TPU v7x, 32 devices: a whole 2x2x4 slice. The times are simulated.
32 devices in a mesh: gx: 4 (over y, x), gy: 2 (over core), ga: 4 (over z).
Axes of the slice: x: 2, y: 2, z: 4, core: 2. Of those that a mesh axis runs over, the one named last changes fastest.
Arguments:
- mixture_fields_initial: float32 [16, 64, 64, 128], P(None, 'gx', ('gy', 'ga')), may hold values from 0 to 1
- flow_speed_vector: float32 [3, 64, 64, 128], P(None, 'gx', ('gy', 'ga')), may hold values from -2 to 2
- thermal_field: float32 [64, 64, 128], P('gx', ('gy', 'ga')), may hold values from 1 to 3
- mass_diffusivity: float32 [16], replicated, may hold values from 0.05 to 0.3
- arrhenius_constant: float32 [16], replicated, may hold values from 0.3 to 3
- arrhenius_energy_temp: float32 [16], replicated, may hold values from 0.5 to 4
- production_coefficients: float32 [16, 16], replicated, may hold values from -1.5 to 1.5
- tucker_factor_east: float32 [64, 64], P('gx'), may hold values from -1 to 1, as said below
- tucker_factor_north: float32 [64, 64], P(('gy', 'ga')), may hold values from -1 to 1, as said below
- tucker_factor_vertical: float32 [128, 32], replicated, may hold values from -1 to 1, as said below
- tucker_factor_component: float32 [16, 8], replicated, may hold values from -1 to 1, as said below
Outputs:
- mixture_fields_final: float32 [16, 64, 64, 128], P(None, 'gx', ('gy', 'ga'))
- residual: float32 [16, 64, 64, 128], P(None, 'gx', ('gy', 'ga'))
- tucker_core: float32 [8, 64, 64, 32], P(None, 'gx', ('gy', 'ga'))
Inputs may be any that keep to these rules, and one draw needn't show every extreme that they name: tucker_factor_east has orthonormal columns. tucker_factor_north has orthonormal columns. tucker_factor_vertical has orthonormal columns. tucker_factor_component has orthonormal columns.
All inputs are finite; a program needn't handle non-finite values.
Results may differ from a plain program's by a relative error of at most 0.0001.
Values sent between devices are 32-bit elements; how exact they have to be, the bound alone decides.
No kernel may reach another device: no remote copies, remote signals or barrier semaphores. Data moves between devices by JAX's collectives and lax.ppermute only.
A program may use at most 64 MiB of HBM per device.

v0:
```python
import jax
import jax.numpy as jnp
from jax import lax
from jax.sharding import PartitionSpec as P

SUB = 2


time_step = 0.5


def padded_2(block, sides, width):
    for axis, dim in sides:
        count = lax.axis_size(axis)
        forward = [(i, i + 1) for i in range(count - 1)]
        backward = [(target, source) for source, target in forward]
        low = lax.ppermute(
            lax.slice_in_dim(block, block.shape[dim] - width, None, axis=dim), axis, forward
        )
        high = lax.ppermute(lax.slice_in_dim(block, 0, width, axis=dim), axis, backward)
        block = jnp.concatenate([low, block, high], axis=dim)
    return block


def advance_solution(
    tensor_elements,
    flow_speed_vector,
    thermal_field,
    mass_diffusivity,
    arrhenius_constant,
    arrhenius_energy_temp,
    production_coefficients,
):
    padded = padded_2(tensor_elements, (("gx", 1), (("gy", "ga"), 2)), 1)
    x_plus = padded[:, 2:, 1:-1, :]
    x_minus = padded[:, :-2, 1:-1, :]
    y_plus = padded[:, 1:-1, 2:, :]
    y_minus = padded[:, 1:-1, :-2, :]
    zero_layer = jnp.zeros_like(tensor_elements[..., :1])
    z_plus = jnp.concatenate([tensor_elements[..., 1:], zero_layer], axis=3)
    z_minus = jnp.concatenate([zero_layer, tensor_elements[..., :-1]], axis=3)
    laplace = x_plus + x_minus + y_plus + y_minus + z_plus + z_minus - 6.0 * tensor_elements
    advect = 0.5 * (
        flow_speed_vector[0] * (x_plus - x_minus)
        + flow_speed_vector[1] * (y_plus - y_minus)
        + flow_speed_vector[2] * (z_plus - z_minus)
    )
    swap_neighbour_halo = jnp.concatenate([tensor_elements[1:], tensor_elements[:1]], axis=0)
    reaction_source_terms = (
        arrhenius_constant[:, None, None, None]
        * jnp.exp(-arrhenius_energy_temp[:, None, None, None] / thermal_field)
        * tensor_elements
        * swap_neighbour_halo
    )
    produced = jnp.einsum(
        "sk,kxyz->sxyz",
        production_coefficients,
        reaction_source_terms,
        precision=lax.Precision.HIGHEST,
    )
    return tensor_elements + time_step * (
        mass_diffusivity[:, None, None, None] * laplace - advect + produced
    )


def compress(
    mixture_snapshot_record,
    tucker_factor_east,
    tucker_factor_north,
    tucker_factor_vertical,
    tucker_factor_component,
):
    highest = lax.Precision.HIGHEST
    projected = jnp.einsum(
        "sxyz,sa->axyz", mixture_snapshot_record, tucker_factor_component, precision=highest
    )
    partial_value = jnp.einsum(
        "axyz,zd->axyd", projected, tucker_factor_vertical, precision=highest
    )
    partial_value = jnp.einsum(
        "axyd,yc->axcd", partial_value, tucker_factor_north, precision=highest
    )
    partial_value = lax.psum_scatter(partial_value, ("gy", "ga"), scatter_dimension=2, tiled=True)
    partial_value = jnp.einsum(
        "axcd,xb->abcd", partial_value, tucker_factor_east, precision=highest
    )
    core_block = lax.psum_scatter(partial_value, "gx", scatter_dimension=1, tiled=True)
    return core_block


def expand(
    core_block,
    tucker_factor_east,
    tucker_factor_north,
    tucker_factor_vertical,
    tucker_factor_component,
):
    highest = lax.Precision.HIGHEST
    columns = tucker_factor_east
    expanded = jnp.einsum(
        "abcd,xb->axcd",
        lax.all_gather(core_block, "gx", axis=1, tiled=True),
        columns,
        precision=highest,
    )
    columns = tucker_factor_north
    expanded = jnp.einsum(
        "axcd,yc->axyd",
        lax.all_gather(expanded, ("gy", "ga"), axis=2, tiled=True),
        columns,
        precision=highest,
    )
    expanded = jnp.einsum("axyd,zd->axyz", expanded, tucker_factor_vertical, precision=highest)
    return jnp.einsum("axyz,sa->sxyz", expanded, tucker_factor_component, precision=highest)


def body(
    mixture_fields_initial,
    flow_speed_vector,
    thermal_field,
    mass_diffusivity,
    arrhenius_constant,
    arrhenius_energy_temp,
    production_coefficients,
    tucker_factor_east,
    tucker_factor_north,
    tucker_factor_vertical,
    tucker_factor_component,
):
    mixture_snapshot_record = mixture_fields_initial
    for substep in range(SUB):
        mixture_snapshot_record = advance_solution(
            mixture_snapshot_record,
            flow_speed_vector,
            thermal_field,
            mass_diffusivity,
            arrhenius_constant,
            arrhenius_energy_temp,
            production_coefficients,
        )
    tucker_core = compress(
        mixture_snapshot_record,
        tucker_factor_east,
        tucker_factor_north,
        tucker_factor_vertical,
        tucker_factor_component,
    )
    residual = mixture_snapshot_record - expand(
        tucker_core,
        tucker_factor_east,
        tucker_factor_north,
        tucker_factor_vertical,
        tucker_factor_component,
    )
    mixture_fields_final = mixture_snapshot_record
    for substep in range(SUB):
        mixture_fields_final = advance_solution(
            mixture_fields_final,
            flow_speed_vector,
            thermal_field,
            mass_diffusivity,
            arrhenius_constant,
            arrhenius_energy_temp,
            production_coefficients,
        )
    return (mixture_fields_final, residual, tucker_core)


def solution(mesh):
    in_specs = (
        P(None, "gx", ("gy", "ga"), None),
        P(None, "gx", ("gy", "ga"), None),
        P("gx", ("gy", "ga"), None),
        P(),
        P(),
        P(),
        P(),
        P("gx", None),
        P(("gy", "ga"), None),
        P(),
        P(),
    )
    out_specs = (
        P(None, "gx", ("gy", "ga"), None),
        P(None, "gx", ("gy", "ga"), None),
        P(None, "gx", ("gy", "ga"), None),
    )
    return jax.shard_map(body, mesh=mesh, in_specs=in_specs, out_specs=out_specs, check_vma=False)
```

profile of v0, /device:TPU:3, one launch (start us, length us, event | category | flops | bytes accessed | tf_op | source)
XLA Modules:
  0.0 237.7 jit_solution(8154288472658362834)
XLA Ops:
  9.1 3.1 %collective-permute-start.1 = (f32[16,1,8,128]{3,0,2,1:T(8,128)S(1)}, f32[16,1,8,128]{3,0,2,1:T(8,128)S(1)}, u32[]{:S(2)}, u32[]{:S(2)}) collective-permute-start(f32[16,1,8,128]{3,0,2,1:T(8,128)S(1)} %get-tuple-element.33), channel_id=1, source_target_pairs={{0,8},{8,16},{16,24},{1,9},{9,17},{17,25},{2,10},{10,18},{18,26},{... | collective-permute-start | bytes 196616 | tf_op jit(solution)/shard_map/ppermute | solution.py:17
  18.2 7.2 %collective-permute-start.2 = (f32[16,18,1,128]{3,0,2,1:T(8,128)S(1)}, f32[16,18,1,128]{3,0,2,1:T(8,128)S(1)}, u32[]{:S(2)}, u32[]{:S(2)}) collective-permute-start(f32[16,18,1,128]{3,0,2,1:T(8,128)S(1)} %get-tuple-element.18), channel_id=1, source_target_pairs={{1,0},{2,1},{3,2},{4,3},{5,4},{6,5},{7,6},{9,8},{10,9},{11,10},{12... | collective-permute-start | bytes 442376 | tf_op jit(solution)/shard_map/ppermute | solution.py:20
  28.1 5.5 %collective-permute-done.3 = f32[16,18,1,128]{3,0,2,1:T(8,128)S(1)} collective-permute-done((f32[16,18,1,128]{3,0,2,1:T(8,128)S(1)}, f32[16,18,1,128]{3,0,2,1:T(8,128)S(1)}, u32[]{:S(2)}, u32[]{:S(2)}) %collective-permute-start.3) | collective-permute-done | bytes 147488 | tf_op jit(solution)/shard_map/ppermute | solution.py:17
  37.6 4.3 %collective-permute-start.5 = (f32[16,1,8,128]{3,0,2,1:T(8,128)S(1)}, f32[16,1,8,128]{3,0,2,1:T(8,128)S(1)}, u32[]{:S(2)}, u32[]{:S(2)}) collective-permute-start(f32[16,1,8,128]{3,0,2,1:T(8,128)S(1)} %get-tuple-element.28), channel_id=1, source_target_pairs={{0,8},{8,16},{16,24},{1,9},{9,17},{17,25},{2,10},{10,18},{18,26},{... | collective-permute-start | bytes 196616 | tf_op jit(solution)/shard_map/ppermute | solution.py:17
  43.2 2.9 %collective-permute-start.6 = (f32[16,18,1,128]{3,0,2,1:T(8,128)S(1)}, f32[16,18,1,128]{3,0,2,1:T(8,128)S(1)}, u32[]{:S(2)}, u32[]{:S(2)}) collective-permute-start(f32[16,18,1,128]{3,0,2,1:T(8,128)S(1)} %get-tuple-element.16), channel_id=1, source_target_pairs={{1,0},{2,1},{3,2},{4,3},{5,4},{6,5},{7,6},{9,8},{10,9},{11,10},{12... | collective-permute-start | bytes 442376 | tf_op jit(solution)/shard_map/ppermute | solution.py:20
  46.1 2.6 %collective-permute-start.7 = (f32[16,18,1,128]{3,0,2,1:T(8,128)S(1)}, f32[16,18,1,128]{3,0,2,1:T(8,128)S(1)}, u32[]{:S(2)}, u32[]{:S(2)}) collective-permute-start(f32[16,18,1,128]{3,0,2,1:T(8,128)S(1)} %get-tuple-element.17), channel_id=1, source_target_pairs={{0,1},{1,2},{2,3},{3,4},{4,5},{5,6},{6,7},{8,9},{9,10},{10,11},{11... | collective-permute-start | bytes 442376 | tf_op jit(solution)/shard_map/ppermute | solution.py:17
  49.4 5.0 %collective-permute-done.7 = f32[16,18,1,128]{3,0,2,1:T(8,128)S(1)} collective-permute-done((f32[16,18,1,128]{3,0,2,1:T(8,128)S(1)}, f32[16,18,1,128]{3,0,2,1:T(8,128)S(1)}, u32[]{:S(2)}, u32[]{:S(2)}) %collective-permute-start.7) | collective-permute-done | bytes 147488 | tf_op jit(solution)/shard_map/ppermute | solution.py:17
  57.7 3.5 %convolution_bitcast_fusion = f32[8,16,64,32]{2,3,1,0:T(8,128)S(1)} fusion(f32[8,16,8,32]{3,2,1,0:T(8,128)S(1)} %fusion.39, f32[8,64]{1,0:T(8,128)S(1)} %copy-done.6), kind=kOutput, calls=%fused_computation.4 | convolution fusion | flops 25165824 | bytes 1181696 | tf_op jit(solution)/shard_map/axyd,yc->axcd/dot_general | solution.py:80
  61.2 4.6 %copy.75 = f32[8,16,64,32]{3,1,0,2:T(8,128)} copy(f32[8,16,64,32]{2,3,1,0:T(8,128)S(1)} %convolution_bitcast_fusion) | data formatting | bytes 2097152
  65.7 4.3 %reshape.16 = f32[64,4096]{1,0:T(8,128)} reshape(f32[64,8,16,32]{3,2,1,0:T(8,128)} %bitcast.104) | data formatting | bytes 2097152
  70.4 34.7 %reduce-scatter.7.cloned.1.call-done = f32[8,4096]{1,0:T(8,128)} async-done(((f32[64,4096]{1,0:T(8,128)}), f32[8,4096]{1,0:T(8,128)}) %reduce-scatter.7.cloned.1.call-update) | async-done | bytes 131088
  108.0 2.8 %copy.59 = f32[8,64,8,32]{3,2,0,1:T(8,128)} copy(f32[8,64,8,32]{1,3,2,0:T(8,128)S(1)} %convolution_bitcast_fusion.2) | data formatting | bytes 1048576 | tf_op jit(solution)/shard_map/axcd,xb->abcd/transpose | solution.py:84
  112.9 4.2 %collective-permute-start.9 = (f32[16,1,8,128]{3,0,2,1:T(8,128)S(1)}, f32[16,1,8,128]{3,0,2,1:T(8,128)S(1)}, u32[]{:S(2)}, u32[]{:S(2)}) collective-permute-start(f32[16,1,8,128]{3,0,2,1:T(8,128)S(1)} %get-tuple-element.24), channel_id=1, source_target_pairs={{0,8},{8,16},{16,24},{1,9},{9,17},{17,25},{2,10},{10,18},{18,26},{... | collective-permute-start | bytes 196616 | tf_op jit(solution)/shard_map/ppermute | solution.py:17
  117.4 2.5 %collective-permute-done.9 = f32[16,1,8,128]{3,0,2,1:T(8,128)S(1)} collective-permute-done((f32[16,1,8,128]{3,0,2,1:T(8,128)S(1)}, f32[16,1,8,128]{3,0,2,1:T(8,128)S(1)}, u32[]{:S(2)}, u32[]{:S(2)}) %collective-permute-start.9) | collective-permute-done | bytes 65568 | tf_op jit(solution)/shard_map/ppermute | solution.py:17
  119.9 3.7 %collective-permute-start.10 = (f32[16,18,1,128]{3,0,2,1:T(8,128)S(1)}, f32[16,18,1,128]{3,0,2,1:T(8,128)S(1)}, u32[]{:S(2)}, u32[]{:S(2)}) collective-permute-start(f32[16,18,1,128]{3,0,2,1:T(8,128)S(1)} %get-tuple-element.14), channel_id=1, source_target_pairs={{1,0},{2,1},{3,2},{4,3},{5,4},{6,5},{7,6},{9,8},{10,9},{11,10},{12... | collective-permute-start | bytes 442376 | tf_op jit(solution)/shard_map/ppermute | solution.py:20
  125.6 19.3 %reduce-scatter.5.cloned.1.call-done = f32[8,16,8,32]{3,2,0,1:T(8,128)} async-done(((f32[8,64,8,32]{3,2,0,1:T(8,128)}), f32[8,16,8,32]{3,2,0,1:T(8,128)}) %reduce-scatter.5.cloned.1.call-update) | async-done | bytes 131088 | tf_op jit(solution)/shard_map/reduce_scatter | solution.py:87
  144.9 20.9 %all_gather.6 = f32[8,64,8,32]{3,2,0,1:T(8,128)S(1)} all-gather(f32[8,16,8,32]{3,2,0,1:T(8,128)} %reduce-scatter.5.cloned.1.call-done), channel_id=1, replica_groups=mesh['gx'=4,'gy'=2,'ga'=4] {'gx'}, dimensions={1}, use_global_device_ids=true | all-gather | bytes 655360 | tf_op jit(solution)/shard_map/all_gather | solution.py:102
  165.7 3.2 %fusion.17 = f32[8,16,8,32]{3,1,2,0:T(8,128)} fusion(f32[8,64,8,32]{3,2,0,1:T(8,128)S(1)} %all_gather.6, f32[16,64]{1,0:T(8,128)S(1)} %copy-done.4), kind=kOutput, calls=%fused_computation.24 | convolution fusion | flops 25165824 | bytes 659456 | tf_op jit(solution)/shard_map/abcd,xb->axcd/dot_general | solution.py:100
  173.4 4.3 %collective-permute-start.13 = (f32[16,1,8,128]{3,0,2,1:T(8,128)S(1)}, f32[16,1,8,128]{3,0,2,1:T(8,128)S(1)}, u32[]{:S(2)}, u32[]{:S(2)}) collective-permute-start(f32[16,1,8,128]{3,0,2,1:T(8,128)S(1)} %get-tuple-element.20), channel_id=1, source_target_pairs={{0,8},{8,16},{16,24},{1,9},{9,17},{17,25},{2,10},{10,18},{18,26},{... | collective-permute-start | bytes 196616 | tf_op jit(solution)/shard_map/ppermute | solution.py:17
  179.0 7.8 %collective-permute-start.14 = (f32[16,18,1,128]{3,0,2,1:T(8,128)S(1)}, f32[16,18,1,128]{3,0,2,1:T(8,128)S(1)}, u32[]{:S(2)}, u32[]{:S(2)}) collective-permute-start(f32[16,18,1,128]{3,0,2,1:T(8,128)S(1)} %get-tuple-element.12), channel_id=1, source_target_pairs={{1,0},{2,1},{3,2},{4,3},{5,4},{6,5},{7,6},{9,8},{10,9},{11,10},{12... | collective-permute-start | bytes 442376 | tf_op jit(solution)/shard_map/ppermute | solution.py:20
  189.5 3.7 %collective-permute-done.14 = f32[16,18,1,128]{3,0,2,1:T(8,128)S(1)} collective-permute-done((f32[16,18,1,128]{3,0,2,1:T(8,128)S(1)}, f32[16,18,1,128]{3,0,2,1:T(8,128)S(1)}, u32[]{:S(2)}, u32[]{:S(2)}) %collective-permute-start.14) | collective-permute-done | bytes 147488 | tf_op jit(solution)/shard_map/ppermute | solution.py:20
  193.2 5.3 %collective-permute-done.15 = f32[16,18,1,128]{3,0,2,1:T(8,128)S(1)} collective-permute-done((f32[16,18,1,128]{3,0,2,1:T(8,128)S(1)}, f32[16,18,1,128]{3,0,2,1:T(8,128)S(1)}, u32[]{:S(2)}, u32[]{:S(2)}) %collective-permute-start.15) | collective-permute-done | bytes 147488 | tf_op jit(solution)/shard_map/ppermute | solution.py:17
  202.7 19.7 %all-gather.2.cloned.1.call-done = f32[8,16,64,32]{3,1,2,0:T(8,128)} async-done(((f32[8,16,8,32]{3,1,2,0:T(8,128)}), f32[8,16,64,32]{3,1,2,0:T(8,128)}) %all-gather.2.cloned.1.call-update) | async-done | bytes 1048592 | tf_op jit(solution)/shard_map/all_gather | solution.py:109
  222.4 5.5 %fusion.20 = f32[8,16,8,32]{3,2,1,0:T(8,128)S(1)} fusion(f32[8,16,64,32]{3,1,2,0:T(8,128)} %all-gather.2.cloned.1.call-done, f32[8,64]{1,0:T(8,128)S(1)} %copy-done.6), kind=kOutput, calls=%fused_computation.25 | convolution fusion | flops 25165824 | bytes 1181696 | tf_op jit(solution)/shard_map/axcd,yc->axyd/dot_general | solution.py:107
  (88 shorter events, 42.8 us)
Async XLA Ops:
  7.2 50.0 %copy-start = (f32[128,32]{0,1:T(8,128)S(1)}, f32[128,32]{0,1:T(8,128)}, u32[]{:S(2)}) copy-start(f32[128,32]{0,1:T(8,128)} %param.20) | copy-start | bytes 49156
  7.2 97.9 %reduce-scatter.7.cloned.1.call-start = ((), (), s32[]{:S(2)}) async-start(), calls=%async_computation.4 | async-start | bytes 1179648
  9.1 6.3 %collective-permute-start.1 = (f32[16,1,8,128]{3,0,2,1:T(8,128)S(1)}, f32[16,1,8,128]{3,0,2,1:T(8,128)S(1)}, u32[]{:S(2)}, u32[]{:S(2)}) collective-permute-start(f32[16,1,8,128]{3,0,2,1:T(8,128)S(1)} %get-tuple-element.33), channel_id=1, source_target_pairs={{0,8},{8,16},{16,24},{1,9},{9,17},{17,25},{2,10},{10,18},{18,26},{... | collective-permute-start | bytes 196616 | tf_op jit(solution)/shard_map/ppermute | solution.py:17
  12.2 5.9 %collective-permute-start = (f32[16,1,8,128]{3,0,2,1:T(8,128)S(1)}, f32[16,1,8,128]{3,0,2,1:T(8,128)S(1)}, u32[]{:S(2)}, u32[]{:S(2)}) collective-permute-start(f32[16,1,8,128]{3,0,2,1:T(8,128)S(1)} %get-tuple-element.32), channel_id=1, source_target_pairs={{8,0},{16,8},{24,16},{9,1},{17,9},{25,17},{10,2},{18,10},{26,18},{... | collective-permute-start | bytes 196616 | tf_op jit(solution)/shard_map/ppermute | solution.py:20
  14.9 18.8 %slice-start = ((f32[16,16,8,128]{3,2,1,0:T(8,128)}), f32[1,16,8,128]{3,2,1,0:T(8,128)S(1)}, s32[]{:S(2)}) async-start(f32[16,16,8,128]{3,2,1,0:T(8,128)} %param.11), calls=%async_computation.5 | async-start | bytes 131072 | tf_op jit(solution)/shard_map/slice | solution.py:48
  14.9 18.8 %copy-start.7 = (f32[16,8,128]{2,1,0:T(8,128)S(1)}, f32[16,8,128]{2,1,0:T(8,128)}, u32[]{:S(2)}) copy-start(f32[16,8,128]{2,1,0:T(8,128)} %param.13) | copy-start | bytes 196612
  14.9 18.7 %copy-start.8 = (f32[16,16]{1,0:T(8,128)S(1)}, f32[16,16]{1,0:T(8,128)}, u32[]{:S(2)}) copy-start(f32[16,16]{1,0:T(8,128)} %param.17) | copy-start | bytes 3076
  18.2 10.0 %collective-permute-start.2 = (f32[16,18,1,128]{3,0,2,1:T(8,128)S(1)}, f32[16,18,1,128]{3,0,2,1:T(8,128)S(1)}, u32[]{:S(2)}, u32[]{:S(2)}) collective-permute-start(f32[16,18,1,128]{3,0,2,1:T(8,128)S(1)} %get-tuple-element.18), channel_id=1, source_target_pairs={{1,0},{2,1},{3,2},{4,3},{5,4},{6,5},{7,6},{9,8},{10,9},{11,10},{12... | collective-permute-start | bytes 442376 | tf_op jit(solution)/shard_map/ppermute | solution.py:20
  25.4 8.3 %collective-permute-start.3 = (f32[16,18,1,128]{3,0,2,1:T(8,128)S(1)}, f32[16,18,1,128]{3,0,2,1:T(8,128)S(1)}, u32[]{:S(2)}, u32[]{:S(2)}) collective-permute-start(f32[16,18,1,128]{3,0,2,1:T(8,128)S(1)} %get-tuple-element.19), channel_id=1, source_target_pairs={{0,1},{1,2},{2,3},{3,4},{4,5},{5,6},{6,7},{8,9},{9,10},{10,11},{11... | collective-permute-start | bytes 442376 | tf_op jit(solution)/shard_map/ppermute | solution.py:17
  35.7 6.2 %collective-permute-start.4 = (f32[16,1,8,128]{3,0,2,1:T(8,128)S(1)}, f32[16,1,8,128]{3,0,2,1:T(8,128)S(1)}, u32[]{:S(2)}, u32[]{:S(2)}) collective-permute-start(f32[16,1,8,128]{3,0,2,1:T(8,128)S(1)} %get-tuple-element.29), channel_id=1, source_target_pairs={{8,0},{16,8},{24,16},{9,1},{17,9},{25,17},{10,2},{18,10},{26,18},{... | collective-permute-start | bytes 196616 | tf_op jit(solution)/shard_map/ppermute | solution.py:20
  37.6 5.6 %collective-permute-start.5 = (f32[16,1,8,128]{3,0,2,1:T(8,128)S(1)}, f32[16,1,8,128]{3,0,2,1:T(8,128)S(1)}, u32[]{:S(2)}, u32[]{:S(2)}) collective-permute-start(f32[16,1,8,128]{3,0,2,1:T(8,128)S(1)} %get-tuple-element.28), channel_id=1, source_target_pairs={{0,8},{8,16},{16,24},{1,9},{9,17},{17,25},{2,10},{10,18},{18,26},{... | collective-permute-start | bytes 196616 | tf_op jit(solution)/shard_map/ppermute | solution.py:17
  43.2 6.2 %collective-permute-start.6 = (f32[16,18,1,128]{3,0,2,1:T(8,128)S(1)}, f32[16,18,1,128]{3,0,2,1:T(8,128)S(1)}, u32[]{:S(2)}, u32[]{:S(2)}) collective-permute-start(f32[16,18,1,128]{3,0,2,1:T(8,128)S(1)} %get-tuple-element.16), channel_id=1, source_target_pairs={{1,0},{2,1},{3,2},{4,3},{5,4},{6,5},{7,6},{9,8},{10,9},{11,10},{12... | collective-permute-start | bytes 442376 | tf_op jit(solution)/shard_map/ppermute | solution.py:20
  46.1 8.3 %collective-permute-start.7 = (f32[16,18,1,128]{3,0,2,1:T(8,128)S(1)}, f32[16,18,1,128]{3,0,2,1:T(8,128)S(1)}, u32[]{:S(2)}, u32[]{:S(2)}) collective-permute-start(f32[16,18,1,128]{3,0,2,1:T(8,128)S(1)} %get-tuple-element.17), channel_id=1, source_target_pairs={{0,1},{1,2},{2,3},{3,4},{4,5},{5,6},{6,7},{8,9},{9,10},{10,11},{11... | collective-permute-start | bytes 442376 | tf_op jit(solution)/shard_map/ppermute | solution.py:17
  65.7 40.4 %copy-start.4 = (f32[16,64]{1,0:T(8,128)S(1)}, f32[16,64]{1,0:T(8,128)}, u32[]{:S(2)}) copy-start(f32[16,64]{1,0:T(8,128)} %param.18) | copy-start | bytes 12292
  70.1 74.8 %reduce-scatter.5.cloned.1.call-start = ((), (), s32[]{:S(2)}) async-start(), calls=%async_computation.2 | async-start | bytes 2621440 | tf_op jit(solution)/shard_map/reduce_scatter | solution.py:87
  110.8 111.6 %all-gather.2.cloned.1.call-start = ((), (), s32[]{:S(2)}) async-start(), calls=%async_computation.3 | async-start | bytes 4718592 | tf_op jit(solution)/shard_map/all_gather | solution.py:109
  110.9 6.4 %collective-permute-start.8 = (f32[16,1,8,128]{3,0,2,1:T(8,128)S(1)}, f32[16,1,8,128]{3,0,2,1:T(8,128)S(1)}, u32[]{:S(2)}, u32[]{:S(2)}) collective-permute-start(f32[16,1,8,128]{3,0,2,1:T(8,128)S(1)} %get-tuple-element.25), channel_id=1, source_target_pairs={{8,0},{16,8},{24,16},{9,1},{17,9},{25,17},{10,2},{18,10},{26,18},{... | collective-permute-start | bytes 196616 | tf_op jit(solution)/shard_map/ppermute | solution.py:20
  112.9 7.0 %collective-permute-start.9 = (f32[16,1,8,128]{3,0,2,1:T(8,128)S(1)}, f32[16,1,8,128]{3,0,2,1:T(8,128)S(1)}, u32[]{:S(2)}, u32[]{:S(2)}) collective-permute-start(f32[16,1,8,128]{3,0,2,1:T(8,128)S(1)} %get-tuple-element.24), channel_id=1, source_target_pairs={{0,8},{8,16},{16,24},{1,9},{9,17},{17,25},{2,10},{10,18},{18,26},{... | collective-permute-start | bytes 196616 | tf_op jit(solution)/shard_map/ppermute | solution.py:17
  119.9 49.6 %collective-permute-start.10 = (f32[16,18,1,128]{3,0,2,1:T(8,128)S(1)}, f32[16,18,1,128]{3,0,2,1:T(8,128)S(1)}, u32[]{:S(2)}, u32[]{:S(2)}) collective-permute-start(f32[16,18,1,128]{3,0,2,1:T(8,128)S(1)} %get-tuple-element.14), channel_id=1, source_target_pairs={{1,0},{2,1},{3,2},{4,3},{5,4},{6,5},{7,6},{9,8},{10,9},{11,10},{12... | collective-permute-start | bytes 442376 | tf_op jit(solution)/shard_map/ppermute | solution.py:20
  123.6 45.8 %collective-permute-start.11 = (f32[16,18,1,128]{3,0,2,1:T(8,128)S(1)}, f32[16,18,1,128]{3,0,2,1:T(8,128)S(1)}, u32[]{:S(2)}, u32[]{:S(2)}) collective-permute-start(f32[16,18,1,128]{3,0,2,1:T(8,128)S(1)} %get-tuple-element.15), channel_id=1, source_target_pairs={{0,1},{1,2},{2,3},{3,4},{4,5},{5,6},{6,7},{8,9},{9,10},{10,11},{11... | collective-permute-start | bytes 442376 | tf_op jit(solution)/shard_map/ppermute | solution.py:17
  171.5 6.2 %collective-permute-start.12 = (f32[16,1,8,128]{3,0,2,1:T(8,128)S(1)}, f32[16,1,8,128]{3,0,2,1:T(8,128)S(1)}, u32[]{:S(2)}, u32[]{:S(2)}) collective-permute-start(f32[16,1,8,128]{3,0,2,1:T(8,128)S(1)} %get-tuple-element.21), channel_id=1, source_target_pairs={{8,0},{16,8},{24,16},{9,1},{17,9},{25,17},{10,2},{18,10},{26,18},{... | collective-permute-start | bytes 196616 | tf_op jit(solution)/shard_map/ppermute | solution.py:20
  173.4 5.6 %collective-permute-start.13 = (f32[16,1,8,128]{3,0,2,1:T(8,128)S(1)}, f32[16,1,8,128]{3,0,2,1:T(8,128)S(1)}, u32[]{:S(2)}, u32[]{:S(2)}) collective-permute-start(f32[16,1,8,128]{3,0,2,1:T(8,128)S(1)} %get-tuple-element.20), channel_id=1, source_target_pairs={{0,8},{8,16},{16,24},{1,9},{9,17},{17,25},{2,10},{10,18},{18,26},{... | collective-permute-start | bytes 196616 | tf_op jit(solution)/shard_map/ppermute | solution.py:17
  179.0 14.2 %collective-permute-start.14 = (f32[16,18,1,128]{3,0,2,1:T(8,128)S(1)}, f32[16,18,1,128]{3,0,2,1:T(8,128)S(1)}, u32[]{:S(2)}, u32[]{:S(2)}) collective-permute-start(f32[16,18,1,128]{3,0,2,1:T(8,128)S(1)} %get-tuple-element.12), channel_id=1, source_target_pairs={{1,0},{2,1},{3,2},{4,3},{5,4},{6,5},{7,6},{9,8},{10,9},{11,10},{12... | collective-permute-start | bytes 442376 | tf_op jit(solution)/shard_map/ppermute | solution.py:20
  186.8 11.7 %collective-permute-start.15 = (f32[16,18,1,128]{3,0,2,1:T(8,128)S(1)}, f32[16,18,1,128]{3,0,2,1:T(8,128)S(1)}, u32[]{:S(2)}, u32[]{:S(2)}) collective-permute-start(f32[16,18,1,128]{3,0,2,1:T(8,128)S(1)} %get-tuple-element.13), channel_id=1, source_target_pairs={{0,1},{1,2},{2,3},{3,4},{4,5},{5,6},{6,7},{8,9},{9,10},{10,11},{11... | collective-permute-start | bytes 442376 | tf_op jit(solution)/shard_map/ppermute | solution.py:17
  (8 other events, 56.5 us)
Sparse Core Ops, SparseCore 0:
  70.2 34.7 reduce-scatter.6
  111.0 33.8 reduce-scatter.4
  169.0 53.3 all-gather.1
where the time goes:
time: 239 us; the launch traced here: 238 us
  waiting for transfers between devices  101 us (42%)
  starting transfers between devices  54.4 us (23%)
  matrix products  25.1 us (11%)
  local copies, waits for them, and re-layouts  21.8 us (9%)
  blocking collectives  20.9 us (9%)
  between operations  14.3 us (6%)
    unnamed x4, waiting for transfers between devices  34.7 us
    ppermute x8, starting transfers between devices, padded_2(): lax.ppermute(lax.slice_in_dim(block, 0, width, axis=dim), axis, backward)  29.6 us
    ppermute x8, starting transfers between devices, padded_2(): lax.ppermute(lax.slice_in_dim(block, block.shape[dim] - width, None, axis...  24.5 us
    ppermute x8, waiting for transfers between devices, padded_2(): lax.ppermute(lax.slice_in_dim(block, block.shape[dim] - width, None, axis...  20.9 us
    all_gather x1, blocking collectives, expand(): lax.all_gather(core_block, 'gx', axis=1, tiled=True)  20.9 us
    all_gather x1, waiting for transfers between devices, expand(): lax.all_gather(expanded, ('gy', 'ga'), axis=2, tiled=True)  19.7 us
    reduce_scatter x1, waiting for transfers between devices, compress(): lax.psum_scatter(partial_value, 'gx', scatter_dimension=1, tiled=True)  19.3 us
    unnamed x33, local copies, waits for them, and re-layouts  16.9 us
  transfers between devices with their start and end apart: 19, of which 14 were waited for; matrix products, arithmetic and copies ran while one was open for 5% of the time, Pallas kernels for 0%

commit v1 on v0

v1 whole, which is shorter than its diff:
```python
import jax
import jax.numpy as jnp
from jax import lax
from jax.sharding import PartitionSpec as P

SUB = 2


time_step = 0.5

ROW = "gx"
COLUMN = ("gy", "ga")
EVERY = ("gx", "gy", "ga")


def faces_beside(low_face, high_face, axes):
    count = lax.axis_size(axes)
    even = lax.axis_index(axes) % 2 == 0

    def swapped(face, first):
        couples = [(i, i + 1) for i in range(first, count - 1, 2)]
        return lax.ppermute(face, axes, couples + [(b, a) for a, b in couples])

    one = swapped(jnp.where(even, high_face, low_face), 0)
    other = swapped(jnp.where(even, low_face, high_face), 1)
    return jnp.where(even, other, one), jnp.where(even, one, other)


def advance_solution(
    tensor_elements,
    flow_speed_vector,
    thermal_field,
    mass_diffusivity,
    arrhenius_constant,
    arrhenius_energy_temp,
    production_coefficients,
):
    y_before, y_after = faces_beside(
        tensor_elements[:, :, :1], tensor_elements[:, :, -1:], COLUMN
    )
    x_before, x_after = faces_beside(tensor_elements[:, :1], tensor_elements[:, -1:], ROW)
    x_plus = jnp.concatenate([tensor_elements[:, 1:], x_after], axis=1)
    x_minus = jnp.concatenate([x_before, tensor_elements[:, :-1]], axis=1)
    y_plus = jnp.concatenate([tensor_elements[:, :, 1:], y_after], axis=2)
    y_minus = jnp.concatenate([y_before, tensor_elements[:, :, :-1]], axis=2)
    zero_layer = jnp.zeros_like(tensor_elements[..., :1])
    z_plus = jnp.concatenate([tensor_elements[..., 1:], zero_layer], axis=3)
    z_minus = jnp.concatenate([zero_layer, tensor_elements[..., :-1]], axis=3)
    laplace = x_plus + x_minus + y_plus + y_minus + z_plus + z_minus - 6.0 * tensor_elements
    advect = 0.5 * (
        flow_speed_vector[0] * (x_plus - x_minus)
        + flow_speed_vector[1] * (y_plus - y_minus)
        + flow_speed_vector[2] * (z_plus - z_minus)
    )
    swap_neighbour_halo = jnp.concatenate([tensor_elements[1:], tensor_elements[:1]], axis=0)
    reaction_source_terms = (
        arrhenius_constant[:, None, None, None]
        * jnp.exp(-arrhenius_energy_temp[:, None, None, None] / thermal_field)
        * tensor_elements
        * swap_neighbour_halo
    )
    produced = jnp.einsum(
        "sk,kxyz->sxyz",
        production_coefficients,
        reaction_source_terms,
        precision=lax.Precision.HIGHEST,
    )
    return tensor_elements + time_step * (
        mass_diffusivity[:, None, None, None] * laplace - advect + produced
    )


def whole_factors(tucker_factor_east, tucker_factor_north):
    rows, columns = lax.axis_size(ROW), lax.axis_size(COLUMN)

    def shares(factor, holders, axes):
        count = -(-factor.shape[0] // holders)
        padded = jnp.pad(factor, ((0, count * holders - factor.shape[0]), (0, 0)))
        return lax.dynamic_slice_in_dim(padded, lax.axis_index(axes) * count, count, 0)

    east = shares(tucker_factor_east, columns, COLUMN)
    north = shares(tucker_factor_north, rows, ROW)
    sent = jnp.concatenate([east.reshape(-1), north.reshape(-1)])
    sent = jnp.pad(sent, (0, -sent.size % 128)).reshape(1, -1, 128)
    sent = jnp.broadcast_to(sent, (rows * columns,) + sent.shape[1:])
    got = lax.all_to_all(sent, EVERY, 0, 0, tiled=True).reshape(rows, columns, -1)
    whole_east = got[:, :, : east.size].reshape(rows, -1, east.shape[1])
    whole_east = whole_east[:, : tucker_factor_east.shape[0]].reshape(-1, east.shape[1])
    whole_north = got[:, :, east.size : east.size + north.size]
    whole_north = whole_north.reshape(rows, columns, *north.shape).transpose(1, 0, 2, 3)
    whole_north = whole_north.reshape(columns, -1, north.shape[1])
    whole_north = whole_north[:, : tucker_factor_north.shape[0]].reshape(-1, north.shape[1])
    return whole_east, whole_north


def compress_and_expand(
    snapshot,
    east,
    north,
    tucker_factor_vertical,
    tucker_factor_component,
):
    highest = lax.Precision.HIGHEST
    rows, columns = lax.axis_size(ROW), lax.axis_size(COLUMN)
    devices = rows * columns
    (_, wide, deep, _), (_, ranks_a) = snapshot.shape, tucker_factor_component.shape
    ranks_d = tucker_factor_vertical.shape[1]
    ranks_b, ranks_c = east.shape[1], north.shape[1]
    projected = jnp.einsum("sxyz,sa->axyz", snapshot, tucker_factor_component, precision=highest)
    projected = jnp.einsum("axyz,zd->dyxa", projected, tucker_factor_vertical, precision=highest)
    pairs = ranks_a * ranks_d
    share = -(-pairs // devices)
    flat = jnp.transpose(projected, (0, 3, 1, 2)).reshape(pairs, deep, wide)
    flat = jnp.pad(flat, ((0, share * devices - pairs), (0, 0), (0, 0)))
    flat = flat.reshape(devices, share, deep, wide).transpose(0, 2, 3, 1)
    flat = lax.all_to_all(
        flat.reshape(devices, deep, wide * share), EVERY, 0, 0, tiled=True
    )
    whole = flat.reshape(rows, columns * deep, wide, share)
    part = jnp.einsum("gyxp,yc->cgxp", whole, north, precision=highest)
    part = part.reshape(ranks_c, rows * wide, share)
    core = jnp.einsum("cxp,xb->cbp", part, east, precision=highest)
    part = jnp.einsum("cbp,xb->cxp", core, east, precision=highest)
    whole = jnp.einsum("cxp,yc->yxp", part, north, precision=highest)
    own_b, own_c = ranks_b // rows, ranks_c // columns

    def pieces(array, tall, broad):
        array = array.reshape(columns, tall, rows, broad, share)
        return array.transpose(2, 0, 1, 3, 4).reshape(devices, tall * broad * share)

    sent = jnp.concatenate([pieces(core, own_c, own_b), pieces(whole, deep, wide)], axis=1)
    sent = jnp.pad(sent, ((0, 0), (0, -sent.shape[1] % 1024)))
    got = lax.all_to_all(
        sent.reshape(devices, -1, 128), EVERY, 0, 0, tiled=True
    ).reshape(devices, -1)

    def ranks_together(array, tall, broad):
        array = array.reshape(devices, tall, broad, share).transpose(0, 3, 2, 1)
        array = array.reshape(devices * share, broad, tall)[:pairs]
        return array.reshape(ranks_d, ranks_a, broad, tall)

    core_size = own_c * own_b * share
    core = ranks_together(got[:, :core_size], own_c, own_b).transpose(1, 2, 3, 0)
    expanded = ranks_together(got[:, core_size : core_size + deep * wide * share], deep, wide)
    expanded = jnp.einsum("daxy,zd->axyz", expanded, tucker_factor_vertical, precision=highest)
    expanded = jnp.einsum("axyz,sa->sxyz", expanded, tucker_factor_component, precision=highest)
    return core, snapshot - expanded


def body(
    mixture_fields_initial,
    flow_speed_vector,
    thermal_field,
    mass_diffusivity,
    arrhenius_constant,
    arrhenius_energy_temp,
    production_coefficients,
    tucker_factor_east,
    tucker_factor_north,
    tucker_factor_vertical,
    tucker_factor_component,
):
    chemistry = (
        flow_speed_vector,
        thermal_field,
        mass_diffusivity,
        arrhenius_constant,
        arrhenius_energy_temp,
        production_coefficients,
    )
    east, north = whole_factors(tucker_factor_east, tucker_factor_north)
    snapshot = mixture_fields_initial
    for substep in range(SUB):
        snapshot = advance_solution(snapshot, *chemistry)
    tucker_core, residual = compress_and_expand(
        snapshot,
        east,
        north,
        tucker_factor_vertical,
        tucker_factor_component,
    )
    mixture_fields_final = snapshot
    for substep in range(SUB):
        mixture_fields_final = advance_solution(mixture_fields_final, *chemistry)
    return (mixture_fields_final, residual, tucker_core)


def solution(mesh):
    in_specs = (
        P(None, "gx", ("gy", "ga"), None),
        P(None, "gx", ("gy", "ga"), None),
        P("gx", ("gy", "ga"), None),
        P(),
        P(),
        P(),
        P(),
        P("gx", None),
        P(("gy", "ga"), None),
        P(),
        P(),
    )
    out_specs = (
        P(None, "gx", ("gy", "ga"), None),
        P(None, "gx", ("gy", "ga"), None),
        P(None, "gx", ("gy", "ga"), None),
    )
    return jax.shard_map(body, mesh=mesh, in_specs=in_specs, out_specs=out_specs, check_vma=False)
```

time: 239 us -> 132 us (0.55)
  waiting for transfers between devices: 101 us -> 5.63 us
  local copies, waits for them, and re-layouts: 21.8 us -> 42.9 us
  blocking collectives: 20.9 us -> 0 us
  between operations: 14.3 us -> 1.4 us
  other arithmetic: 0.06 us -> 7.39 us
  starting transfers between devices: 54.4 us -> 48.6 us
    unnamed x4 -> x0, waiting for transfers between devices: 34.7 us -> none
    ppermute x16, waiting for transfers between devices: 27.3 us -> 3.06 us  [swapped(): return lax.ppermute(face, axes, couples + [(b, a) for a, b in couples])]
    all_gather x1 -> x0, blocking collectives: 20.9 us -> none  [expand(): lax.all_gather(core_block, 'gx', axis=1, tiled=True)]
    all_gather x1 -> x0, waiting for transfers between devices: 19.7 us -> none  [expand(): lax.all_gather(expanded, ('gy', 'ga'), axis=2, tiled=True)]
    reduce_scatter x1 -> x0, waiting for transfers between devices: 19.3 us -> none  [compress(): lax.psum_scatter(partial_value, 'gx', scatter_dimension=1, tiled=True)]
    ppermute x16, starting transfers between devices: 54.1 us -> 40.4 us  [swapped(): return lax.ppermute(face, axes, couples + [(b, a) for a, b in couples])]
    unnamed x33 -> x36, local copies, waits for them, and re-layouts: 16.9 us -> 5.6 us
    dot_general x8, matrix products: 17.1 us -> 7.32 us  [the longest x1 2.37 us: compress_and_expand(): whole = jnp.einsum('cxp,yc->yxp', part, north, precision=highest)]
  transfers between devices with their start and end apart: 19 -> 19, of which waited for: 14 -> 3; matrix products, arithmetic and copies ran while one was open for 5% -> 41% of each run, Pallas kernels for 0% -> 0%
where the time goes in v1:
time: 132 us; the launch traced here: 129 us
  starting transfers between devices  48.6 us (37%)
  local copies, waits for them, and re-layouts  42.9 us (32%)
  matrix products  23.5 us (18%)
  other arithmetic  7.39 us (6%)
  waiting for transfers between devices  5.63 us (4%)
  between operations  1.4 us (1%)
    ppermute x16, starting transfers between devices, swapped(): return lax.ppermute(face, axes, couples + [(b, a) for a, b in couples])  40.4 us
    dot_general x4, matrix products, advance_solution(): jnp.einsum('sk,kxyz->sxyz', production_coefficients, reaction_source_term...  16.2 us
    unnamed x36, local copies, waits for them, and re-layouts  5.6 us
    concatenate x2, local copies, waits for them, and re-layouts, compress_and_expand(): jnp.concatenate([pieces(core, own_c, own_b), pieces(whole, deep, wide)],...  5.39 us
    slice x4, local copies, waits for them, and re-layouts, advance_solution(): z_plus = jnp.concatenate([tensor_elements[..., 1:], zero_layer], axis=3)  5.36 us
    slice x4, local copies, waits for them, and re-layouts, advance_solution(): x_plus = jnp.concatenate([tensor_elements[:, 1:], x_after], axis=1)  4.88 us
    select_n x8, other arithmetic, faces_beside(): return (jnp.where(even, other, one), jnp.where(even, one, other))  4.42 us
    slice x4, local copies, waits for them, and re-layouts, advance_solution(): y_plus = jnp.concatenate([tensor_elements[:, :, 1:], y_after], axis=2)  4.3 us
  transfers between devices with their start and end apart: 19, of which 3 were waited for; matrix products, arithmetic and copies ran while one was open for 41% of the time, Pallas kernels for 0%

profile of v1, /device:TPU:3, one launch (start us, length us, event | category | flops | bytes accessed | tf_op | source)
XLA Modules:
  0.0 129.4 jit_solution(17172985078733048749)
XLA Ops:
  0.7 1.8 %copy.112 = f32[16,16,8,128]{3,0,2,1:T(8,128)S(1)} copy(f32[16,16,8,128]{3,2,1,0:T(8,128)} %param.11) | data formatting | bytes 2097152 | tf_op args[0]
  4.5 4.9 %collective-permute-start.3 = (f32[16,16,1,128]{3,0,2,1:T(8,128)}, f32[16,16,1,128]{3,0,2,1:T(8,128)}, u32[]{:S(2)}, u32[]{:S(2)}) collective-permute-start(f32[16,16,1,128]{3,0,2,1:T(8,128)} %get-tuple-element.54), channel_id=1, source_target_pairs={{1,2},{3,4},{5,6},{2,1},{4,3},{6,5},{9,10},{11,12},{13,14},{10,9},... | collective-permute-start | bytes 393224 | tf_op jit(solution)/shard_map/ppermute | solution.py:22
  10.4 4.1 %collective-permute-start.1 = (f32[16,1,8,128]{3,0,2,1:T(8,128)}, f32[16,1,8,128]{3,0,2,1:T(8,128)}, u32[]{:S(2)}, u32[]{:S(2)}) collective-permute-start(f32[16,1,8,128]{3,0,2,1:T(8,128)} %get-tuple-element.50), channel_id=1, source_target_pairs={{8,16},{16,8},{9,17},{17,9},{10,18},{18,10},{11,19},{19,11},{12,20... | collective-permute-start | bytes 196616 | tf_op jit(solution)/shard_map/ppermute | solution.py:22
  16.7 2.8 %all-to-all-start = ((f32[32,2,128]{2,1,0:T(2,128)}), f32[32,2,128]{2,1,0:T(2,128)S(1)}, u32[]{:S(2)}, u32[]{:S(2)}) async-start(f32[32,2,128]{2,1,0:T(2,128)} %broadcast_in_dim.5), calls=%async_computation | async-start | bytes 65536 | tf_op jit(solution)/shard_map/all_to_all | solution.py:86
  27.7 4.6 %fusion.11 = f32[16,16,8,128]{3,0,2,1:T(8,128)S(1)} fusion(f32[1,16,8,128]{3,0,2,1:T(1,128)S(1)} %bitcast.131, f32[15,16,8,128]{3,0,2,1:T(8,128)S(1)} %slice.239, f32[16,16,8,127]{3,0,2,1:T(8,128)} %get-tuple-element.56, f32[16,16,8,127]{3,0,2,1:T(8,128)} %get-tuple-element.55, f32[16,16,7,128]{3,0,2,1:T(8,128)} %get-tuple-element.52, ...), kind=kOutput, calls=%fused_computation.17 | convolution fusion | flops 58195968 | bytes 9684160 | tf_op jit(solution)/shard_map/sk,kxyz->sxyz/dot_general | solution.py:62
  34.1 3.0 %collective-permute-start.5 = (f32[16,1,8,128]{3,0,2,1:T(8,128)S(1)}, f32[16,1,8,128]{3,0,2,1:T(8,128)S(1)}, u32[]{:S(2)}, u32[]{:S(2)}) collective-permute-start(f32[16,1,8,128]{3,0,2,1:T(8,128)S(1)} %get-tuple-element.40), channel_id=1, source_target_pairs={{8,16},{16,8},{9,17},{17,9},{10,18},{18,10},{11,19},{19,11},{12,20... | collective-permute-start | bytes 196616 | tf_op jit(solution)/shard_map/ppermute | solution.py:22
  38.5 5.1 %collective-permute-start.7 = (f32[16,16,1,128]{3,0,2,1:T(8,128)S(1)}, f32[16,16,1,128]{3,0,2,1:T(8,128)S(1)}, u32[]{:S(2)}, u32[]{:S(2)}) collective-permute-start(f32[16,16,1,128]{3,0,2,1:T(8,128)S(1)} %get-tuple-element.44), channel_id=1, source_target_pairs={{1,2},{3,4},{5,6},{2,1},{4,3},{6,5},{9,10},{11,12},{13,14},{10,9},... | collective-permute-start | bytes 393224 | tf_op jit(solution)/shard_map/ppermute | solution.py:22
  43.7 3.0 %collective-permute-done.7 = f32[16,16,1,128]{3,0,2,1:T(8,128)S(1)} collective-permute-done((f32[16,16,1,128]{3,0,2,1:T(8,128)S(1)}, f32[16,16,1,128]{3,0,2,1:T(8,128)S(1)}, u32[]{:S(2)}, u32[]{:S(2)}) %collective-permute-start.7) | collective-permute-done | bytes 131104 | tf_op jit(solution)/shard_map/ppermute | solution.py:22
  46.8 2.1 %fusion.8 = f32[16,16,8,128]{3,0,2,1:T(8,128)S(1)} fusion(f32[16,16,8,128]{3,0,2,1:T(8,128)S(1)} %fusion.11, f32[1,16,8,128]{3,0,2,1:T(1,128)S(1)} %slice.251, f32[15,16,8,128]{3,0,2,1:T(8,128)S(1)} %slice.250, f32[16,16,8,127]{3,0,2,1:T(8,128)S(1)} %get-tuple-element.46, f32[16,16,8,127]{3,0,2,1:T(8,128)S(1)} %get-tuple-element.45, ...), kind=kOutput, calls=%fused_computation.13 | convolution fusion | flops 58195968 | bytes 9684160 | tf_op jit(solution)/shard_map/sk,kxyz->sxyz/dot_general | solution.py:62
  54.4 6.7 %collective-permute-start.11 = (f32[16,16,1,128]{3,0,2,1:T(8,128)S(1)}, f32[16,16,1,128]{3,0,2,1:T(8,128)S(1)}, u32[]{:S(2)}, u32[]{:S(2)}) collective-permute-start(f32[16,16,1,128]{3,0,2,1:T(8,128)S(1)} %get-tuple-element.34), channel_id=1, source_target_pairs={{1,2},{3,4},{5,6},{2,1},{4,3},{6,5},{9,10},{11,12},{13,14},{10,9},... | collective-permute-start | bytes 393224 | tf_op jit(solution)/shard_map/ppermute | solution.py:22
  61.2 2.1 %collective-permute-start.9 = (f32[16,1,8,128]{3,0,2,1:T(8,128)S(1)}, f32[16,1,8,128]{3,0,2,1:T(8,128)}, u32[]{:S(2)}, u32[]{:S(2)}) collective-permute-start(f32[16,1,8,128]{3,0,2,1:T(8,128)S(1)} %get-tuple-element.30), channel_id=1, source_target_pairs={{8,16},{16,8},{9,17},{17,9},{10,18},{18,10},{11,19},{19,11},{12,20... | collective-permute-start | bytes 196616 | tf_op jit(solution)/shard_map/ppermute | solution.py:22
  65.7 2.8 %all-to-all-start.1 = ((f32[32,8,128]{2,1,0:T(8,128)}), f32[32,8,128]{2,1,0:T(8,128)S(1)}, u32[]{:S(2)}, u32[]{:S(2)}) async-start(f32[32,8,128]{2,1,0:T(8,128)} %copy.116), calls=%async_computation.1 | async-start | bytes 262144 | tf_op jit(solution)/shard_map/all_to_all | solution.py:116
  69.6 4.6 %fusion.5 = f32[16,16,8,128]{3,0,2,1:T(8,128)S(1)} fusion(f32[16,16,8,128]{3,0,2,1:T(8,128)S(1)} %fusion.8, f32[1,16,8,128]{3,0,2,1:T(1,128)} %slice.263, f32[15,16,8,128]{3,0,2,1:T(8,128)S(1)} %slice.262, f32[16,16,8,127]{3,0,2,1:T(8,128)} %get-tuple-element.36, f32[16,16,8,127]{3,0,2,1:T(8,128)} %get-tuple-element.35, ...), kind=kOutput, calls=%fused_computation.9 | convolution fusion | flops 58195968 | bytes 9684160 | tf_op jit(solution)/shard_map/sk,kxyz->sxyz/dot_general | solution.py:62
  79.0 4.0 %collective-permute-start.13 = (f32[16,1,8,128]{3,0,2,1:T(8,128)S(1)}, f32[16,1,8,128]{3,0,2,1:T(8,128)S(1)}, u32[]{:S(2)}, u32[]{:S(2)}) collective-permute-start(f32[16,1,8,128]{3,0,2,1:T(8,128)S(1)} %get-tuple-element.20), channel_id=1, source_target_pairs={{8,16},{16,8},{9,17},{17,9},{10,18},{18,10},{11,19},{19,11},{12,20... | collective-permute-start | bytes 196616 | tf_op jit(solution)/shard_map/ppermute | solution.py:22
  86.8 5.1 %collective-permute-start.15 = (f32[16,16,1,128]{3,0,2,1:T(8,128)}, f32[16,16,1,128]{3,0,2,1:T(8,128)}, u32[]{:S(2)}, u32[]{:S(2)}) collective-permute-start(f32[16,16,1,128]{3,0,2,1:T(8,128)} %get-tuple-element.24), channel_id=1, source_target_pairs={{1,2},{3,4},{5,6},{2,1},{4,3},{6,5},{9,10},{11,12},{13,14},{10,9},... | collective-permute-start | bytes 393224 | tf_op jit(solution)/shard_map/ppermute | solution.py:22
  92.6 2.5 %reshape.64 = f32[4,64,16,8]{3,2,1,0:T(8,128)} reshape(f32[32,8,128]{2,1,0:T(8,128)S(1)} %all-to-all-done.1) | data formatting | bytes 262144 | tf_op jit(solution)/shard_map/reshape | solution.py:119
  95.0 2.3 %copy.117 = f32[4,16,8,64]{3,2,1,0:T(8,128)S(1)} copy(f32[4,16,8,64]{2,1,3,0:T(8,128)} %bitcast.125) | data formatting | bytes 262144 | tf_op jit(solution)/shard_map/gyxp,yc->cgxp/dot_general | solution.py:120
  99.5 2.4 %convolution_bitcast_fusion.1 = f32[4,8,8,16,8]{3,2,4,0,1:T(8,128)S(1)} fusion(f32[8,8,64,1,1]{2,1,4,3,0:T(8,128)S(1)} %bitcast.135, f32[4,16,8,64]{3,1,0,2:T(8,128)S(1)} %bitcast.133), kind=kOutput, calls=%fused_computation.1 | convolution fusion | flops 25165824 | bytes 278528 | tf_op jit(solution)/shard_map/cxp,yc->yxp/dot_general | solution.py:124
  102.7 2.0 %copy.125 = f32[4,8,8,16,8]{4,3,2,1,0:T(8,128)} copy(f32[4,8,8,16,8]{3,2,4,0,1:T(8,128)S(1)} %convolution_bitcast_fusion.1) | data formatting | bytes 262144 | tf_op jit(solution)/shard_map/transpose | solution.py:129
  104.7 2.6 %concatenate.125 = f32[32,8,128]{2,1,0:T(8,128)S(1)} reshape(f32[4,8,8,16,8]{4,3,2,1,0:T(8,128)} %copy.125) | data formatting | bytes 262144 | tf_op jit(solution)/shard_map/concatenate | solution.py:131
  109.7 2.7 %concatenate.124 = f32[32,8,128]{2,1,0:T(8,128)S(1)} reshape(f32[4,8,8,16,8]{4,3,2,1,0:T(8,128)} %copy.122) | data formatting | bytes 262144 | tf_op jit(solution)/shard_map/concatenate | solution.py:131
  113.1 2.6 %all-to-all-start.2 = ((f32[32,16,128]{2,1,0:T(8,128)}), f32[32,16,128]{2,1,0:T(8,128)S(1)}, u32[]{:S(2)}, u32[]{:S(2)}) async-start(f32[32,16,128]{2,1,0:T(8,128)} %pad_maximum_fusion.16), calls=%async_computation.2 | async-start | bytes 524288 | tf_op jit(solution)/shard_map/all_to_all | solution.py:133
  116.7 4.8 %fusion.2 = f32[16,16,8,128]{3,0,2,1:T(8,128)S(1)} fusion(f32[16,16,8,128]{3,0,2,1:T(8,128)S(1)} %fusion.5, f32[1,16,8,128]{3,0,2,1:T(1,128)} %slice.275, f32[15,16,8,128]{3,0,2,1:T(8,128)S(1)} %copy-done.3, f32[16,16,8,127]{3,0,2,1:T(8,128)} %get-tuple-element.26, f32[16,16,8,127]{3,0,2,1:T(8,128)} %get-tuple-element.25, ...), kind=kOutput, calls=%fused_computation.5 | convolution fusion | flops 58195968 | bytes 9684160 | tf_op jit(solution)/shard_map/sk,kxyz->sxyz/dot_general | solution.py:62
  122.8 2.1 %all-to-all-done.2 = f32[32,16,128]{2,1,0:T(8,128)S(1)} async-done(((f32[32,16,128]{2,1,0:T(8,128)}), f32[32,16,128]{2,1,0:T(8,128)S(1)}, u32[]{:S(2)}, u32[]{:S(2)}) %all-to-all-start.2) | async-done | bytes 262176 | tf_op jit(solution)/shard_map/all_to_all | solution.py:133
  (126 shorter events, 47.0 us)
Async XLA Ops:
  0.6 63.4 %copy-start = (f32[128,32]{0,1:T(8,128)S(1)}, f32[128,32]{0,1:T(8,128)}, u32[]{:S(2)}) copy-start(f32[128,32]{0,1:T(8,128)} %param.20) | copy-start | bytes 49156
  3.2 23.5 %collective-permute-start.2 = (f32[16,16,1,128]{3,0,2,1:T(8,128)}, f32[16,16,1,128]{3,0,2,1:T(8,128)S(1)}, u32[]{:S(2)}, u32[]{:S(2)}) collective-permute-start(f32[16,16,1,128]{3,0,2,1:T(8,128)} %get-tuple-element.53), channel_id=1, source_target_pairs={{0,1},{2,3},{4,5},{6,7},{1,0},{3,2},{5,4},{7,6},{8,9},{10,11},{12,... | collective-permute-start | bytes 393224 | tf_op jit(solution)/shard_map/ppermute | solution.py:22
  4.5 22.2 %collective-permute-start.3 = (f32[16,16,1,128]{3,0,2,1:T(8,128)}, f32[16,16,1,128]{3,0,2,1:T(8,128)}, u32[]{:S(2)}, u32[]{:S(2)}) collective-permute-start(f32[16,16,1,128]{3,0,2,1:T(8,128)} %get-tuple-element.54), channel_id=1, source_target_pairs={{1,2},{3,4},{5,6},{2,1},{4,3},{6,5},{9,10},{11,12},{13,14},{10,9},... | collective-permute-start | bytes 393224 | tf_op jit(solution)/shard_map/ppermute | solution.py:22
  10.2 15.6 %collective-permute-start = (f32[16,1,8,128]{3,0,2,1:T(8,128)}, f32[16,1,8,128]{3,0,2,1:T(8,128)}, u32[]{:S(2)}, u32[]{:S(2)}) collective-permute-start(f32[16,1,8,128]{3,0,2,1:T(8,128)} %get-tuple-element.49), channel_id=1, source_target_pairs={{0,8},{16,24},{8,0},{24,16},{1,9},{17,25},{9,1},{25,17},{2,10},{18... | collective-permute-start | bytes 196616 | tf_op jit(solution)/shard_map/ppermute | solution.py:22
  10.4 15.4 %collective-permute-start.1 = (f32[16,1,8,128]{3,0,2,1:T(8,128)}, f32[16,1,8,128]{3,0,2,1:T(8,128)}, u32[]{:S(2)}, u32[]{:S(2)}) collective-permute-start(f32[16,1,8,128]{3,0,2,1:T(8,128)} %get-tuple-element.50), channel_id=1, source_target_pairs={{8,16},{16,8},{9,17},{17,9},{10,18},{18,10},{11,19},{19,11},{12,20... | collective-permute-start | bytes 196616 | tf_op jit(solution)/shard_map/ppermute | solution.py:22
  16.7 8.8 %all-to-all-start = ((f32[32,2,128]{2,1,0:T(2,128)}), f32[32,2,128]{2,1,0:T(2,128)S(1)}, u32[]{:S(2)}, u32[]{:S(2)}) async-start(f32[32,2,128]{2,1,0:T(2,128)} %broadcast_in_dim.5), calls=%async_computation | async-start | bytes 65536 | tf_op jit(solution)/shard_map/all_to_all | solution.py:86
  25.1 44.5 %copy-start.15 = (f32[16]{0:T(128)}, f32[16]{0:T(128)S(1)}, u32[]{:S(2)}) copy-start(f32[16]{0:T(128)S(1)} %neg.3) | copy-start | bytes 196
  33.1 13.6 %copy-start.5 = (f32[16,8,128]{2,1,0:T(8,128)S(1)}, f32[16,8,128]{2,1,0:T(8,128)}, u32[]{:S(2)}) copy-start(f32[16,8,128]{2,1,0:T(8,128)} %get-tuple-element.65) | copy-start | bytes 196612
  33.1 13.6 %copy-start.6 = (f32[16,8,128]{2,1,0:T(8,128)S(1)}, f32[16,8,128]{2,1,0:T(8,128)}, u32[]{:S(2)}) copy-start(f32[16,8,128]{2,1,0:T(8,128)} %get-tuple-element.66) | copy-start | bytes 196612
  33.1 13.6 %copy-start.7 = (f32[16,8,128]{2,1,0:T(8,128)S(1)}, f32[16,8,128]{2,1,0:T(8,128)}, u32[]{:S(2)}) copy-start(f32[16,8,128]{2,1,0:T(8,128)} %get-tuple-element.67) | copy-start | bytes 196612
  33.2 10.4 %collective-permute-start.4 = (f32[16,1,8,128]{3,0,2,1:T(8,128)S(1)}, f32[16,1,8,128]{3,0,2,1:T(8,128)S(1)}, u32[]{:S(2)}, u32[]{:S(2)}) collective-permute-start(f32[16,1,8,128]{3,0,2,1:T(8,128)S(1)} %get-tuple-element.39), channel_id=1, source_target_pairs={{0,8},{16,24},{8,0},{24,16},{1,9},{17,25},{9,1},{25,17},{2,10},{18... | collective-permute-start | bytes 196616 | tf_op jit(solution)/shard_map/ppermute | solution.py:22
  34.1 9.5 %collective-permute-start.5 = (f32[16,1,8,128]{3,0,2,1:T(8,128)S(1)}, f32[16,1,8,128]{3,0,2,1:T(8,128)S(1)}, u32[]{:S(2)}, u32[]{:S(2)}) collective-permute-start(f32[16,1,8,128]{3,0,2,1:T(8,128)S(1)} %get-tuple-element.40), channel_id=1, source_target_pairs={{8,16},{16,8},{9,17},{17,9},{10,18},{18,10},{11,19},{19,11},{12,20... | collective-permute-start | bytes 196616 | tf_op jit(solution)/shard_map/ppermute | solution.py:22
  37.3 6.4 %collective-permute-start.6 = (f32[16,16,1,128]{3,0,2,1:T(8,128)S(1)}, f32[16,16,1,128]{3,0,2,1:T(8,128)S(1)}, u32[]{:S(2)}, u32[]{:S(2)}) collective-permute-start(f32[16,16,1,128]{3,0,2,1:T(8,128)S(1)} %get-tuple-element.43), channel_id=1, source_target_pairs={{0,1},{2,3},{4,5},{6,7},{1,0},{3,2},{5,4},{7,6},{8,9},{10,11},{12,... | collective-permute-start | bytes 393224 | tf_op jit(solution)/shard_map/ppermute | solution.py:22
  38.5 8.2 %collective-permute-start.7 = (f32[16,16,1,128]{3,0,2,1:T(8,128)S(1)}, f32[16,16,1,128]{3,0,2,1:T(8,128)S(1)}, u32[]{:S(2)}, u32[]{:S(2)}) collective-permute-start(f32[16,16,1,128]{3,0,2,1:T(8,128)S(1)} %get-tuple-element.44), channel_id=1, source_target_pairs={{1,2},{3,4},{5,6},{2,1},{4,3},{6,5},{9,10},{11,12},{13,14},{10,9},... | collective-permute-start | bytes 393224 | tf_op jit(solution)/shard_map/ppermute | solution.py:22
  54.3 15.2 %collective-permute-start.10 = (f32[16,16,1,128]{3,0,2,1:T(8,128)S(1)}, f32[16,16,1,128]{3,0,2,1:T(8,128)S(1)}, u32[]{:S(2)}, u32[]{:S(2)}) collective-permute-start(f32[16,16,1,128]{3,0,2,1:T(8,128)S(1)} %get-tuple-element.33), channel_id=1, source_target_pairs={{0,1},{2,3},{4,5},{6,7},{1,0},{3,2},{5,4},{7,6},{8,9},{10,11},{12,... | collective-permute-start | bytes 393224 | tf_op jit(solution)/shard_map/ppermute | solution.py:22
  54.4 15.1 %collective-permute-start.11 = (f32[16,16,1,128]{3,0,2,1:T(8,128)S(1)}, f32[16,16,1,128]{3,0,2,1:T(8,128)S(1)}, u32[]{:S(2)}, u32[]{:S(2)}) collective-permute-start(f32[16,16,1,128]{3,0,2,1:T(8,128)S(1)} %get-tuple-element.34), channel_id=1, source_target_pairs={{1,2},{3,4},{5,6},{2,1},{4,3},{6,5},{9,10},{11,12},{13,14},{10,9},... | collective-permute-start | bytes 393224 | tf_op jit(solution)/shard_map/ppermute | solution.py:22
  61.1 7.5 %collective-permute-start.8 = (f32[16,1,8,128]{3,0,2,1:T(8,128)S(1)}, f32[16,1,8,128]{3,0,2,1:T(8,128)}, u32[]{:S(2)}, u32[]{:S(2)}) collective-permute-start(f32[16,1,8,128]{3,0,2,1:T(8,128)S(1)} %get-tuple-element.29), channel_id=1, source_target_pairs={{0,8},{16,24},{8,0},{24,16},{1,9},{17,25},{9,1},{25,17},{2,10},{18... | collective-permute-start | bytes 196616 | tf_op jit(solution)/shard_map/ppermute | solution.py:22
  61.2 7.4 %collective-permute-start.9 = (f32[16,1,8,128]{3,0,2,1:T(8,128)S(1)}, f32[16,1,8,128]{3,0,2,1:T(8,128)}, u32[]{:S(2)}, u32[]{:S(2)}) collective-permute-start(f32[16,1,8,128]{3,0,2,1:T(8,128)S(1)} %get-tuple-element.30), channel_id=1, source_target_pairs={{8,16},{16,8},{9,17},{17,9},{10,18},{18,10},{11,19},{19,11},{12,20... | collective-permute-start | bytes 196616 | tf_op jit(solution)/shard_map/ppermute | solution.py:22
  65.7 26.8 %all-to-all-start.1 = ((f32[32,8,128]{2,1,0:T(8,128)}), f32[32,8,128]{2,1,0:T(8,128)S(1)}, u32[]{:S(2)}, u32[]{:S(2)}) async-start(f32[32,8,128]{2,1,0:T(8,128)} %copy.116), calls=%async_computation.1 | async-start | bytes 262144 | tf_op jit(solution)/shard_map/all_to_all | solution.py:116
  78.8 13.1 %collective-permute-start.12 = (f32[16,1,8,128]{3,0,2,1:T(8,128)S(1)}, f32[16,1,8,128]{3,0,2,1:T(8,128)S(1)}, u32[]{:S(2)}, u32[]{:S(2)}) collective-permute-start(f32[16,1,8,128]{3,0,2,1:T(8,128)S(1)} %get-tuple-element.19), channel_id=1, source_target_pairs={{0,8},{16,24},{8,0},{24,16},{1,9},{17,25},{9,1},{25,17},{2,10},{18... | collective-permute-start | bytes 196616 | tf_op jit(solution)/shard_map/ppermute | solution.py:22
  79.0 12.8 %collective-permute-start.13 = (f32[16,1,8,128]{3,0,2,1:T(8,128)S(1)}, f32[16,1,8,128]{3,0,2,1:T(8,128)S(1)}, u32[]{:S(2)}, u32[]{:S(2)}) collective-permute-start(f32[16,1,8,128]{3,0,2,1:T(8,128)S(1)} %get-tuple-element.20), channel_id=1, source_target_pairs={{8,16},{16,8},{9,17},{17,9},{10,18},{18,10},{11,19},{19,11},{12,20... | collective-permute-start | bytes 196616 | tf_op jit(solution)/shard_map/ppermute | solution.py:22
  85.6 30.1 %collective-permute-start.14 = (f32[16,16,1,128]{3,0,2,1:T(8,128)}, f32[16,16,1,128]{3,0,2,1:T(8,128)}, u32[]{:S(2)}, u32[]{:S(2)}) collective-permute-start(f32[16,16,1,128]{3,0,2,1:T(8,128)} %get-tuple-element.23), channel_id=1, source_target_pairs={{0,1},{2,3},{4,5},{6,7},{1,0},{3,2},{5,4},{7,6},{8,9},{10,11},{12,... | collective-permute-start | bytes 393224 | tf_op jit(solution)/shard_map/ppermute | solution.py:22
  86.8 29.0 %collective-permute-start.15 = (f32[16,16,1,128]{3,0,2,1:T(8,128)}, f32[16,16,1,128]{3,0,2,1:T(8,128)}, u32[]{:S(2)}, u32[]{:S(2)}) collective-permute-start(f32[16,16,1,128]{3,0,2,1:T(8,128)} %get-tuple-element.24), channel_id=1, source_target_pairs={{1,2},{3,4},{5,6},{2,1},{4,3},{6,5},{9,10},{11,12},{13,14},{10,9},... | collective-permute-start | bytes 393224 | tf_op jit(solution)/shard_map/ppermute | solution.py:22
  113.1 11.8 %all-to-all-start.2 = ((f32[32,16,128]{2,1,0:T(8,128)}), f32[32,16,128]{2,1,0:T(8,128)S(1)}, u32[]{:S(2)}, u32[]{:S(2)}) async-start(f32[32,16,128]{2,1,0:T(8,128)} %pad_maximum_fusion.16), calls=%async_computation.2 | async-start | bytes 524288 | tf_op jit(solution)/shard_map/all_to_all | solution.py:133
  (12 other events, 59.0 us)

commit v2 on v1

v2 whole, which is shorter than its diff:
```python
import functools

import jax
import jax.numpy as jnp
from jax import lax
from jax.experimental import pallas as pl
from jax.experimental.pallas import tpu as pltpu
from jax.sharding import PartitionSpec as P

SUB = 2


time_step = 0.5

ROW = "gx"
COLUMN = ("gy", "ga")
EVERY = ("gx", "gy", "ga")
HIGHEST = lax.Precision.HIGHEST
HIGH = lax.Precision.HIGH
VMEM_LIMIT = 8 * 1024 * 1024


def vmem_call(kernel, outs, in_smem, n_in, flops=0, moved=0, exps=0, scratch=()):
    vmem = pl.BlockSpec(memory_space=pltpu.VMEM)
    smem = pl.BlockSpec(memory_space=pltpu.SMEM)
    return pl.pallas_call(
        kernel,
        in_specs=[smem] * in_smem + [vmem] * (n_in - in_smem),
        out_specs=[vmem] * len(outs),
        out_shape=[jax.ShapeDtypeStruct(shape, jnp.float32) for shape in outs],
        scratch_shapes=[pltpu.VMEM(shape, jnp.float32) for shape in scratch],
        compiler_params=pltpu.CompilerParams(vmem_limit_bytes=VMEM_LIMIT),
        cost_estimate=pl.CostEstimate(flops=flops, bytes_accessed=moved, transcendentals=exps),
    )


def planes_of_species(ref, species, plane, at):
    return jnp.concatenate(
        [ref[pl.ds(first * plane + at, 8, stride=plane), :] for first in range(0, species, 8)], axis=0
    )


def store_planes_of_species(ref, species, plane, at, value):
    for first in range(0, species, 8):
        ref[pl.ds(first * plane + at, 8, stride=plane), :] = value[first : first + 8]


def faces_kernel(shape, even_ref, rows_ref, x_one, x_other, y_one, y_other):
    wide, deep, species, _ = shape
    even_x, even_y = even_ref[0] == 1, even_ref[1] == 1
    plane = wide * deep
    for y in range(deep):
        low = planes_of_species(rows_ref, species, plane, y)
        high = planes_of_species(rows_ref, species, plane, (wide - 1) * deep + y)
        x_one[y] = jnp.where(even_x, high, low)
        x_other[y] = jnp.where(even_x, low, high)
    for x in range(wide):
        low = planes_of_species(rows_ref, species, plane, x * deep)
        high = planes_of_species(rows_ref, species, plane, x * deep + deep - 1)
        y_one[x] = jnp.where(even_y, high, low)
        y_other[x] = jnp.where(even_y, low, high)


def prepare_kernel(shape, given, thermal_ref, constant_ref, energy_ref, field, rates):
    wide, deep, species, up = shape
    constant = jnp.broadcast_to(constant_ref[...], (species, up))
    energy = jnp.broadcast_to(energy_ref[...], (species, up))
    for x in range(wide):
        inverse = -1.0 / thermal_ref[x]
        field[x] = jnp.swapaxes(given[:, x], 0, 1)
        for y in range(deep):
            rates[x, y] = constant * jnp.exp(energy * inverse[y : y + 1])


def blocks_on_diagonal(matrix, count):
    high, wide = matrix.shape
    tall, broad = count * high, count * wide

    def picks(rows, size):
        row = lax.broadcasted_iota(jnp.int32, (rows, size), 0) % size
        return (row == lax.broadcasted_iota(jnp.int32, (rows, size), 1)).astype(jnp.float32)

    full = jnp.dot(picks(tall, high), matrix, precision=HIGHEST, preferred_element_type=jnp.float32)
    full = lax.dot_general(
        full, picks(broad, wide), (((1,), (1,)), ((), ())), precision=HIGHEST,
        preferred_element_type=jnp.float32,
    )
    row = lax.broadcasted_iota(jnp.int32, (tall, broad), 0) // high
    column = lax.broadcasted_iota(jnp.int32, (tall, broad), 1) // wide
    return jnp.where(row == column, full, 0.0)


def matrices_kernel(
    together, wide, own_ref, production, component, component_turned, east, north,
    mix, squeeze, widen, factor_rows,
):
    mix[...] = blocks_on_diagonal(time_step * production[...], together)
    squeeze[...] = blocks_on_diagonal(component_turned[...], wide)
    widen[...] = blocks_on_diagonal(component[...], wide)

    def two_rows(ref, at):
        return jnp.concatenate([ref[pl.ds(2 * at + row, 1), :] for row in range(2)], axis=1)

    if factor_rows is not None:
        factor_rows[0:1] = two_rows(east, own_ref[3])
        factor_rows[1:2] = two_rows(north, own_ref[2])


def _without_rows(kernel, *refs):
    kernel(*refs, None)


def step(shape, refs, emit):
    wide, deep, species, up = shape
    even_ref, field, x_one, x_other, y_one, y_other, rates, flow, diffusivity_ref, mix_ref = refs
    even_x, even_y = even_ref[0] == 1, even_ref[1] == 1
    diffusivity = jnp.broadcast_to(diffusivity_ref[...] * time_step, (species, up))
    mix = mix_ref[...]
    lane = lax.broadcasted_iota(jnp.int32, (deep, species, up), 2)
    first, last = lane == 0, lane == up - 1
    together = 4 if wide % 4 == 0 else 1
    half = max(together // 2, 1)
    x_before = jnp.where(even_x, x_other[...], x_one[...])
    x_after = jnp.where(even_x, x_one[...], x_other[...])
    for x0 in range(0, wide, together):
        made = []
        for x in range(x0, x0 + together):
            here = field[x]
            ahead = pltpu.roll(here.reshape(deep, species, up), species - 1, 1)
            made.append((rates[x] * here * ahead).reshape(deep * species, up))
        if together == 4:
            right = jnp.concatenate(
                [jnp.concatenate(made[:2], axis=0), jnp.concatenate(made[2:], axis=0)], axis=1
            )
        else:
            right = made[0]
        produced = jnp.dot(mix, right, precision=HIGH, preferred_element_type=jnp.float32)
        for x in range(x0, x0 + together):
            here = field[x]
            x_minus = field[x - 1] if x > 0 else x_before
            x_plus = field[x + 1] if x < wide - 1 else x_after
            before = jnp.where(even_y, y_other[x], y_one[x])
            after = jnp.where(even_y, y_one[x], y_other[x])
            y_minus = jnp.concatenate([before[None], here[:-1]], axis=0)
            y_plus = jnp.concatenate([here[1:], after[None]], axis=0)
            z_minus = jnp.where(first, 0.0, pltpu.roll(here, 1, 2))
            z_plus = jnp.where(last, 0.0, pltpu.roll(here, up - 1, 2))

            def speed(d):
                return jnp.stack(
                    [jnp.broadcast_to(flow[d, x, pl.ds(y, 1), :], (species, up)) for y in range(deep)]
                )

            laplace = (x_plus + x_minus) + (y_plus + y_minus) + (z_plus + z_minus) - 6.0 * here
            advect = (
                speed(0) * (x_plus - x_minus)
                + speed(1) * (y_plus - y_minus)
                + speed(2) * (z_plus - z_minus)
            )
            part = (x - x0) % half if together == 4 else 0
            group = (x - x0) // half if together == 4 else 0
            size = deep * species
            reacted = produced[part * size : (part + 1) * size, group * up : (group + 1) * up]
            emit(
                x,
                here
                + diffusivity[None] * laplace
                - (0.5 * time_step) * advect
                + reacted.reshape(deep, species, up),
            )


def emit_faces(shape, even_ref, x, plane, x_one, x_other, y_one, y_other):
    wide, deep, _, _ = shape
    even_x, even_y = even_ref[0] == 1, even_ref[1] == 1
    low, high = plane[0], plane[deep - 1]
    y_one[x] = jnp.where(even_y, high, low)
    y_other[x] = jnp.where(even_y, low, high)
    if x == 0:
        @pl.when(even_x)
        def _():
            x_other[...] = plane

        @pl.when(jnp.logical_not(even_x))
        def _():
            x_one[...] = plane
    if x == wide - 1:
        @pl.when(even_x)
        def _():
            x_one[...] = plane

        @pl.when(jnp.logical_not(even_x))
        def _():
            x_other[...] = plane


def advance_kernel(shape, *refs):
    even_ref, (out, x_one, x_other, y_one, y_other) = refs[0], refs[10:]

    def emit(x, plane):
        out[x] = plane
        emit_faces(shape, even_ref, x, plane, x_one, x_other, y_one, y_other)

    step(shape, refs[:10], emit)


def final_kernel(shape, *refs):
    out = refs[10]

    def emit(x, plane):
        out[:, x] = jnp.swapaxes(plane, 0, 1)

    step(shape, refs[:10], emit)


def project_kernel(shape, ranks, field, component, vertical, factor_rows, out):
    wide, deep, species, up = shape
    ranks_a, ranks_d = ranks
    each = deep + 2
    for y in range(deep):
        rows = field[:, y].reshape(wide * species, up)
        on_a = jnp.dot(component[...], rows, precision=HIGHEST, preferred_element_type=jnp.float32)
        on_d = lax.dot_general(
            vertical[...], on_a, (((1,), (1,)), ((), ())), precision=HIGHEST,
            preferred_element_type=jnp.float32,
        )
        out[pl.ds(y, ranks_d, stride=each), :] = on_d
    for row in range(2):
        out[pl.ds(deep + row, ranks_d, stride=each), :] = jnp.broadcast_to(
            factor_rows[row : row + 1], (ranks_d, 128)
        )


def core_kernel(counts, got, out):
    rows, columns, ranks_a, tall, deep = counts
    devices, each = rows * columns, deep + 2
    whole = jnp.concatenate(
        [
            jnp.concatenate(
                [got[pl.ds((row * columns + column) * each, deep), :] for column in range(columns)],
                axis=0,
            )
            for row in range(rows)
        ],
        axis=1,
    )

    def halves(at):
        both = got[pl.ds(at, devices, stride=each), :]
        return jnp.concatenate([both[:, :64], both[:, 64:]], axis=0)

    def is_at(shape, row_place, column_place):
        row = lax.broadcasted_iota(jnp.int32, shape, 0)
        column = lax.broadcasted_iota(jnp.int32, shape, 1)
        return row_place(row) == column_place(column)

    def dot(a, b, contract, precision=HIGH):
        return lax.dot_general(
            a, b, ((contract[:1], contract[1:]), ((), ())), precision=precision,
            preferred_element_type=jnp.float32,
        )

    high = 2 * devices
    broad = high * ranks_a
    own = 128 // ranks_a

    def of_east(at):
        x = at // ranks_a
        return (x % 2) * devices + x // 2

    def column_b(at):
        return at // 128 * own + at % own

    def column_a(at):
        return at // own % ranks_a

    def same(at):
        return at

    pick = is_at((broad, high), of_east, same).astype(jnp.float32)
    east = dot(pick, halves(deep), (1, 0))
    widen = is_at((high, broad), same, column_b).astype(jnp.float32)
    east = dot(east, widen, (1, 0))
    east = jnp.where(is_at((broad, broad), lambda at: at % ranks_a, column_a), east, 0.0)

    def of_north(at):
        column, row = at // deep, at % deep // 2
        return (at % 2) * devices + row * columns + column

    pick = is_at((high, high), of_north, same).astype(jnp.float32)
    north = dot(pick, halves(deep + 1), (1, 0), HIGHEST)

    half = dot(north, whole, (0, 0))
    core = dot(half, east, (1, 0))
    half = dot(core, east, (1, 1))
    whole = dot(north, half, (1, 0))
    for row in range(rows):
        for column in range(columns):
            at = row * columns + column
            out[at, 0:tall] = core[column * tall : (column + 1) * tall, row * 128 : (row + 1) * 128]
            out[at, tall : tall + deep] = whole[
                column * deep : (column + 1) * deep, row * 128 : (row + 1) * 128
            ]


def expand_kernel(shape, ranks, tall, got, field, component, vertical, residual, core, full):
    wide, deep, species, up = shape
    ranks_a, ranks_d = ranks
    each = tall + deep
    for y in range(deep):
        on_d = got[pl.ds(tall + y, ranks_d, stride=each), :]
        on_a = lax.dot_general(
            on_d, vertical[...], (((0,), (0,)), ((), ())), precision=HIGH,
            preferred_element_type=jnp.float32,
        )
        full[y] = jnp.dot(component[...], on_a, precision=HIGH, preferred_element_type=jnp.float32)
    for x in range(wide):
        residual[:, x] = jnp.swapaxes(
            field[x] - full[:, x * species : (x + 1) * species, :], 0, 1
        )
    turned = [got[pl.ds(c, ranks_d, stride=each), :].T for c in range(tall)]
    core[...] = jnp.swapaxes(jnp.stack(turned), 0, 1)


def faces_beside(faces):
    def swapped(face, axes, first):
        couples = [(i, i + 1) for i in range(first, lax.axis_size(axes) - 1, 2)]
        return lax.ppermute(face, axes, couples + [(b, a) for a, b in couples])

    x_one, x_other, y_one, y_other = faces
    y_one, y_other = swapped(y_one, COLUMN, 0), swapped(y_other, COLUMN, 1)
    x_one, x_other = swapped(x_one, ROW, 0), swapped(x_other, ROW, 1)
    return x_one, x_other, y_one, y_other


def whole_factors(tucker_factor_east, tucker_factor_north):
    rows, columns = lax.axis_size(ROW), lax.axis_size(COLUMN)

    def shares(factor, holders, axes):
        count = -(-factor.shape[0] // holders)
        padded = jnp.pad(factor, ((0, count * holders - factor.shape[0]), (0, 0)))
        return lax.dynamic_slice_in_dim(padded, lax.axis_index(axes) * count, count, 0)

    east = shares(tucker_factor_east, columns, COLUMN)
    north = shares(tucker_factor_north, rows, ROW)
    sent = jnp.concatenate([east.reshape(-1), north.reshape(-1)])
    sent = jnp.pad(sent, (0, -sent.size % 128)).reshape(1, -1, 128)
    sent = jnp.broadcast_to(sent, (rows * columns,) + sent.shape[1:])
    got = lax.all_to_all(sent, EVERY, 0, 0, tiled=True).reshape(rows, columns, -1)
    whole_east = got[:, :, : east.size].reshape(rows, -1, east.shape[1])
    whole_east = whole_east[:, : tucker_factor_east.shape[0]].reshape(-1, east.shape[1])
    whole_north = got[:, :, east.size : east.size + north.size]
    whole_north = whole_north.reshape(rows, columns, *north.shape).transpose(1, 0, 2, 3)
    whole_north = whole_north.reshape(columns, -1, north.shape[1])
    whole_north = whole_north[:, : tucker_factor_north.shape[0]].reshape(-1, north.shape[1])
    return whole_east, whole_north


def compress_and_expand(snapshot, east, north, vertical, component):
    rows, columns = lax.axis_size(ROW), lax.axis_size(COLUMN)
    devices = rows * columns
    (wide, deep, _, _), (_, ranks_a) = snapshot.shape, component.shape
    ranks_d = vertical.shape[1]
    ranks_b, ranks_c = east.shape[1], north.shape[1]
    projected = jnp.einsum("xysz,sa->xyaz", snapshot, component, precision=HIGHEST)
    projected = jnp.einsum("xyaz,zd->dyxa", projected, vertical, precision=HIGHEST)
    pairs = ranks_a * ranks_d
    share = -(-pairs // devices)
    flat = jnp.transpose(projected, (0, 3, 1, 2)).reshape(pairs, deep, wide)
    flat = jnp.pad(flat, ((0, share * devices - pairs), (0, 0), (0, 0)))
    flat = flat.reshape(devices, share, deep, wide).transpose(0, 2, 3, 1)
    flat = lax.all_to_all(
        flat.reshape(devices, deep, wide * share), EVERY, 0, 0, tiled=True
    )
    whole = flat.reshape(rows, columns * deep, wide, share)
    part = jnp.einsum("gyxp,yc->cgxp", whole, north, precision=HIGHEST)
    part = part.reshape(ranks_c, rows * wide, share)
    core = jnp.einsum("cxp,xb->cbp", part, east, precision=HIGHEST)
    part = jnp.einsum("cbp,xb->cxp", core, east, precision=HIGHEST)
    whole = jnp.einsum("cxp,yc->yxp", part, north, precision=HIGHEST)
    own_b, own_c = ranks_b // rows, ranks_c // columns

    def pieces(array, tall, broad):
        array = array.reshape(columns, tall, rows, broad, share)
        return array.transpose(2, 0, 1, 3, 4).reshape(devices, tall * broad * share)

    sent = jnp.concatenate([pieces(core, own_c, own_b), pieces(whole, deep, wide)], axis=1)
    sent = jnp.pad(sent, ((0, 0), (0, -sent.shape[1] % 1024)))
    got = lax.all_to_all(
        sent.reshape(devices, -1, 128), EVERY, 0, 0, tiled=True
    ).reshape(devices, -1)

    def ranks_together(array, tall, broad):
        array = array.reshape(devices, tall, broad, share).transpose(0, 3, 2, 1)
        array = array.reshape(devices * share, broad, tall)[:pairs]
        return array.reshape(ranks_d, ranks_a, broad, tall)

    core_size = own_c * own_b * share
    core = ranks_together(got[:, :core_size], own_c, own_b).transpose(1, 2, 3, 0)
    expanded = ranks_together(got[:, core_size : core_size + deep * wide * share], deep, wide)
    expanded = jnp.einsum("daxy,zd->axyz", expanded, vertical, precision=HIGHEST)
    expanded = jnp.einsum("axyz,sa->sxyz", expanded, component, precision=HIGHEST)
    return core, snapshot.transpose(2, 0, 1, 3) - expanded


def body(
    mixture_fields_initial,
    flow_speed_vector,
    thermal_field,
    mass_diffusivity,
    arrhenius_constant,
    arrhenius_energy_temp,
    production_coefficients,
    tucker_factor_east,
    tucker_factor_north,
    tucker_factor_vertical,
    tucker_factor_component,
):
    species, wide, deep, up = mixture_fields_initial.shape
    shape = (wide, deep, species, up)
    cells = wide * deep * species * up
    rows, columns = lax.axis_size(ROW), lax.axis_size(COLUMN)
    devices = rows * columns
    ranks_a, ranks_d = tucker_factor_component.shape[1], tucker_factor_vertical.shape[1]
    ranks_b, ranks_c = tucker_factor_east.shape[1], tucker_factor_north.shape[1]
    own_b, own_c = ranks_b // rows, ranks_c // columns
    kernels_fit = (
        ranks_d == devices
        and wide * ranks_a == 128
        and own_b * ranks_a == 128
        and deep == own_c == 8
        and ranks_b == ranks_c == 64
        and wide == 2 * columns
        and deep == 2 * rows
    )

    row, column = lax.axis_index(ROW), lax.axis_index(COLUMN)
    own = jnp.stack([1 - row % 2, 1 - column % 2, row, column]).astype(jnp.int32)
    face_shapes = [(deep, species, up)] * 2 + [(wide, species, up)] * 2
    field_rows = mixture_fields_initial.reshape(species * wide * deep, up)
    faces = vmem_call(functools.partial(faces_kernel, shape), face_shapes, 1, 2)(own, field_rows)
    faces = faces_beside(faces)
    field, rates = vmem_call(
        functools.partial(prepare_kernel, shape), [shape, shape], 0, 4,
        flops=4 * cells, moved=12 * cells, exps=cells,
    )(
        mixture_fields_initial,
        thermal_field,
        arrhenius_constant[:, None],
        arrhenius_energy_temp[:, None],
    )
    together = 2 if wide % 4 == 0 else 1
    both = together * deep
    matrices = functools.partial(matrices_kernel, both, wide)
    matrix_shapes = [
        (both * species,) * 2, (wide * ranks_a, wide * species), (wide * species, wide * ranks_a)
    ]
    if kernels_fit:
        matrix_shapes.append((2, 128))
    else:
        matrices = functools.partial(_without_rows, matrices)
    mix, squeeze, widen, *factor_rows = vmem_call(
        matrices, matrix_shapes, 1, 6, flops=cells, moved=cells,
    )(
        own,
        production_coefficients,
        tucker_factor_component,
        tucker_factor_component.T,
        tucker_factor_east,
        tucker_factor_north,
    )
    fixed = (rates, flow_speed_vector, mass_diffusivity[:, None], mix)
    advance = vmem_call(
        functools.partial(advance_kernel, shape), [shape] + face_shapes, 1, 10,
        flops=60 * cells, moved=8 * cells,
    )
    final = vmem_call(
        functools.partial(final_kernel, shape), [mixture_fields_initial.shape], 1, 10,
        flops=60 * cells, moved=8 * cells,
    )
    for substep in range(SUB):
        if substep:
            faces = faces_beside(faces)
        field, *faces = advance(own, field, *faces, *fixed)
    snapshot = field

    if kernels_fit:
        (sent,) = vmem_call(
            functools.partial(project_kernel, shape, (ranks_a, ranks_d)),
            [(devices * (deep + 2), 128)], 0, 4, flops=60 * cells, moved=4 * cells,
        )(snapshot, squeeze, tucker_factor_vertical.T, *factor_rows)
        got = lax.all_to_all(
            sent.reshape(devices, (deep + 2) // 2, 2, 128), EVERY, 0, 0, tiled=True
        )
        for substep in range(SUB - 1):
            faces = faces_beside(faces)
            field, *faces = advance(own, field, *faces, *fixed)
        got, field = lax.optimization_barrier((got, field))
        (sent,) = vmem_call(
            functools.partial(core_kernel, (rows, columns, ranks_a, own_c, deep)),
            [(devices, own_c + deep, 128)], 0, 1, flops=60 * cells, moved=4 * cells,
        )(got.reshape(devices * (deep + 2), 128))
        got = lax.all_to_all(sent, EVERY, 0, 0, tiled=True)
    else:
        east, north = whole_factors(tucker_factor_east, tucker_factor_north)
        tucker_core, residual = compress_and_expand(
            snapshot, east, north, tucker_factor_vertical, tucker_factor_component
        )
        for substep in range(SUB - 1):
            faces = faces_beside(faces)
            field, *faces = advance(own, field, *faces, *fixed)
    faces = faces_beside(faces)
    (mixture_fields_final,) = final(own, field, *faces, *fixed)
    if kernels_fit:
        residual, tucker_core = vmem_call(
            functools.partial(expand_kernel, shape, (ranks_a, ranks_d), own_c),
            [mixture_fields_initial.shape, (ranks_a * own_b, own_c, ranks_d)], 0, 4,
            flops=60 * cells, moved=8 * cells, scratch=[(deep, wide * species, up)],
        )(
            got.reshape(devices * (own_c + deep), 128),
            snapshot,
            widen,
            tucker_factor_vertical.T,
        )
        tucker_core = tucker_core.reshape(ranks_a, own_b, own_c, ranks_d)
    return (mixture_fields_final, residual, tucker_core)


def solution(mesh):
    in_specs = (
        P(None, "gx", ("gy", "ga"), None),
        P(None, "gx", ("gy", "ga"), None),
        P("gx", ("gy", "ga"), None),
        P(),
        P(),
        P(),
        P(),
        P("gx", None),
        P(("gy", "ga"), None),
        P(),
        P(),
    )
    out_specs = (
        P(None, "gx", ("gy", "ga"), None),
        P(None, "gx", ("gy", "ga"), None),
        P(None, "gx", ("gy", "ga"), None),
    )
    return jax.shard_map(body, mesh=mesh, in_specs=in_specs, out_specs=out_specs, check_vma=False)
```

time: 132 us -> 81.7 us (0.62)
  local copies, waits for them, and re-layouts: 42.9 us -> 4.32 us
  matrix products: 23.5 us -> 0 us
  Pallas kernels: 0 us -> 20.6 us
  other arithmetic: 7.39 us -> 0.08 us
    dot_general x12 -> x0, matrix products: 23.5 us -> none  [the longest x4 16.2 us: advance_solution(): jnp.einsum('sk,kxyz->sxyz', production_coefficients, reaction_source_term...]
    pallas_call x0 -> x10, Pallas kernels: none -> 20.6 us  [the longest x3 6 us: body(): field, *faces = advance(own, field, *faces, *fixed)]
    slice x23 -> x0, local copies, waits for them, and re-layouts: 17.3 us -> none  [the longest x4 5.36 us: advance_solution(): z_plus = jnp.concatenate([tensor_elements[..., 1:], zero_layer], axis=3)]
    select_n x16 -> x0, other arithmetic: 6.65 us -> none  [the longest x8 4.42 us: faces_beside(): return (jnp.where(even, other, one), jnp.where(even, one, other))]
    concatenate x2 -> x0, local copies, waits for them, and re-layouts: 5.39 us -> none  [compress_and_expand(): jnp.concatenate([pieces(core, own_c, own_b), pieces(whole, deep, wide)],...]
    transpose x4 -> x0, local copies, waits for them, and re-layouts: 4.97 us -> none  [the longest x2 3.82 us: pieces(): return array.transpose(2, 0, 1, 3, 4).reshape(devices, tall * broad * share)]
    reshape x9 -> x0, local copies, waits for them, and re-layouts: 4.39 us -> none  [the longest x1 2.48 us: compress_and_expand(): whole = flat.reshape(rows, columns * deep, wide, share)]
    ppermute x16, waiting for transfers between devices: 3.06 us -> 6.42 us  [swapped(): return lax.ppermute(face, axes, couples + [(b, a) for a, b in couples])]
  transfers between devices with their start and end apart: 19 -> 18, of which waited for: 3 -> 4; matrix products, arithmetic and copies ran while one was open for 41% -> 0% of each run, Pallas kernels for 0% -> 9%
where the time goes in v2:
time: 81.7 us; the launch traced here: 80.3 us
  starting transfers between devices  47.9 us (59%)
  Pallas kernels  20.6 us (25%)
  waiting for transfers between devices  6.43 us (8%)
  local copies, waits for them, and re-layouts  4.32 us (5%)
  between operations  0.93 us (1%)
    ppermute x16, starting transfers between devices, swapped(): return lax.ppermute(face, axes, couples + [(b, a) for a, b in couples])  38.9 us
    ppermute x16, waiting for transfers between devices, swapped(): return lax.ppermute(face, axes, couples + [(b, a) for a, b in couples])  6.42 us
    pallas_call x3, Pallas kernels, body(): field, *faces = advance(own, field, *faces, *fixed)  6 us
    all_to_all x1, starting transfers between devices, body(): got = lax.all_to_all(sent, EVERY, 0, 0, tiled=True)  4.86 us
    all_to_all x1, starting transfers between devices, body(): lax.all_to_all(sent.reshape(devices, (deep + 2) // 2, 2, 128), EVERY, 0,...  4.17 us
    unnamed x29, local copies, waits for them, and re-layouts  4.07 us
    pallas_call x1, Pallas kernels, body(): mixture_fields_final, = final(own, field, *faces, *fixed)  2.99 us
    pallas_call x1, Pallas kernels, body(): vmem_call(functools.partial(core_kernel, (rows, columns, ranks_a, own_c,...  2.91 us
  transfers between devices with their start and end apart: 18, of which 4 were waited for; matrix products, arithmetic and copies ran while one was open for 0% of the time, Pallas kernels for 9%

profile of v2, /device:TPU:3, one launch (start us, length us, event | category | flops | bytes accessed | tf_op | source)
XLA Modules:
  0.0 80.3 jit_solution(15035250329052333287)
XLA Ops:
  2.0 1.4 %shard_map.131 = (f32[8,16,128]{2,1,0:T(8,128)}, f32[8,16,128]{2,1,0:T(8,128)S(1)}, f32[16,16,128]{2,1,0:T(8,128)}, f32[16,16,128]{2,1,0:T(8,128)S(1)}) custom-call(s32[4]{0:T(128)S(1)} %pad_add_fusion.even_ref.own_ref.refs_0_, f32[2048,128]{1,0:T(8,128)S(1)} %bitcast.14), custom_call_target="tpu_custom_call" | custom-call | tf_op jit(solution)/shard_map/pallas_call | solution.py:441
  3.5 1.3 %collective-permute-start.2 = (f32[16,16,128]{2,1,0:T(8,128)}, f32[16,16,128]{2,1,0:T(8,128)S(1)}, u32[]{:S(2)}, u32[]{:S(2)}) collective-permute-start(f32[16,16,128]{2,1,0:T(8,128)} %get-tuple-element.35), channel_id=1, source_target_pairs={{0,1},{2,3},{4,5},{6,7},{1,0},{3,2},{5,4},{7,6},{8,9},{10,11},{12,... | collective-permute-start | bytes 393224 | tf_op jit(solution)/shard_map/ppermute | solution.py:328
  4.7 4.9 %collective-permute-start.3 = (f32[16,16,128]{2,1,0:T(8,128)S(1)}, f32[16,16,128]{2,1,0:T(8,128)S(1)}, u32[]{:S(2)}, u32[]{:S(2)}) collective-permute-start(f32[16,16,128]{2,1,0:T(8,128)S(1)} %get-tuple-element.36), channel_id=1, source_target_pairs={{1,2},{3,4},{5,6},{2,1},{4,3},{6,5},{9,10},{11,12},{13,14},{10,9},... | collective-permute-start | bytes 393224 | tf_op jit(solution)/shard_map/ppermute | solution.py:328
  10.0 4.1 %collective-permute-start.1 = (f32[8,16,128]{2,1,0:T(8,128)S(1)}, f32[8,16,128]{2,1,0:T(8,128)S(1)}, u32[]{:S(2)}, u32[]{:S(2)}) collective-permute-start(f32[8,16,128]{2,1,0:T(8,128)S(1)} %get-tuple-element.34), channel_id=1, source_target_pairs={{8,16},{16,8},{9,17},{17,9},{10,18},{18,10},{11,19},{19,11},{12,20... | collective-permute-start | bytes 196616 | tf_op jit(solution)/shard_map/ppermute | solution.py:328
  14.2 1.8 %shard_map.132 = (f32[256,256]{1,0:T(8,128)S(1)}, f32[128,256]{1,0:T(8,128)S(1)}, f32[256,128]{1,0:T(8,128)S(1)}, f32[2,128]{1,0:T(2,128)S(1)}) custom-call(s32[4]{0:T(128)S(1)} %pad_add_fusion.even_ref.own_ref.refs_0_, f32[16,16]{1,0:T(8,128)S(1)} %copy-done.8, f32[16,8]{1,0:T(8,128)S(1)} %copy.16.component, f32[8,16]{1,0:T(8,128)S(1)} %bitcast.19, ...), custom_call_target="tpu_custom_call" | custom-call | flops 262144 | bytes 262144 | tf_op jit(solution)/shard_map/pallas_call | solution.py:462
  17.2 1.9 %shard_map.133 = (f32[16,8,16,128]{3,2,1,0:T(8,128)S(1)}, f32[8,16,128]{2,1,0:T(8,128)S(1)}, f32[8,16,128]{2,1,0:T(8,128)S(1)}, f32[16,16,128]{2,1,0:T(8,128)S(1)}, f32[16,16,128]{2,1,0:T(8,128)S(1)}) custom-call(s32[4]{0:T(128)S(1)} %pad_add_fusion.even_ref.own_ref.refs_0_, f32[16,8,16,128]{3,2,1,0:T(8,128)S(1)} %get-tuple-element.32.refs_1_, ...), custom_call_target="tpu_custom_call" | custom-call | flops 15728640 | bytes 2097152 | tf_op jit(solution)/shard_map/pallas_call | solution.py:484
  19.2 4.0 %collective-permute-start.7 = (f32[16,16,128]{2,1,0:T(8,128)S(1)}, f32[16,16,128]{2,1,0:T(8,128)S(1)}, u32[]{:S(2)}, u32[]{:S(2)}) collective-permute-start(f32[16,16,128]{2,1,0:T(8,128)S(1)} %get-tuple-element.43), channel_id=1, source_target_pairs={{1,2},{3,4},{5,6},{2,1},{4,3},{6,5},{9,10},{11,12},{13,14},{10,9},... | collective-permute-start | bytes 393224 | tf_op jit(solution)/shard_map/ppermute | solution.py:328
  23.3 3.7 %collective-permute-start.5 = (f32[8,16,128]{2,1,0:T(8,128)S(1)}, f32[8,16,128]{2,1,0:T(8,128)S(1)}, u32[]{:S(2)}, u32[]{:S(2)}) collective-permute-start(f32[8,16,128]{2,1,0:T(8,128)S(1)} %get-tuple-element.41), channel_id=1, source_target_pairs={{8,16},{16,8},{9,17},{17,9},{10,18},{18,10},{11,19},{19,11},{12,20... | collective-permute-start | bytes 196616 | tf_op jit(solution)/shard_map/ppermute | solution.py:328
  27.0 2.2 %collective-permute-done.5.refs_3_ = f32[8,16,128]{2,1,0:T(8,128)S(1)} collective-permute-done((f32[8,16,128]{2,1,0:T(8,128)S(1)}, f32[8,16,128]{2,1,0:T(8,128)S(1)}, u32[]{:S(2)}, u32[]{:S(2)}) %collective-permute-start.5) | collective-permute-done | bytes 65568 | tf_op jit(solution)/shard_map/ppermute | solution.py:328
  29.3 2.1 %shard_map.134 = (f32[16,8,16,128]{3,2,1,0:T(8,128)S(1)}, f32[8,16,128]{2,1,0:T(8,128)S(1)}, f32[8,16,128]{2,1,0:T(8,128)S(1)}, f32[16,16,128]{2,1,0:T(8,128)S(1)}, f32[16,16,128]{2,1,0:T(8,128)S(1)}) custom-call(s32[4]{0:T(128)S(1)} %pad_add_fusion.even_ref.own_ref.refs_0_, f32[16,8,16,128]{3,2,1,0:T(8,128)S(1)} %get-tuple-element.39.refs_1_, ...), custom_call_target="tpu_custom_call" | custom-call | flops 15728640 | bytes 2097152 | tf_op jit(solution)/shard_map/pallas_call | solution.py:484
  31.4 2.7 %shard_map.135 = f32[320,128]{1,0:T(8,128)} custom-call(f32[16,8,16,128]{3,2,1,0:T(8,128)S(1)} %get-tuple-element.44.field.refs_1_, f32[128,256]{1,0:T(8,128)S(1)} %get-tuple-element.45.component, f32[32,128]{1,0:T(8,128)S(1)} %bitcast.17, f32[2,128]{1,0:T(2,128)S(1)} %get-tuple-element.46.factor_rows), custom_call_target="tpu_custom_call" | custom-call | flops 15728640 | bytes 1048576 | tf_op jit(solution)/shard_map/pallas_call | solution.py:488
  34.1 4.2 %all-to-all-start = ((f32[32,5,2,128]{3,2,1,0:T(2,128)}), f32[32,5,2,128]{3,2,1,0:T(2,128)S(1)}, u32[]{:S(2)}, u32[]{:S(2)}) async-start(f32[32,5,2,128]{3,2,1,0:T(2,128)} %bitcast.10), calls=%async_computation | async-start | bytes 327680 | tf_op jit(solution)/shard_map/all_to_all | solution.py:492
  38.3 1.3 %collective-permute-start.10 = (f32[16,16,128]{2,1,0:T(8,128)S(1)}, f32[16,16,128]{2,1,0:T(8,128)S(1)}, u32[]{:S(2)}, u32[]{:S(2)}) collective-permute-start(f32[16,16,128]{2,1,0:T(8,128)S(1)} %get-tuple-element.49), channel_id=1, source_target_pairs={{0,1},{2,3},{4,5},{6,7},{1,0},{3,2},{5,4},{7,6},{8,9},{10,11},{12,... | collective-permute-start | bytes 393224 | tf_op jit(solution)/shard_map/ppermute | solution.py:328
  39.5 4.5 %collective-permute-start.11 = (f32[16,16,128]{2,1,0:T(8,128)S(1)}, f32[16,16,128]{2,1,0:T(8,128)S(1)}, u32[]{:S(2)}, u32[]{:S(2)}) collective-permute-start(f32[16,16,128]{2,1,0:T(8,128)S(1)} %get-tuple-element.50), channel_id=1, source_target_pairs={{1,2},{3,4},{5,6},{2,1},{4,3},{6,5},{9,10},{11,12},{13,14},{10,9},... | collective-permute-start | bytes 393224 | tf_op jit(solution)/shard_map/ppermute | solution.py:328
  44.4 4.0 %collective-permute-start.9 = (f32[8,16,128]{2,1,0:T(8,128)S(1)}, f32[8,16,128]{2,1,0:T(8,128)S(1)}, u32[]{:S(2)}, u32[]{:S(2)}) collective-permute-start(f32[8,16,128]{2,1,0:T(8,128)S(1)} %get-tuple-element.48), channel_id=1, source_target_pairs={{8,16},{16,8},{9,17},{17,9},{10,18},{18,10},{11,19},{19,11},{12,20... | collective-permute-start | bytes 196616 | tf_op jit(solution)/shard_map/ppermute | solution.py:328
  48.4 1.9 %collective-permute-done.9.refs_3_ = f32[8,16,128]{2,1,0:T(8,128)S(1)} collective-permute-done((f32[8,16,128]{2,1,0:T(8,128)S(1)}, f32[8,16,128]{2,1,0:T(8,128)S(1)}, u32[]{:S(2)}, u32[]{:S(2)}) %collective-permute-start.9) | collective-permute-done | bytes 65568 | tf_op jit(solution)/shard_map/ppermute | solution.py:328
  50.3 2.0 %shard_map.136 = (f32[16,8,16,128]{3,2,1,0:T(8,128)S(1)}, f32[8,16,128]{2,1,0:T(8,128)S(1)}, f32[8,16,128]{2,1,0:T(8,128)S(1)}, f32[16,16,128]{2,1,0:T(8,128)S(1)}, f32[16,16,128]{2,1,0:T(8,128)S(1)}) custom-call(s32[4]{0:T(128)S(1)} %pad_add_fusion.even_ref.own_ref.refs_0_, f32[16,8,16,128]{3,2,1,0:T(8,128)S(1)} %get-tuple-element.44.field.refs_1_, ...), custom_call_target="tpu_custom_call" | custom-call | flops 15728640 | bytes 2097152 | tf_op jit(solution)/shard_map/pallas_call | solution.py:497
  53.2 2.9 %shard_map.138 = f32[32,16,128]{2,1,0:T(8,128)} custom-call(f32[320,128]{1,0:T(8,128)S(1)} %bitcast.16), custom_call_target="tpu_custom_call" | custom-call | flops 15728640 | bytes 1048576 | tf_op jit(solution)/shard_map/pallas_call | solution.py:499
  56.1 4.9 %all-to-all-start.1 = ((f32[32,16,128]{2,1,0:T(8,128)}), f32[32,16,128]{2,1,0:T(8,128)S(1)}, u32[]{:S(2)}, u32[]{:S(2)}) async-start(f32[32,16,128]{2,1,0:T(8,128)} %shard_map.138), calls=%async_computation.1 | async-start | bytes 524288 | tf_op jit(solution)/shard_map/all_to_all | solution.py:503
  62.2 4.5 %collective-permute-start.15 = (f32[16,16,128]{2,1,0:T(8,128)S(1)}, f32[16,16,128]{2,1,0:T(8,128)S(1)}, u32[]{:S(2)}, u32[]{:S(2)}) collective-permute-start(f32[16,16,128]{2,1,0:T(8,128)S(1)} %get-tuple-element.56), channel_id=1, source_target_pairs={{1,2},{3,4},{5,6},{2,1},{4,3},{6,5},{9,10},{11,12},{13,14},{10,9},... | collective-permute-start | bytes 393224 | tf_op jit(solution)/shard_map/ppermute | solution.py:328
  67.1 4.2 %collective-permute-start.13 = (f32[8,16,128]{2,1,0:T(8,128)S(1)}, f32[8,16,128]{2,1,0:T(8,128)S(1)}, u32[]{:S(2)}, u32[]{:S(2)}) collective-permute-start(f32[8,16,128]{2,1,0:T(8,128)S(1)} %get-tuple-element.54), channel_id=1, source_target_pairs={{8,16},{16,8},{9,17},{17,9},{10,18},{18,10},{11,19},{19,11},{12,20... | collective-permute-start | bytes 196616 | tf_op jit(solution)/shard_map/ppermute | solution.py:328
  71.3 1.7 %collective-permute-done.13.refs_3_ = f32[8,16,128]{2,1,0:T(8,128)S(1)} collective-permute-done((f32[8,16,128]{2,1,0:T(8,128)S(1)}, f32[8,16,128]{2,1,0:T(8,128)S(1)}, u32[]{:S(2)}, u32[]{:S(2)}) %collective-permute-start.13) | collective-permute-done | bytes 65568 | tf_op jit(solution)/shard_map/ppermute | solution.py:328
  74.8 3.0 %shard_map.137 = f32[16,16,8,128]{3,2,1,0:T(8,128)} custom-call(s32[4]{0:T(128)S(1)} %pad_add_fusion.even_ref.own_ref.refs_0_, f32[16,8,16,128]{3,2,1,0:T(8,128)S(1)} %copy-done.4, f32[8,16,128]{2,1,0:T(8,128)S(1)} %collective-permute-done.12.refs_2_, f32[8,16,128]{2,1,0:T(8,128)S(1)} %collective-permute-done.13.refs_3_, ...), custom_call_target="tpu_custom_call" | custom-call | flops 15728640 | bytes 2097152 | tf_op jit(solution)/shard_map/pallas_call | solution.py:513
  77.8 2.5 %shard_map.139 = (f32[16,16,8,128]{3,2,1,0:T(8,128)}, f32[128,8,32]{2,1,0:T(8,128)}) custom-call(f32[512,128]{1,0:T(8,128)S(1)} %bitcast.15, f32[16,8,16,128]{3,2,1,0:T(8,128)S(1)} %get-tuple-element.44.field.refs_1_, f32[256,128]{1,0:T(8,128)S(1)} %get-tuple-element.58.component, f32[32,128]{1,0:T(8,128)S(1)} %bitcast.18), custom_call_target="tpu_custom_call" | custom-call | flops 15728640 | bytes 2097152 | tf_op jit(solution)/shard_map/pallas_call | solution.py:515
  (55 shorter events, 7.8 us)
Async XLA Ops:
  0.7 13.5 %copy-start.10 = (f32[8,64]{1,0:T(8,128)S(1)}, f32[8,64]{1,0:T(8,128)}, u32[]{:S(2)}) copy-start(f32[8,64]{1,0:T(8,128)} %north.1) | copy-start | bytes 6148
  2.0 14.0 %copy-start.11 = (f32[16]{0:T(128)S(1)}, f32[16]{0:T(128)}, u32[]{:S(2)}) copy-start(f32[16]{0:T(128)} %param.15) | copy-start | bytes 196
  2.0 14.1 %copy-start.12 = (f32[16]{0:T(128)S(1)}, f32[16]{0:T(128)}, u32[]{:S(2)}) copy-start(f32[16]{0:T(128)} %param.16) | copy-start | bytes 196
  2.0 14.2 %copy-start.13 = (f32[16]{0:T(128)S(1)}, f32[16]{0:T(128)}, u32[]{:S(2)}) copy-start(f32[16]{0:T(128)} %param.14) | copy-start | bytes 196
  2.0 14.3 %copy-start.1 = (f32[16,16,8,128]{3,2,1,0:T(8,128)S(1)}, f32[16,16,8,128]{3,2,1,0:T(8,128)}, u32[]{:S(2)}) copy-start(f32[16,16,8,128]{3,2,1,0:T(8,128)} %given.1) | copy-start | bytes 3145732
  3.4 12.8 %copy-start.6 = (f32[16,8,128]{2,1,0:T(8,128)S(1)}, f32[16,8,128]{2,1,0:T(8,128)}, u32[]{:S(2)}) copy-start(f32[16,8,128]{2,1,0:T(8,128)} %thermal_ref.1) | copy-start | bytes 196612
  3.5 13.2 %collective-permute-start.2 = (f32[16,16,128]{2,1,0:T(8,128)}, f32[16,16,128]{2,1,0:T(8,128)S(1)}, u32[]{:S(2)}, u32[]{:S(2)}) collective-permute-start(f32[16,16,128]{2,1,0:T(8,128)} %get-tuple-element.35), channel_id=1, source_target_pairs={{0,1},{2,3},{4,5},{6,7},{1,0},{3,2},{5,4},{7,6},{8,9},{10,11},{12,... | collective-permute-start | bytes 393224 | tf_op jit(solution)/shard_map/ppermute | solution.py:328
  4.7 11.9 %collective-permute-start.3 = (f32[16,16,128]{2,1,0:T(8,128)S(1)}, f32[16,16,128]{2,1,0:T(8,128)S(1)}, u32[]{:S(2)}, u32[]{:S(2)}) collective-permute-start(f32[16,16,128]{2,1,0:T(8,128)S(1)} %get-tuple-element.36), channel_id=1, source_target_pairs={{1,2},{3,4},{5,6},{2,1},{4,3},{6,5},{9,10},{11,12},{13,14},{10,9},... | collective-permute-start | bytes 393224 | tf_op jit(solution)/shard_map/ppermute | solution.py:328
  9.7 6.9 %collective-permute-start = (f32[8,16,128]{2,1,0:T(8,128)}, f32[8,16,128]{2,1,0:T(8,128)S(1)}, u32[]{:S(2)}, u32[]{:S(2)}) collective-permute-start(f32[8,16,128]{2,1,0:T(8,128)} %get-tuple-element.33), channel_id=1, source_target_pairs={{0,8},{16,24},{8,0},{24,16},{1,9},{17,25},{9,1},{25,17},{2,10},{18... | collective-permute-start | bytes 196616 | tf_op jit(solution)/shard_map/ppermute | solution.py:328
  10.0 6.6 %collective-permute-start.1 = (f32[8,16,128]{2,1,0:T(8,128)S(1)}, f32[8,16,128]{2,1,0:T(8,128)S(1)}, u32[]{:S(2)}, u32[]{:S(2)}) collective-permute-start(f32[8,16,128]{2,1,0:T(8,128)S(1)} %get-tuple-element.34), channel_id=1, source_target_pairs={{8,16},{16,8},{9,17},{17,9},{10,18},{18,10},{11,19},{19,11},{12,20... | collective-permute-start | bytes 196616 | tf_op jit(solution)/shard_map/ppermute | solution.py:328
  19.1 10.1 %collective-permute-start.6 = (f32[16,16,128]{2,1,0:T(8,128)S(1)}, f32[16,16,128]{2,1,0:T(8,128)S(1)}, u32[]{:S(2)}, u32[]{:S(2)}) collective-permute-start(f32[16,16,128]{2,1,0:T(8,128)S(1)} %get-tuple-element.42), channel_id=1, source_target_pairs={{0,1},{2,3},{4,5},{6,7},{1,0},{3,2},{5,4},{7,6},{8,9},{10,11},{12,... | collective-permute-start | bytes 393224 | tf_op jit(solution)/shard_map/ppermute | solution.py:328
  19.2 10.0 %collective-permute-start.7 = (f32[16,16,128]{2,1,0:T(8,128)S(1)}, f32[16,16,128]{2,1,0:T(8,128)S(1)}, u32[]{:S(2)}, u32[]{:S(2)}) collective-permute-start(f32[16,16,128]{2,1,0:T(8,128)S(1)} %get-tuple-element.43), channel_id=1, source_target_pairs={{1,2},{3,4},{5,6},{2,1},{4,3},{6,5},{9,10},{11,12},{13,14},{10,9},... | collective-permute-start | bytes 393224 | tf_op jit(solution)/shard_map/ppermute | solution.py:328
  23.3 3.8 %collective-permute-start.4 = (f32[8,16,128]{2,1,0:T(8,128)S(1)}, f32[8,16,128]{2,1,0:T(8,128)S(1)}, u32[]{:S(2)}, u32[]{:S(2)}) collective-permute-start(f32[8,16,128]{2,1,0:T(8,128)S(1)} %get-tuple-element.40), channel_id=1, source_target_pairs={{0,8},{16,24},{8,0},{24,16},{1,9},{17,25},{9,1},{25,17},{2,10},{18... | collective-permute-start | bytes 196616 | tf_op jit(solution)/shard_map/ppermute | solution.py:328
  23.3 5.9 %collective-permute-start.5 = (f32[8,16,128]{2,1,0:T(8,128)S(1)}, f32[8,16,128]{2,1,0:T(8,128)S(1)}, u32[]{:S(2)}, u32[]{:S(2)}) collective-permute-start(f32[8,16,128]{2,1,0:T(8,128)S(1)} %get-tuple-element.41), channel_id=1, source_target_pairs={{8,16},{16,8},{9,17},{17,9},{10,18},{18,10},{11,19},{19,11},{12,20... | collective-permute-start | bytes 196616 | tf_op jit(solution)/shard_map/ppermute | solution.py:328
  34.1 19.1 %all-to-all-start = ((f32[32,5,2,128]{3,2,1,0:T(2,128)}), f32[32,5,2,128]{3,2,1,0:T(2,128)S(1)}, u32[]{:S(2)}, u32[]{:S(2)}) async-start(f32[32,5,2,128]{3,2,1,0:T(2,128)} %bitcast.10), calls=%async_computation | async-start | bytes 327680 | tf_op jit(solution)/shard_map/all_to_all | solution.py:492
  38.3 12.0 %collective-permute-start.10 = (f32[16,16,128]{2,1,0:T(8,128)S(1)}, f32[16,16,128]{2,1,0:T(8,128)S(1)}, u32[]{:S(2)}, u32[]{:S(2)}) collective-permute-start(f32[16,16,128]{2,1,0:T(8,128)S(1)} %get-tuple-element.49), channel_id=1, source_target_pairs={{0,1},{2,3},{4,5},{6,7},{1,0},{3,2},{5,4},{7,6},{8,9},{10,11},{12,... | collective-permute-start | bytes 393224 | tf_op jit(solution)/shard_map/ppermute | solution.py:328
  39.5 10.8 %collective-permute-start.11 = (f32[16,16,128]{2,1,0:T(8,128)S(1)}, f32[16,16,128]{2,1,0:T(8,128)S(1)}, u32[]{:S(2)}, u32[]{:S(2)}) collective-permute-start(f32[16,16,128]{2,1,0:T(8,128)S(1)} %get-tuple-element.50), channel_id=1, source_target_pairs={{1,2},{3,4},{5,6},{2,1},{4,3},{6,5},{9,10},{11,12},{13,14},{10,9},... | collective-permute-start | bytes 393224 | tf_op jit(solution)/shard_map/ppermute | solution.py:328
  44.0 4.4 %collective-permute-start.8 = (f32[8,16,128]{2,1,0:T(8,128)S(1)}, f32[8,16,128]{2,1,0:T(8,128)S(1)}, u32[]{:S(2)}, u32[]{:S(2)}) collective-permute-start(f32[8,16,128]{2,1,0:T(8,128)S(1)} %get-tuple-element.47), channel_id=1, source_target_pairs={{0,8},{16,24},{8,0},{24,16},{1,9},{17,25},{9,1},{25,17},{2,10},{18... | collective-permute-start | bytes 196616 | tf_op jit(solution)/shard_map/ppermute | solution.py:328
  44.4 5.9 %collective-permute-start.9 = (f32[8,16,128]{2,1,0:T(8,128)S(1)}, f32[8,16,128]{2,1,0:T(8,128)S(1)}, u32[]{:S(2)}, u32[]{:S(2)}) collective-permute-start(f32[8,16,128]{2,1,0:T(8,128)S(1)} %get-tuple-element.48), channel_id=1, source_target_pairs={{8,16},{16,8},{9,17},{17,9},{10,18},{18,10},{11,19},{19,11},{12,20... | collective-permute-start | bytes 196616 | tf_op jit(solution)/shard_map/ppermute | solution.py:328
  56.1 21.7 %all-to-all-start.1 = ((f32[32,16,128]{2,1,0:T(8,128)}), f32[32,16,128]{2,1,0:T(8,128)S(1)}, u32[]{:S(2)}, u32[]{:S(2)}) async-start(f32[32,16,128]{2,1,0:T(8,128)} %shard_map.138), calls=%async_computation.1 | async-start | bytes 524288 | tf_op jit(solution)/shard_map/all_to_all | solution.py:503
  61.0 12.0 %collective-permute-start.14 = (f32[16,16,128]{2,1,0:T(8,128)S(1)}, f32[16,16,128]{2,1,0:T(8,128)S(1)}, u32[]{:S(2)}, u32[]{:S(2)}) collective-permute-start(f32[16,16,128]{2,1,0:T(8,128)S(1)} %get-tuple-element.55), channel_id=1, source_target_pairs={{0,1},{2,3},{4,5},{6,7},{1,0},{3,2},{5,4},{7,6},{8,9},{10,11},{12,... | collective-permute-start | bytes 393224 | tf_op jit(solution)/shard_map/ppermute | solution.py:328
  62.2 11.4 %collective-permute-start.15 = (f32[16,16,128]{2,1,0:T(8,128)S(1)}, f32[16,16,128]{2,1,0:T(8,128)S(1)}, u32[]{:S(2)}, u32[]{:S(2)}) collective-permute-start(f32[16,16,128]{2,1,0:T(8,128)S(1)} %get-tuple-element.56), channel_id=1, source_target_pairs={{1,2},{3,4},{5,6},{2,1},{4,3},{6,5},{9,10},{11,12},{13,14},{10,9},... | collective-permute-start | bytes 393224 | tf_op jit(solution)/shard_map/ppermute | solution.py:328
  66.8 4.5 %collective-permute-start.12 = (f32[8,16,128]{2,1,0:T(8,128)S(1)}, f32[8,16,128]{2,1,0:T(8,128)S(1)}, u32[]{:S(2)}, u32[]{:S(2)}) collective-permute-start(f32[8,16,128]{2,1,0:T(8,128)S(1)} %get-tuple-element.53), channel_id=1, source_target_pairs={{0,8},{16,24},{8,0},{24,16},{1,9},{17,25},{9,1},{25,17},{2,10},{18... | collective-permute-start | bytes 196616 | tf_op jit(solution)/shard_map/ppermute | solution.py:328
  67.1 5.9 %collective-permute-start.13 = (f32[8,16,128]{2,1,0:T(8,128)S(1)}, f32[8,16,128]{2,1,0:T(8,128)S(1)}, u32[]{:S(2)}, u32[]{:S(2)}) collective-permute-start(f32[8,16,128]{2,1,0:T(8,128)S(1)} %get-tuple-element.54), channel_id=1, source_target_pairs={{8,16},{16,8},{9,17},{17,9},{10,18},{18,10},{11,19},{19,11},{12,20... | collective-permute-start | bytes 196616 | tf_op jit(solution)/shard_map/ppermute | solution.py:328
  (8 other events, 43.0 us)

commit v3 on v2

v3 whole, which is shorter than its diff:
```python
import functools

import jax
import jax.numpy as jnp
from jax import lax
from jax.experimental import pallas as pl
from jax.experimental.pallas import tpu as pltpu
from jax.sharding import PartitionSpec as P

SUB = 2


time_step = 0.5

ROW = "gx"
COLUMN = ("gy", "ga")
EVERY = ("gx", "gy", "ga")
HIGHEST = lax.Precision.HIGHEST
HIGH = lax.Precision.HIGH
VMEM_LIMIT = 8 * 1024 * 1024


def vmem_call(kernel, outs, in_smem, n_in, flops=0, moved=0, exps=0, scratch=()):
    vmem = pl.BlockSpec(memory_space=pltpu.VMEM)
    smem = pl.BlockSpec(memory_space=pltpu.SMEM)
    return pl.pallas_call(
        kernel,
        in_specs=[smem] * in_smem + [vmem] * (n_in - in_smem),
        out_specs=[vmem] * len(outs),
        out_shape=[jax.ShapeDtypeStruct(shape, jnp.float32) for shape in outs],
        scratch_shapes=[pltpu.VMEM(shape, jnp.float32) for shape in scratch],
        compiler_params=pltpu.CompilerParams(vmem_limit_bytes=VMEM_LIMIT),
        cost_estimate=pl.CostEstimate(flops=flops, bytes_accessed=moved, transcendentals=exps),
    )


def planes_of_species(ref, species, plane, at):
    return jnp.concatenate(
        [ref[pl.ds(first * plane + at, 8, stride=plane), :] for first in range(0, species, 8)], axis=0
    )


def store_planes_of_species(ref, species, plane, at, value):
    for first in range(0, species, 8):
        ref[pl.ds(first * plane + at, 8, stride=plane), :] = value[first : first + 8]


def faces_kernel(shape, even_ref, rows_ref, x_one, x_other, y_one, y_other):
    wide, deep, species, _ = shape
    even_x, even_y = even_ref[0] == 1, even_ref[1] == 1
    plane = wide * deep
    for y in range(deep):
        low = planes_of_species(rows_ref, species, plane, y)
        high = planes_of_species(rows_ref, species, plane, (wide - 1) * deep + y)
        x_one[y] = jnp.where(even_x, high, low)
        x_other[y] = jnp.where(even_x, low, high)
    for x in range(wide):
        low = planes_of_species(rows_ref, species, plane, x * deep)
        high = planes_of_species(rows_ref, species, plane, x * deep + deep - 1)
        y_one[x] = jnp.where(even_y, high, low)
        y_other[x] = jnp.where(even_y, low, high)


def tiled(matrix, count):
    size = matrix.shape[1]
    column = lax.broadcasted_iota(jnp.int32, (size, size * count), 1) % size
    pick = (column == lax.broadcasted_iota(jnp.int32, (size, size * count), 0)).astype(jnp.float32)
    return jnp.dot(matrix, pick, precision=HIGHEST, preferred_element_type=jnp.float32)


def where_equal(matrix, of_row, of_column):
    row = lax.broadcasted_iota(jnp.int32, matrix.shape, 0)
    column = lax.broadcasted_iota(jnp.int32, matrix.shape, 1)
    return jnp.where(of_row(row) == of_column(column), matrix, 0.0)


def prepare_kernel(shape, ranks, own_ref, given, *refs):
    wide, deep, species, up = shape
    ranks_a, _ = ranks
    held, semaphores, refs = refs[-11:-1], refs[-1], refs[:-11]
    copies = [
        pltpu.make_async_copy(source, target, semaphores.at[at])
        for at, (source, target) in enumerate(zip(refs[:10], held))
    ]
    for copy in copies:
        copy.start()
    (flow, thermal, diffusivity, constant, energy, production, turned, vertical, east,
     north) = held
    (field, rates, speeds, coefficients, mix, squeeze, wide_rows, upright,
     *factor_rows) = refs[10:]
    for x in range(wide):
        field[x] = jnp.swapaxes(given[:, x], 0, 1)
    for copy in copies:
        copy.wait()
    eye = (
        lax.broadcasted_iota(jnp.int32, (species, species), 0)
        == lax.broadcasted_iota(jnp.int32, (species, species), 1)
    )
    for at, ref in enumerate((diffusivity, constant, energy)):
        column = jnp.sum(jnp.where(eye, ref[...], 0.0), axis=1, keepdims=True)
        coefficients[at] = jnp.broadcast_to(time_step * column if at == 0 else column, (species, up))
    for x in range(wide):
        speeds[3, x] = thermal[x]
        inverse = -1.0 / thermal[x]
        for d in range(3):
            speeds[d, x] = (0.5 * time_step) * flow[d, x]
        for y in range(deep):
            rates[x, y] = coefficients[1] * jnp.exp(coefficients[2] * inverse[y : y + 1])
    count = mix.shape[0] // species
    full = jnp.concatenate([tiled(time_step * production[...], count)] * count, axis=0)
    mix[...] = where_equal(full, lambda at: at // species, lambda at: at // species)
    full = tiled(turned[...], wide)
    full = [jnp.broadcast_to(full[a : a + 1], (wide, full.shape[1])) for a in range(ranks_a)]
    full = jnp.concatenate(full, axis=0)
    squeeze[...] = where_equal(full, lambda at: at % wide, lambda at: at // species)
    pick = lax.broadcasted_iota(jnp.int32, (ranks_a, ranks_a * wide), 1) // wide
    pick = pick == lax.broadcasted_iota(jnp.int32, pick.shape, 0)
    wide_rows[...] = lax.dot_general(
        turned[...], pick.astype(jnp.float32), (((0,), (0,)), ((), ())), precision=HIGHEST,
        preferred_element_type=jnp.float32,
    )
    upright[...] = vertical[...]
    if factor_rows:
        def two_rows(ref, at):
            return jnp.concatenate([ref[pl.ds(2 * at + row, 1), :] for row in range(2)], axis=1)

        factor_rows[0][0:1] = two_rows(east, own_ref[3])
        factor_rows[0][1:2] = two_rows(north, own_ref[2])


def reacted(cells, mix):
    species = cells[0].shape[0]
    group = mix.shape[0] // species
    made = []
    for first in range(0, len(cells), 2 * group):
        some = cells[first : first + 2 * group]
        some = some + [jnp.zeros_like(some[0])] * (-len(some) % group)
        right = [
            jnp.concatenate(some[at : at + group], axis=0) for at in range(0, len(some), group)
        ]
        up = right[0].shape[1]
        produced = jnp.dot(
            mix, jnp.concatenate(right, axis=1), precision=HIGH, preferred_element_type=jnp.float32
        )
        for at in range(len(right)):
            for cell in range(group):
                made.append(
                    produced[cell * species : (cell + 1) * species, at * up : (at + 1) * up]
                )
    return made[: len(cells)]


def sources(here, rates):
    made = rates * here * pltpu.roll(here, here.shape[1] - 1, 1)
    return [made[cell] for cell in range(here.shape[0])]


def advanced(here, x_minus, x_plus, y_minus, y_plus, speeds, diffusivity, produced):
    up = here.shape[2]
    lane = lax.broadcasted_iota(jnp.int32, here.shape, 2)
    z_minus = jnp.where(lane == 0, 0.0, pltpu.roll(here, 1, 2))
    z_plus = jnp.where(lane == up - 1, 0.0, pltpu.roll(here, up - 1, 2))
    laplace = (x_plus + x_minus) + (y_plus + y_minus) + (z_plus + z_minus) - 6.0 * here
    advect = (
        speeds[0] * (x_plus - x_minus)
        + speeds[1] * (y_plus - y_minus)
        + speeds[2] * (z_plus - z_minus)
    )
    return here + diffusivity * laplace - advect + jnp.stack(produced)


def rows_for_species(rows, species):
    return jnp.stack([jnp.broadcast_to(row, (species, row.shape[1])) for row in rows])


def own_speeds(flow, x, deep):
    return [[flow[d, x, pl.ds(y, 1), :] for y in range(deep)] for d in range(3)]


def planes_advanced(planes, here, x_beside, y_beside, rates, speeds, diffusivity, mix, emit, together=4):
    for at in range(0, len(planes), together):
        some = planes[at : at + together]
        cells, counts = [], []
        for x in some:
            made = sources(here(x), rates(x))
            counts.append((len(cells), len(cells) + len(made)))
            cells += made
        produced = reacted(cells, mix)
        for x, (start, end) in zip(some, counts):
            emit(
                x,
                advanced(
                    here(x), x_beside(x, 0), x_beside(x, 1), y_beside(x, 0), y_beside(x, 1),
                    speeds(x), diffusivity, produced[start:end],
                ),
            )


def block_kernel(shape, field, rates, flow, coefficients, mix_ref, out):
    wide, deep, species, up = shape

    def x_beside(x, side):
        at = x + 2 * side - 1
        return field[at] if 0 <= at < wide else jnp.zeros((deep, species, up), jnp.float32)

    def y_beside(x, side):
        here, none = field[x], jnp.zeros((1, species, up), jnp.float32)
        return jnp.concatenate([here[1:], none] if side else [none, here[:-1]], axis=0)

    def emit(x, plane):
        out[x] = plane

    planes_advanced(
        range(wide), lambda x: field[x], x_beside, y_beside, lambda x: rates[x],
        lambda x: [rows_for_species(speed, species) for speed in own_speeds(flow, x, deep)],
        coefficients[0][None], mix_ref[...], emit,
    )


def from_beyond(value, side, speed, diffusivity):
    across = speed * value
    return diffusivity * value - across if side else diffusivity * value + across


def finish(shape, refs, emit):
    wide, deep, species, up = shape
    own_ref, block, x_one, x_other, y_one, y_other, flow, coefficients = refs
    even_x, even_y = own_ref[0] == 1, own_ref[1] == 1
    diffusivity = coefficients[0][None]

    def row(d, x, y):
        return jnp.broadcast_to(flow[d, x, pl.ds(y, 1), :], (species, up))

    for x in range(wide):
        plane = block[x]
        before = jnp.where(even_y, y_other[x], y_one[x])
        after = jnp.where(even_y, y_one[x], y_other[x])
        before = from_beyond(before, 0, row(1, x, 0), diffusivity[0])
        after = from_beyond(after, 1, row(1, x, deep - 1), diffusivity[0])
        plane = jnp.concatenate(
            [(plane[0] + before)[None], plane[1:-1], (plane[-1] + after)[None]], axis=0
        )
        for side in range(2):
            if x == (wide - 1 if side else 0):
                one, other = (x_one, x_other) if side else (x_other, x_one)
                value = jnp.where(even_x, one[...], other[...])
                speed = rows_for_species(own_speeds(flow, x, deep)[0], species)
                plane = plane + from_beyond(value, side, speed, diffusivity)
        emit(x, plane)


def to_one_or_other(even, one, other, high, value):
    first = even if high else jnp.logical_not(even)

    @pl.when(first)
    def _():
        one[...] = value

    @pl.when(jnp.logical_not(first))
    def _():
        other[...] = value


def advance_kernel(shape, *refs):
    wide, deep, _, _ = shape
    own_ref, (out, x_one, x_other, y_one, y_other) = refs[0], refs[8:]
    even_x, even_y = own_ref[0] == 1, own_ref[1] == 1

    def emit(x, plane):
        out[x] = plane
        low, high = plane[0], plane[deep - 1]
        y_one[x] = jnp.where(even_y, high, low)
        y_other[x] = jnp.where(even_y, low, high)
        if x == 0:
            to_one_or_other(even_x, x_one, x_other, False, plane)
        if x == wide - 1:
            to_one_or_other(even_x, x_one, x_other, True, plane)

    finish(shape, refs[:8], emit)


def snapshot_kernel(shape, *refs):
    _, deep, species, _ = shape
    own_ref, flow, (out, y_one, y_other) = refs[0], refs[6], refs[8:]
    even_y = own_ref[1] == 1

    def emit(x, plane):
        out[x] = plane

        def others(y):
            rows = [flow[d, x, pl.ds(y, 1), :] for d in range(4)]
            return jnp.concatenate(rows * 2, axis=0)

        low = jnp.concatenate([plane[0], plane[1], others(0)], axis=0)
        high = jnp.concatenate([plane[deep - 1], plane[deep - 2], others(deep - 1)], axis=0)
        y_one[x] = jnp.where(even_y, high, low)
        y_other[x] = jnp.where(even_y, low, high)

    finish(shape, refs[:8], emit)


def wide_faces_kernel(shape, own_ref, field, y_one, y_other, flow, x_one, x_other):
    wide, deep, species, _ = shape
    even_x, even_y = own_ref[0] == 1, own_ref[1] == 1
    first, second = slice(0, species), slice(species, 2 * species)
    rest = slice(2 * species, 2 * species + 8)

    def face(outer, inner, out):
        for y in range(deep):
            out[y, first] = field[outer, y]
            out[y, second] = field[inner, y]
            rows = [flow[d, outer, y : y + 1, :] for d in range(4)]
            out[y, rest] = jnp.concatenate(rows * 2, axis=0)
        out[deep, first] = jnp.where(even_y, y_other[outer, first], y_one[outer, first])
        out[deep, second] = jnp.where(even_y, y_one[outer, first], y_other[outer, first])
        out[deep, rest] = jnp.zeros_like(out[deep, rest])

    @pl.when(even_x)
    def _():
        face(wide - 1, wide - 2, x_one)
        face(0, 1, x_other)

    @pl.when(jnp.logical_not(even_x))
    def _():
        face(0, 1, x_one)
        face(wide - 1, wide - 2, x_other)


def choose(even, one, other, side, at):
    first, second = (one, other) if side else (other, one)
    return jnp.where(even, first[at], second[at])


def rate_of(temperature, coefficients):
    return coefficients[1] * jnp.exp(coefficients[2] * (-1.0 / temperature))


def third_step_kernel(
    shape, counts, own_ref, block, field, y_one, y_other, rates, flow, coefficients, mix_ref,
    inner, middle,
):
    wide, deep, species, up = shape
    _, columns = counts
    even_y, column = own_ref[1] == 1, own_ref[3]
    inside = (column > 0, column < columns - 1)
    diffusivity, mix = coefficients[0][None], mix_ref[...]
    first, second = slice(0, species), slice(species, 2 * species)
    rest = slice(2 * species, 2 * species + 8)

    def beside(side, x, at):
        return choose(even_y, y_one, y_other, side, (x, at))

    def here(x):
        return jnp.stack([beside(0, x, first), beside(1, x, first)])

    def x_beside(x, side):
        at = x + 2 * side - 1
        return here(at) if 0 <= at < wide else jnp.zeros((2, species, up), jnp.float32)

    def y_beside(x, side):
        outer = beside(side, x, second)
        return jnp.stack([field[x, 0], outer] if side else [outer, field[x, deep - 1]])

    def other_rows(x):
        return [beside(side, x, rest) for side in range(2)]

    def emit(x, plane):
        inner[x, 0] = jnp.where(inside[0], plane[0], 0.0)
        inner[x, deep + 1] = jnp.where(inside[1], plane[1], 0.0)

    planes_advanced(
        range(wide), here, x_beside, y_beside,
        lambda x: jnp.stack(
            [rate_of(rows[3:4], coefficients) for rows in other_rows(x)]
        ),
        lambda x: [
            rows_for_species([rows[d : d + 1] for rows in other_rows(x)], species) for d in range(3)
        ],
        diffusivity, mix, emit, 16,
    )

    def row(x, y):
        return jnp.broadcast_to(flow[1, x, pl.ds(y, 1), :], (species, up))

    for x in range(wide):
        low = from_beyond(beside(0, x, first), 0, row(x, 0), diffusivity[0])
        high = from_beyond(beside(1, x, first), 1, row(x, deep - 1), diffusivity[0])
        inner[x, 1] = block[x, 0] + low
        inner[x, 2:deep] = block[x, 1 : deep - 1]
        inner[x, deep] = block[x, deep - 1] + high

    def emit_last(x, plane):
        middle[:, x - 2] = jnp.swapaxes(plane, 0, 1)

    planes_advanced(
        range(2, wide - 2),
        lambda x: inner[x, 1 : deep + 1],
        lambda x, side: inner[x + 2 * side - 1, 1 : deep + 1],
        lambda x, side: inner[x, 2 * side : 2 * side + deep],
        lambda x: rates[x],
        lambda x: [rows_for_species(speed, species) for speed in own_speeds(flow, x, deep)],
        diffusivity, mix, emit_last,
    )


def fourth_step_kernel(
    shape, counts, own_ref, inner, middle, field, x_one, x_other, y_one, y_other, rates, flow,
    coefficients, mix_ref, out, edge, x_sides,
):
    wide, deep, species, up = shape
    rows, _ = counts
    even_x, even_y, row = own_ref[0] == 1, own_ref[1] == 1, own_ref[2]
    inside = (row > 0, row < rows - 1)
    diffusivity, mix = coefficients[0][None], mix_ref[...]
    first, second = slice(0, species), slice(species, 2 * species)
    rest = slice(2 * species, 2 * species + 8)
    cells = slice(0, deep)

    out[:, 2 : wide - 2] = middle[...]

    def beside(side, at, of=cells):
        return choose(even_x, x_one, x_other, side, (of, at))

    def corners(side):
        return [beside(side, at, deep) for at in (first, second)]

    def last(side):
        return wide - 1 if side else 0

    def y_beside(side, to):
        here, corner = beside(side, first), corners(side)[to][None]
        return jnp.concatenate([here[1:], corner] if to else [corner, here[:-1]], axis=0)

    def other_rows(side):
        others = beside(side, rest)
        return [others[y] for y in range(deep)]

    def emit(side, plane):
        x_sides[side] = jnp.where(inside[side], plane, 0.0)

    planes_advanced(
        range(2), lambda side: beside(side, first),
        lambda side, to: beside(side, second) if side == to else field[last(side)],
        y_beside,
        lambda side: jnp.stack(
            [rate_of(rows[3:4], coefficients) for rows in other_rows(side)]
        ),
        lambda side: [
            rows_for_species([rows[d : d + 1] for rows in other_rows(side)], species)
            for d in range(3)
        ],
        diffusivity, mix, emit,
    )
    for side in range(2):
        x = last(side)
        low, high = corners(side)
        value = jnp.concatenate([low[None], beside(side, first), high[None]], axis=0)
        ends = [choose(even_y, y_one, y_other, to, (x, rest))[0:1] for to in range(2)]
        speed = rows_for_species([ends[0]] + own_speeds(flow, x, deep)[0] + [ends[1]], species)
        edge[side] = inner[x] + from_beyond(value, side, speed, diffusivity)

    def plane_of(x):
        if x < 0 or x >= wide:
            return x_sides[0 if x < 0 else 1]
        if x == 0 or x == wide - 1:
            return edge[0 if x == 0 else 1, 1 : deep + 1]
        return inner[x, 1 : deep + 1]

    def y_of(x, side):
        at = slice(2 * side, 2 * side + deep)
        return edge[0 if x == 0 else 1, at] if x in (0, wide - 1) else inner[x, at]

    def emit_last(x, plane):
        out[:, x] = jnp.swapaxes(plane, 0, 1)

    planes_advanced(
        [0, 1, wide - 2, wide - 1], plane_of, lambda x, side: plane_of(x + 2 * side - 1), y_of,
        lambda x: rates[x],
        lambda x: [rows_for_species(speed, species) for speed in own_speeds(flow, x, deep)],
        diffusivity, mix, emit_last,
    )


def project_kernel(shape, ranks, field, component, vertical, factor_rows, out):
    wide, deep, species, up = shape
    ranks_a, ranks_d = ranks
    each = deep + 2
    for y in range(deep):
        rows = field[:, y].reshape(wide * species, up)
        on_a = jnp.dot(component[...], rows, precision=HIGHEST, preferred_element_type=jnp.float32)
        on_d = lax.dot_general(
            vertical[...], on_a, (((1,), (1,)), ((), ())), precision=HIGHEST,
            preferred_element_type=jnp.float32,
        )
        out[pl.ds(y, ranks_d, stride=each), :] = on_d
    for row in range(2):
        out[pl.ds(deep + row, ranks_d, stride=each), :] = jnp.broadcast_to(
            factor_rows[row : row + 1], (ranks_d, 128)
        )


def core_kernel(counts, got, out):
    rows, columns, ranks_a, tall, deep = counts
    devices, each = rows * columns, deep + 2
    own = 128 // ranks_a

    def dot(a, b, contract, precision=HIGHEST):
        return lax.dot_general(
            a, b, ((contract[:1], contract[1:]), ((), ())), precision=precision,
            preferred_element_type=jnp.float32,
        )

    whole = jnp.concatenate(
        [
            jnp.concatenate(
                [got[pl.ds((row * columns + column) * each, deep), :] for column in range(columns)],
                axis=0,
            )
            for row in range(rows)
        ],
        axis=1,
    )

    def in_order(at, of_row):
        both = got[pl.ds(at, devices, stride=each), :]
        halves = jnp.concatenate([both[:, :64], both[:, 64:]], axis=0)
        pick = jnp.full((2 * devices, 2 * devices), 1.0, jnp.float32)
        return dot(where_equal(pick, of_row, lambda at: at), halves, (1, 0))

    east = in_order(deep, lambda at: at % 2 * devices + at // 2)
    north = in_order(
        deep + 1, lambda at: at % 2 * devices + at % deep // 2 * columns + at // deep
    )

    def by_rank(array):
        return jnp.concatenate(
            [
                jnp.concatenate(
                    [
                        array[(row * ranks_a + a) * own : (row * ranks_a + a + 1) * own]
                        for row in range(rows)
                    ],
                    axis=0,
                )
                for a in range(ranks_a)
            ],
            axis=1,
        )

    def by_row(parts):
        return jnp.concatenate(
            [
                parts[a][row * own : (row + 1) * own]
                for row in range(rows)
                for a in range(ranks_a)
            ],
            axis=0,
        ).T

    half = by_rank(dot(whole, north, (0, 0)))
    core = dot(east, half, (0, 0))
    half = dot(east, core, (1, 0))
    ranks_c = north.shape[1]
    split = [slice(a * ranks_c, (a + 1) * ranks_c) for a in range(ranks_a)]
    core = by_row([core[:, at] for at in split])
    whole = by_row([dot(half[:, at], north, (1, 1)) for at in split])
    for row in range(rows):
        for column in range(columns):
            at = row * columns + column
            out[at, 0:tall] = core[column * tall : (column + 1) * tall, row * 128 : (row + 1) * 128]
            out[at, tall : tall + deep] = whole[
                column * deep : (column + 1) * deep, row * 128 : (row + 1) * 128
            ]


def expand_kernel(shape, ranks, tall, got, field, wide_rows, vertical, residual, core, full):
    wide, deep, species, up = shape
    ranks_a, ranks_d = ranks
    each = tall + deep
    component = where_equal(
        jnp.concatenate([wide_rows[...]] * wide, axis=0),
        lambda at: at // species,
        lambda at: at % wide,
    )
    for y in range(deep):
        on_d = got[pl.ds(tall + y, ranks_d, stride=each), :]
        on_a = lax.dot_general(
            on_d, vertical[...], (((0,), (0,)), ((), ())), precision=HIGH,
            preferred_element_type=jnp.float32,
        )
        full[y] = jnp.dot(component, on_a, precision=HIGH, preferred_element_type=jnp.float32)
    for x in range(wide):
        residual[:, x] = jnp.swapaxes(
            field[x] - full[:, x * species : (x + 1) * species, :], 0, 1
        )
    turned = [got[pl.ds(c, ranks_d, stride=each), :].T for c in range(tall)]
    core[...] = jnp.swapaxes(jnp.stack(turned), 0, 1)


def swapped(one, other, axes):
    got = []
    for first, face in enumerate((one, other)):
        couples = [(i, i + 1) for i in range(first, lax.axis_size(axes) - 1, 2)]
        got.append(lax.ppermute(face, axes, couples + [(b, a) for a, b in couples]))
    return got


def faces_beside(faces):
    x_one, x_other, y_one, y_other = faces
    y_one, y_other = swapped(y_one, y_other, COLUMN)
    x_one, x_other = swapped(x_one, x_other, ROW)
    return x_one, x_other, y_one, y_other


def whole_factors(tucker_factor_east, tucker_factor_north):
    rows, columns = lax.axis_size(ROW), lax.axis_size(COLUMN)

    def shares(factor, holders, axes):
        count = -(-factor.shape[0] // holders)
        padded = jnp.pad(factor, ((0, count * holders - factor.shape[0]), (0, 0)))
        return lax.dynamic_slice_in_dim(padded, lax.axis_index(axes) * count, count, 0)

    east = shares(tucker_factor_east, columns, COLUMN)
    north = shares(tucker_factor_north, rows, ROW)
    sent = jnp.concatenate([east.reshape(-1), north.reshape(-1)])
    sent = jnp.pad(sent, (0, -sent.size % 128)).reshape(1, -1, 128)
    sent = jnp.broadcast_to(sent, (rows * columns,) + sent.shape[1:])
    got = lax.all_to_all(sent, EVERY, 0, 0, tiled=True).reshape(rows, columns, -1)
    whole_east = got[:, :, : east.size].reshape(rows, -1, east.shape[1])
    whole_east = whole_east[:, : tucker_factor_east.shape[0]].reshape(-1, east.shape[1])
    whole_north = got[:, :, east.size : east.size + north.size]
    whole_north = whole_north.reshape(rows, columns, *north.shape).transpose(1, 0, 2, 3)
    whole_north = whole_north.reshape(columns, -1, north.shape[1])
    whole_north = whole_north[:, : tucker_factor_north.shape[0]].reshape(-1, north.shape[1])
    return whole_east, whole_north


def compress_and_expand(snapshot, east, north, vertical, component):
    rows, columns = lax.axis_size(ROW), lax.axis_size(COLUMN)
    devices = rows * columns
    (wide, deep, _, _), (_, ranks_a) = snapshot.shape, component.shape
    ranks_d = vertical.shape[1]
    ranks_b, ranks_c = east.shape[1], north.shape[1]
    projected = jnp.einsum("xysz,sa->xyaz", snapshot, component, precision=HIGHEST)
    projected = jnp.einsum("xyaz,zd->dyxa", projected, vertical, precision=HIGHEST)
    pairs = ranks_a * ranks_d
    share = -(-pairs // devices)
    flat = jnp.transpose(projected, (0, 3, 1, 2)).reshape(pairs, deep, wide)
    flat = jnp.pad(flat, ((0, share * devices - pairs), (0, 0), (0, 0)))
    flat = flat.reshape(devices, share, deep, wide).transpose(0, 2, 3, 1)
    flat = lax.all_to_all(
        flat.reshape(devices, deep, wide * share), EVERY, 0, 0, tiled=True
    )
    whole = flat.reshape(rows, columns * deep, wide, share)
    part = jnp.einsum("gyxp,yc->cgxp", whole, north, precision=HIGHEST)
    part = part.reshape(ranks_c, rows * wide, share)
    core = jnp.einsum("cxp,xb->cbp", part, east, precision=HIGHEST)
    part = jnp.einsum("cbp,xb->cxp", core, east, precision=HIGHEST)
    whole = jnp.einsum("cxp,yc->yxp", part, north, precision=HIGHEST)
    own_b, own_c = ranks_b // rows, ranks_c // columns

    def pieces(array, tall, broad):
        array = array.reshape(columns, tall, rows, broad, share)
        return array.transpose(2, 0, 1, 3, 4).reshape(devices, tall * broad * share)

    sent = jnp.concatenate([pieces(core, own_c, own_b), pieces(whole, deep, wide)], axis=1)
    sent = jnp.pad(sent, ((0, 0), (0, -sent.shape[1] % 1024)))
    got = lax.all_to_all(
        sent.reshape(devices, -1, 128), EVERY, 0, 0, tiled=True
    ).reshape(devices, -1)

    def ranks_together(array, tall, broad):
        array = array.reshape(devices, tall, broad, share).transpose(0, 3, 2, 1)
        array = array.reshape(devices * share, broad, tall)[:pairs]
        return array.reshape(ranks_d, ranks_a, broad, tall)

    core_size = own_c * own_b * share
    core = ranks_together(got[:, :core_size], own_c, own_b).transpose(1, 2, 3, 0)
    expanded = ranks_together(got[:, core_size : core_size + deep * wide * share], deep, wide)
    expanded = jnp.einsum("daxy,zd->axyz", expanded, vertical, precision=HIGHEST)
    expanded = jnp.einsum("axyz,sa->sxyz", expanded, component, precision=HIGHEST)
    return core, snapshot.transpose(2, 0, 1, 3) - expanded


def body(
    mixture_fields_initial,
    flow_speed_vector,
    thermal_field,
    mass_diffusivity,
    arrhenius_constant,
    arrhenius_energy_temp,
    production_coefficients,
    tucker_factor_east,
    tucker_factor_north,
    tucker_factor_vertical,
    tucker_factor_component,
):
    species, wide, deep, up = mixture_fields_initial.shape
    shape = (wide, deep, species, up)
    cells = wide * deep * species * up
    rows, columns = lax.axis_size(ROW), lax.axis_size(COLUMN)
    devices = rows * columns
    ranks_a, ranks_d = tucker_factor_component.shape[1], tucker_factor_vertical.shape[1]
    ranks_b, ranks_c = tucker_factor_east.shape[1], tucker_factor_north.shape[1]
    own_b, own_c = ranks_b // rows, ranks_c // columns
    kernels_fit = (
        ranks_d == devices
        and wide * ranks_a == 128
        and own_b * ranks_a == 128
        and deep == own_c == 8
        and ranks_b == ranks_c == 64
        and wide == 2 * columns
        and deep == 2 * rows
    )

    row, column = lax.axis_index(ROW), lax.axis_index(COLUMN)
    own = jnp.stack([1 - row % 2, 1 - column % 2, row, column]).astype(jnp.int32)
    face_shapes = [(deep, species, up)] * 2 + [(wide, species, up)] * 2
    field_rows = mixture_fields_initial.reshape(species * wide * deep, up)
    faces = vmem_call(functools.partial(faces_kernel, shape), face_shapes, 1, 2)(own, field_rows)
    faces = faces_beside(faces)
    both = 16
    out_shapes = [
        shape, shape, (4, wide, deep, up), (3, species, up), (both * species,) * 2,
        (wide * ranks_a, wide * species), (species, wide * ranks_a), (ranks_d, up),
    ] + [(2, 128)] * kernels_fit
    small = (
        flow_speed_vector, thermal_field, mass_diffusivity[None], arrhenius_constant[None],
        arrhenius_energy_temp[None], production_coefficients,
        tucker_factor_component.T, tucker_factor_vertical.T, tucker_factor_east,
        tucker_factor_north,
    )
    vmem, smem = (pl.BlockSpec(memory_space=space) for space in (pltpu.VMEM, pltpu.SMEM))
    (field, rates, speeds, coefficients, mix, squeeze, wide_rows, upright,
     *factor_rows) = pl.pallas_call(
        functools.partial(prepare_kernel, shape, (ranks_a, ranks_d)),
        in_specs=[smem, vmem] + [pl.BlockSpec(memory_space=pltpu.HBM)] * len(small),
        out_specs=[vmem] * len(out_shapes),
        out_shape=[jax.ShapeDtypeStruct(out, jnp.float32) for out in out_shapes],
        scratch_shapes=[pltpu.VMEM(array.shape, jnp.float32) for array in small]
        + [pltpu.SemaphoreType.DMA((len(small),))],
        compiler_params=pltpu.CompilerParams(vmem_limit_bytes=VMEM_LIMIT),
        cost_estimate=pl.CostEstimate(
            flops=4 * cells, bytes_accessed=12 * cells, transcendentals=cells
        ),
    )(
        own, mixture_fields_initial,
        *(pltpu.with_memory_space_constraint(array, pltpu.HBM) for array in small),
    )
    block = vmem_call(
        functools.partial(block_kernel, shape), [shape], 0, 5, flops=60 * cells, moved=8 * cells
    )
    advance = vmem_call(
        functools.partial(advance_kernel, shape), [shape] + face_shapes, 1, 8,
        flops=4 * cells, moved=8 * cells,
    )
    fixed = (rates, speeds, coefficients, mix)
    for substep in range(SUB - 1):
        field, *faces = advance(
            own, *block(field, *fixed), *faces, speeds, coefficients
        )
        faces = faces_beside(faces)
    high = 2 * species + 8
    snapshot, *y_faces = vmem_call(
        functools.partial(snapshot_kernel, shape), [shape] + [(wide, high, up)] * 2, 1, 8,
        flops=4 * cells, moved=8 * cells,
    )(own, *block(field, *fixed), *faces, speeds, coefficients)
    y_faces = swapped(*y_faces, COLUMN)
    x_faces = vmem_call(
        functools.partial(wide_faces_kernel, shape), [(deep + 1, high, up)] * 2, 1, 5,
        flops=cells, moved=cells,
    )(own, snapshot, *y_faces, speeds)
    x_faces = swapped(*x_faces, ROW)
    inner, middle = vmem_call(
        functools.partial(third_step_kernel, shape, (rows, columns)),
        [(wide, deep + 2, species, up), (species, wide - 4, deep, up)], 1, 9,
        flops=120 * cells, moved=16 * cells,
    )(own, *block(snapshot, *fixed), snapshot, *y_faces, *fixed)
    if kernels_fit:
        (sent,) = vmem_call(
            functools.partial(project_kernel, shape, (ranks_a, ranks_d)),
            [(devices * (deep + 2), 128)], 0, 4, flops=60 * cells, moved=4 * cells,
        )(snapshot, squeeze, upright, *factor_rows)
        got = lax.all_to_all(
            sent.reshape(devices, (deep + 2) // 2, 2, 128), EVERY, 0, 0, tiled=True
        )
        (sent,) = vmem_call(
            functools.partial(core_kernel, (rows, columns, ranks_a, own_c, deep)),
            [(devices, own_c + deep, 128)], 0, 1, flops=60 * cells, moved=4 * cells,
        )(got.reshape(devices * (deep + 2), 128))
        got = lax.all_to_all(sent, EVERY, 0, 0, tiled=True)
        residual, tucker_core = vmem_call(
            functools.partial(expand_kernel, shape, (ranks_a, ranks_d), own_c),
            [mixture_fields_initial.shape, (ranks_a * own_b, own_c, ranks_d)], 0, 4,
            flops=60 * cells, moved=8 * cells, scratch=[(deep, wide * species, up)],
        )(
            got.reshape(devices * (own_c + deep), 128),
            snapshot,
            wide_rows,
            upright,
        )
        tucker_core = tucker_core.reshape(ranks_a, own_b, own_c, ranks_d)
    else:
        east, north = whole_factors(tucker_factor_east, tucker_factor_north)
        tucker_core, residual = compress_and_expand(
            snapshot, east, north, tucker_factor_vertical, tucker_factor_component
        )
    own_last, _ = lax.optimization_barrier((own, tucker_core))
    (mixture_fields_final,) = vmem_call(
        functools.partial(fourth_step_kernel, shape, (rows, columns)),
        [mixture_fields_initial.shape], 1, 12,
        flops=60 * cells, moved=8 * cells,
        scratch=[(2, deep + 2, species, up), (2, deep, species, up)],
    )(own_last, inner, middle, snapshot, *x_faces, *y_faces, *fixed)
    return (mixture_fields_final, residual, tucker_core)


def solution(mesh):
    in_specs = (
        P(None, "gx", ("gy", "ga"), None),
        P(None, "gx", ("gy", "ga"), None),
        P("gx", ("gy", "ga"), None),
        P(),
        P(),
        P(),
        P(),
        P("gx", None),
        P(("gy", "ga"), None),
        P(),
        P(),
    )
    out_specs = (
        P(None, "gx", ("gy", "ga"), None),
        P(None, "gx", ("gy", "ga"), None),
        P(None, "gx", ("gy", "ga"), None),
    )
    return jax.shard_map(body, mesh=mesh, in_specs=in_specs, out_specs=out_specs, check_vma=False)
```

time: 81.7 us -> 72.6 us (0.89)
  starting transfers between devices: 47.9 us -> 37.6 us
  Pallas kernels: 20.6 us -> 23.2 us
  waiting for transfers between devices: 6.43 us -> 5.05 us
    ppermute x16 -> x12, starting transfers between devices: 38.9 us -> 28.5 us  [swapped(): got.append(lax.ppermute(face, axes, couples + [(b, a) for a, b in couples]))]
    pallas_call x6 -> x9, Pallas kernels: 11.1 us -> 14.3 us  [the longest x2 2.7 us: body(): block(field, *fixed)]
    ppermute x16 -> x12, waiting for transfers between devices: 6.42 us -> 3.61 us  [swapped(): got.append(lax.ppermute(face, axes, couples + [(b, a) for a, b in couples]))]
    all_to_all x1, waiting for transfers between devices: 0.01 us -> 1.44 us  [body(): lax.all_to_all(sent.reshape(devices, (deep + 2) // 2, 2, 128), EVERY, 0,...]
    pallas_call x1, Pallas kernels: 2.47 us -> 3.53 us  [body(): vmem_call(functools.partial(expand_kernel, shape, (ranks_a, ranks_d), own...]
    unnamed x29 -> x14, local copies, waits for them, and re-layouts: 4.07 us -> 5.04 us
    pallas_call x1, Pallas kernels: 2.91 us -> 1.94 us  [body(): vmem_call(functools.partial(core_kernel, (rows, columns, ranks_a, own_c,...]
  transfers between devices with their start and end apart: 18 -> 14, of which waited for: 4 -> 3; matrix products, arithmetic and copies ran while one was open for 0% -> 0% of each run, Pallas kernels for 9% -> 21%
where the time goes in v3:
time: 72.6 us; the launch traced here: 71.8 us
  starting transfers between devices  37.6 us (52%)
  Pallas kernels  23.2 us (32%)
  waiting for transfers between devices  5.05 us (7%)
  local copies, waits for them, and re-layouts  5.04 us (7%)
  between operations  0.88 us (1%)
    ppermute x12, starting transfers between devices, swapped(): got.append(lax.ppermute(face, axes, couples + [(b, a) for a, b in couples]))  28.5 us
    unnamed x14, local copies, waits for them, and re-layouts  5.04 us
    all_to_all x1, starting transfers between devices, body(): got = lax.all_to_all(sent, EVERY, 0, 0, tiled=True)  4.91 us
    all_to_all x1, starting transfers between devices, body(): lax.all_to_all(sent.reshape(devices, (deep + 2) // 2, 2, 128), EVERY, 0,...  4.18 us
    ppermute x12, waiting for transfers between devices, swapped(): got.append(lax.ppermute(face, axes, couples + [(b, a) for a, b in couples]))  3.61 us
    pallas_call x1, Pallas kernels, body(): vmem_call(functools.partial(expand_kernel, shape, (ranks_a, ranks_d), own...  3.53 us
    pallas_call x2, Pallas kernels, body(): block(field, *fixed)  2.7 us
    pallas_call x1, Pallas kernels, body(): vmem_call(functools.partial(project_kernel, shape, (ranks_a, ranks_d)), [...  2.69 us
  transfers between devices with their start and end apart: 14, of which 3 were waited for; matrix products, arithmetic and copies ran while one was open for 0% of the time, Pallas kernels for 21%

profile of v3, /device:TPU:3, one launch (start us, length us, event | category | flops | bytes accessed | tf_op | source)
XLA Modules:
  0.0 71.8 jit_solution(17306392906337220736)
XLA Ops:
  0.7 1.2 %copy-done = f32[16,16,8,128]{3,2,1,0:T(8,128)S(1)} copy-done((f32[16,16,8,128]{3,2,1,0:T(8,128)S(1)}, f32[16,16,8,128]{3,2,1,0:T(8,128)}, u32[]{:S(2)}) %copy-start) | copy-done | bytes 1048600
  2.7 1.4 %collective-permute-start.2 = (f32[16,16,128]{2,1,0:T(8,128)S(1)}, f32[16,16,128]{2,1,0:T(8,128)S(1)}, u32[]{:S(2)}, u32[]{:S(2)}) collective-permute-start(f32[16,16,128]{2,1,0:T(8,128)S(1)} %get-tuple-element.38), channel_id=1, source_target_pairs={{0,1},{2,3},{4,5},{6,7},{1,0},{3,2},{5,4},{7,6},{8,9},{10,11},{12,... | collective-permute-start | bytes 393224 | tf_op jit(solution)/shard_map/ppermute | solution.py:604
  4.1 4.9 %collective-permute-start.3 = (f32[16,16,128]{2,1,0:T(8,128)S(1)}, f32[16,16,128]{2,1,0:T(8,128)S(1)}, u32[]{:S(2)}, u32[]{:S(2)}) collective-permute-start(f32[16,16,128]{2,1,0:T(8,128)S(1)} %get-tuple-element.39), channel_id=1, source_target_pairs={{1,2},{3,4},{5,6},{2,1},{4,3},{6,5},{9,10},{11,12},{13,14},{10,9},... | collective-permute-start | bytes 393224 | tf_op jit(solution)/shard_map/ppermute | solution.py:604
  9.3 4.1 %collective-permute-start.1 = (f32[8,16,128]{2,1,0:T(8,128)S(1)}, f32[8,16,128]{2,1,0:T(8,128)S(1)}, u32[]{:S(2)}, u32[]{:S(2)}) collective-permute-start(f32[8,16,128]{2,1,0:T(8,128)S(1)} %get-tuple-element.37), channel_id=1, source_target_pairs={{8,16},{16,8},{9,17},{17,9},{10,18},{18,10},{11,19},{19,11},{12,20... | collective-permute-start | bytes 196616 | tf_op jit(solution)/shard_map/ppermute | solution.py:604
  13.4 2.0 %shard_map.130 = (f32[16,8,16,128]{3,2,1,0:T(8,128)S(1)}, f32[16,8,16,128]{3,2,1,0:T(8,128)S(1)}, f32[4,16,8,128]{3,2,1,0:T(8,128)S(1)}, f32[3,16,128]{2,1,0:T(8...) custom-call(s32[4]{0:T(128)S(1)} %pad_add_fusion.own_ref.even_ref.re, ...), custom_call_target="tpu_custom_call" | custom-call | flops 1048576 | bytes 3145728 | tf_op jit(solution)/shard_map/pallas_call | solution.py:735
  15.4 1.4 %shard_map.131.refs_1_ = f32[16,8,16,128]{3,2,1,0:T(8,128)S(1)} custom-call(f32[16,8,16,128]{3,2,1,0:T(8,128)S(1)} %get-tuple-element.31.field, f32[16,8,16,128]{3,2,1,0:T(8,128)S(1)} %get-tuple-element.32.rates, f32[4,16,8,128]{3,2,1,0:T(8,128)S(1)} %get-tuple-element.33.flow.refs_6_, f32[3,16,128]{2,1,0:T(8,128)S(1)} %get-tuple-element.34.coefficients.refs_7_, ...), custom_call_target="tpu_custom_call" | custom-call | flops 15728640 | bytes 2097152 | tf_op jit(solution)/shard_map/pallas_call | solution.py:760
  17.5 4.0 %collective-permute-start.7 = (f32[16,16,128]{2,1,0:T(8,128)S(1)}, f32[16,16,128]{2,1,0:T(8,128)S(1)}, u32[]{:S(2)}, u32[]{:S(2)}) collective-permute-start(f32[16,16,128]{2,1,0:T(8,128)S(1)} %get-tuple-element.44), channel_id=1, source_target_pairs={{1,2},{3,4},{5,6},{2,1},{4,3},{6,5},{9,10},{11,12},{13,14},{10,9},... | collective-permute-start | bytes 393224 | tf_op jit(solution)/shard_map/ppermute | solution.py:604
  21.6 3.4 %collective-permute-start.5 = (f32[8,16,128]{2,1,0:T(8,128)S(1)}, f32[8,16,128]{2,1,0:T(8,128)S(1)}, u32[]{:S(2)}, u32[]{:S(2)}) collective-permute-start(f32[8,16,128]{2,1,0:T(8,128)S(1)} %get-tuple-element.42), channel_id=1, source_target_pairs={{8,16},{16,8},{9,17},{17,9},{10,18},{18,10},{11,19},{19,11},{12,20... | collective-permute-start | bytes 196616 | tf_op jit(solution)/shard_map/ppermute | solution.py:604
  25.1 1.4 %shard_map.134.refs_1_ = f32[16,8,16,128]{3,2,1,0:T(8,128)S(1)} custom-call(f32[16,8,16,128]{3,2,1,0:T(8,128)S(1)} %get-tuple-element.40.field, f32[16,8,16,128]{3,2,1,0:T(8,128)S(1)} %get-tuple-element.32.rates, f32[4,16,8,128]{3,2,1,0:T(8,128)S(1)} %get-tuple-element.33.flow.refs_6_, f32[3,16,128]{2,1,0:T(8,128)S(1)} %get-tuple-element.34.coefficients.refs_7_, ...), custom_call_target="tpu_custom_call" | custom-call | flops 15728640 | bytes 2097152 | tf_op jit(solution)/shard_map/pallas_call | solution.py:767
  27.6 1.4 %shard_map.135 = (f32[16,8,16,128]{3,2,1,0:T(8,128)S(1)}, f32[16,40,128]{2,1,0:T(8,128)}, f32[16,40,128]{2,1,0:T(8,128)S(1)}) custom-call(s32[4]{0:T(128)S(1)} %pad_add_fusion.own_ref.even_ref.refs_0_, f32[16,8,16,128]{3,2,1,0:T(8,128)S(1)} %shard_map.134.refs_1_, f32[8,16,128]{2,1,0:T(8,128)S(1)} %collective-permute-done.4.refs_2_, ...), custom_call_target="tpu_custom_call" | custom-call | flops 1048576 | bytes 2097152 | tf_op jit(solution)/shard_map/pallas_call | solution.py:764
  29.0 2.7 %shard_map.136 = f32[320,128]{1,0:T(8,128)} custom-call(f32[16,8,16,128]{3,2,1,0:T(8,128)S(1)} %get-tuple-element.45.field, f32[128,256]{1,0:T(8,128)S(1)} %get-tuple-element.46.component, f32[32,128]{1,0:T(8,128)S(1)} %get-tuple-element.47.vertical, f32[2,128]{1,0:T(2,128)S(1)} %get-tuple-element.48.factor_rows), custom_call_target="tpu_custom_call" | custom-call | flops 15728640 | bytes 1048576 | tf_op jit(solution)/shard_map/pallas_call | solution.py:780
  31.7 4.2 %all-to-all-start = ((f32[32,5,2,128]{3,2,1,0:T(2,128)}), f32[32,5,2,128]{3,2,1,0:T(2,128)S(1)}, u32[]{:S(2)}, u32[]{:S(2)}) async-start(f32[32,5,2,128]{3,2,1,0:T(2,128)} %bitcast.10), calls=%async_computation | async-start | bytes 327680 | tf_op jit(solution)/shard_map/all_to_all | solution.py:784
  35.9 1.3 %collective-permute-start.8 = (f32[16,40,128]{2,1,0:T(8,128)}, f32[16,40,128]{2,1,0:T(8,128)S(1)}, u32[]{:S(2)}, u32[]{:S(2)}) collective-permute-start(f32[16,40,128]{2,1,0:T(8,128)} %get-tuple-element.52), channel_id=1, source_target_pairs={{0,1},{2,3},{4,5},{6,7},{1,0},{3,2},{5,4},{7,6},{8,9},{10,11},{12,... | collective-permute-start | bytes 983048 | tf_op jit(solution)/shard_map/ppermute | solution.py:604
  37.1 4.5 %collective-permute-start.9 = (f32[16,40,128]{2,1,0:T(8,128)}, f32[16,40,128]{2,1,0:T(8,128)S(1)}, u32[]{:S(2)}, u32[]{:S(2)}) collective-permute-start(f32[16,40,128]{2,1,0:T(8,128)} %copy-done.6), channel_id=1, source_target_pairs={{1,2},{3,4},{5,6},{2,1},{4,3},{6,5},{9,10},{11,12},{13,14},{10,9},... | collective-permute-start | bytes 983048 | tf_op jit(solution)/shard_map/ppermute | solution.py:604
  41.6 1.4 %all-to-all-done = f32[32,5,2,128]{3,2,1,0:T(2,128)S(1)} async-done(((f32[32,5,2,128]{3,2,1,0:T(2,128)}), f32[32,5,2,128]{3,2,1,0:T(2,128)S(1)}, u32[]{:S(2)}, u32[]{:S(2)}) %all-to-all-start) | async-done | bytes 163872 | tf_op jit(solution)/shard_map/all_to_all | solution.py:784
  43.1 1.9 %shard_map.137 = f32[32,16,128]{2,1,0:T(8,128)S(1)} custom-call(f32[320,128]{1,0:T(8,128)S(1)} %bitcast.15), custom_call_target="tpu_custom_call" | custom-call | flops 15728640 | bytes 1048576 | tf_op jit(solution)/shard_map/pallas_call | solution.py:787
  45.8 4.9 %all-to-all-start.1 = ((f32[32,16,128]{2,1,0:T(8,128)}), f32[32,16,128]{2,1,0:T(8,128)}, u32[]{:S(2)}, u32[]{:S(2)}) async-start(f32[32,16,128]{2,1,0:T(8,128)} %copy-done.3), calls=%async_computation.1 | async-start | bytes 524288 | tf_op jit(solution)/shard_map/all_to_all | solution.py:791
  50.7 2.5 %collective-permute-done.9.y_other = f32[16,40,128]{2,1,0:T(8,128)S(1)} collective-permute-done((f32[16,40,128]{2,1,0:T(8,128)}, f32[16,40,128]{2,1,0:T(8,128)S(1)}, u32[]{:S(2)}, u32[]{:S(2)}) %collective-permute-start.9) | collective-permute-done | bytes 327712 | tf_op jit(solution)/shard_map/ppermute | solution.py:604
  53.1 1.3 %shard_map.141 = (f32[9,40,128]{2,1,0:T(8,128)}, f32[9,40,128]{2,1,0:T(8,128)}) custom-call(s32[4]{0:T(128)S(1)} %pad_add_fusion.own_ref.even_ref.refs_0_, f32[16,8,16,128]{3,2,1,0:T(8,128)S(1)} %get-tuple-element.45.field, f32[16,40,128]{2,1,0:T(8,128)S(1)} %collective-permute-done.8.y_one, f32[16,40,128]{2,1,0:T(8,128)S(1)} %collective-permute-done.9.y_other, ...), custom_call_target="tpu_custom_call" | custom-call | flops 262144 | bytes 262144 | tf_op jit(solution)/shard_map/pallas_call | solution.py:769
  54.7 4.2 %collective-permute-start.11 = (f32[9,40,128]{2,1,0:T(8,128)}, f32[9,40,128]{2,1,0:T(8,128)}, u32[]{:S(2)}, u32[]{:S(2)}) collective-permute-start(f32[9,40,128]{2,1,0:T(8,128)} %get-tuple-element.57), channel_id=1, source_target_pairs={{8,16},{16,8},{9,17},{17,9},{10,18},{18,10},{11,19},{19,11},{12,20... | collective-permute-start | bytes 552968 | tf_op jit(solution)/shard_map/ppermute | solution.py:604
  59.0 1.3 %shard_map.139.block = f32[16,8,16,128]{3,2,1,0:T(8,128)S(1)} custom-call(f32[16,8,16,128]{3,2,1,0:T(8,128)S(1)} %get-tuple-element.45.field, f32[16,8,16,128]{3,2,1,0:T(8,128)S(1)} %get-tuple-element.32.rates, f32[4,16,8,128]{3,2,1,0:T(8,128)S(1)} %get-tuple-element.33.flow.refs_6_, f32[3,16,128]{2,1,0:T(8,128)S(1)} %get-tuple-element.34.coefficients.refs_7_, ...), custom_call_target="tpu_custom_call" | custom-call | flops 15728640 | bytes 2097152 | tf_op jit(solution)/shard_map/pallas_call | solution.py:778
  60.3 2.2 %shard_map.140 = (f32[16,10,16,128]{3,2,1,0:T(8,128)S(1)}, f32[16,12,8,128]{3,2,1,0:T(8,128)S(1)}) custom-call(s32[4]{0:T(128)S(1)} %pad_add_fusion.own_ref.even_ref.refs_0_, f32[16,8,16,128]{3,2,1,0:T(8,128)S(1)} %shard_map.139.block, f32[16,8,16,128]{3,2,1,0:T(8,128)S(1)} %get-tuple-element.45.field, f32[16,40,128]{2,1,0:T(8,128)S(1)} %collective-permute-done.8.y_one, ...), custom_call_target="tpu_custom_call" | custom-call | flops 31457280 | bytes 4194304 | tf_op jit(solution)/shard_map/pallas_call | solution.py:774
  64.5 3.5 %shard_map.138 = (f32[16,16,8,128]{3,2,1,0:T(8,128)}, f32[128,8,32]{2,1,0:T(8,128)}) custom-call(f32[512,128]{1,0:T(8,128)} %bitcast.12.got, f32[16,8,16,128]{3,2,1,0:T(8,128)S(1)} %get-tuple-element.45.field, f32[16,128]{1,0:T(8,128)S(1)} %get-tuple-element.49.wide_rows, f32[32,128]{1,0:T(8,128)S(1)} %get-tuple-element.47.vertical), custom_call_target="tpu_custom_call" | custom-call | flops 15728640 | bytes 2097152 | tf_op jit(solution)/shard_map/pallas_call | solution.py:792
  69.2 2.6 %shard_map.142 = f32[16,16,8,128]{3,2,1,0:T(8,128)} custom-call(s32[4]{0:T(128)S(1)} %pad_add_fusion.own_ref.even_ref.refs_0_, f32[16,10,16,128]{3,2,1,0:T(8,128)S(1)} %copy-done.2, f32[16,12,8,128]{3,2,1,0:T(8,128)S(1)} %copy-done.5, f32[16,8,16,128]{3,2,1,0:T(8,128)S(1)} %get-tuple-element.45.field, f32[9,40,128]{2,1,0:T(8,128)S(1)} %collective-permute-done.10.x_one, ...), custom_call_target="tpu_custom_call" | custom-call | flops 15728640 | bytes 2097152 | tf_op jit(solution)/shard_map/pallas_call | solution.py:809
  (32 shorter events, 7.2 us)
Async XLA Ops:
  0.7 1.2 %copy-start = (f32[16,16,8,128]{3,2,1,0:T(8,128)S(1)}, f32[16,16,8,128]{3,2,1,0:T(8,128)}, u32[]{:S(2)}) copy-start(f32[16,16,8,128]{3,2,1,0:T(8,128)} %given.1) | copy-start | bytes 3145732
  2.7 14.0 %collective-permute-start.2 = (f32[16,16,128]{2,1,0:T(8,128)S(1)}, f32[16,16,128]{2,1,0:T(8,128)S(1)}, u32[]{:S(2)}, u32[]{:S(2)}) collective-permute-start(f32[16,16,128]{2,1,0:T(8,128)S(1)} %get-tuple-element.38), channel_id=1, source_target_pairs={{0,1},{2,3},{4,5},{6,7},{1,0},{3,2},{5,4},{7,6},{8,9},{10,11},{12,... | collective-permute-start | bytes 393224 | tf_op jit(solution)/shard_map/ppermute | solution.py:604
  4.1 12.7 %collective-permute-start.3 = (f32[16,16,128]{2,1,0:T(8,128)S(1)}, f32[16,16,128]{2,1,0:T(8,128)S(1)}, u32[]{:S(2)}, u32[]{:S(2)}) collective-permute-start(f32[16,16,128]{2,1,0:T(8,128)S(1)} %get-tuple-element.39), channel_id=1, source_target_pairs={{1,2},{3,4},{5,6},{2,1},{4,3},{6,5},{9,10},{11,12},{13,14},{10,9},... | collective-permute-start | bytes 393224 | tf_op jit(solution)/shard_map/ppermute | solution.py:604
  9.0 7.7 %collective-permute-start = (f32[8,16,128]{2,1,0:T(8,128)S(1)}, f32[8,16,128]{2,1,0:T(8,128)S(1)}, u32[]{:S(2)}, u32[]{:S(2)}) collective-permute-start(f32[8,16,128]{2,1,0:T(8,128)S(1)} %get-tuple-element.36), channel_id=1, source_target_pairs={{0,8},{16,24},{8,0},{24,16},{1,9},{17,25},{9,1},{25,17},{2,10},{18... | collective-permute-start | bytes 196616 | tf_op jit(solution)/shard_map/ppermute | solution.py:604
  9.3 7.4 %collective-permute-start.1 = (f32[8,16,128]{2,1,0:T(8,128)S(1)}, f32[8,16,128]{2,1,0:T(8,128)S(1)}, u32[]{:S(2)}, u32[]{:S(2)}) collective-permute-start(f32[8,16,128]{2,1,0:T(8,128)S(1)} %get-tuple-element.37), channel_id=1, source_target_pairs={{8,16},{16,8},{9,17},{17,9},{10,18},{18,10},{11,19},{19,11},{12,20... | collective-permute-start | bytes 196616 | tf_op jit(solution)/shard_map/ppermute | solution.py:604
  17.5 10.1 %collective-permute-start.6 = (f32[16,16,128]{2,1,0:T(8,128)S(1)}, f32[16,16,128]{2,1,0:T(8,128)S(1)}, u32[]{:S(2)}, u32[]{:S(2)}) collective-permute-start(f32[16,16,128]{2,1,0:T(8,128)S(1)} %get-tuple-element.43), channel_id=1, source_target_pairs={{0,1},{2,3},{4,5},{6,7},{1,0},{3,2},{5,4},{7,6},{8,9},{10,11},{12,... | collective-permute-start | bytes 393224 | tf_op jit(solution)/shard_map/ppermute | solution.py:604
  17.5 10.0 %collective-permute-start.7 = (f32[16,16,128]{2,1,0:T(8,128)S(1)}, f32[16,16,128]{2,1,0:T(8,128)S(1)}, u32[]{:S(2)}, u32[]{:S(2)}) collective-permute-start(f32[16,16,128]{2,1,0:T(8,128)S(1)} %get-tuple-element.44), channel_id=1, source_target_pairs={{1,2},{3,4},{5,6},{2,1},{4,3},{6,5},{9,10},{11,12},{13,14},{10,9},... | collective-permute-start | bytes 393224 | tf_op jit(solution)/shard_map/ppermute | solution.py:604
  21.6 4.9 %collective-permute-start.4 = (f32[8,16,128]{2,1,0:T(8,128)S(1)}, f32[8,16,128]{2,1,0:T(8,128)S(1)}, u32[]{:S(2)}, u32[]{:S(2)}) collective-permute-start(f32[8,16,128]{2,1,0:T(8,128)S(1)} %get-tuple-element.41), channel_id=1, source_target_pairs={{0,8},{16,24},{8,0},{24,16},{1,9},{17,25},{9,1},{25,17},{2,10},{18... | collective-permute-start | bytes 196616 | tf_op jit(solution)/shard_map/ppermute | solution.py:604
  21.6 5.9 %collective-permute-start.5 = (f32[8,16,128]{2,1,0:T(8,128)S(1)}, f32[8,16,128]{2,1,0:T(8,128)S(1)}, u32[]{:S(2)}, u32[]{:S(2)}) collective-permute-start(f32[8,16,128]{2,1,0:T(8,128)S(1)} %get-tuple-element.42), channel_id=1, source_target_pairs={{8,16},{16,8},{9,17},{17,9},{10,18},{18,10},{11,19},{19,11},{12,20... | collective-permute-start | bytes 196616 | tf_op jit(solution)/shard_map/ppermute | solution.py:604
  29.0 2.7 %copy-start.6 = (f32[16,40,128]{2,1,0:T(8,128)}, f32[16,40,128]{2,1,0:T(8,128)S(1)}, u32[]{:S(2)}) copy-start(f32[16,40,128]{2,1,0:T(8,128)S(1)} %get-tuple-element.53) | copy-start | bytes 983044
  31.7 11.4 %all-to-all-start = ((f32[32,5,2,128]{3,2,1,0:T(2,128)}), f32[32,5,2,128]{3,2,1,0:T(2,128)S(1)}, u32[]{:S(2)}, u32[]{:S(2)}) async-start(f32[32,5,2,128]{3,2,1,0:T(2,128)} %bitcast.10), calls=%async_computation | async-start | bytes 327680 | tf_op jit(solution)/shard_map/all_to_all | solution.py:784
  35.9 14.8 %collective-permute-start.8 = (f32[16,40,128]{2,1,0:T(8,128)}, f32[16,40,128]{2,1,0:T(8,128)S(1)}, u32[]{:S(2)}, u32[]{:S(2)}) collective-permute-start(f32[16,40,128]{2,1,0:T(8,128)} %get-tuple-element.52), channel_id=1, source_target_pairs={{0,1},{2,3},{4,5},{6,7},{1,0},{3,2},{5,4},{7,6},{8,9},{10,11},{12,... | collective-permute-start | bytes 983048 | tf_op jit(solution)/shard_map/ppermute | solution.py:604
  37.1 16.0 %collective-permute-start.9 = (f32[16,40,128]{2,1,0:T(8,128)}, f32[16,40,128]{2,1,0:T(8,128)S(1)}, u32[]{:S(2)}, u32[]{:S(2)}) collective-permute-start(f32[16,40,128]{2,1,0:T(8,128)} %copy-done.6), channel_id=1, source_target_pairs={{1,2},{3,4},{5,6},{2,1},{4,3},{6,5},{9,10},{11,12},{13,14},{10,9},... | collective-permute-start | bytes 983048 | tf_op jit(solution)/shard_map/ppermute | solution.py:604
  45.0 0.7 %copy-start.3 = (f32[32,16,128]{2,1,0:T(8,128)}, f32[32,16,128]{2,1,0:T(8,128)S(1)}, u32[]{:S(2)}) copy-start(f32[32,16,128]{2,1,0:T(8,128)S(1)} %shard_map.137) | copy-start | bytes 786436
  45.8 18.7 %all-to-all-start.1 = ((f32[32,16,128]{2,1,0:T(8,128)}), f32[32,16,128]{2,1,0:T(8,128)}, u32[]{:S(2)}, u32[]{:S(2)}) async-start(f32[32,16,128]{2,1,0:T(8,128)} %copy-done.3), calls=%async_computation.1 | async-start | bytes 524288 | tf_op jit(solution)/shard_map/all_to_all | solution.py:791
  54.5 13.5 %collective-permute-start.10 = (f32[9,40,128]{2,1,0:T(8,128)}, f32[9,40,128]{2,1,0:T(8,128)S(1)}, u32[]{:S(2)}, u32[]{:S(2)}) collective-permute-start(f32[9,40,128]{2,1,0:T(8,128)} %get-tuple-element.56), channel_id=1, source_target_pairs={{0,8},{16,24},{8,0},{24,16},{1,9},{17,25},{9,1},{25,17},{2,10},{18... | collective-permute-start | bytes 552968 | tf_op jit(solution)/shard_map/ppermute | solution.py:604
  54.7 13.3 %collective-permute-start.11 = (f32[9,40,128]{2,1,0:T(8,128)}, f32[9,40,128]{2,1,0:T(8,128)}, u32[]{:S(2)}, u32[]{:S(2)}) collective-permute-start(f32[9,40,128]{2,1,0:T(8,128)} %get-tuple-element.57), channel_id=1, source_target_pairs={{8,16},{16,8},{9,17},{17,9},{10,18},{18,10},{11,19},{19,11},{12,20... | collective-permute-start | bytes 552968 | tf_op jit(solution)/shard_map/ppermute | solution.py:604
  62.5 1.1 %copy-start.1 = (f32[16,10,16,128]{3,2,1,0:T(8,128)}, f32[16,10,16,128]{3,2,1,0:T(8,128)S(1)}, u32[]{:S(2)}) copy-start(f32[16,10,16,128]{3,2,1,0:T(8,128)S(1)} %get-tuple-element.54.inner) | copy-start | bytes 3932164
  63.6 0.9 %copy-start.4 = (f32[16,12,8,128]{3,2,1,0:T(8,128)}, f32[16,12,8,128]{3,2,1,0:T(8,128)S(1)}, u32[]{:S(2)}) copy-start(f32[16,12,8,128]{3,2,1,0:T(8,128)S(1)} %get-tuple-element.55.middle) | copy-start | bytes 2359300
  64.5 3.5 %copy-start.2 = (f32[16,10,16,128]{3,2,1,0:T(8,128)S(1)}, f32[16,10,16,128]{3,2,1,0:T(8,128)}, u32[]{:S(2)}) copy-start(f32[16,10,16,128]{3,2,1,0:T(8,128)} %copy-done.1) | copy-start | bytes 3932164
  68.0 1.1 %copy-start.5 = (f32[16,12,8,128]{3,2,1,0:T(8,128)S(1)}, f32[16,12,8,128]{3,2,1,0:T(8,128)}, u32[]{:S(2)}) copy-start(f32[16,12,8,128]{3,2,1,0:T(8,128)} %copy-done.4) | copy-start | bytes 2359300

commit v4 on v3

--- a/solution.py
+++ b/solution.py
@@ -16,19 +16,25 @@
 COLUMN = ("gy", "ga")
 EVERY = ("gx", "gy", "ga")
 HIGHEST = lax.Precision.HIGHEST
-HIGH = lax.Precision.HIGH
-VMEM_LIMIT = 8 * 1024 * 1024
-
-
-def vmem_call(kernel, outs, in_smem, n_in, flops=0, moved=0, exps=0, scratch=()):
+VMEM_LIMIT = 4 * 1024 * 1024
+
+
+def vmem_call(
+    kernel, outs, in_smem, n_in, flops=0, moved=0, exps=0, scratch=(), placed=(), copies=0, aliases={}
+):
     vmem = pl.BlockSpec(memory_space=pltpu.VMEM)
     smem = pl.BlockSpec(memory_space=pltpu.SMEM)
+    anywhere = pl.BlockSpec(memory_space=pl.ANY)
+    ins = [smem] * in_smem + [vmem] * (n_in - in_smem)
+    specs = [anywhere if at in placed else spec for at, spec in enumerate(ins + [vmem] * len(outs))]
     return pl.pallas_call(
         kernel,
-        in_specs=[smem] * in_smem + [vmem] * (n_in - in_smem),
-        out_specs=[vmem] * len(outs),
+        in_specs=specs[:n_in],
+        out_specs=specs[n_in:],
         out_shape=[jax.ShapeDtypeStruct(shape, jnp.float32) for shape in outs],
-        scratch_shapes=[pltpu.VMEM(shape, jnp.float32) for shape in scratch],
+        scratch_shapes=[pltpu.VMEM(shape, jnp.float32) for shape in scratch]
+        + [pltpu.SemaphoreType.DMA((copies,))] * (copies > 0),
+        input_output_aliases=aliases,
         compiler_params=pltpu.CompilerParams(vmem_limit_bytes=VMEM_LIMIT),
         cost_estimate=pl.CostEstimate(flops=flops, bytes_accessed=moved, transcendentals=exps),
     )
@@ -106,9 +112,7 @@
             speeds[d, x] = (0.5 * time_step) * flow[d, x]
         for y in range(deep):
             rates[x, y] = coefficients[1] * jnp.exp(coefficients[2] * inverse[y : y + 1])
-    count = mix.shape[0] // species
-    full = jnp.concatenate([tiled(time_step * production[...], count)] * count, axis=0)
-    mix[...] = where_equal(full, lambda at: at // species, lambda at: at // species)
+    mix[...] = tiled(time_step * production[...], mix.shape[1] // species)
     full = tiled(turned[...], wide)
     full = [jnp.broadcast_to(full[a : a + 1], (wide, full.shape[1])) for a in range(ranks_a)]
     full = jnp.concatenate(full, axis=0)
@@ -128,26 +132,49 @@
         factor_rows[0][1:2] = two_rows(north, own_ref[2])
 
 
+def halves_of(value):
+    high = value.astype(jnp.bfloat16)
+    return high, (value - high.astype(jnp.float32)).astype(jnp.bfloat16)
+
+
+def product(a, b, contract):
+    def dot(left, right):
+        return lax.dot_general(
+            left, right, ((contract[:1], contract[1:]), ((), ())),
+            preferred_element_type=jnp.float32,
+        )
+
+    (a_high, a_low), (b_high, b_low) = halves_of(a), halves_of(b)
+    return dot(a_high, b_high) + (dot(a_high, b_low) + dot(a_low, b_high))
+
+
+def mixing(rows):
+    species, size = rows.shape
+    full = jnp.concatenate([rows] * (size // species), axis=0)
+    high, low = halves_of(
+        where_equal(full, lambda at: at // species, lambda at: at // species)
+    )
+    return jnp.concatenate(
+        [jnp.concatenate([high, high], axis=1), jnp.concatenate([low, low], axis=1)], axis=0
+    )
+
+
 def reacted(cells, mix):
-    species = cells[0].shape[0]
-    group = mix.shape[0] // species
-    made = []
-    for first in range(0, len(cells), 2 * group):
-        some = cells[first : first + 2 * group]
-        some = some + [jnp.zeros_like(some[0])] * (-len(some) % group)
-        right = [
-            jnp.concatenate(some[at : at + group], axis=0) for at in range(0, len(some), group)
-        ]
-        up = right[0].shape[1]
-        produced = jnp.dot(
-            mix, jnp.concatenate(right, axis=1), precision=HIGH, preferred_element_type=jnp.float32
-        )
-        for at in range(len(right)):
-            for cell in range(group):
-                made.append(
-                    produced[cell * species : (cell + 1) * species, at * up : (at + 1) * up]
-                )
-    return made[: len(cells)]
+    species, up = cells[0].shape
+    size = mix.shape[0] // 2
+    group = size // species
+    cells = cells + [jnp.zeros_like(cells[0])] * (-len(cells) % group)
+    right = []
+    for at in range(0, len(cells), group):
+        high, low = halves_of(jnp.concatenate(cells[at : at + group], axis=0))
+        right.append(jnp.concatenate([high, low], axis=0))
+    produced = jnp.dot(mix, jnp.concatenate(right, axis=1), preferred_element_type=jnp.float32)
+    produced = produced[:size] + produced[size:]
+    return [
+        produced[cell * species : (cell + 1) * species, at * up : (at + 1) * up]
+        for at in range(len(right))
+        for cell in range(group)
+    ]
 
 
 def sources(here, rates):
@@ -196,6 +223,17 @@
             )
 
 
+def rate_of(temperature, coefficients):
+    return coefficients[1] * jnp.exp(coefficients[2] * (-1.0 / temperature))
+
+
+def own_rates(flow, coefficients, x, deep):
+    inverse = -1.0 / flow[3, x]
+    return jnp.stack(
+        [coefficients[1] * jnp.exp(coefficients[2] * inverse[y : y + 1]) for y in range(deep)]
+    )
+
+
 def block_kernel(shape, field, rates, flow, coefficients, mix_ref, out):
     wide, deep, species, up = shape
 
@@ -211,9 +249,10 @@
         out[x] = plane
 
     planes_advanced(
-        range(wide), lambda x: field[x], x_beside, y_beside, lambda x: rates[x],
+        range(wide), lambda x: field[x], x_beside, y_beside,
+        lambda x: rates[x],
         lambda x: [rows_for_species(speed, species) for speed in own_speeds(flow, x, deep)],
-        coefficients[0][None], mix_ref[...], emit,
+        coefficients[0][None], mixing(mix_ref[...]), emit,
     )
 
 
@@ -279,22 +318,36 @@
     finish(shape, refs[:8], emit)
 
 
+def outer_of(cell, species):
+    return slice(2 * cell * species, (2 * cell + 1) * species)
+
+
+def inner_of(cell, species):
+    return slice((2 * cell + 1) * species, (2 * cell + 2) * species)
+
+
+def flow_of(cell, count, species):
+    return slice(2 * count * species + 4 * cell, 2 * count * species + 4 * cell + 4)
+
+
 def snapshot_kernel(shape, *refs):
-    _, deep, species, _ = shape
+    wide, deep, species, _ = shape
     own_ref, flow, (out, y_one, y_other) = refs[0], refs[6], refs[8:]
     even_y = own_ref[1] == 1
 
     def emit(x, plane):
         out[x] = plane
 
+        def put(low, high, at):
+            y_one[at] = jnp.where(even_y, high, low)
+            y_other[at] = jnp.where(even_y, low, high)
+
         def others(y):
-            rows = [flow[d, x, pl.ds(y, 1), :] for d in range(4)]
-            return jnp.concatenate(rows * 2, axis=0)
-
-        low = jnp.concatenate([plane[0], plane[1], others(0)], axis=0)
-        high = jnp.concatenate([plane[deep - 1], plane[deep - 2], others(deep - 1)], axis=0)
-        y_one[x] = jnp.where(even_y, high, low)
-        y_other[x] = jnp.where(even_y, low, high)
+            return jnp.concatenate([flow[d, x, pl.ds(y, 1), :] for d in range(4)], axis=0)
+
+        put(plane[0], plane[deep - 1], outer_of(x, species))
+        put(plane[1], plane[deep - 2], inner_of(x, species))
+        put(others(0), others(deep - 1), flow_of(x, wide, species))
 
     finish(shape, refs[:8], emit)
 
@@ -302,18 +355,17 @@
 def wide_faces_kernel(shape, own_ref, field, y_one, y_other, flow, x_one, x_other):
     wide, deep, species, _ = shape
     even_x, even_y = own_ref[0] == 1, own_ref[1] == 1
-    first, second = slice(0, species), slice(species, 2 * species)
-    rest = slice(2 * species, 2 * species + 8)
 
     def face(outer, inner, out):
         for y in range(deep):
-            out[y, first] = field[outer, y]
-            out[y, second] = field[inner, y]
-            rows = [flow[d, outer, y : y + 1, :] for d in range(4)]
-            out[y, rest] = jnp.concatenate(rows * 2, axis=0)
-        out[deep, first] = jnp.where(even_y, y_other[outer, first], y_one[outer, first])
-        out[deep, second] = jnp.where(even_y, y_one[outer, first], y_other[outer, first])
-        out[deep, rest] = jnp.zeros_like(out[deep, rest])
+            out[outer_of(y, species)] = field[outer, y]
+            out[inner_of(y, species)] = field[inner, y]
+            out[flow_of(y, deep + 1, species)] = jnp.concatenate(
+                [flow[d, outer, y : y + 1, :] for d in range(4)], axis=0
+            )
+        at = outer_of(outer, species)
+        out[outer_of(deep, species)] = choose(even_y, y_one, y_other, 0, at)
+        out[inner_of(deep, species)] = choose(even_y, y_one, y_other, 1, at)
 
     @pl.when(even_x)
     def _():
@@ -326,121 +378,134 @@
         face(wide - 1, wide - 2, x_other)
 
 
+def planes_copied(groups, ready, out, semaphores):
+    copies, at = {}, 0
+    for group in groups:
+        copies[group[-1]] = pltpu.make_async_copy(
+            ready.at[:, pl.ds(at, len(group))],
+            out.at[:, pl.ds(group[0], len(group))],
+            semaphores.at[len(copies)],
+        )
+        at += len(group)
+    return copies
+
+
 def choose(even, one, other, side, at):
     first, second = (one, other) if side else (other, one)
     return jnp.where(even, first[at], second[at])
 
 
-def rate_of(temperature, coefficients):
-    return coefficients[1] * jnp.exp(coefficients[2] * (-1.0 / temperature))
-
-
 def third_step_kernel(
-    shape, counts, own_ref, block, field, y_one, y_other, rates, flow, coefficients, mix_ref,
-    inner, middle,
+    shape, counts, own_ref, field, y_one, y_other, flow, coefficients, mix_ref, edges, ends, out,
+    inner, ready, semaphores,
 ):
     wide, deep, species, up = shape
     _, columns = counts
     even_y, column = own_ref[1] == 1, own_ref[3]
     inside = (column > 0, column < columns - 1)
-    diffusivity, mix = coefficients[0][None], mix_ref[...]
-    first, second = slice(0, species), slice(species, 2 * species)
-    rest = slice(2 * species, 2 * species + 8)
-
-    def beside(side, x, at):
-        return choose(even_y, y_one, y_other, side, (x, at))
+    diffusivity, mix = coefficients[0][None], mixing(mix_ref[...])
+
+    def beside(side, x, rows):
+        return choose(even_y, y_one, y_other, side, rows)
 
     def here(x):
-        return jnp.stack([beside(0, x, first), beside(1, x, first)])
+        at = outer_of(x, species)
+        return jnp.concatenate(
+            [beside(0, x, at)[None], field[x], beside(1, x, at)[None]], axis=0
+        )
 
     def x_beside(x, side):
         at = x + 2 * side - 1
-        return here(at) if 0 <= at < wide else jnp.zeros((2, species, up), jnp.float32)
+        return here(at) if 0 <= at < wide else jnp.zeros((deep + 2, species, up), jnp.float32)
 
     def y_beside(x, side):
-        outer = beside(side, x, second)
-        return jnp.stack([field[x, 0], outer] if side else [outer, field[x, deep - 1]])
-
-    def other_rows(x):
-        return [beside(side, x, rest) for side in range(2)]
+        plane, beyond = here(x), beside(side, x, inner_of(x, species))[None]
+        return jnp.concatenate([plane[1:], beyond] if side else [beyond, plane[:-1]], axis=0)
+
+    def others(side, x):
+        return beside(side, x, flow_of(x, wide, species))
+
+    def rates(x):
+        sides = [rate_of(others(side, x)[3:4], coefficients)[None] for side in range(2)]
+        return jnp.concatenate([sides[0], own_rates(flow, coefficients, x, deep), sides[1]], axis=0)
+
+    def speeds(x):
+        ends, own = [others(side, x) for side in range(2)], own_speeds(flow, x, deep)
+        return [
+            rows_for_species([ends[0][d : d + 1]] + own[d] + [ends[1][d : d + 1]], species)
+            for d in range(3)
+        ]
 
     def emit(x, plane):
         inner[x, 0] = jnp.where(inside[0], plane[0], 0.0)
-        inner[x, deep + 1] = jnp.where(inside[1], plane[1], 0.0)
+        inner[x, 1 : deep + 1] = plane[1 : deep + 1]
+        inner[x, deep + 1] = jnp.where(inside[1], plane[deep + 1], 0.0)
+        if x < 3 or x >= wide - 3:
+            edges[x if x < 3 else x - wide + 6] = inner[x]
+        if x in (0, wide - 1):
+            for side in range(2):
+                ends[0 if x == 0 else 1, side, 0:4] = others(side, x)
+
+    planes_advanced(range(wide), here, x_beside, y_beside, rates, speeds, diffusivity, mix, emit)
+
+    inmost = range(2, wide - 2)
+    copies = planes_copied(
+        [inmost[at : at + 4] for at in range(0, len(inmost), 4)], ready, out, semaphores
+    )
+
+    def emit_last(x, plane):
+        ready[:, x - 2] = jnp.swapaxes(plane, 0, 1)
+        if x in copies:
+            copies[x].start()
 
     planes_advanced(
-        range(wide), here, x_beside, y_beside,
-        lambda x: jnp.stack(
-            [rate_of(rows[3:4], coefficients) for rows in other_rows(x)]
-        ),
-        lambda x: [
-            rows_for_species([rows[d : d + 1] for rows in other_rows(x)], species) for d in range(3)
-        ],
-        diffusivity, mix, emit, 16,
-    )
-
-    def row(x, y):
-        return jnp.broadcast_to(flow[1, x, pl.ds(y, 1), :], (species, up))
-
-    for x in range(wide):
-        low = from_beyond(beside(0, x, first), 0, row(x, 0), diffusivity[0])
-        high = from_beyond(beside(1, x, first), 1, row(x, deep - 1), diffusivity[0])
-        inner[x, 1] = block[x, 0] + low
-        inner[x, 2:deep] = block[x, 1 : deep - 1]
-        inner[x, deep] = block[x, deep - 1] + high
-
-    def emit_last(x, plane):
-        middle[:, x - 2] = jnp.swapaxes(plane, 0, 1)
-
-    planes_advanced(
-        range(2, wide - 2),
+        inmost,
         lambda x: inner[x, 1 : deep + 1],
         lambda x, side: inner[x + 2 * side - 1, 1 : deep + 1],
         lambda x, side: inner[x, 2 * side : 2 * side + deep],
-        lambda x: rates[x],
+        lambda x: own_rates(flow, coefficients, x, deep),
         lambda x: [rows_for_species(speed, species) for speed in own_speeds(flow, x, deep)],
         diffusivity, mix, emit_last,
     )
+    for copy in copies.values():
+        copy.wait()
 
 
 def fourth_step_kernel(
-    shape, counts, own_ref, inner, middle, field, x_one, x_other, y_one, y_other, rates, flow,
-    coefficients, mix_ref, out, edge, x_sides,
+    shape, counts, own_ref, edges, ends, _, field, x_one, x_other, flow, coefficients, mix_ref,
+    out, edge, x_sides, ready, semaphores,
 ):
     wide, deep, species, up = shape
     rows, _ = counts
-    even_x, even_y, row = own_ref[0] == 1, own_ref[1] == 1, own_ref[2]
+    even_x, row = own_ref[0] == 1, own_ref[2]
     inside = (row > 0, row < rows - 1)
-    diffusivity, mix = coefficients[0][None], mix_ref[...]
-    first, second = slice(0, species), slice(species, 2 * species)
-    rest = slice(2 * species, 2 * species + 8)
-    cells = slice(0, deep)
-
-    out[:, 2 : wide - 2] = middle[...]
-
-    def beside(side, at, of=cells):
-        return choose(even_x, x_one, x_other, side, (of, at))
+    diffusivity, mix = coefficients[0][None], mixing(mix_ref[...])
+    def beside(side, rows_of, cells=range(deep)):
+        return jnp.stack(
+            [choose(even_x, x_one, x_other, side, rows_of(cell, species)) for cell in cells]
+        )
 
     def corners(side):
-        return [beside(side, at, deep) for at in (first, second)]
+        return [beside(side, rows_of, [deep])[0] for rows_of in (outer_of, inner_of)]
 
     def last(side):
         return wide - 1 if side else 0
 
     def y_beside(side, to):
-        here, corner = beside(side, first), corners(side)[to][None]
+        here, corner = beside(side, outer_of), corners(side)[to][None]
         return jnp.concatenate([here[1:], corner] if to else [corner, here[:-1]], axis=0)
 
     def other_rows(side):
-        others = beside(side, rest)
-        return [others[y] for y in range(deep)]
+        return [
+            choose(even_x, x_one, x_other, side, flow_of(y, deep + 1, species)) for y in range(deep)
+        ]
 
     def emit(side, plane):
         x_sides[side] = jnp.where(inside[side], plane, 0.0)
 
     planes_advanced(
-        range(2), lambda side: beside(side, first),
-        lambda side, to: beside(side, second) if side == to else field[last(side)],
+        range(2), lambda side: beside(side, outer_of),
+        lambda side, to: beside(side, inner_of) if side == to else field[last(side)],
         y_beside,
         lambda side: jnp.stack(
             [rate_of(rows[3:4], coefficients) for rows in other_rows(side)]
@@ -454,45 +519,63 @@
     for side in range(2):
         x = last(side)
         low, high = corners(side)
-        value = jnp.concatenate([low[None], beside(side, first), high[None]], axis=0)
-        ends = [choose(even_y, y_one, y_other, to, (x, rest))[0:1] for to in range(2)]
-        speed = rows_for_species([ends[0]] + own_speeds(flow, x, deep)[0] + [ends[1]], species)
-        edge[side] = inner[x] + from_beyond(value, side, speed, diffusivity)
+        value = jnp.concatenate([low[None], beside(side, outer_of), high[None]], axis=0)
+        speed = rows_for_species(
+            [ends[side, 0, 0:1]] + own_speeds(flow, x, deep)[0] + [ends[side, 1, 0:1]], species
+        )
+        edge[side] = edges[5 * side] + from_beyond(value, side, speed, diffusivity)
 
     def plane_of(x):
         if x < 0 or x >= wide:
             return x_sides[0 if x < 0 else 1]
         if x == 0 or x == wide - 1:
             return edge[0 if x == 0 else 1, 1 : deep + 1]
-        return inner[x, 1 : deep + 1]
+        return edges[x if x < 3 else x - wide + 6, 1 : deep + 1]
 
     def y_of(x, side):
         at = slice(2 * side, 2 * side + deep)
-        return edge[0 if x == 0 else 1, at] if x in (0, wide - 1) else inner[x, at]
+        if x in (0, wide - 1):
+            return edge[0 if x == 0 else 1, at]
+        return edges[x if x < 3 else x - wide + 6, at]
+
+    outermost = [0, 1, wide - 2, wide - 1]
+    copies = planes_copied([outermost[:2], outermost[2:]], ready, out, semaphores)
 
     def emit_last(x, plane):
-        out[:, x] = jnp.swapaxes(plane, 0, 1)
+        ready[:, outermost.index(x)] = jnp.swapaxes(plane, 0, 1)
+        if x in copies:
+            copies[x].start()
 
     planes_advanced(
-        [0, 1, wide - 2, wide - 1], plane_of, lambda x, side: plane_of(x + 2 * side - 1), y_of,
-        lambda x: rates[x],
+        outermost, plane_of, lambda x, side: plane_of(x + 2 * side - 1), y_of,
+        lambda x: own_rates(flow, coefficients, x, deep),
         lambda x: [rows_for_species(speed, species) for speed in own_speeds(flow, x, deep)],
         diffusivity, mix, emit_last,
     )
+    for copy in copies.values():
+        copy.wait()
 
 
 def project_kernel(shape, ranks, field, component, vertical, factor_rows, out):
     wide, deep, species, up = shape
     ranks_a, ranks_d = ranks
     each = deep + 2
+    cells = [field[x, y] for y in range(deep) for x in range(wide)]
+    high, low = halves_of(jnp.concatenate(cells, axis=0))
+    both = jnp.concatenate([high, low], axis=1)
+    high, low = halves_of(vertical[...])
+    left = jnp.concatenate(
+        [jnp.concatenate([high, high], axis=1), jnp.concatenate([low, low], axis=1)], axis=0
+    )
+    on_d = lax.dot_general(
+        left, both, (((1,), (1,)), ((), ())), preferred_element_type=jnp.float32
+    )
+    on_d = on_d[:ranks_d] + on_d[ranks_d:]
+    size = wide * species
+    on_d = jnp.concatenate([on_d[:, y * size : (y + 1) * size] for y in range(deep)], axis=0)
+    on_both = product(on_d, component[...], (1, 1))
     for y in range(deep):
-        rows = field[:, y].reshape(wide * species, up)
-        on_a = jnp.dot(component[...], rows, precision=HIGHEST, preferred_element_type=jnp.float32)
-        on_d = lax.dot_general(
-            vertical[...], on_a, (((1,), (1,)), ((), ())), precision=HIGHEST,
-            preferred_element_type=jnp.float32,
-        )
-        out[pl.ds(y, ranks_d, stride=each), :] = on_d
+        out[pl.ds(y, ranks_d, stride=each), :] = on_both[y * ranks_d : (y + 1) * ranks_d]
     for row in range(2):
         out[pl.ds(deep + row, ranks_d, stride=each), :] = jnp.broadcast_to(
             factor_rows[row : row + 1], (ranks_d, 128)
@@ -503,12 +586,6 @@
     rows, columns, ranks_a, tall, deep = counts
     devices, each = rows * columns, deep + 2
     own = 128 // ranks_a
-
-    def dot(a, b, contract, precision=HIGHEST):
-        return lax.dot_general(
-            a, b, ((contract[:1], contract[1:]), ((), ())), precision=precision,
-            preferred_element_type=jnp.float32,
-        )
 
     whole = jnp.concatenate(
         [
@@ -525,7 +602,7 @@
         both = got[pl.ds(at, devices, stride=each), :]
         halves = jnp.concatenate([both[:, :64], both[:, 64:]], axis=0)
         pick = jnp.full((2 * devices, 2 * devices), 1.0, jnp.float32)
-        return dot(where_equal(pick, of_row, lambda at: at), halves, (1, 0))
+        return product(where_equal(pick, of_row, lambda at: at), halves, (1, 0))
 
     east = in_order(deep, lambda at: at % 2 * devices + at // 2)
     north = in_order(
@@ -557,13 +634,13 @@
             axis=0,
         ).T
 
-    half = by_rank(dot(whole, north, (0, 0)))
-    core = dot(east, half, (0, 0))
-    half = dot(east, core, (1, 0))
+    half = by_rank(product(whole, north, (0, 0)))
+    core = product(east, half, (0, 0))
+    half = product(east, core, (1, 0))
     ranks_c = north.shape[1]
     split = [slice(a * ranks_c, (a + 1) * ranks_c) for a in range(ranks_a)]
     core = by_row([core[:, at] for at in split])
-    whole = by_row([dot(half[:, at], north, (1, 1)) for at in split])
+    whole = by_row([product(half[:, at], north, (1, 1)) for at in split])
     for row in range(rows):
         for column in range(columns):
             at = row * columns + column
@@ -584,11 +661,8 @@
     )
     for y in range(deep):
         on_d = got[pl.ds(tall + y, ranks_d, stride=each), :]
-        on_a = lax.dot_general(
-            on_d, vertical[...], (((0,), (0,)), ((), ())), precision=HIGH,
-            preferred_element_type=jnp.float32,
-        )
-        full[y] = jnp.dot(component, on_a, precision=HIGH, preferred_element_type=jnp.float32)
+        on_a = product(on_d, vertical[...], (0, 0))
+        full[y] = product(component, on_a, (1, 0))
     for x in range(wide):
         residual[:, x] = jnp.swapaxes(
             field[x] - full[:, x * species : (x + 1) * species, :], 0, 1
@@ -719,9 +793,8 @@
     field_rows = mixture_fields_initial.reshape(species * wide * deep, up)
     faces = vmem_call(functools.partial(faces_kernel, shape), face_shapes, 1, 2)(own, field_rows)
     faces = faces_beside(faces)
-    both = 16
     out_shapes = [
-        shape, shape, (4, wide, deep, up), (3, species, up), (both * species,) * 2,
+        shape, shape, (4, wide, deep, up), (3, species, up), (species, 128),
         (wide * ranks_a, wide * species), (species, wide * ranks_a), (ranks_d, up),
     ] + [(2, 128)] * kernels_fit
     small = (
@@ -760,22 +833,17 @@
             own, *block(field, *fixed), *faces, speeds, coefficients
         )
         faces = faces_beside(faces)
-    high = 2 * species + 8
+    high = 2 * species + 4
     snapshot, *y_faces = vmem_call(
-        functools.partial(snapshot_kernel, shape), [shape] + [(wide, high, up)] * 2, 1, 8,
+        functools.partial(snapshot_kernel, shape), [shape] + [(wide * high + 64, up)] * 2, 1, 8,
         flops=4 * cells, moved=8 * cells,
     )(own, *block(field, *fixed), *faces, speeds, coefficients)
     y_faces = swapped(*y_faces, COLUMN)
     x_faces = vmem_call(
-        functools.partial(wide_faces_kernel, shape), [(deep + 1, high, up)] * 2, 1, 5,
+        functools.partial(wide_faces_kernel, shape), [((deep + 1) * high + 36, up)] * 2, 1, 5,
         flops=cells, moved=cells,
     )(own, snapshot, *y_faces, speeds)
     x_faces = swapped(*x_faces, ROW)
-    inner, middle = vmem_call(
-        functools.partial(third_step_kernel, shape, (rows, columns)),
-        [(wide, deep + 2, species, up), (species, wide - 4, deep, up)], 1, 9,
-        flops=120 * cells, moved=16 * cells,
-    )(own, *block(snapshot, *fixed), snapshot, *y_faces, *fixed)
     if kernels_fit:
         (sent,) = vmem_call(
             functools.partial(project_kernel, shape, (ranks_a, ranks_d)),
@@ -792,7 +860,8 @@
         residual, tucker_core = vmem_call(
             functools.partial(expand_kernel, shape, (ranks_a, ranks_d), own_c),
             [mixture_fields_initial.shape, (ranks_a * own_b, own_c, ranks_d)], 0, 4,
-            flops=60 * cells, moved=8 * cells, scratch=[(deep, wide * species, up)],
+            flops=60 * cells, moved=8 * cells,
+            scratch=[(deep, wide * species, up)],
         )(
             got.reshape(devices * (own_c + deep), 128),
             snapshot,
@@ -805,13 +874,22 @@
         tucker_core, residual = compress_and_expand(
             snapshot, east, north, tucker_factor_vertical, tucker_factor_component
         )
-    own_last, _ = lax.optimization_barrier((own, tucker_core))
+    fixed = fixed[1:]
+    edges, ends, inmost = vmem_call(
+        functools.partial(third_step_kernel, shape, (rows, columns)),
+        [(6, deep + 2, species, up), (2, 2, 8, up), mixture_fields_initial.shape], 1, 7,
+        flops=120 * cells, moved=16 * cells,
+        scratch=[(wide, deep + 2, species, up), (species, wide - 4, deep, up)], placed=[9],
+        copies=-(-(wide - 4) // 4),
+    )(own, snapshot, *y_faces, *fixed)
+    own, _ = lax.optimization_barrier((own, tucker_core))
     (mixture_fields_final,) = vmem_call(
         functools.partial(fourth_step_kernel, shape, (rows, columns)),
-        [mixture_fields_initial.shape], 1, 12,
+        [mixture_fields_initial.shape], 1, 10,
         flops=60 * cells, moved=8 * cells,
-        scratch=[(2, deep + 2, species, up), (2, deep, species, up)],
-    )(own_last, inner, middle, snapshot, *x_faces, *y_faces, *fixed)
+        scratch=[(2, deep + 2, species, up), (2, deep, species, up), (species, 4, deep, up)],
+        placed=[3, 10], copies=2, aliases={3: 0},
+    )(own, edges, ends, inmost, snapshot, *x_faces, *fixed)
     return (mixture_fields_final, residual, tucker_core)
 
 

time: 72.6 us -> 67.7 us (0.933)
  the two profiles are of different devices: /device:TPU:3 before, /device:TPU:18 now
where the time goes in v4:
time: 67.7 us; the launch traced here: 67.3 us
  starting transfers between devices  35.3 us (52%)
  Pallas kernels  18.9 us (28%)
  waiting for transfers between devices  11 us (16%)
  local copies, waits for them, and re-layouts  1.23 us (2%)
  between operations  0.83 us (1%)
    ppermute x12, starting transfers between devices, swapped(): got.append(lax.ppermute(face, axes, couples + [(b, a) for a, b in couples]))  24.9 us
    ppermute x12, waiting for transfers between devices, swapped(): got.append(lax.ppermute(face, axes, couples + [(b, a) for a, b in couples]))  8.59 us
    all_to_all x1, starting transfers between devices, body(): got = lax.all_to_all(sent, EVERY, 0, 0, tiled=True)  5.73 us
    all_to_all x1, starting transfers between devices, body(): lax.all_to_all(sent.reshape(devices, (deep + 2) // 2, 2, 128), EVERY, 0,...  4.73 us
    pallas_call x1, Pallas kernels, body(): vmem_call(functools.partial(third_step_kernel, shape, (rows, columns)), [...  4.04 us
    pallas_call x1, Pallas kernels, body(): vmem_call(functools.partial(expand_kernel, shape, (ranks_a, ranks_d), own...  2.43 us
    all_to_all x1, waiting for transfers between devices, body(): lax.all_to_all(sent.reshape(devices, (deep + 2) // 2, 2, 128), EVERY, 0,...  2.36 us
    pallas_call x2, Pallas kernels, body(): block(field, *fixed)  2.31 us
  transfers between devices with their start and end apart: 14, of which 3 were waited for; matrix products, arithmetic and copies ran while one was open for 0% of the time, Pallas kernels for 20%

profile of v4, /device:TPU:18, one launch (start us, length us, event | category | flops | bytes accessed | tf_op | source)
XLA Modules:
  0.0 67.3 jit_solution(8815539081369209762)
XLA Ops:
  0.7 1.2 %copy-done = f32[16,16,8,128]{3,2,1,0:T(8,128)S(1)} copy-done((f32[16,16,8,128]{3,2,1,0:T(8,128)S(1)}, f32[16,16,8,128]{3,2,1,0:T(8,128)}, u32[]{:S(2)}) %copy-start) | copy-done | bytes 1048600
  2.0 0.8 %shard_map.132 = (f32[8,16,128]{2,1,0:T(8,128)S(1)}, f32[8,16,128]{2,1,0:T(8,128)S(1)}, f32[16,16,128]{2,1,0:T(8,128)S(1)}, f32[16,16,128]{2,1,0:T(8,128)S(1)}) custom-call(s32[4]{0:T(128)S(1)} %pad_add_fusion.own_ref.even_ref.refs_0_, f32[2048,128]{1,0:T(8,128)S(1)} %bitcast.14), custom_call_target="tpu_custom_call" | custom-call | tf_op jit(solution)/shard_map/pallas_call | solution.py:794
  2.7 1.6 %collective-permute-start.2 = (f32[16,16,128]{2,1,0:T(8,128)S(1)}, f32[16,16,128]{2,1,0:T(8,128)S(1)}, u32[]{:S(2)}, u32[]{:S(2)}) collective-permute-start(f32[16,16,128]{2,1,0:T(8,128)S(1)} %get-tuple-element.39), channel_id=1, source_target_pairs={{0,1},{2,3},{4,5},{6,7},{1,0},{3,2},{5,4},{7,6},{8,9},{10,11},{12,... | collective-permute-start | bytes 393224 | tf_op jit(solution)/shard_map/ppermute | solution.py:678
  4.4 1.9 %collective-permute-start.3 = (f32[16,16,128]{2,1,0:T(8,128)S(1)}, f32[16,16,128]{2,1,0:T(8,128)S(1)}, u32[]{:S(2)}, u32[]{:S(2)}) collective-permute-start(f32[16,16,128]{2,1,0:T(8,128)S(1)} %get-tuple-element.40), channel_id=1, source_target_pairs={{1,2},{3,4},{5,6},{2,1},{4,3},{6,5},{9,10},{11,12},{13,14},{10,9},... | collective-permute-start | bytes 393224 | tf_op jit(solution)/shard_map/ppermute | solution.py:678
  6.9 4.3 %collective-permute-start.1 = (f32[8,16,128]{2,1,0:T(8,128)S(1)}, f32[8,16,128]{2,1,0:T(8,128)S(1)}, u32[]{:S(2)}, u32[]{:S(2)}) collective-permute-start(f32[8,16,128]{2,1,0:T(8,128)S(1)} %get-tuple-element.38), channel_id=1, source_target_pairs={{8,16},{16,8},{9,17},{17,9},{10,18},{18,10},{11,19},{19,11},{12,20... | collective-permute-start | bytes 196616 | tf_op jit(solution)/shard_map/ppermute | solution.py:678
  11.2 1.9 %shard_map.130 = (f32[16,8,16,128]{3,2,1,0:T(8,128)S(1)}, f32[16,8,16,128]{3,2,1,0:T(8,128)S(1)}, f32[4,16,8,128]{3,2,1,0:T(8,128)S(1)}, f32[3,16,128]{2,1,0:T(8...) custom-call(s32[4]{0:T(128)S(1)} %pad_add_fusion.own_ref.even_ref.re, ...), custom_call_target="tpu_custom_call" | custom-call | flops 1048576 | bytes 3145728 | tf_op jit(solution)/shard_map/pallas_call | solution.py:808
  13.2 1.2 %shard_map.131.refs_1_ = f32[16,8,16,128]{3,2,1,0:T(8,128)S(1)} custom-call(f32[16,8,16,128]{3,2,1,0:T(8,128)S(1)} %get-tuple-element.32.field, f32[16,8,16,128]{3,2,1,0:T(8,128)S(1)} %get-tuple-element.33.rates, f32[4,16,8,128]{3,2,1,0:T(8,128)S(1)} %get-tuple-element.34.flow.refs_6_, f32[3,16,128]{2,1,0:T(8,128)S(1)} %get-tuple-element.35.coefficients.refs_7_, ...), custom_call_target="tpu_custom_call" | custom-call | flops 15728640 | bytes 2097152 | tf_op jit(solution)/shard_map/pallas_call | solution.py:833
  15.1 1.0 %collective-permute-start.6 = (f32[16,16,128]{2,1,0:T(8,128)S(1)}, f32[16,16,128]{2,1,0:T(8,128)S(1)}, u32[]{:S(2)}, u32[]{:S(2)}) collective-permute-start(f32[16,16,128]{2,1,0:T(8,128)S(1)} %get-tuple-element.44), channel_id=1, source_target_pairs={{0,1},{2,3},{4,5},{6,7},{1,0},{3,2},{5,4},{7,6},{8,9},{10,11},{12,... | collective-permute-start | bytes 393224 | tf_op jit(solution)/shard_map/ppermute | solution.py:678
  16.1 3.0 %collective-permute-start.7 = (f32[16,16,128]{2,1,0:T(8,128)S(1)}, f32[16,16,128]{2,1,0:T(8,128)S(1)}, u32[]{:S(2)}, u32[]{:S(2)}) collective-permute-start(f32[16,16,128]{2,1,0:T(8,128)S(1)} %get-tuple-element.45), channel_id=1, source_target_pairs={{1,2},{3,4},{5,6},{2,1},{4,3},{6,5},{9,10},{11,12},{13,14},{10,9},... | collective-permute-start | bytes 393224 | tf_op jit(solution)/shard_map/ppermute | solution.py:678
  19.2 3.9 %collective-permute-start.5 = (f32[8,16,128]{2,1,0:T(8,128)S(1)}, f32[8,16,128]{2,1,0:T(8,128)S(1)}, u32[]{:S(2)}, u32[]{:S(2)}) collective-permute-start(f32[8,16,128]{2,1,0:T(8,128)S(1)} %get-tuple-element.43), channel_id=1, source_target_pairs={{8,16},{16,8},{9,17},{17,9},{10,18},{18,10},{11,19},{19,11},{12,20... | collective-permute-start | bytes 196616 | tf_op jit(solution)/shard_map/ppermute | solution.py:678
  23.1 1.1 %shard_map.134.refs_1_ = f32[16,8,16,128]{3,2,1,0:T(8,128)S(1)} custom-call(f32[16,8,16,128]{3,2,1,0:T(8,128)S(1)} %get-tuple-element.41.field, f32[16,8,16,128]{3,2,1,0:T(8,128)S(1)} %get-tuple-element.33.rates, f32[4,16,8,128]{3,2,1,0:T(8,128)S(1)} %get-tuple-element.34.flow.refs_6_, f32[3,16,128]{2,1,0:T(8,128)S(1)} %get-tuple-element.35.coefficients.refs_7_, ...), custom_call_target="tpu_custom_call" | custom-call | flops 15728640 | bytes 2097152 | tf_op jit(solution)/shard_map/pallas_call | solution.py:840
  24.2 2.0 %collective-permute-done.5.refs_3_ = f32[8,16,128]{2,1,0:T(8,128)S(1)} collective-permute-done((f32[8,16,128]{2,1,0:T(8,128)S(1)}, f32[8,16,128]{2,1,0:T(8,128)S(1)}, u32[]{:S(2)}, u32[]{:S(2)}) %collective-permute-start.5) | collective-permute-done | bytes 65568 | tf_op jit(solution)/shard_map/ppermute | solution.py:678
  27.0 1.4 %shard_map.136 = f32[320,128]{1,0:T(8,128)} custom-call(f32[16,8,16,128]{3,2,1,0:T(8,128)S(1)} %get-tuple-element.46.field, f32[128,256]{1,0:T(8,128)S(1)} %get-tuple-element.47.component, f32[32,128]{1,0:T(8,128)S(1)} %get-tuple-element.48.vertical, f32[2,128]{1,0:T(2,128)S(1)} %get-tuple-element.49.factor_rows), custom_call_target="tpu_custom_call" | custom-call | flops 15728640 | bytes 1048576 | tf_op jit(solution)/shard_map/pallas_call | solution.py:848
  28.4 4.7 %all-to-all-start = ((f32[32,5,2,128]{3,2,1,0:T(2,128)}), f32[32,5,2,128]{3,2,1,0:T(2,128)S(1)}, u32[]{:S(2)}, u32[]{:S(2)}) async-start(f32[32,5,2,128]{3,2,1,0:T(2,128)} %bitcast.10), calls=%async_computation | async-start | bytes 327680 | tf_op jit(solution)/shard_map/all_to_all | solution.py:852
  33.1 1.6 %collective-permute-start.8 = (f32[640,128]{1,0:T(8,128)S(1)}, f32[640,128]{1,0:T(8,128)S(1)}, u32[]{:S(2)}, u32[]{:S(2)}) collective-permute-start(f32[640,128]{1,0:T(8,128)S(1)} %get-tuple-element.53), channel_id=1, source_target_pairs={{0,1},{2,3},{4,5},{6,7},{1,0},{3,2},{5,4},{7,6},{8,9},{10,11},{12,... | collective-permute-start | bytes 983048 | tf_op jit(solution)/shard_map/ppermute | solution.py:678
  34.7 1.9 %collective-permute-start.9 = (f32[640,128]{1,0:T(8,128)S(1)}, f32[640,128]{1,0:T(8,128)S(1)}, u32[]{:S(2)}, u32[]{:S(2)}) collective-permute-start(f32[640,128]{1,0:T(8,128)S(1)} %get-tuple-element.54), channel_id=1, source_target_pairs={{1,2},{3,4},{5,6},{2,1},{4,3},{6,5},{9,10},{11,12},{13,14},{10,9},... | collective-permute-start | bytes 983048 | tf_op jit(solution)/shard_map/ppermute | solution.py:678
  36.6 2.4 %all-to-all-done = f32[32,5,2,128]{3,2,1,0:T(2,128)S(1)} async-done(((f32[32,5,2,128]{3,2,1,0:T(2,128)}), f32[32,5,2,128]{3,2,1,0:T(2,128)S(1)}, u32[]{:S(2)}, u32[]{:S(2)}) %all-to-all-start) | async-done | bytes 163872 | tf_op jit(solution)/shard_map/all_to_all | solution.py:852
  39.0 2.2 %shard_map.137 = f32[32,16,128]{2,1,0:T(8,128)} custom-call(f32[320,128]{1,0:T(8,128)S(1)} %bitcast.16), custom_call_target="tpu_custom_call" | custom-call | flops 15728640 | bytes 1048576 | tf_op jit(solution)/shard_map/pallas_call | solution.py:855
  41.2 5.7 %all-to-all-start.1 = ((f32[32,16,128]{2,1,0:T(8,128)}), f32[32,16,128]{2,1,0:T(8,128)S(1)}, u32[]{:S(2)}, u32[]{:S(2)}) async-start(f32[32,16,128]{2,1,0:T(8,128)} %shard_map.137), calls=%async_computation.1 | async-start | bytes 524288 | tf_op jit(solution)/shard_map/all_to_all | solution.py:859
  46.9 6.5 %collective-permute-done.9.y_other = f32[640,128]{1,0:T(8,128)S(1)} collective-permute-done((f32[640,128]{1,0:T(8,128)S(1)}, f32[640,128]{1,0:T(8,128)S(1)}, u32[]{:S(2)}, u32[]{:S(2)}) %collective-permute-start.9) | collective-permute-done | bytes 327712 | tf_op jit(solution)/shard_map/ppermute | solution.py:678
  54.7 4.2 %collective-permute-start.11 = (f32[360,128]{1,0:T(8,128)S(1)}, f32[360,128]{1,0:T(8,128)S(1)}, u32[]{:S(2)}, u32[]{:S(2)}) collective-permute-start(f32[360,128]{1,0:T(8,128)S(1)} %get-tuple-element.59), channel_id=1, source_target_pairs={{8,16},{16,8},{9,17},{17,9},{10,18},{18,10},{11,19},{19,11},{12,20... | collective-permute-start | bytes 552968 | tf_op jit(solution)/shard_map/ppermute | solution.py:678
  58.9 4.0 %shard_map.139 = (f32[6,10,16,128]{3,2,1,0:T(8,128)S(1)}, f32[2,2,8,128]{3,2,1,0:T(8,128)S(1)}, f32[16,16,8,128]{3,2,1,0:T(8,128)}) custom-call(s32[4]{0:T(128)S(1)} %pad_add_fusion.own_ref.even_ref.refs_0_, f32[16,8,16,128]{3,2,1,0:T(8,128)S(1)} %get-tuple-element.46.field, f32[640,128]{1,0:T(8,128)S(1)} %collective-permute-done.8.y_one, ...), custom_call_target="tpu_custom_call" | custom-call | flops 31457280 | bytes 4194304 | tf_op jit(solution)/shard_map/pallas_call | solution.py:878
  63.0 2.4 %shard_map.138 = (f32[16,16,8,128]{3,2,1,0:T(8,128)}, f32[128,8,32]{2,1,0:T(8,128)}) custom-call(f32[512,128]{1,0:T(8,128)S(1)} %bitcast.15, f32[16,8,16,128]{3,2,1,0:T(8,128)S(1)} %get-tuple-element.46.field, f32[16,128]{1,0:T(8,128)S(1)} %get-tuple-element.50.wide_rows, f32[32,128]{1,0:T(8,128)S(1)} %get-tuple-element.48.vertical), custom_call_target="tpu_custom_call" | custom-call | flops 15728640 | bytes 2097152 | tf_op jit(solution)/shard_map/pallas_call | solution.py:860
  65.5 1.9 %shard_map.141 = f32[16,16,8,128]{3,2,1,0:T(8,128)} custom-call(s32[4]{0:T(128)S(1)} %pad_add_fusion.own_ref.even_ref.refs_0_, f32[6,10,16,128]{3,2,1,0:T(8,128)S(1)} %get-tuple-element.55.edges, f32[2,2,8,128]{3,2,1,0:T(8,128)S(1)} %get-tuple-element.56.ends, f32[16,16,8,128]{3,2,1,0:T(8,128)} %get-tuple-element.57._, ...), custom_call_target="tpu_custom_call", output_to_operand_aliasing={{}: (3, {})} | custom-call | flops 15728640 | bytes 2097152 | tf_op jit(solution)/shard_map/pallas_call | solution.py:886
  (19 shorter events, 3.4 us)
Async XLA Ops:
  0.7 1.2 %copy-start = (f32[16,16,8,128]{3,2,1,0:T(8,128)S(1)}, f32[16,16,8,128]{3,2,1,0:T(8,128)}, u32[]{:S(2)}) copy-start(f32[16,16,8,128]{3,2,1,0:T(8,128)} %given.1) | copy-start | bytes 3145732
  2.7 11.7 %collective-permute-start.2 = (f32[16,16,128]{2,1,0:T(8,128)S(1)}, f32[16,16,128]{2,1,0:T(8,128)S(1)}, u32[]{:S(2)}, u32[]{:S(2)}) collective-permute-start(f32[16,16,128]{2,1,0:T(8,128)S(1)} %get-tuple-element.39), channel_id=1, source_target_pairs={{0,1},{2,3},{4,5},{6,7},{1,0},{3,2},{5,4},{7,6},{8,9},{10,11},{12,... | collective-permute-start | bytes 393224 | tf_op jit(solution)/shard_map/ppermute | solution.py:678
  4.4 10.0 %collective-permute-start.3 = (f32[16,16,128]{2,1,0:T(8,128)S(1)}, f32[16,16,128]{2,1,0:T(8,128)S(1)}, u32[]{:S(2)}, u32[]{:S(2)}) collective-permute-start(f32[16,16,128]{2,1,0:T(8,128)S(1)} %get-tuple-element.40), channel_id=1, source_target_pairs={{1,2},{3,4},{5,6},{2,1},{4,3},{6,5},{9,10},{11,12},{13,14},{10,9},... | collective-permute-start | bytes 393224 | tf_op jit(solution)/shard_map/ppermute | solution.py:678
  6.3 8.1 %collective-permute-start = (f32[8,16,128]{2,1,0:T(8,128)S(1)}, f32[8,16,128]{2,1,0:T(8,128)S(1)}, u32[]{:S(2)}, u32[]{:S(2)}) collective-permute-start(f32[8,16,128]{2,1,0:T(8,128)S(1)} %get-tuple-element.37), channel_id=1, source_target_pairs={{0,8},{16,24},{8,0},{24,16},{1,9},{17,25},{9,1},{25,17},{2,10},{18... | collective-permute-start | bytes 196616 | tf_op jit(solution)/shard_map/ppermute | solution.py:678
  6.9 7.5 %collective-permute-start.1 = (f32[8,16,128]{2,1,0:T(8,128)S(1)}, f32[8,16,128]{2,1,0:T(8,128)S(1)}, u32[]{:S(2)}, u32[]{:S(2)}) collective-permute-start(f32[8,16,128]{2,1,0:T(8,128)S(1)} %get-tuple-element.38), channel_id=1, source_target_pairs={{8,16},{16,8},{9,17},{17,9},{10,18},{18,10},{11,19},{19,11},{12,20... | collective-permute-start | bytes 196616 | tf_op jit(solution)/shard_map/ppermute | solution.py:678
  15.1 11.2 %collective-permute-start.6 = (f32[16,16,128]{2,1,0:T(8,128)S(1)}, f32[16,16,128]{2,1,0:T(8,128)S(1)}, u32[]{:S(2)}, u32[]{:S(2)}) collective-permute-start(f32[16,16,128]{2,1,0:T(8,128)S(1)} %get-tuple-element.44), channel_id=1, source_target_pairs={{0,1},{2,3},{4,5},{6,7},{1,0},{3,2},{5,4},{7,6},{8,9},{10,11},{12,... | collective-permute-start | bytes 393224 | tf_op jit(solution)/shard_map/ppermute | solution.py:678
  16.1 10.2 %collective-permute-start.7 = (f32[16,16,128]{2,1,0:T(8,128)S(1)}, f32[16,16,128]{2,1,0:T(8,128)S(1)}, u32[]{:S(2)}, u32[]{:S(2)}) collective-permute-start(f32[16,16,128]{2,1,0:T(8,128)S(1)} %get-tuple-element.45), channel_id=1, source_target_pairs={{1,2},{3,4},{5,6},{2,1},{4,3},{6,5},{9,10},{11,12},{13,14},{10,9},... | collective-permute-start | bytes 393224 | tf_op jit(solution)/shard_map/ppermute | solution.py:678
  19.1 5.1 %collective-permute-start.4 = (f32[8,16,128]{2,1,0:T(8,128)S(1)}, f32[8,16,128]{2,1,0:T(8,128)S(1)}, u32[]{:S(2)}, u32[]{:S(2)}) collective-permute-start(f32[8,16,128]{2,1,0:T(8,128)S(1)} %get-tuple-element.42), channel_id=1, source_target_pairs={{0,8},{16,24},{8,0},{24,16},{1,9},{17,25},{9,1},{25,17},{2,10},{18... | collective-permute-start | bytes 196616 | tf_op jit(solution)/shard_map/ppermute | solution.py:678
  19.2 7.1 %collective-permute-start.5 = (f32[8,16,128]{2,1,0:T(8,128)S(1)}, f32[8,16,128]{2,1,0:T(8,128)S(1)}, u32[]{:S(2)}, u32[]{:S(2)}) collective-permute-start(f32[8,16,128]{2,1,0:T(8,128)S(1)} %get-tuple-element.43), channel_id=1, source_target_pairs={{8,16},{16,8},{9,17},{17,9},{10,18},{18,10},{11,19},{19,11},{12,20... | collective-permute-start | bytes 196616 | tf_op jit(solution)/shard_map/ppermute | solution.py:678
  28.4 10.6 %all-to-all-start = ((f32[32,5,2,128]{3,2,1,0:T(2,128)}), f32[32,5,2,128]{3,2,1,0:T(2,128)S(1)}, u32[]{:S(2)}, u32[]{:S(2)}) async-start(f32[32,5,2,128]{3,2,1,0:T(2,128)} %bitcast.10), calls=%async_computation | async-start | bytes 327680 | tf_op jit(solution)/shard_map/all_to_all | solution.py:852
  33.1 13.8 %collective-permute-start.8 = (f32[640,128]{1,0:T(8,128)S(1)}, f32[640,128]{1,0:T(8,128)S(1)}, u32[]{:S(2)}, u32[]{:S(2)}) collective-permute-start(f32[640,128]{1,0:T(8,128)S(1)} %get-tuple-element.53), channel_id=1, source_target_pairs={{0,1},{2,3},{4,5},{6,7},{1,0},{3,2},{5,4},{7,6},{8,9},{10,11},{12,... | collective-permute-start | bytes 983048 | tf_op jit(solution)/shard_map/ppermute | solution.py:678
  34.7 18.7 %collective-permute-start.9 = (f32[640,128]{1,0:T(8,128)S(1)}, f32[640,128]{1,0:T(8,128)S(1)}, u32[]{:S(2)}, u32[]{:S(2)}) collective-permute-start(f32[640,128]{1,0:T(8,128)S(1)} %get-tuple-element.54), channel_id=1, source_target_pairs={{1,2},{3,4},{5,6},{2,1},{4,3},{6,5},{9,10},{11,12},{13,14},{10,9},... | collective-permute-start | bytes 983048 | tf_op jit(solution)/shard_map/ppermute | solution.py:678
  41.2 21.8 %all-to-all-start.1 = ((f32[32,16,128]{2,1,0:T(8,128)}), f32[32,16,128]{2,1,0:T(8,128)S(1)}, u32[]{:S(2)}, u32[]{:S(2)}) async-start(f32[32,16,128]{2,1,0:T(8,128)} %shard_map.137), calls=%async_computation.1 | async-start | bytes 524288 | tf_op jit(solution)/shard_map/all_to_all | solution.py:859
  54.0 11.4 %collective-permute-start.10 = (f32[360,128]{1,0:T(8,128)S(1)}, f32[360,128]{1,0:T(8,128)S(1)}, u32[]{:S(2)}, u32[]{:S(2)}) collective-permute-start(f32[360,128]{1,0:T(8,128)S(1)} %get-tuple-element.58), channel_id=1, source_target_pairs={{0,8},{16,24},{8,0},{24,16},{1,9},{17,25},{9,1},{25,17},{2,10},{18... | collective-permute-start | bytes 552968 | tf_op jit(solution)/shard_map/ppermute | solution.py:678
  54.7 10.7 %collective-permute-start.11 = (f32[360,128]{1,0:T(8,128)S(1)}, f32[360,128]{1,0:T(8,128)S(1)}, u32[]{:S(2)}, u32[]{:S(2)}) collective-permute-start(f32[360,128]{1,0:T(8,128)S(1)} %get-tuple-element.59), channel_id=1, source_target_pairs={{8,16},{16,8},{9,17},{17,9},{10,18},{18,10},{11,19},{19,11},{12,20... | collective-permute-start | bytes 552968 | tf_op jit(solution)/shard_map/ppermute | solution.py:678

commit v5 on v4

--- a/solution.py
+++ b/solution.py
@@ -17,6 +17,9 @@
 EVERY = ("gx", "gy", "ga")
 HIGHEST = lax.Precision.HIGHEST
 VMEM_LIMIT = 4 * 1024 * 1024
+FACE_COPIES = 4
+
+SPARE_Y, SPARE_X = 24, 160
 
 
 def vmem_call(
@@ -51,20 +54,28 @@
         ref[pl.ds(first * plane + at, 8, stride=plane), :] = value[first : first + 8]
 
 
-def faces_kernel(shape, even_ref, rows_ref, x_one, x_other, y_one, y_other):
-    wide, deep, species, _ = shape
-    even_x, even_y = even_ref[0] == 1, even_ref[1] == 1
-    plane = wide * deep
-    for y in range(deep):
-        low = planes_of_species(rows_ref, species, plane, y)
-        high = planes_of_species(rows_ref, species, plane, (wide - 1) * deep + y)
-        x_one[y] = jnp.where(even_x, high, low)
-        x_other[y] = jnp.where(even_x, low, high)
+def faces_kernel(shape, own_ref, given, x_one, x_other, y_one, y_other, held, semaphores):
+    wide, deep, species, up = shape
+    even_x, even_y = own_ref[0] == 1, own_ref[1] == 1
+    plane, together = wide * deep, -(-wide // FACE_COPIES)
+    copies = {}
+    for x in range(0, wide, together):
+        some = pl.ds(x, min(together, wide - x))
+        copies[x] = pltpu.make_async_copy(
+            given.at[:, some], held.at[:, some], semaphores.at[x // together]
+        )
+        copies[x].start()
+    rows = held.reshape(species * plane, up)
     for x in range(wide):
-        low = planes_of_species(rows_ref, species, plane, x * deep)
-        high = planes_of_species(rows_ref, species, plane, x * deep + deep - 1)
+        if x in copies:
+            copies[x].wait()
+        low = planes_of_species(rows, species, plane, x * deep)
+        high = planes_of_species(rows, species, plane, x * deep + deep - 1)
         y_one[x] = jnp.where(even_y, high, low)
         y_other[x] = jnp.where(even_y, low, high)
+        if x in (0, wide - 1):
+            face = jnp.swapaxes(held[:, x], 0, 1)
+            to_one_or_other(even_x, x_one, x_other, x > 0, face)
 
 
 def tiled(matrix, count):
@@ -80,20 +91,22 @@
     return jnp.where(of_row(row) == of_column(column), matrix, 0.0)
 
 
-def prepare_kernel(shape, ranks, own_ref, given, *refs):
-    wide, deep, species, up = shape
-    ranks_a, _ = ranks
-    held, semaphores, refs = refs[-11:-1], refs[-1], refs[:-11]
+def fetched(sources, held, semaphores):
     copies = [
         pltpu.make_async_copy(source, target, semaphores.at[at])
-        for at, (source, target) in enumerate(zip(refs[:10], held))
+        for at, (source, target) in enumerate(zip(sources, held))
     ]
     for copy in copies:
         copy.start()
-    (flow, thermal, diffusivity, constant, energy, production, turned, vertical, east,
-     north) = held
-    (field, rates, speeds, coefficients, mix, squeeze, wide_rows, upright,
-     *factor_rows) = refs[10:]
+    return copies
+
+
+def prepare_kernel(shape, given, *refs):
+    wide, deep, species, up = shape
+    held, semaphores = refs[-7:-1], refs[-1]
+    copies = fetched(refs[:6], held, semaphores)
+    flow, thermal, diffusivity, constant, energy, production = held
+    field, rates, speeds, coefficients, mix = refs[6:-7]
     for x in range(wide):
         field[x] = jnp.swapaxes(given[:, x], 0, 1)
     for copy in copies:
@@ -113,6 +126,17 @@
         for y in range(deep):
             rates[x, y] = coefficients[1] * jnp.exp(coefficients[2] * inverse[y : y + 1])
     mix[...] = tiled(time_step * production[...], mix.shape[1] // species)
+
+
+def matrices_kernel(shape, own_ref, *refs):
+    wide, _, species, _ = shape
+    held, semaphores = refs[-5:-1], refs[-1]
+    copies = fetched(refs[:4], held, semaphores)
+    turned, vertical, east, north = held
+    squeeze, wide_rows, upright, factor_rows = refs[4:-5]
+    for copy in copies:
+        copy.wait()
+    ranks_a = turned.shape[0]
     full = tiled(turned[...], wide)
     full = [jnp.broadcast_to(full[a : a + 1], (wide, full.shape[1])) for a in range(ranks_a)]
     full = jnp.concatenate(full, axis=0)
@@ -124,12 +148,12 @@
         preferred_element_type=jnp.float32,
     )
     upright[...] = vertical[...]
-    if factor_rows:
-        def two_rows(ref, at):
-            return jnp.concatenate([ref[pl.ds(2 * at + row, 1), :] for row in range(2)], axis=1)
-
-        factor_rows[0][0:1] = two_rows(east, own_ref[3])
-        factor_rows[0][1:2] = two_rows(north, own_ref[2])
+
+    def two_rows(ref, at):
+        return jnp.concatenate([ref[pl.ds(2 * at + row, 1), :] for row in range(2)], axis=1)
+
+    factor_rows[0:1] = two_rows(east, own_ref[3])
+    factor_rows[1:2] = two_rows(north, own_ref[2])
 
 
 def halves_of(value):
@@ -234,8 +258,9 @@
     )
 
 
-def block_kernel(shape, field, rates, flow, coefficients, mix_ref, out):
+def block_kernel(shape, held, field, *refs):
     wide, deep, species, up = shape
+    rates, (flow, coefficients, mix_ref, out) = refs[0] if held else None, refs[held:]
 
     def x_beside(x, side):
         at = x + 2 * side - 1
@@ -250,7 +275,7 @@
 
     planes_advanced(
         range(wide), lambda x: field[x], x_beside, y_beside,
-        lambda x: rates[x],
+        lambda x: rates[x] if held else own_rates(flow, coefficients, x, deep),
         lambda x: [rows_for_species(speed, species) for speed in own_speeds(flow, x, deep)],
         coefficients[0][None], mixing(mix_ref[...]), emit,
     )
@@ -396,8 +421,8 @@
 
 
 def third_step_kernel(
-    shape, counts, own_ref, field, y_one, y_other, flow, coefficients, mix_ref, edges, ends, out,
-    inner, ready, semaphores,
+    shape, counts, own_ref, block, field, y_one, y_other, flow, coefficients, mix_ref, edges, ends,
+    out, inner, ready, semaphores,
 ):
     wide, deep, species, up = shape
     _, columns = counts
@@ -405,48 +430,51 @@
     inside = (column > 0, column < columns - 1)
     diffusivity, mix = coefficients[0][None], mixing(mix_ref[...])
 
-    def beside(side, x, rows):
-        return choose(even_y, y_one, y_other, side, rows)
+    def outer(side, x):
+        return choose(even_y, y_one, y_other, side, outer_of(x, species))
+
+    def others(side, x):
+        return choose(even_y, y_one, y_other, side, flow_of(x, wide, species))
 
     def here(x):
-        at = outer_of(x, species)
-        return jnp.concatenate(
-            [beside(0, x, at)[None], field[x], beside(1, x, at)[None]], axis=0
-        )
+        return jnp.stack([outer(0, x), outer(1, x)])
 
     def x_beside(x, side):
         at = x + 2 * side - 1
-        return here(at) if 0 <= at < wide else jnp.zeros((deep + 2, species, up), jnp.float32)
+        return here(at) if 0 <= at < wide else jnp.zeros((2, species, up), jnp.float32)
 
     def y_beside(x, side):
-        plane, beyond = here(x), beside(side, x, inner_of(x, species))[None]
-        return jnp.concatenate([plane[1:], beyond] if side else [beyond, plane[:-1]], axis=0)
-
-    def others(side, x):
-        return beside(side, x, flow_of(x, wide, species))
-
-    def rates(x):
-        sides = [rate_of(others(side, x)[3:4], coefficients)[None] for side in range(2)]
-        return jnp.concatenate([sides[0], own_rates(flow, coefficients, x, deep), sides[1]], axis=0)
-
-    def speeds(x):
-        ends, own = [others(side, x) for side in range(2)], own_speeds(flow, x, deep)
-        return [
-            rows_for_species([ends[0][d : d + 1]] + own[d] + [ends[1][d : d + 1]], species)
+        beyond = choose(even_y, y_one, y_other, side, inner_of(x, species))
+        return jnp.stack([field[x, 0], beyond] if side else [beyond, field[x, deep - 1]])
+
+    def emit(x, plane):
+        for side in range(2):
+            inner[x, side * (deep + 1)] = jnp.where(inside[side], plane[side], 0.0)
+
+    planes_advanced(
+        range(wide), here, x_beside, y_beside,
+        lambda x: jnp.stack([rate_of(others(side, x)[3:4], coefficients) for side in range(2)]),
+        lambda x: [
+            rows_for_species([others(side, x)[d : d + 1] for side in range(2)], species)
             for d in range(3)
-        ]
-
-    def emit(x, plane):
-        inner[x, 0] = jnp.where(inside[0], plane[0], 0.0)
-        inner[x, 1 : deep + 1] = plane[1 : deep + 1]
-        inner[x, deep + 1] = jnp.where(inside[1], plane[deep + 1], 0.0)
+        ],
+        diffusivity, mix, emit, 16,
+    )
+
+    def row(x, y):
+        return jnp.broadcast_to(flow[1, x, pl.ds(y, 1), :], (species, up))
+
+    for x in range(wide):
+        inner[x, 1] = block[x, 0] + from_beyond(outer(0, x), 0, row(x, 0), diffusivity[0])
+        inner[x, 2:deep] = block[x, 1 : deep - 1]
+        inner[x, deep] = block[x, deep - 1] + from_beyond(
+            outer(1, x), 1, row(x, deep - 1), diffusivity[0]
+        )
         if x < 3 or x >= wide - 3:
             edges[x if x < 3 else x - wide + 6] = inner[x]
         if x in (0, wide - 1):
             for side in range(2):
                 ends[0 if x == 0 else 1, side, 0:4] = others(side, x)
-
-    planes_advanced(range(wide), here, x_beside, y_beside, rates, speeds, diffusivity, mix, emit)
 
     inmost = range(2, wide - 2)
     copies = planes_copied(
@@ -790,38 +818,37 @@
     row, column = lax.axis_index(ROW), lax.axis_index(COLUMN)
     own = jnp.stack([1 - row % 2, 1 - column % 2, row, column]).astype(jnp.int32)
     face_shapes = [(deep, species, up)] * 2 + [(wide, species, up)] * 2
-    field_rows = mixture_fields_initial.reshape(species * wide * deep, up)
-    faces = vmem_call(functools.partial(faces_kernel, shape), face_shapes, 1, 2)(own, field_rows)
+    faces = vmem_call(
+        functools.partial(faces_kernel, shape), face_shapes, 1, 2,
+        scratch=[mixture_fields_initial.shape], placed=[1], copies=FACE_COPIES,
+    )(own, pltpu.with_memory_space_constraint(mixture_fields_initial, pltpu.HBM))
     faces = faces_beside(faces)
-    out_shapes = [
-        shape, shape, (4, wide, deep, up), (3, species, up), (species, 128),
-        (wide * ranks_a, wide * species), (species, wide * ranks_a), (ranks_d, up),
-    ] + [(2, 128)] * kernels_fit
-    small = (
-        flow_speed_vector, thermal_field, mass_diffusivity[None], arrhenius_constant[None],
-        arrhenius_energy_temp[None], production_coefficients,
-        tucker_factor_component.T, tucker_factor_vertical.T, tucker_factor_east,
-        tucker_factor_north,
-    )
-    vmem, smem = (pl.BlockSpec(memory_space=space) for space in (pltpu.VMEM, pltpu.SMEM))
-    (field, rates, speeds, coefficients, mix, squeeze, wide_rows, upright,
-     *factor_rows) = pl.pallas_call(
-        functools.partial(prepare_kernel, shape, (ranks_a, ranks_d)),
-        in_specs=[smem, vmem] + [pl.BlockSpec(memory_space=pltpu.HBM)] * len(small),
-        out_specs=[vmem] * len(out_shapes),
-        out_shape=[jax.ShapeDtypeStruct(out, jnp.float32) for out in out_shapes],
-        scratch_shapes=[pltpu.VMEM(array.shape, jnp.float32) for array in small]
-        + [pltpu.SemaphoreType.DMA((len(small),))],
-        compiler_params=pltpu.CompilerParams(vmem_limit_bytes=VMEM_LIMIT),
-        cost_estimate=pl.CostEstimate(
-            flops=4 * cells, bytes_accessed=12 * cells, transcendentals=cells
+    def with_fetches(kernel, given, small, outs, **cost):
+        call = vmem_call(
+            kernel, outs, int(given is own), 1 + len(small),
+            scratch=[array.shape for array in small], placed=range(1, 1 + len(small)),
+            copies=len(small), **cost,
+        )
+        return call(
+            given, *(pltpu.with_memory_space_constraint(array, pltpu.HBM) for array in small)
+        )
+
+    field, rates, speeds, coefficients, mix = with_fetches(
+        functools.partial(prepare_kernel, shape),
+        mixture_fields_initial,
+        (
+            flow_speed_vector, thermal_field, mass_diffusivity[None], arrhenius_constant[None],
+            arrhenius_energy_temp[None], production_coefficients,
         ),
-    )(
-        own, mixture_fields_initial,
-        *(pltpu.with_memory_space_constraint(array, pltpu.HBM) for array in small),
-    )
-    block = vmem_call(
-        functools.partial(block_kernel, shape), [shape], 0, 5, flops=60 * cells, moved=8 * cells
+        [shape, shape, (4, wide, deep, up), (3, species, up), (species, 128)],
+        flops=4 * cells, moved=12 * cells, exps=cells,
+    )
+    block, last_block = (
+        vmem_call(
+            functools.partial(block_kernel, shape, held), [shape], 0, 4 + held,
+            flops=60 * cells, moved=8 * cells,
+        )
+        for held in (1, 0)
     )
     advance = vmem_call(
         functools.partial(advance_kernel, shape), [shape] + face_shapes, 1, 8,
@@ -832,19 +859,28 @@
         field, *faces = advance(
             own, *block(field, *fixed), *faces, speeds, coefficients
         )
+        first = field
         faces = faces_beside(faces)
     high = 2 * species + 4
     snapshot, *y_faces = vmem_call(
-        functools.partial(snapshot_kernel, shape), [shape] + [(wide * high + 64, up)] * 2, 1, 8,
+        functools.partial(snapshot_kernel, shape), [shape] + [(wide * high + SPARE_Y, up)] * 2, 1, 8,
         flops=4 * cells, moved=8 * cells,
     )(own, *block(field, *fixed), *faces, speeds, coefficients)
     y_faces = swapped(*y_faces, COLUMN)
-    x_faces = vmem_call(
-        functools.partial(wide_faces_kernel, shape), [((deep + 1) * high + 36, up)] * 2, 1, 5,
-        flops=cells, moved=cells,
-    )(own, snapshot, *y_faces, speeds)
-    x_faces = swapped(*x_faces, ROW)
     if kernels_fit:
+        own, _ = lax.optimization_barrier((own, first))
+        squeeze, wide_rows, upright, *factor_rows = with_fetches(
+            functools.partial(matrices_kernel, shape),
+            own,
+            (
+                tucker_factor_component.T, tucker_factor_vertical.T, tucker_factor_east,
+                tucker_factor_north,
+            ),
+            [
+                (wide * ranks_a, wide * species), (species, wide * ranks_a), (ranks_d, up),
+                (2, 128),
+            ],
+        )
         (sent,) = vmem_call(
             functools.partial(project_kernel, shape, (ranks_a, ranks_d)),
             [(devices * (deep + 2), 128)], 0, 4, flops=60 * cells, moved=4 * cells,
@@ -856,6 +892,7 @@
             functools.partial(core_kernel, (rows, columns, ranks_a, own_c, deep)),
             [(devices, own_c + deep, 128)], 0, 1, flops=60 * cells, moved=4 * cells,
         )(got.reshape(devices * (deep + 2), 128))
+        sent, later = lax.optimization_barrier((sent, snapshot))
         got = lax.all_to_all(sent, EVERY, 0, 0, tiled=True)
         residual, tucker_core = vmem_call(
             functools.partial(expand_kernel, shape, (ranks_a, ranks_d), own_c),
@@ -874,14 +911,23 @@
         tucker_core, residual = compress_and_expand(
             snapshot, east, north, tucker_factor_vertical, tucker_factor_component
         )
+        later = snapshot
     fixed = fixed[1:]
+    (third,) = last_block(later, *fixed)
+    own_wide, third = lax.optimization_barrier((own, third))
+    x_faces = vmem_call(
+        functools.partial(wide_faces_kernel, shape),
+        [((deep + 1) * high - 4 + spare, up) for spare in (SPARE_X, 0)], 1, 5,
+        flops=cells, moved=cells,
+    )(own_wide, snapshot, *y_faces, speeds)
+    x_faces = swapped(*x_faces, ROW)
     edges, ends, inmost = vmem_call(
         functools.partial(third_step_kernel, shape, (rows, columns)),
-        [(6, deep + 2, species, up), (2, 2, 8, up), mixture_fields_initial.shape], 1, 7,
+        [(6, deep + 2, species, up), (2, 2, 8, up), mixture_fields_initial.shape], 1, 8,
         flops=120 * cells, moved=16 * cells,
-        scratch=[(wide, deep + 2, species, up), (species, wide - 4, deep, up)], placed=[9],
+        scratch=[(wide, deep + 2, species, up), (species, wide - 4, deep, up)], placed=[10],
         copies=-(-(wide - 4) // 4),
-    )(own, snapshot, *y_faces, *fixed)
+    )(own, third, snapshot, *y_faces, *fixed)
     own, _ = lax.optimization_barrier((own, tucker_core))
     (mixture_fields_final,) = vmem_call(
         functools.partial(fourth_step_kernel, shape, (rows, columns)),

time: 67.7 us -> 65.4 us (0.966)
  the two profiles are of different devices: /device:TPU:18 before, /device:TPU:3 now
where the time goes in v5:
time: 65.4 us; the launch traced here: 65 us
  starting transfers between devices  36.9 us (56%)
  Pallas kernels  21.5 us (33%)
  waiting for transfers between devices  5.6 us (9%)
  between operations  0.89 us (1%)
    ppermute x12, starting transfers between devices, swapped(): got.append(lax.ppermute(face, axes, couples + [(b, a) for a, b in couples]))  29.3 us
    all_to_all x1, starting transfers between devices, body(): got = lax.all_to_all(sent, EVERY, 0, 0, tiled=True)  4.26 us
    ppermute x12, waiting for transfers between devices, swapped(): got.append(lax.ppermute(face, axes, couples + [(b, a) for a, b in couples]))  4.16 us
    all_to_all x1, starting transfers between devices, body(): lax.all_to_all(sent.reshape(devices, (deep + 2) // 2, 2, 128), EVERY, 0,...  3.39 us
    pallas_call x1, Pallas kernels, body(): vmem_call(functools.partial(third_step_kernel, shape, (rows, columns)), [...  2.92 us
    pallas_call x2, Pallas kernels, with_fetches(): call(given, *(pltpu.with_memory_space_constraint(array, pltpu.HBM) for ar...  2.8 us
    pallas_call x1, Pallas kernels, body(): vmem_call(functools.partial(expand_kernel, shape, (ranks_a, ranks_d), own...  2.44 us
    pallas_call x2, Pallas kernels, body(): block(field, *fixed)  2.25 us
  transfers between devices with their start and end apart: 14, of which 3 were waited for; matrix products, arithmetic and copies ran while one was open for 0% of the time, Pallas kernels for 23%

profile of v5, /device:TPU:3, one launch (start us, length us, event | category | flops | bytes accessed | tf_op | source)
XLA Modules:
  0.0 65.0 jit_solution(10470614150068262462)
XLA Ops:
  0.7 1.8 %shard_map.132 = (f32[8,16,128]{2,1,0:T(8,128)S(1)}, f32[8,16,128]{2,1,0:T(8,128)S(1)}, f32[16,16,128]{2,1,0:T(8,128)S(1)}, f32[16,16,128]{2,1,0:T(8,128)S(1)}) custom-call(s32[4]{0:T(128)S(1)} %pad_add_fusion.own_ref.refs_0_, f32[16,16,8,128]{3,2,1,0:T(8,128)} %given.3), custom_call_target="tpu_custom_call" | custom-call | tf_op jit(solution)/shard_map/pallas_call | solution.py:821
  2.6 1.4 %collective-permute-start.2 = (f32[16,16,128]{2,1,0:T(8,128)S(1)}, f32[16,16,128]{2,1,0:T(8,128)S(1)}, u32[]{:S(2)}, u32[]{:S(2)}) collective-permute-start(f32[16,16,128]{2,1,0:T(8,128)S(1)} %get-tuple-element.44), channel_id=1, source_target_pairs={{0,1},{2,3},{4,5},{6,7},{1,0},{3,2},{5,4},{7,6},{8,9},{10,11},{12,... | collective-permute-start | bytes 393224 | tf_op jit(solution)/shard_map/ppermute | solution.py:706
  3.9 4.9 %collective-permute-start.3 = (f32[16,16,128]{2,1,0:T(8,128)S(1)}, f32[16,16,128]{2,1,0:T(8,128)S(1)}, u32[]{:S(2)}, u32[]{:S(2)}) collective-permute-start(f32[16,16,128]{2,1,0:T(8,128)S(1)} %get-tuple-element.45), channel_id=1, source_target_pairs={{1,2},{3,4},{5,6},{2,1},{4,3},{6,5},{9,10},{11,12},{13,14},{10,9},... | collective-permute-start | bytes 393224 | tf_op jit(solution)/shard_map/ppermute | solution.py:706
  9.2 4.1 %collective-permute-start.1 = (f32[8,16,128]{2,1,0:T(8,128)S(1)}, f32[8,16,128]{2,1,0:T(8,128)S(1)}, u32[]{:S(2)}, u32[]{:S(2)}) collective-permute-start(f32[8,16,128]{2,1,0:T(8,128)S(1)} %get-tuple-element.43), channel_id=1, source_target_pairs={{8,16},{16,8},{9,17},{17,9},{10,18},{18,10},{11,19},{19,11},{12,20... | collective-permute-start | bytes 196616 | tf_op jit(solution)/shard_map/ppermute | solution.py:706
  13.3 1.3 %shard_map.130 = (f32[16,8,16,128]{3,2,1,0:T(8,128)S(1)}, f32[16,8,16,128]{3,2,1,0:T(8,128)S(1)}, f32[4,16,8,128]{3,2,1,0:T(8,128)S(1)}, f32[3,16,128]{2,1,0:T(8,128)S(1)}, f32[16,128]{1,0:T(8,128)S(1)}) custom-call(f32[16,16,8,128]{3,2,1,0:T(8,128)S(1)} %copy-done, f32[3,16,8,128]{3,2,1,0:T(8,128)} %refs_0_.1, f32[16,8,128]{2,1,0:T(8,128)} %refs_1_.1, ...), custom_call_target="tpu_custom_call" | custom-call | flops 1048576 | bytes 3145728 | tf_op jit(solution)/shard_map/pallas_call | solution.py:832
  16.4 4.3 %collective-permute-start.7 = (f32[16,16,128]{2,1,0:T(8,128)S(1)}, f32[16,16,128]{2,1,0:T(8,128)S(1)}, u32[]{:S(2)}, u32[]{:S(2)}) collective-permute-start(f32[16,16,128]{2,1,0:T(8,128)S(1)} %get-tuple-element.51), channel_id=1, source_target_pairs={{1,2},{3,4},{5,6},{2,1},{4,3},{6,5},{9,10},{11,12},{13,14},{10,9},... | collective-permute-start | bytes 393224 | tf_op jit(solution)/shard_map/ppermute | solution.py:706
  20.8 4.1 %collective-permute-start.5 = (f32[8,16,128]{2,1,0:T(8,128)S(1)}, f32[8,16,128]{2,1,0:T(8,128)S(1)}, u32[]{:S(2)}, u32[]{:S(2)}) collective-permute-start(f32[8,16,128]{2,1,0:T(8,128)S(1)} %get-tuple-element.49), channel_id=1, source_target_pairs={{8,16},{16,8},{9,17},{17,9},{10,18},{18,10},{11,19},{19,11},{12,20... | collective-permute-start | bytes 196616 | tf_op jit(solution)/shard_map/ppermute | solution.py:706
  24.9 1.5 %shard_map.136 = (f32[128,256]{1,0:T(8,128)S(1)}, f32[16,128]{1,0:T(8,128)S(1)}, f32[32,128]{1,0:T(8,128)S(1)}, f32[2,128]{1,0:T(2,128)S(1)}) custom-call(s32[4]{0:T(128)S(1)} %pad_add_fusion.own_ref.refs_0_, f32[8,16]{1,0:T(8,128)} %bitcast.16, f32[32,128]{1,0:T(8,128)} %bitcast.15, f32[16,64]{1,0:T(8,128)} %refs_2_.1, f32[8,64]{1,0:T(8,128)} %refs_3_.1), custom_call_target="tpu_custom_call" | custom-call | tf_op jit(solution)/shard_map/pallas_call | solution.py:832
  26.5 1.2 %shard_map.134.refs_1_ = f32[16,8,16,128]{3,2,1,0:T(8,128)S(1)} custom-call(f32[16,8,16,128]{3,2,1,0:T(8,128)S(1)} %get-tuple-element.46.field, f32[16,8,16,128]{3,2,1,0:T(8,128)S(1)} %get-tuple-element.38.refs_0_, f32[4,16,8,128]{3,2,1,0:T(8,128)S(1)} %get-tuple-element.39.refs_1_.refs_6_.refs_0_.flow, ...), custom_call_target="tpu_custom_call" | custom-call | flops 15728640 | bytes 2097152 | tf_op jit(solution)/shard_map/pallas_call | solution.py:868
  28.4 1.4 %shard_map.137 = f32[320,128]{1,0:T(8,128)} custom-call(f32[16,8,16,128]{3,2,1,0:T(8,128)S(1)} %get-tuple-element.60.field, f32[128,256]{1,0:T(8,128)S(1)} %get-tuple-element.53.component, f32[32,128]{1,0:T(8,128)S(1)} %get-tuple-element.54.vertical, f32[2,128]{1,0:T(2,128)S(1)} %get-tuple-element.55.factor_rows), custom_call_target="tpu_custom_call" | custom-call | flops 15728640 | bytes 1048576 | tf_op jit(solution)/shard_map/pallas_call | solution.py:884
  29.8 3.4 %all-to-all-start = ((f32[32,5,2,128]{3,2,1,0:T(2,128)}), f32[32,5,2,128]{3,2,1,0:T(2,128)S(1)}, u32[]{:S(2)}, u32[]{:S(2)}) async-start(f32[32,5,2,128]{3,2,1,0:T(2,128)} %bitcast.9), calls=%async_computation | async-start | bytes 327680 | tf_op jit(solution)/shard_map/all_to_all | solution.py:888
  33.2 1.3 %collective-permute-start.8 = (f32[600,128]{1,0:T(8,128)S(1)}, f32[600,128]{1,0:T(8,128)S(1)}, u32[]{:S(2)}, u32[]{:S(2)}) collective-permute-start(f32[600,128]{1,0:T(8,128)S(1)} %get-tuple-element.62), channel_id=1, source_target_pairs={{0,1},{2,3},{4,5},{6,7},{1,0},{3,2},{5,4},{7,6},{8,9},{10,11},{12,... | collective-permute-start | bytes 921608 | tf_op jit(solution)/shard_map/ppermute | solution.py:706
  34.4 4.5 %collective-permute-start.9 = (f32[600,128]{1,0:T(8,128)S(1)}, f32[600,128]{1,0:T(8,128)S(1)}, u32[]{:S(2)}, u32[]{:S(2)}) collective-permute-start(f32[600,128]{1,0:T(8,128)S(1)} %get-tuple-element.63), channel_id=1, source_target_pairs={{1,2},{3,4},{5,6},{2,1},{4,3},{6,5},{9,10},{11,12},{13,14},{10,9},... | collective-permute-start | bytes 921608 | tf_op jit(solution)/shard_map/ppermute | solution.py:706
  38.9 1.4 %all-to-all-done = f32[32,5,2,128]{3,2,1,0:T(2,128)S(1)} async-done(((f32[32,5,2,128]{3,2,1,0:T(2,128)}), f32[32,5,2,128]{3,2,1,0:T(2,128)S(1)}, u32[]{:S(2)}, u32[]{:S(2)}) %all-to-all-start) | async-done | bytes 163872 | tf_op jit(solution)/shard_map/all_to_all | solution.py:888
  40.4 2.2 %shard_map.138 = f32[32,16,128]{2,1,0:T(8,128)} custom-call(f32[320,128]{1,0:T(8,128)S(1)} %bitcast.14), custom_call_target="tpu_custom_call" | custom-call | flops 15728640 | bytes 1048576 | tf_op jit(solution)/shard_map/pallas_call | solution.py:891
  42.6 4.3 %all-to-all-start.1 = ((f32[32,16,128]{2,1,0:T(8,128)}), f32[32,16,128]{2,1,0:T(8,128)S(1)}, u32[]{:S(2)}, u32[]{:S(2)}) async-start(f32[32,16,128]{2,1,0:T(8,128)} %shard_map.138), calls=%async_computation.1 | async-start | bytes 524288 | tf_op jit(solution)/shard_map/all_to_all | solution.py:896
  46.8 1.2 %shard_map.140.block = f32[16,8,16,128]{3,2,1,0:T(8,128)S(1)} custom-call(f32[16,8,16,128]{3,2,1,0:T(8,128)S(1)} %get-tuple-element.60.field, f32[4,16,8,128]{3,2,1,0:T(8,128)S(1)} %get-tuple-element.39.refs_1_.refs_6_.refs_0_.flow, f32[3,16,128]{2,1,0:T(8,128)S(1)} %get-tuple-element.40.refs_2_.refs_7_.refs_1_.coefficients, ...), custom_call_target="tpu_custom_call" | custom-call | flops 15728640 | bytes 2097152 | tf_op jit(solution)/shard_map/pallas_call | solution.py:916
  48.1 1.8 %collective-permute-done.9.y_other = f32[600,128]{1,0:T(8,128)S(1)} collective-permute-done((f32[600,128]{1,0:T(8,128)S(1)}, f32[600,128]{1,0:T(8,128)S(1)}, u32[]{:S(2)}, u32[]{:S(2)}) %collective-permute-start.9) | collective-permute-done | bytes 307232 | tf_op jit(solution)/shard_map/ppermute | solution.py:706
  49.9 1.2 %shard_map.142 = (f32[480,128]{1,0:T(8,128)S(1)}, f32[320,128]{1,0:T(8,128)}) custom-call(s32[4]{0:T(128)S(1)} %pad_add_fusion.own_ref.refs_0_, f32[16,8,16,128]{3,2,1,0:T(8,128)S(1)} %get-tuple-element.60.field, f32[600,128]{1,0:T(8,128)S(1)} %collective-permute-done.8.y_one, f32[600,128]{1,0:T(8,128)S(1)} %collective-permute-done.9.y_other, ...), custom_call_target="tpu_custom_call" | custom-call | flops 262144 | bytes 262144 | tf_op jit(solution)/shard_map/pallas_call | solution.py:918
  51.4 4.0 %collective-permute-start.11 = (f32[320,128]{1,0:T(8,128)}, f32[320,128]{1,0:T(8,128)S(1)}, u32[]{:S(2)}, u32[]{:S(2)}) collective-permute-start(f32[320,128]{1,0:T(8,128)} %get-tuple-element.69), channel_id=1, source_target_pairs={{8,16},{16,8},{9,17},{17,9},{10,18},{18,10},{11,19},{19,11},{12,20... | collective-permute-start | bytes 491528 | tf_op jit(solution)/shard_map/ppermute | solution.py:706
  55.4 2.9 %shard_map.141 = (f32[6,10,16,128]{3,2,1,0:T(8,128)S(1)}, f32[2,2,8,128]{3,2,1,0:T(8,128)S(1)}, f32[16,16,8,128]{3,2,1,0:T(8,128)}) custom-call(s32[4]{0:T(128)S(1)} %pad_add_fusion.own_ref.refs_0_, f32[16,8,16,128]{3,2,1,0:T(8,128)S(1)} %shard_map.140.block, f32[16,8,16,128]{3,2,1,0:T(8,128)S(1)} %get-tuple-element.60.field, ...), custom_call_target="tpu_custom_call" | custom-call | flops 31457280 | bytes 4194304 | tf_op jit(solution)/shard_map/pallas_call | solution.py:924
  58.3 2.4 %shard_map.139 = (f32[16,16,8,128]{3,2,1,0:T(8,128)}, f32[128,8,32]{2,1,0:T(8,128)}) custom-call(f32[512,128]{1,0:T(8,128)S(1)} %bitcast.13, f32[16,8,16,128]{3,2,1,0:T(8,128)S(1)} %get-tuple-element.60.field, f32[16,128]{1,0:T(8,128)S(1)} %get-tuple-element.57.wide_rows, f32[32,128]{1,0:T(8,128)S(1)} %get-tuple-element.54.vertical), custom_call_target="tpu_custom_call" | custom-call | flops 15728640 | bytes 2097152 | tf_op jit(solution)/shard_map/pallas_call | solution.py:897
  60.8 2.3 %collective-permute-done.11.x_other = f32[320,128]{1,0:T(8,128)S(1)} collective-permute-done((f32[320,128]{1,0:T(8,128)}, f32[320,128]{1,0:T(8,128)S(1)}, u32[]{:S(2)}, u32[]{:S(2)}) %collective-permute-start.11) | collective-permute-done | bytes 163872 | tf_op jit(solution)/shard_map/ppermute | solution.py:706
  63.1 1.8 %shard_map.143 = f32[16,16,8,128]{3,2,1,0:T(8,128)} custom-call(s32[4]{0:T(128)S(1)} %pad_add_fusion.own_ref.refs_0_, f32[6,10,16,128]{3,2,1,0:T(8,128)S(1)} %get-tuple-element.64.edges, f32[2,2,8,128]{3,2,1,0:T(8,128)S(1)} %get-tuple-element.65.ends, f32[16,16,8,128]{3,2,1,0:T(8,128)} %get-tuple-element.66._, ...), custom_call_target="tpu_custom_call", output_to_operand_aliasing={{}: (3, {})} | custom-call | flops 15728640 | bytes 2097152 | tf_op jit(solution)/shard_map/pallas_call | solution.py:932
  (21 shorter events, 3.3 us)
Async XLA Ops:
  0.6 12.6 %copy-start = (f32[16,16,8,128]{3,2,1,0:T(8,128)S(1)}, f32[16,16,8,128]{3,2,1,0:T(8,128)}, u32[]{:S(2)}) copy-start(f32[16,16,8,128]{3,2,1,0:T(8,128)} %given.3) | copy-start | bytes 3145732
  2.6 13.1 %collective-permute-start.2 = (f32[16,16,128]{2,1,0:T(8,128)S(1)}, f32[16,16,128]{2,1,0:T(8,128)S(1)}, u32[]{:S(2)}, u32[]{:S(2)}) collective-permute-start(f32[16,16,128]{2,1,0:T(8,128)S(1)} %get-tuple-element.44), channel_id=1, source_target_pairs={{0,1},{2,3},{4,5},{6,7},{1,0},{3,2},{5,4},{7,6},{8,9},{10,11},{12,... | collective-permute-start | bytes 393224 | tf_op jit(solution)/shard_map/ppermute | solution.py:706
  3.9 11.7 %collective-permute-start.3 = (f32[16,16,128]{2,1,0:T(8,128)S(1)}, f32[16,16,128]{2,1,0:T(8,128)S(1)}, u32[]{:S(2)}, u32[]{:S(2)}) collective-permute-start(f32[16,16,128]{2,1,0:T(8,128)S(1)} %get-tuple-element.45), channel_id=1, source_target_pairs={{1,2},{3,4},{5,6},{2,1},{4,3},{6,5},{9,10},{11,12},{13,14},{10,9},... | collective-permute-start | bytes 393224 | tf_op jit(solution)/shard_map/ppermute | solution.py:706
  8.9 6.8 %collective-permute-start = (f32[8,16,128]{2,1,0:T(8,128)S(1)}, f32[8,16,128]{2,1,0:T(8,128)S(1)}, u32[]{:S(2)}, u32[]{:S(2)}) collective-permute-start(f32[8,16,128]{2,1,0:T(8,128)S(1)} %get-tuple-element.42), channel_id=1, source_target_pairs={{0,8},{16,24},{8,0},{24,16},{1,9},{17,25},{9,1},{25,17},{2,10},{18... | collective-permute-start | bytes 196616 | tf_op jit(solution)/shard_map/ppermute | solution.py:706
  9.2 6.5 %collective-permute-start.1 = (f32[8,16,128]{2,1,0:T(8,128)S(1)}, f32[8,16,128]{2,1,0:T(8,128)S(1)}, u32[]{:S(2)}, u32[]{:S(2)}) collective-permute-start(f32[8,16,128]{2,1,0:T(8,128)S(1)} %get-tuple-element.43), channel_id=1, source_target_pairs={{8,16},{16,8},{9,17},{17,9},{10,18},{18,10},{11,19},{19,11},{12,20... | collective-permute-start | bytes 196616 | tf_op jit(solution)/shard_map/ppermute | solution.py:706
  16.4 11.3 %collective-permute-start.6 = (f32[16,16,128]{2,1,0:T(8,128)S(1)}, f32[16,16,128]{2,1,0:T(8,128)S(1)}, u32[]{:S(2)}, u32[]{:S(2)}) collective-permute-start(f32[16,16,128]{2,1,0:T(8,128)S(1)} %get-tuple-element.50), channel_id=1, source_target_pairs={{0,1},{2,3},{4,5},{6,7},{1,0},{3,2},{5,4},{7,6},{8,9},{10,11},{12,... | collective-permute-start | bytes 393224 | tf_op jit(solution)/shard_map/ppermute | solution.py:706
  16.4 11.2 %collective-permute-start.7 = (f32[16,16,128]{2,1,0:T(8,128)S(1)}, f32[16,16,128]{2,1,0:T(8,128)S(1)}, u32[]{:S(2)}, u32[]{:S(2)}) collective-permute-start(f32[16,16,128]{2,1,0:T(8,128)S(1)} %get-tuple-element.51), channel_id=1, source_target_pairs={{1,2},{3,4},{5,6},{2,1},{4,3},{6,5},{9,10},{11,12},{13,14},{10,9},... | collective-permute-start | bytes 393224 | tf_op jit(solution)/shard_map/ppermute | solution.py:706
  20.8 6.9 %collective-permute-start.4 = (f32[8,16,128]{2,1,0:T(8,128)S(1)}, f32[8,16,128]{2,1,0:T(8,128)S(1)}, u32[]{:S(2)}, u32[]{:S(2)}) collective-permute-start(f32[8,16,128]{2,1,0:T(8,128)S(1)} %get-tuple-element.48), channel_id=1, source_target_pairs={{0,8},{16,24},{8,0},{24,16},{1,9},{17,25},{9,1},{25,17},{2,10},{18... | collective-permute-start | bytes 196616 | tf_op jit(solution)/shard_map/ppermute | solution.py:706
  20.8 6.8 %collective-permute-start.5 = (f32[8,16,128]{2,1,0:T(8,128)S(1)}, f32[8,16,128]{2,1,0:T(8,128)S(1)}, u32[]{:S(2)}, u32[]{:S(2)}) collective-permute-start(f32[8,16,128]{2,1,0:T(8,128)S(1)} %get-tuple-element.49), channel_id=1, source_target_pairs={{8,16},{16,8},{9,17},{17,9},{10,18},{18,10},{11,19},{19,11},{12,20... | collective-permute-start | bytes 196616 | tf_op jit(solution)/shard_map/ppermute | solution.py:706
  29.8 10.6 %all-to-all-start = ((f32[32,5,2,128]{3,2,1,0:T(2,128)}), f32[32,5,2,128]{3,2,1,0:T(2,128)S(1)}, u32[]{:S(2)}, u32[]{:S(2)}) async-start(f32[32,5,2,128]{3,2,1,0:T(2,128)} %bitcast.9), calls=%async_computation | async-start | bytes 327680 | tf_op jit(solution)/shard_map/all_to_all | solution.py:888
  33.2 14.9 %collective-permute-start.8 = (f32[600,128]{1,0:T(8,128)S(1)}, f32[600,128]{1,0:T(8,128)S(1)}, u32[]{:S(2)}, u32[]{:S(2)}) collective-permute-start(f32[600,128]{1,0:T(8,128)S(1)} %get-tuple-element.62), channel_id=1, source_target_pairs={{0,1},{2,3},{4,5},{6,7},{1,0},{3,2},{5,4},{7,6},{8,9},{10,11},{12,... | collective-permute-start | bytes 921608 | tf_op jit(solution)/shard_map/ppermute | solution.py:706
  34.4 15.4 %collective-permute-start.9 = (f32[600,128]{1,0:T(8,128)S(1)}, f32[600,128]{1,0:T(8,128)S(1)}, u32[]{:S(2)}, u32[]{:S(2)}) collective-permute-start(f32[600,128]{1,0:T(8,128)S(1)} %get-tuple-element.63), channel_id=1, source_target_pairs={{1,2},{3,4},{5,6},{2,1},{4,3},{6,5},{9,10},{11,12},{13,14},{10,9},... | collective-permute-start | bytes 921608 | tf_op jit(solution)/shard_map/ppermute | solution.py:706
  42.6 15.8 %all-to-all-start.1 = ((f32[32,16,128]{2,1,0:T(8,128)}), f32[32,16,128]{2,1,0:T(8,128)S(1)}, u32[]{:S(2)}, u32[]{:S(2)}) async-start(f32[32,16,128]{2,1,0:T(8,128)} %shard_map.138), calls=%async_computation.1 | async-start | bytes 524288 | tf_op jit(solution)/shard_map/all_to_all | solution.py:896
  51.1 12.0 %collective-permute-start.10 = (f32[480,128]{1,0:T(8,128)S(1)}, f32[480,128]{1,0:T(8,128)S(1)}, u32[]{:S(2)}, u32[]{:S(2)}) collective-permute-start(f32[480,128]{1,0:T(8,128)S(1)} %get-tuple-element.68), channel_id=1, source_target_pairs={{0,8},{16,24},{8,0},{24,16},{1,9},{17,25},{9,1},{25,17},{2,10},{18... | collective-permute-start | bytes 737288 | tf_op jit(solution)/shard_map/ppermute | solution.py:706
  51.4 11.8 %collective-permute-start.11 = (f32[320,128]{1,0:T(8,128)}, f32[320,128]{1,0:T(8,128)S(1)}, u32[]{:S(2)}, u32[]{:S(2)}) collective-permute-start(f32[320,128]{1,0:T(8,128)} %get-tuple-element.69), channel_id=1, source_target_pairs={{8,16},{16,8},{9,17},{17,9},{10,18},{18,10},{11,19},{19,11},{12,20... | collective-permute-start | bytes 491528 | tf_op jit(solution)/shard_map/ppermute | solution.py:706

commit v6 on v5

--- a/solution.py
+++ b/solution.py
@@ -19,7 +19,7 @@
 VMEM_LIMIT = 4 * 1024 * 1024
 FACE_COPIES = 4
 
-SPARE_Y, SPARE_X = 24, 160
+SPARE_X = 104
 
 
 def vmem_call(
@@ -422,7 +422,7 @@
 
 def third_step_kernel(
     shape, counts, own_ref, block, field, y_one, y_other, flow, coefficients, mix_ref, edges, ends,
-    out, inner, ready, semaphores,
+    nearly, out, inner, ready, semaphores,
 ):
     wide, deep, species, up = shape
     _, columns = counts
@@ -470,8 +470,8 @@
         inner[x, deep] = block[x, deep - 1] + from_beyond(
             outer(1, x), 1, row(x, deep - 1), diffusivity[0]
         )
-        if x < 3 or x >= wide - 3:
-            edges[x if x < 3 else x - wide + 6] = inner[x]
+        if x < 2 or x >= wide - 2:
+            edges[x if x < 2 else x - wide + 4] = inner[x]
         if x in (0, wide - 1):
             for side in range(2):
                 ends[0 if x == 0 else 1, side, 0:4] = others(side, x)
@@ -482,14 +482,23 @@
     )
 
     def emit_last(x, plane):
-        ready[:, x - 2] = jnp.swapaxes(plane, 0, 1)
+        if x in (1, wide - 2):
+            nearly[0 if x == 1 else 1] = plane
+        else:
+            ready[:, x - 2] = jnp.swapaxes(plane, 0, 1)
         if x in copies:
             copies[x].start()
 
+    def last_beside(x, side):
+        at = x + 2 * side - 1
+        if at in (0, wide - 1):
+            return jnp.zeros((deep, species, up), jnp.float32)
+        return inner[at, 1 : deep + 1]
+
     planes_advanced(
-        inmost,
+        range(1, wide - 1),
         lambda x: inner[x, 1 : deep + 1],
-        lambda x, side: inner[x + 2 * side - 1, 1 : deep + 1],
+        last_beside,
         lambda x, side: inner[x, 2 * side : 2 * side + deep],
         lambda x: own_rates(flow, coefficients, x, deep),
         lambda x: [rows_for_species(speed, species) for speed in own_speeds(flow, x, deep)],
@@ -500,8 +509,8 @@
 
 
 def fourth_step_kernel(
-    shape, counts, own_ref, edges, ends, _, field, x_one, x_other, flow, coefficients, mix_ref,
-    out, edge, x_sides, ready, semaphores,
+    shape, counts, own_ref, edges, ends, nearly, _, field, x_one, x_other, flow, coefficients,
+    mix_ref, out, edge, x_sides, ready, semaphores,
 ):
     wide, deep, species, up = shape
     rows, _ = counts
@@ -527,6 +536,31 @@
         return [
             choose(even_x, x_one, x_other, side, flow_of(y, deep + 1, species)) for y in range(deep)
         ]
+
+    outermost = [[0], [1], [wide - 2], [wide - 1]]
+    copies = planes_copied(outermost, ready, out, semaphores)
+
+    def emit_last(x, plane):
+        ready[:, outermost.index([x])] = jnp.swapaxes(plane, 0, 1)
+        copies[x].start()
+
+    def speeds_of(x):
+        return [rows_for_species(speed, species) for speed in own_speeds(flow, x, deep)]
+
+    for side in range(2):
+        x = last(side)
+        low, high = corners(side)
+        value = jnp.concatenate([low[None], beside(side, outer_of), high[None]], axis=0)
+        speed = rows_for_species(
+            [ends[side, 0, 0:1]] + own_speeds(flow, x, deep)[0] + [ends[side, 1, 0:1]], species
+        )
+        edge[side] = edges[3 * side] + from_beyond(value, side, speed, diffusivity)
+        inner = wide - 2 if side else 1
+        emit_last(
+            inner,
+            nearly[side]
+            + from_beyond(edge[side, 1 : deep + 1], side, speeds_of(inner)[0], diffusivity),
+        )
 
     def emit(side, plane):
         x_sides[side] = jnp.where(inside[side], plane, 0.0)
@@ -544,41 +578,14 @@
         ],
         diffusivity, mix, emit,
     )
-    for side in range(2):
-        x = last(side)
-        low, high = corners(side)
-        value = jnp.concatenate([low[None], beside(side, outer_of), high[None]], axis=0)
-        speed = rows_for_species(
-            [ends[side, 0, 0:1]] + own_speeds(flow, x, deep)[0] + [ends[side, 1, 0:1]], species
-        )
-        edge[side] = edges[5 * side] + from_beyond(value, side, speed, diffusivity)
-
-    def plane_of(x):
-        if x < 0 or x >= wide:
-            return x_sides[0 if x < 0 else 1]
-        if x == 0 or x == wide - 1:
-            return edge[0 if x == 0 else 1, 1 : deep + 1]
-        return edges[x if x < 3 else x - wide + 6, 1 : deep + 1]
-
-    def y_of(x, side):
-        at = slice(2 * side, 2 * side + deep)
-        if x in (0, wide - 1):
-            return edge[0 if x == 0 else 1, at]
-        return edges[x if x < 3 else x - wide + 6, at]
-
-    outermost = [0, 1, wide - 2, wide - 1]
-    copies = planes_copied([outermost[:2], outermost[2:]], ready, out, semaphores)
-
-    def emit_last(x, plane):
-        ready[:, outermost.index(x)] = jnp.swapaxes(plane, 0, 1)
-        if x in copies:
-            copies[x].start()
-
     planes_advanced(
-        outermost, plane_of, lambda x, side: plane_of(x + 2 * side - 1), y_of,
-        lambda x: own_rates(flow, coefficients, x, deep),
-        lambda x: [rows_for_species(speed, species) for speed in own_speeds(flow, x, deep)],
-        diffusivity, mix, emit_last,
+        range(2),
+        lambda side: edge[side, 1 : deep + 1],
+        lambda side, to: x_sides[side] if side == to else edges[1 + side, 1 : deep + 1],
+        lambda side, to: edge[side, 2 * to : 2 * to + deep],
+        lambda side: own_rates(flow, coefficients, last(side), deep),
+        lambda side: speeds_of(last(side)),
+        diffusivity, mix, lambda side, plane: emit_last(last(side), plane),
     )
     for copy in copies.values():
         copy.wait()
@@ -863,7 +870,7 @@
         faces = faces_beside(faces)
     high = 2 * species + 4
     snapshot, *y_faces = vmem_call(
-        functools.partial(snapshot_kernel, shape), [shape] + [(wide * high + SPARE_Y, up)] * 2, 1, 8,
+        functools.partial(snapshot_kernel, shape), [shape] + [(wide * high, up)] * 2, 1, 8,
         flops=4 * cells, moved=8 * cells,
     )(own, *block(field, *fixed), *faces, speeds, coefficients)
     y_faces = swapped(*y_faces, COLUMN)
@@ -914,28 +921,30 @@
         later = snapshot
     fixed = fixed[1:]
     (third,) = last_block(later, *fixed)
-    own_wide, third = lax.optimization_barrier((own, third))
     x_faces = vmem_call(
         functools.partial(wide_faces_kernel, shape),
         [((deep + 1) * high - 4 + spare, up) for spare in (SPARE_X, 0)], 1, 5,
         flops=cells, moved=cells,
-    )(own_wide, snapshot, *y_faces, speeds)
+    )(own, snapshot, *y_faces, speeds)
     x_faces = swapped(*x_faces, ROW)
-    edges, ends, inmost = vmem_call(
+    edges, ends, nearly, inmost = vmem_call(
         functools.partial(third_step_kernel, shape, (rows, columns)),
-        [(6, deep + 2, species, up), (2, 2, 8, up), mixture_fields_initial.shape], 1, 8,
+        [
+            (4, deep + 2, species, up), (2, 2, 8, up), (2, deep, species, up),
+            mixture_fields_initial.shape,
+        ], 1, 8,
         flops=120 * cells, moved=16 * cells,
-        scratch=[(wide, deep + 2, species, up), (species, wide - 4, deep, up)], placed=[10],
+        scratch=[(wide, deep + 2, species, up), (species, wide - 4, deep, up)], placed=[11],
         copies=-(-(wide - 4) // 4),
     )(own, third, snapshot, *y_faces, *fixed)
     own, _ = lax.optimization_barrier((own, tucker_core))
     (mixture_fields_final,) = vmem_call(
         functools.partial(fourth_step_kernel, shape, (rows, columns)),
-        [mixture_fields_initial.shape], 1, 10,
+        [mixture_fields_initial.shape], 1, 11,
         flops=60 * cells, moved=8 * cells,
         scratch=[(2, deep + 2, species, up), (2, deep, species, up), (species, 4, deep, up)],
-        placed=[3, 10], copies=2, aliases={3: 0},
-    )(own, edges, ends, inmost, snapshot, *x_faces, *fixed)
+        placed=[4, 11], copies=4, aliases={4: 0},
+    )(own, edges, ends, nearly, inmost, snapshot, *x_faces, *fixed)
     return (mixture_fields_final, residual, tucker_core)
 
 

time: 65.4 us -> 63.4 us (0.969)
  waiting for transfers between devices: 5.6 us -> 4.13 us
  Pallas kernels: 21.5 us -> 20.8 us
    ppermute x12, waiting for transfers between devices: 4.16 us -> 2.69 us  [swapped(): got.append(lax.ppermute(face, axes, couples + [(b, a) for a, b in couples]))]
    pallas_call x1, Pallas kernels: 1.25 us -> 0.59 us  [body(): vmem_call(functools.partial(wide_faces_kernel, shape), [((deep + 1) * hig...]
where the time goes in v6:
time: 63.4 us; the launch traced here: 62.9 us
  starting transfers between devices  37 us (58%)
  Pallas kernels  20.8 us (33%)
  waiting for transfers between devices  4.13 us (7%)
  between operations  0.89 us (1%)
    ppermute x12, starting transfers between devices, swapped(): got.append(lax.ppermute(face, axes, couples + [(b, a) for a, b in couples]))  29.4 us
    all_to_all x1, starting transfers between devices, body(): got = lax.all_to_all(sent, EVERY, 0, 0, tiled=True)  4.26 us
    all_to_all x1, starting transfers between devices, body(): lax.all_to_all(sent.reshape(devices, (deep + 2) // 2, 2, 128), EVERY, 0,...  3.42 us
    pallas_call x1, Pallas kernels, body(): vmem_call(functools.partial(third_step_kernel, shape, (rows, columns)), [...  3.05 us
    pallas_call x2, Pallas kernels, with_fetches(): call(given, *(pltpu.with_memory_space_constraint(array, pltpu.HBM) for ar...  2.8 us
    ppermute x12, waiting for transfers between devices, swapped(): got.append(lax.ppermute(face, axes, couples + [(b, a) for a, b in couples]))  2.69 us
    pallas_call x1, Pallas kernels, body(): vmem_call(functools.partial(expand_kernel, shape, (ranks_a, ranks_d), own...  2.43 us
    pallas_call x2, Pallas kernels, body(): block(field, *fixed)  2.2 us
  transfers between devices with their start and end apart: 14, of which 3 were waited for; matrix products, arithmetic and copies ran while one was open for 0% of the time, Pallas kernels for 23%

profile of v6, /device:TPU:3, one launch (start us, length us, event | category | flops | bytes accessed | tf_op | source)
XLA Modules:
  0.0 62.9 jit_solution(2154943449472176901)
XLA Ops:
  0.7 1.8 %shard_map.132 = (f32[8,16,128]{2,1,0:T(8,128)S(1)}, f32[8,16,128]{2,1,0:T(8,128)S(1)}, f32[16,16,128]{2,1,0:T(8,128)S(1)}, f32[16,16,128]{2,1,0:T(8,128)S(1)}) custom-call(s32[4]{0:T(128)S(1)} %pad_add_fusion.own_ref.refs_0_, f32[16,16,8,128]{3,2,1,0:T(8,128)} %given.3), custom_call_target="tpu_custom_call" | custom-call | tf_op jit(solution)/shard_map/pallas_call | solution.py:828
  2.6 1.4 %collective-permute-start.2 = (f32[16,16,128]{2,1,0:T(8,128)S(1)}, f32[16,16,128]{2,1,0:T(8,128)S(1)}, u32[]{:S(2)}, u32[]{:S(2)}) collective-permute-start(f32[16,16,128]{2,1,0:T(8,128)S(1)} %get-tuple-element.43), channel_id=1, source_target_pairs={{0,1},{2,3},{4,5},{6,7},{1,0},{3,2},{5,4},{7,6},{8,9},{10,11},{12,... | collective-permute-start | bytes 393224 | tf_op jit(solution)/shard_map/ppermute | solution.py:713
  3.9 4.9 %collective-permute-start.3 = (f32[16,16,128]{2,1,0:T(8,128)S(1)}, f32[16,16,128]{2,1,0:T(8,128)S(1)}, u32[]{:S(2)}, u32[]{:S(2)}) collective-permute-start(f32[16,16,128]{2,1,0:T(8,128)S(1)} %get-tuple-element.44), channel_id=1, source_target_pairs={{1,2},{3,4},{5,6},{2,1},{4,3},{6,5},{9,10},{11,12},{13,14},{10,9},... | collective-permute-start | bytes 393224 | tf_op jit(solution)/shard_map/ppermute | solution.py:713
  9.2 4.1 %collective-permute-start.1 = (f32[8,16,128]{2,1,0:T(8,128)S(1)}, f32[8,16,128]{2,1,0:T(8,128)S(1)}, u32[]{:S(2)}, u32[]{:S(2)}) collective-permute-start(f32[8,16,128]{2,1,0:T(8,128)S(1)} %get-tuple-element.42), channel_id=1, source_target_pairs={{8,16},{16,8},{9,17},{17,9},{10,18},{18,10},{11,19},{19,11},{12,20... | collective-permute-start | bytes 196616 | tf_op jit(solution)/shard_map/ppermute | solution.py:713
  13.3 1.3 %shard_map.130 = (f32[16,8,16,128]{3,2,1,0:T(8,128)S(1)}, f32[16,8,16,128]{3,2,1,0:T(8,128)S(1)}, f32[4,16,8,128]{3,2,1,0:T(8,128)S(1)}, f32[3,16,128]{2,1,0:T(8,128)S(1)}, f32[16,128]{1,0:T(8,128)S(1)}) custom-call(f32[16,16,8,128]{3,2,1,0:T(8,128)S(1)} %copy-done, f32[3,16,8,128]{3,2,1,0:T(8,128)} %refs_0_.1, f32[16,8,128]{2,1,0:T(8,128)} %refs_1_.1, ...), custom_call_target="tpu_custom_call" | custom-call | flops 1048576 | bytes 3145728 | tf_op jit(solution)/shard_map/pallas_call | solution.py:839
  14.5 1.1 %shard_map.131.refs_1_ = f32[16,8,16,128]{3,2,1,0:T(8,128)S(1)} custom-call(f32[16,8,16,128]{3,2,1,0:T(8,128)S(1)} %get-tuple-element.36.field, f32[16,8,16,128]{3,2,1,0:T(8,128)S(1)} %get-tuple-element.37.refs_0_, f32[4,16,8,128]{3,2,1,0:T(8,128)S(1)} %get-tuple-element.38.refs_1_.refs_6_.refs_0_.flow, ...), custom_call_target="tpu_custom_call" | custom-call | flops 15728640 | bytes 2097152 | tf_op jit(solution)/shard_map/pallas_call | solution.py:867
  16.4 4.3 %collective-permute-start.7 = (f32[16,16,128]{2,1,0:T(8,128)S(1)}, f32[16,16,128]{2,1,0:T(8,128)S(1)}, u32[]{:S(2)}, u32[]{:S(2)}) collective-permute-start(f32[16,16,128]{2,1,0:T(8,128)S(1)} %get-tuple-element.50), channel_id=1, source_target_pairs={{1,2},{3,4},{5,6},{2,1},{4,3},{6,5},{9,10},{11,12},{13,14},{10,9},... | collective-permute-start | bytes 393224 | tf_op jit(solution)/shard_map/ppermute | solution.py:713
  20.8 4.1 %collective-permute-start.5 = (f32[8,16,128]{2,1,0:T(8,128)S(1)}, f32[8,16,128]{2,1,0:T(8,128)S(1)}, u32[]{:S(2)}, u32[]{:S(2)}) collective-permute-start(f32[8,16,128]{2,1,0:T(8,128)S(1)} %get-tuple-element.48), channel_id=1, source_target_pairs={{8,16},{16,8},{9,17},{17,9},{10,18},{18,10},{11,19},{19,11},{12,20... | collective-permute-start | bytes 196616 | tf_op jit(solution)/shard_map/ppermute | solution.py:713
  24.9 1.5 %shard_map.136 = (f32[128,256]{1,0:T(8,128)S(1)}, f32[16,128]{1,0:T(8,128)S(1)}, f32[32,128]{1,0:T(8,128)S(1)}, f32[2,128]{1,0:T(2,128)S(1)}) custom-call(s32[4]{0:T(128)S(1)} %pad_add_fusion.own_ref.refs_0_, f32[8,16]{1,0:T(8,128)} %bitcast.16, f32[32,128]{1,0:T(8,128)} %bitcast.15, f32[16,64]{1,0:T(8,128)} %refs_2_.1, f32[8,64]{1,0:T(8,128)} %refs_3_.1), custom_call_target="tpu_custom_call" | custom-call | tf_op jit(solution)/shard_map/pallas_call | solution.py:839
  26.5 1.1 %shard_map.134.refs_1_ = f32[16,8,16,128]{3,2,1,0:T(8,128)S(1)} custom-call(f32[16,8,16,128]{3,2,1,0:T(8,128)S(1)} %get-tuple-element.45.field, f32[16,8,16,128]{3,2,1,0:T(8,128)S(1)} %get-tuple-element.37.refs_0_, f32[4,16,8,128]{3,2,1,0:T(8,128)S(1)} %get-tuple-element.38.refs_1_.refs_6_.refs_0_.flow, ...), custom_call_target="tpu_custom_call" | custom-call | flops 15728640 | bytes 2097152 | tf_op jit(solution)/shard_map/pallas_call | solution.py:875
  27.7 0.7 %shard_map.135 = (f32[16,8,16,128]{3,2,1,0:T(8,128)S(1)}, f32[576,128]{1,0:T(8,128)S(1)}, f32[576,128]{1,0:T(8,128)S(1)}) custom-call(s32[4]{0:T(128)S(1)} %pad_add_fusion.own_ref.refs_0_, f32[16,8,16,128]{3,2,1,0:T(8,128)S(1)} %shard_map.134.refs_1_, f32[8,16,128]{2,1,0:T(8,128)S(1)} %collective-permute-done.4.refs_2_, ...), custom_call_target="tpu_custom_call" | custom-call | flops 1048576 | bytes 2097152 | tf_op jit(solution)/shard_map/pallas_call | solution.py:872
  28.4 1.4 %shard_map.137 = f32[320,128]{1,0:T(8,128)} custom-call(f32[16,8,16,128]{3,2,1,0:T(8,128)S(1)} %get-tuple-element.59.field, f32[128,256]{1,0:T(8,128)S(1)} %get-tuple-element.52.component, f32[32,128]{1,0:T(8,128)S(1)} %get-tuple-element.53.vertical, f32[2,128]{1,0:T(2,128)S(1)} %get-tuple-element.54.factor_rows), custom_call_target="tpu_custom_call" | custom-call | flops 15728640 | bytes 1048576 | tf_op jit(solution)/shard_map/pallas_call | solution.py:891
  29.7 3.4 %all-to-all-start = ((f32[32,5,2,128]{3,2,1,0:T(2,128)}), f32[32,5,2,128]{3,2,1,0:T(2,128)S(1)}, u32[]{:S(2)}, u32[]{:S(2)}) async-start(f32[32,5,2,128]{3,2,1,0:T(2,128)} %bitcast.9), calls=%async_computation | async-start | bytes 327680 | tf_op jit(solution)/shard_map/all_to_all | solution.py:895
  33.2 1.3 %collective-permute-start.8 = (f32[576,128]{1,0:T(8,128)S(1)}, f32[576,128]{1,0:T(8,128)S(1)}, u32[]{:S(2)}, u32[]{:S(2)}) collective-permute-start(f32[576,128]{1,0:T(8,128)S(1)} %get-tuple-element.60), channel_id=1, source_target_pairs={{0,1},{2,3},{4,5},{6,7},{1,0},{3,2},{5,4},{7,6},{8,9},{10,11},{12,... | collective-permute-start | bytes 884744 | tf_op jit(solution)/shard_map/ppermute | solution.py:713
  34.4 4.5 %collective-permute-start.9 = (f32[576,128]{1,0:T(8,128)S(1)}, f32[576,128]{1,0:T(8,128)S(1)}, u32[]{:S(2)}, u32[]{:S(2)}) collective-permute-start(f32[576,128]{1,0:T(8,128)S(1)} %get-tuple-element.61), channel_id=1, source_target_pairs={{1,2},{3,4},{5,6},{2,1},{4,3},{6,5},{9,10},{11,12},{13,14},{10,9},... | collective-permute-start | bytes 884744 | tf_op jit(solution)/shard_map/ppermute | solution.py:713
  38.9 1.4 %all-to-all-done = f32[32,5,2,128]{3,2,1,0:T(2,128)S(1)} async-done(((f32[32,5,2,128]{3,2,1,0:T(2,128)}), f32[32,5,2,128]{3,2,1,0:T(2,128)S(1)}, u32[]{:S(2)}, u32[]{:S(2)}) %all-to-all-start) | async-done | bytes 163872 | tf_op jit(solution)/shard_map/all_to_all | solution.py:895
  40.4 2.2 %shard_map.138 = f32[32,16,128]{2,1,0:T(8,128)} custom-call(f32[320,128]{1,0:T(8,128)S(1)} %bitcast.14), custom_call_target="tpu_custom_call" | custom-call | flops 15728640 | bytes 1048576 | tf_op jit(solution)/shard_map/pallas_call | solution.py:898
  42.5 4.3 %all-to-all-start.1 = ((f32[32,16,128]{2,1,0:T(8,128)}), f32[32,16,128]{2,1,0:T(8,128)S(1)}, u32[]{:S(2)}, u32[]{:S(2)}) async-start(f32[32,16,128]{2,1,0:T(8,128)} %shard_map.138), calls=%async_computation.1 | async-start | bytes 524288 | tf_op jit(solution)/shard_map/all_to_all | solution.py:903
  46.8 2.6 %collective-permute-done.9.y_other = f32[576,128]{1,0:T(8,128)S(1)} collective-permute-done((f32[576,128]{1,0:T(8,128)S(1)}, f32[576,128]{1,0:T(8,128)S(1)}, u32[]{:S(2)}, u32[]{:S(2)}) %collective-permute-start.9) | collective-permute-done | bytes 294944 | tf_op jit(solution)/shard_map/ppermute | solution.py:713
  50.3 4.0 %collective-permute-start.11 = (f32[320,128]{1,0:T(8,128)S(1)}, f32[320,128]{1,0:T(8,128)S(1)}, u32[]{:S(2)}, u32[]{:S(2)}) collective-permute-start(f32[320,128]{1,0:T(8,128)S(1)} %get-tuple-element.67), channel_id=1, source_target_pairs={{8,16},{16,8},{9,17},{17,9},{10,18},{18,10},{11,19},{19,11},{12,20... | collective-permute-start | bytes 491528 | tf_op jit(solution)/shard_map/ppermute | solution.py:713
  54.4 1.2 %shard_map.140.block = f32[16,8,16,128]{3,2,1,0:T(8,128)S(1)} custom-call(f32[16,8,16,128]{3,2,1,0:T(8,128)S(1)} %get-tuple-element.59.field, f32[4,16,8,128]{3,2,1,0:T(8,128)S(1)} %get-tuple-element.38.refs_1_.refs_6_.refs_0_.flow, f32[3,16,128]{2,1,0:T(8,128)S(1)} %get-tuple-element.39.refs_2_.refs_7_.refs_1_.coefficients, ...), custom_call_target="tpu_custom_call" | custom-call | flops 15728640 | bytes 2097152 | tf_op jit(solution)/shard_map/pallas_call | solution.py:923
  55.6 3.0 %shard_map.141 = (f32[4,10,16,128]{3,2,1,0:T(8,128)S(1)}, f32[2,2,8,128]{3,2,1,0:T(8,128)S(1)}, f32[2,8,16,128]{3,2,1,0:T(8,128)S(1)}, f32[16,16,8,128]{3,2,1,0:T(8,128)}) custom-call(s32[4]{0:T(128)S(1)} %pad_add_fusion.own_ref.refs_0_, f32[16,8,16,128]{3,2,1,0:T(8,128)S(1)} %shard_map.140.block, f32[16,8,16,128]{3,2,1,0:T(8,128)S(1)} %get-tuple-element.59.field, ...), custom_call_target="tpu_custom_call" | custom-call | flops 31457280 | bytes 4194304 | tf_op jit(solution)/shard_map/pallas_call | solution.py:930
  58.7 2.4 %shard_map.139 = (f32[16,16,8,128]{3,2,1,0:T(8,128)}, f32[128,8,32]{2,1,0:T(8,128)}) custom-call(f32[512,128]{1,0:T(8,128)S(1)} %bitcast.13, f32[16,8,16,128]{3,2,1,0:T(8,128)S(1)} %get-tuple-element.59.field, f32[16,128]{1,0:T(8,128)S(1)} %get-tuple-element.56.wide_rows, f32[32,128]{1,0:T(8,128)S(1)} %get-tuple-element.53.vertical), custom_call_target="tpu_custom_call" | custom-call | flops 15728640 | bytes 2097152 | tf_op jit(solution)/shard_map/pallas_call | solution.py:904
  61.2 1.8 %shard_map.143 = f32[16,16,8,128]{3,2,1,0:T(8,128)} custom-call(s32[4]{0:T(128)S(1)} %pad_add_fusion.own_ref.refs_0_, f32[4,10,16,128]{3,2,1,0:T(8,128)S(1)} %get-tuple-element.62.edges, f32[2,2,8,128]{3,2,1,0:T(8,128)S(1)} %get-tuple-element.63.ends, f32[2,8,16,128]{3,2,1,0:T(8,128)S(1)} %get-tuple-element.64.nearly, ...), custom_call_target="tpu_custom_call", output_to_operand_aliasing={{}: (4, {})} | custom-call | flops 15728640 | bytes 2097152 | tf_op jit(solution)/shard_map/pallas_call | solution.py:941
  (21 shorter events, 2.3 us)
Async XLA Ops:
  0.6 12.6 %copy-start = (f32[16,16,8,128]{3,2,1,0:T(8,128)S(1)}, f32[16,16,8,128]{3,2,1,0:T(8,128)}, u32[]{:S(2)}) copy-start(f32[16,16,8,128]{3,2,1,0:T(8,128)} %given.3) | copy-start | bytes 3145732
  2.6 13.1 %collective-permute-start.2 = (f32[16,16,128]{2,1,0:T(8,128)S(1)}, f32[16,16,128]{2,1,0:T(8,128)S(1)}, u32[]{:S(2)}, u32[]{:S(2)}) collective-permute-start(f32[16,16,128]{2,1,0:T(8,128)S(1)} %get-tuple-element.43), channel_id=1, source_target_pairs={{0,1},{2,3},{4,5},{6,7},{1,0},{3,2},{5,4},{7,6},{8,9},{10,11},{12,... | collective-permute-start | bytes 393224 | tf_op jit(solution)/shard_map/ppermute | solution.py:713
  3.9 11.7 %collective-permute-start.3 = (f32[16,16,128]{2,1,0:T(8,128)S(1)}, f32[16,16,128]{2,1,0:T(8,128)S(1)}, u32[]{:S(2)}, u32[]{:S(2)}) collective-permute-start(f32[16,16,128]{2,1,0:T(8,128)S(1)} %get-tuple-element.44), channel_id=1, source_target_pairs={{1,2},{3,4},{5,6},{2,1},{4,3},{6,5},{9,10},{11,12},{13,14},{10,9},... | collective-permute-start | bytes 393224 | tf_op jit(solution)/shard_map/ppermute | solution.py:713
  8.9 6.7 %collective-permute-start = (f32[8,16,128]{2,1,0:T(8,128)S(1)}, f32[8,16,128]{2,1,0:T(8,128)S(1)}, u32[]{:S(2)}, u32[]{:S(2)}) collective-permute-start(f32[8,16,128]{2,1,0:T(8,128)S(1)} %get-tuple-element.41), channel_id=1, source_target_pairs={{0,8},{16,24},{8,0},{24,16},{1,9},{17,25},{9,1},{25,17},{2,10},{18... | collective-permute-start | bytes 196616 | tf_op jit(solution)/shard_map/ppermute | solution.py:713
  9.2 6.4 %collective-permute-start.1 = (f32[8,16,128]{2,1,0:T(8,128)S(1)}, f32[8,16,128]{2,1,0:T(8,128)S(1)}, u32[]{:S(2)}, u32[]{:S(2)}) collective-permute-start(f32[8,16,128]{2,1,0:T(8,128)S(1)} %get-tuple-element.42), channel_id=1, source_target_pairs={{8,16},{16,8},{9,17},{17,9},{10,18},{18,10},{11,19},{19,11},{12,20... | collective-permute-start | bytes 196616 | tf_op jit(solution)/shard_map/ppermute | solution.py:713
  16.3 11.3 %collective-permute-start.6 = (f32[16,16,128]{2,1,0:T(8,128)S(1)}, f32[16,16,128]{2,1,0:T(8,128)S(1)}, u32[]{:S(2)}, u32[]{:S(2)}) collective-permute-start(f32[16,16,128]{2,1,0:T(8,128)S(1)} %get-tuple-element.49), channel_id=1, source_target_pairs={{0,1},{2,3},{4,5},{6,7},{1,0},{3,2},{5,4},{7,6},{8,9},{10,11},{12,... | collective-permute-start | bytes 393224 | tf_op jit(solution)/shard_map/ppermute | solution.py:713
  16.4 11.2 %collective-permute-start.7 = (f32[16,16,128]{2,1,0:T(8,128)S(1)}, f32[16,16,128]{2,1,0:T(8,128)S(1)}, u32[]{:S(2)}, u32[]{:S(2)}) collective-permute-start(f32[16,16,128]{2,1,0:T(8,128)S(1)} %get-tuple-element.50), channel_id=1, source_target_pairs={{1,2},{3,4},{5,6},{2,1},{4,3},{6,5},{9,10},{11,12},{13,14},{10,9},... | collective-permute-start | bytes 393224 | tf_op jit(solution)/shard_map/ppermute | solution.py:713
  20.8 6.9 %collective-permute-start.4 = (f32[8,16,128]{2,1,0:T(8,128)S(1)}, f32[8,16,128]{2,1,0:T(8,128)S(1)}, u32[]{:S(2)}, u32[]{:S(2)}) collective-permute-start(f32[8,16,128]{2,1,0:T(8,128)S(1)} %get-tuple-element.47), channel_id=1, source_target_pairs={{0,8},{16,24},{8,0},{24,16},{1,9},{17,25},{9,1},{25,17},{2,10},{18... | collective-permute-start | bytes 196616 | tf_op jit(solution)/shard_map/ppermute | solution.py:713
  20.8 6.8 %collective-permute-start.5 = (f32[8,16,128]{2,1,0:T(8,128)S(1)}, f32[8,16,128]{2,1,0:T(8,128)S(1)}, u32[]{:S(2)}, u32[]{:S(2)}) collective-permute-start(f32[8,16,128]{2,1,0:T(8,128)S(1)} %get-tuple-element.48), channel_id=1, source_target_pairs={{8,16},{16,8},{9,17},{17,9},{10,18},{18,10},{11,19},{19,11},{12,20... | collective-permute-start | bytes 196616 | tf_op jit(solution)/shard_map/ppermute | solution.py:713
  29.7 10.6 %all-to-all-start = ((f32[32,5,2,128]{3,2,1,0:T(2,128)}), f32[32,5,2,128]{3,2,1,0:T(2,128)S(1)}, u32[]{:S(2)}, u32[]{:S(2)}) async-start(f32[32,5,2,128]{3,2,1,0:T(2,128)} %bitcast.9), calls=%async_computation | async-start | bytes 327680 | tf_op jit(solution)/shard_map/all_to_all | solution.py:895
  33.2 13.7 %collective-permute-start.8 = (f32[576,128]{1,0:T(8,128)S(1)}, f32[576,128]{1,0:T(8,128)S(1)}, u32[]{:S(2)}, u32[]{:S(2)}) collective-permute-start(f32[576,128]{1,0:T(8,128)S(1)} %get-tuple-element.60), channel_id=1, source_target_pairs={{0,1},{2,3},{4,5},{6,7},{1,0},{3,2},{5,4},{7,6},{8,9},{10,11},{12,... | collective-permute-start | bytes 884744 | tf_op jit(solution)/shard_map/ppermute | solution.py:713
  34.4 15.0 %collective-permute-start.9 = (f32[576,128]{1,0:T(8,128)S(1)}, f32[576,128]{1,0:T(8,128)S(1)}, u32[]{:S(2)}, u32[]{:S(2)}) collective-permute-start(f32[576,128]{1,0:T(8,128)S(1)} %get-tuple-element.61), channel_id=1, source_target_pairs={{1,2},{3,4},{5,6},{2,1},{4,3},{6,5},{9,10},{11,12},{13,14},{10,9},... | collective-permute-start | bytes 884744 | tf_op jit(solution)/shard_map/ppermute | solution.py:713
  42.5 16.1 %all-to-all-start.1 = ((f32[32,16,128]{2,1,0:T(8,128)}), f32[32,16,128]{2,1,0:T(8,128)S(1)}, u32[]{:S(2)}, u32[]{:S(2)}) async-start(f32[32,16,128]{2,1,0:T(8,128)} %shard_map.138), calls=%async_computation.1 | async-start | bytes 524288 | tf_op jit(solution)/shard_map/all_to_all | solution.py:903
  50.0 11.2 %collective-permute-start.10 = (f32[424,128]{1,0:T(8,128)S(1)}, f32[424,128]{1,0:T(8,128)S(1)}, u32[]{:S(2)}, u32[]{:S(2)}) collective-permute-start(f32[424,128]{1,0:T(8,128)S(1)} %get-tuple-element.66), channel_id=1, source_target_pairs={{0,8},{16,24},{8,0},{24,16},{1,9},{17,25},{9,1},{25,17},{2,10},{18... | collective-permute-start | bytes 651272 | tf_op jit(solution)/shard_map/ppermute | solution.py:713
  50.3 10.8 %collective-permute-start.11 = (f32[320,128]{1,0:T(8,128)S(1)}, f32[320,128]{1,0:T(8,128)S(1)}, u32[]{:S(2)}, u32[]{:S(2)}) collective-permute-start(f32[320,128]{1,0:T(8,128)S(1)} %get-tuple-element.67), channel_id=1, source_target_pairs={{8,16},{16,8},{9,17},{17,9},{10,18},{18,10},{11,19},{19,11},{12,20... | collective-permute-start | bytes 491528 | tf_op jit(solution)/shard_map/ppermute | solution.py:713

commit v7 on v6

--- a/solution.py
+++ b/solution.py
@@ -103,10 +103,10 @@
 
 def prepare_kernel(shape, given, *refs):
     wide, deep, species, up = shape
-    held, semaphores = refs[-7:-1], refs[-1]
-    copies = fetched(refs[:6], held, semaphores)
-    flow, thermal, diffusivity, constant, energy, production = held
-    field, rates, speeds, coefficients, mix = refs[6:-7]
+    held, semaphores = refs[-11:-1], refs[-1]
+    copies = fetched(refs[:10], held, semaphores)
+    flow, thermal, diffusivity, constant, energy, production = held[:6]
+    field, rates, speeds, coefficients, mix = refs[10:15]
     for x in range(wide):
         field[x] = jnp.swapaxes(given[:, x], 0, 1)
     for copy in copies:
@@ -126,28 +126,27 @@
         for y in range(deep):
             rates[x, y] = coefficients[1] * jnp.exp(coefficients[2] * inverse[y : y + 1])
     mix[...] = tiled(time_step * production[...], mix.shape[1] // species)
-
-
-def matrices_kernel(shape, own_ref, *refs):
+    for target, source in zip(refs[15:19], held[6:]):
+        target[...] = source[...]
+
+
+def x_of(lane, wide):
+    return 2 * (lane % (wide // 2)) + lane % wide // (wide // 2)
+
+
+def matrices_kernel(shape, own_ref, turned, east, north, squeeze, wide_rows, factor_rows):
     wide, _, species, _ = shape
-    held, semaphores = refs[-5:-1], refs[-1]
-    copies = fetched(refs[:4], held, semaphores)
-    turned, vertical, east, north = held
-    squeeze, wide_rows, upright, factor_rows = refs[4:-5]
-    for copy in copies:
-        copy.wait()
     ranks_a = turned.shape[0]
     full = tiled(turned[...], wide)
     full = [jnp.broadcast_to(full[a : a + 1], (wide, full.shape[1])) for a in range(ranks_a)]
     full = jnp.concatenate(full, axis=0)
-    squeeze[...] = where_equal(full, lambda at: at % wide, lambda at: at // species)
+    squeeze[...] = where_equal(full, lambda at: x_of(at, wide), lambda at: at // species)
     pick = lax.broadcasted_iota(jnp.int32, (ranks_a, ranks_a * wide), 1) // wide
     pick = pick == lax.broadcasted_iota(jnp.int32, pick.shape, 0)
     wide_rows[...] = lax.dot_general(
         turned[...], pick.astype(jnp.float32), (((0,), (0,)), ((), ())), precision=HIGHEST,
         preferred_element_type=jnp.float32,
     )
-    upright[...] = vertical[...]
 
     def two_rows(ref, at):
         return jnp.concatenate([ref[pl.ds(2 * at + row, 1), :] for row in range(2)], axis=1)
@@ -478,7 +477,7 @@
 
     inmost = range(2, wide - 2)
     copies = planes_copied(
-        [inmost[at : at + 4] for at in range(0, len(inmost), 4)], ready, out, semaphores
+        [inmost[at : at + 6] for at in range(0, len(inmost), 6)], ready, out, semaphores
     )
 
     def emit_last(x, plane):
@@ -496,7 +495,7 @@
         return inner[at, 1 : deep + 1]
 
     planes_advanced(
-        range(1, wide - 1),
+        [*inmost, 1, wide - 2],
         lambda x: inner[x, 1 : deep + 1],
         last_beside,
         lambda x, side: inner[x, 2 * side : 2 * side + deep],
@@ -619,13 +618,17 @@
 
 def core_kernel(counts, got, out):
     rows, columns, ranks_a, tall, deep = counts
-    devices, each = rows * columns, deep + 2
+    devices, each, all_of = rows * columns, deep + 2, tall + deep
     own = 128 // ranks_a
+    in_order = [(r, g) for r in range(2) for g in range(rows)]
 
     whole = jnp.concatenate(
         [
             jnp.concatenate(
-                [got[pl.ds((row * columns + column) * each, deep), :] for column in range(columns)],
+                [
+                    got[pl.ds(row * columns * each + 2 * g + r, columns, stride=each), :]
+                    for r, g in in_order
+                ],
                 axis=0,
             )
             for row in range(rows)
@@ -633,55 +636,50 @@
         axis=1,
     )
 
-    def in_order(at, of_row):
+    def factor(at):
         both = got[pl.ds(at, devices, stride=each), :]
-        halves = jnp.concatenate([both[:, :64], both[:, 64:]], axis=0)
-        pick = jnp.full((2 * devices, 2 * devices), 1.0, jnp.float32)
-        return product(where_equal(pick, of_row, lambda at: at), halves, (1, 0))
-
-    east = in_order(deep, lambda at: at % 2 * devices + at // 2)
-    north = in_order(
-        deep + 1, lambda at: at % 2 * devices + at % deep // 2 * columns + at // deep
-    )
-
-    def by_rank(array):
-        return jnp.concatenate(
-            [
-                jnp.concatenate(
-                    [
-                        array[(row * ranks_a + a) * own : (row * ranks_a + a + 1) * own]
-                        for row in range(rows)
-                    ],
-                    axis=0,
-                )
-                for a in range(ranks_a)
-            ],
-            axis=1,
-        )
-
-    def by_row(parts):
-        return jnp.concatenate(
-            [
-                parts[a][row * own : (row + 1) * own]
-                for row in range(rows)
-                for a in range(ranks_a)
-            ],
-            axis=0,
-        ).T
-
-    half = by_rank(product(whole, north, (0, 0)))
+        return jnp.concatenate([both[:, :64], both[:, 64:]], axis=0)
+
+    east, north = factor(deep), factor(deep + 1)
+    half = product(whole, north, (0, 0))
+
+    def part(array, a, r, g):
+        at = (g * ranks_a + a) * own + r * columns
+        return array[at : at + columns]
+
+    half = jnp.concatenate(
+        [
+            jnp.concatenate([part(half, a, r, g) for r, g in in_order], axis=0)
+            for a in range(ranks_a)
+        ],
+        axis=1,
+    )
     core = product(east, half, (0, 0))
     half = product(east, core, (1, 0))
-    ranks_c = north.shape[1]
+    ranks_c, size = north.shape[1], len(in_order) * columns
     split = [slice(a * ranks_c, (a + 1) * ranks_c) for a in range(ranks_a)]
-    core = by_row([core[:, at] for at in split])
-    whole = by_row([product(half[:, at], north, (1, 1)) for at in split])
+    core = jnp.concatenate(
+        [core[row * own : (row + 1) * own, at] for row in range(rows) for at in split], axis=0
+    ).T
+    whole = product(jnp.concatenate([half[:, at] for at in split], axis=0), north, (1, 1))
+    whole = jnp.concatenate(
+        [
+            whole[at : at + columns]
+            for row in range(rows)
+            for a in range(ranks_a)
+            for r in range(2)
+            for at in [a * size + (r * rows + row) * columns]
+        ],
+        axis=0,
+    ).T
+    flat = out.reshape(devices * all_of, 128)
     for row in range(rows):
+        lanes = slice(row * 128, (row + 1) * 128)
         for column in range(columns):
-            at = row * columns + column
-            out[at, 0:tall] = core[column * tall : (column + 1) * tall, row * 128 : (row + 1) * 128]
-            out[at, tall : tall + deep] = whole[
-                column * deep : (column + 1) * deep, row * 128 : (row + 1) * 128
+            out[row * columns + column, 0:tall] = core[column * tall : (column + 1) * tall, lanes]
+        for at, (r, g) in enumerate(in_order):
+            flat[pl.ds(row * columns * all_of + tall + 2 * g + r, columns, stride=all_of), :] = whole[
+                at * columns : (at + 1) * columns, lanes
             ]
 
 
@@ -692,7 +690,7 @@
     component = where_equal(
         jnp.concatenate([wide_rows[...]] * wide, axis=0),
         lambda at: at // species,
-        lambda at: at % wide,
+        lambda at: x_of(at, wide),
     )
     for y in range(deep):
         on_d = got[pl.ds(tall + y, ranks_d, stride=each), :]
@@ -832,7 +830,7 @@
     faces = faces_beside(faces)
     def with_fetches(kernel, given, small, outs, **cost):
         call = vmem_call(
-            kernel, outs, int(given is own), 1 + len(small),
+            kernel, outs, 0, 1 + len(small),
             scratch=[array.shape for array in small], placed=range(1, 1 + len(small)),
             copies=len(small), **cost,
         )
@@ -840,14 +838,18 @@
             given, *(pltpu.with_memory_space_constraint(array, pltpu.HBM) for array in small)
         )
 
-    field, rates, speeds, coefficients, mix = with_fetches(
+    field, rates, speeds, coefficients, mix, turned, upright, east, north = with_fetches(
         functools.partial(prepare_kernel, shape),
         mixture_fields_initial,
         (
             flow_speed_vector, thermal_field, mass_diffusivity[None], arrhenius_constant[None],
-            arrhenius_energy_temp[None], production_coefficients,
+            arrhenius_energy_temp[None], production_coefficients, tucker_factor_component.T,
+            tucker_factor_vertical.T, tucker_factor_east, tucker_factor_north,
         ),
-        [shape, shape, (4, wide, deep, up), (3, species, up), (species, 128)],
+        [
+            shape, shape, (4, wide, deep, up), (3, species, up), (species, 128),
+            (ranks_a, species), (ranks_d, up), tucker_factor_east.shape, tucker_factor_north.shape,
+        ],
         flops=4 * cells, moved=12 * cells, exps=cells,
     )
     block, last_block = (
@@ -876,22 +878,14 @@
     y_faces = swapped(*y_faces, COLUMN)
     if kernels_fit:
         own, _ = lax.optimization_barrier((own, first))
-        squeeze, wide_rows, upright, *factor_rows = with_fetches(
+        squeeze, wide_rows, factor_rows = vmem_call(
             functools.partial(matrices_kernel, shape),
-            own,
-            (
-                tucker_factor_component.T, tucker_factor_vertical.T, tucker_factor_east,
-                tucker_factor_north,
-            ),
-            [
-                (wide * ranks_a, wide * species), (species, wide * ranks_a), (ranks_d, up),
-                (2, 128),
-            ],
-        )
+            [(wide * ranks_a, wide * species), (species, wide * ranks_a), (2, 128)], 1, 4,
+        )(own, turned, east, north)
         (sent,) = vmem_call(
             functools.partial(project_kernel, shape, (ranks_a, ranks_d)),
             [(devices * (deep + 2), 128)], 0, 4, flops=60 * cells, moved=4 * cells,
-        )(snapshot, squeeze, upright, *factor_rows)
+        )(snapshot, squeeze, upright, factor_rows)
         got = lax.all_to_all(
             sent.reshape(devices, (deep + 2) // 2, 2, 128), EVERY, 0, 0, tiled=True
         )

time: 63.4 us -> 63.6 us (level)
  Pallas kernels: 20.8 us -> 19.8 us
  starting transfers between devices: 37 us -> 37.8 us
    pallas_call x2 -> x1, Pallas kernels: 2.8 us -> 1.32 us  [with_fetches(): call(given, *(pltpu.with_memory_space_constraint(array, pltpu.HBM) for ar...]
    all_to_all x1, starting transfers between devices: 3.42 us -> 4.19 us  [body(): lax.all_to_all(sent.reshape(devices, (deep + 2) // 2, 2, 128), EVERY, 0,...]
    pallas_call x0 -> x1, Pallas kernels: none -> 0.75 us  [body(): vmem_call(functools.partial(matrices_kernel, shape), [(wide * ranks_a, wi...]
  transfers between devices with their start and end apart: 14 -> 14, of which waited for: 3 -> 2; matrix products, arithmetic and copies ran while one was open for 0% -> 0% of each run, Pallas kernels for 23% -> 21%
where the time goes in v7:
time: 63.6 us; the launch traced here: 62.9 us
  starting transfers between devices  37.8 us (59%)
  Pallas kernels  19.8 us (31%)
  waiting for transfers between devices  4.3 us (7%)
  between operations  0.88 us (1%)
    ppermute x12, starting transfers between devices, swapped(): got.append(lax.ppermute(face, axes, couples + [(b, a) for a, b in couples]))  29.3 us
    all_to_all x1, starting transfers between devices, body(): got = lax.all_to_all(sent, EVERY, 0, 0, tiled=True)  4.26 us
    all_to_all x1, starting transfers between devices, body(): lax.all_to_all(sent.reshape(devices, (deep + 2) // 2, 2, 128), EVERY, 0,...  4.19 us
    pallas_call x1, Pallas kernels, body(): vmem_call(functools.partial(third_step_kernel, shape, (rows, columns)), [...  3.03 us
    ppermute x12, waiting for transfers between devices, swapped(): got.append(lax.ppermute(face, axes, couples + [(b, a) for a, b in couples]))  2.86 us
    pallas_call x1, Pallas kernels, body(): vmem_call(functools.partial(expand_kernel, shape, (ranks_a, ranks_d), own...  2.43 us
    pallas_call x2, Pallas kernels, body(): block(field, *fixed)  2.2 us
    pallas_call x1, Pallas kernels, body(): vmem_call(functools.partial(core_kernel, (rows, columns, ranks_a, own_c,...  1.94 us
  transfers between devices with their start and end apart: 14, of which 2 were waited for; matrix products, arithmetic and copies ran while one was open for 0% of the time, Pallas kernels for 21%

profile of v7, /device:TPU:3, one launch (start us, length us, event | category | flops | bytes accessed | tf_op | source)
XLA Modules:
  0.0 62.9 jit_solution(2162416275212014968)
XLA Ops:
  0.7 1.8 %shard_map.132 = (f32[8,16,128]{2,1,0:T(8,128)S(1)}, f32[8,16,128]{2,1,0:T(8,128)S(1)}, f32[16,16,128]{2,1,0:T(8,128)S(1)}, f32[16,16,128]{2,1,0:T(8,128)S(1)}) custom-call(s32[4]{0:T(128)S(1)} %pad_add_fusion.own_ref.refs_0_, f32[16,16,8,128]{3,2,1,0:T(8,128)} %given.3), custom_call_target="tpu_custom_call" | custom-call | tf_op jit(solution)/shard_map/pallas_call | solution.py:826
  2.6 1.4 %collective-permute-start.2 = (f32[16,16,128]{2,1,0:T(8,128)S(1)}, f32[16,16,128]{2,1,0:T(8,128)S(1)}, u32[]{:S(2)}, u32[]{:S(2)}) collective-permute-start(f32[16,16,128]{2,1,0:T(8,128)S(1)} %get-tuple-element.46), channel_id=1, source_target_pairs={{0,1},{2,3},{4,5},{6,7},{1,0},{3,2},{5,4},{7,6},{8,9},{10,11},{12,... | collective-permute-start | bytes 393224 | tf_op jit(solution)/shard_map/ppermute | solution.py:711
  3.9 4.9 %collective-permute-start.3 = (f32[16,16,128]{2,1,0:T(8,128)S(1)}, f32[16,16,128]{2,1,0:T(8,128)S(1)}, u32[]{:S(2)}, u32[]{:S(2)}) collective-permute-start(f32[16,16,128]{2,1,0:T(8,128)S(1)} %get-tuple-element.47), channel_id=1, source_target_pairs={{1,2},{3,4},{5,6},{2,1},{4,3},{6,5},{9,10},{11,12},{13,14},{10,9},... | collective-permute-start | bytes 393224 | tf_op jit(solution)/shard_map/ppermute | solution.py:711
  9.2 4.1 %collective-permute-start.1 = (f32[8,16,128]{2,1,0:T(8,128)S(1)}, f32[8,16,128]{2,1,0:T(8,128)S(1)}, u32[]{:S(2)}, u32[]{:S(2)}) collective-permute-start(f32[8,16,128]{2,1,0:T(8,128)S(1)} %get-tuple-element.45), channel_id=1, source_target_pairs={{8,16},{16,8},{9,17},{17,9},{10,18},{18,10},{11,19},{19,11},{12,20... | collective-permute-start | bytes 196616 | tf_op jit(solution)/shard_map/ppermute | solution.py:711
  13.3 1.3 %shard_map.130 = (f32[16,8,16,128]{3,2,1,0:T(8,128)S(1)}, f32[16,8,16,128]{3,2,1,0:T(8,128)S(1)}, f32[4,16,8,128]{3,2,1,0:T(8,128)S(1)}, f32[3,16,128]{2,1,0:T(8...) custom-call(f32[16,16,8,128]{3,2,1,0:T(8,128)S(1)} %copy-done, ...), custom_call_target="tpu_custom_call" | custom-call | flops 1048576 | bytes 3145728 | tf_op jit(solution)/shard_map/pallas_call | solution.py:837
  14.6 1.1 %shard_map.131.refs_1_ = f32[16,8,16,128]{3,2,1,0:T(8,128)S(1)} custom-call(f32[16,8,16,128]{3,2,1,0:T(8,128)S(1)} %get-tuple-element.39.field, f32[16,8,16,128]{3,2,1,0:T(8,128)S(1)} %get-tuple-element.40.refs_0_, f32[4,16,8,128]{3,2,1,0:T(8,128)S(1)} %get-tuple-element.41.refs_1_.refs_6_.refs_0_.flow, ...), custom_call_target="tpu_custom_call" | custom-call | flops 15728640 | bytes 2097152 | tf_op jit(solution)/shard_map/pallas_call | solution.py:869
  16.5 4.3 %collective-permute-start.7 = (f32[16,16,128]{2,1,0:T(8,128)S(1)}, f32[16,16,128]{2,1,0:T(8,128)S(1)}, u32[]{:S(2)}, u32[]{:S(2)}) collective-permute-start(f32[16,16,128]{2,1,0:T(8,128)S(1)} %get-tuple-element.53), channel_id=1, source_target_pairs={{1,2},{3,4},{5,6},{2,1},{4,3},{6,5},{9,10},{11,12},{13,14},{10,9},... | collective-permute-start | bytes 393224 | tf_op jit(solution)/shard_map/ppermute | solution.py:711
  20.8 4.1 %collective-permute-start.5 = (f32[8,16,128]{2,1,0:T(8,128)S(1)}, f32[8,16,128]{2,1,0:T(8,128)S(1)}, u32[]{:S(2)}, u32[]{:S(2)}) collective-permute-start(f32[8,16,128]{2,1,0:T(8,128)S(1)} %get-tuple-element.51), channel_id=1, source_target_pairs={{8,16},{16,8},{9,17},{17,9},{10,18},{18,10},{11,19},{19,11},{12,20... | collective-permute-start | bytes 196616 | tf_op jit(solution)/shard_map/ppermute | solution.py:711
  24.9 0.8 %shard_map.136 = (f32[128,256]{1,0:T(8,128)S(1)}, f32[16,128]{1,0:T(8,128)S(1)}, f32[2,128]{1,0:T(2,128)S(1)}) custom-call(s32[4]{0:T(128)S(1)} %pad_add_fusion.own_ref.refs_0_, f32[8,16]{1,0:T(8,128)S(1)} %get-tuple-element.55.turned, f32[16,64]{1,0:T(8,128)S(1)} %get-tuple-element.56.east, f32[8,64]{1,0:T(8,128)S(1)} %get-tuple-element.57.north), custom_call_target="tpu_custom_call" | custom-call | tf_op jit(solution)/shard_map/pallas_call | solution.py:881
  25.7 1.1 %shard_map.134.refs_1_ = f32[16,8,16,128]{3,2,1,0:T(8,128)S(1)} custom-call(f32[16,8,16,128]{3,2,1,0:T(8,128)S(1)} %get-tuple-element.48.field, f32[16,8,16,128]{3,2,1,0:T(8,128)S(1)} %get-tuple-element.40.refs_0_, f32[4,16,8,128]{3,2,1,0:T(8,128)S(1)} %get-tuple-element.41.refs_1_.refs_6_.refs_0_.flow, ...), custom_call_target="tpu_custom_call" | custom-call | flops 15728640 | bytes 2097152 | tf_op jit(solution)/shard_map/pallas_call | solution.py:877
  26.9 0.7 %shard_map.135 = (f32[16,8,16,128]{3,2,1,0:T(8,128)S(1)}, f32[576,128]{1,0:T(8,128)S(1)}, f32[576,128]{1,0:T(8,128)S(1)}) custom-call(s32[4]{0:T(128)S(1)} %pad_add_fusion.own_ref.refs_0_, f32[16,8,16,128]{3,2,1,0:T(8,128)S(1)} %shard_map.134.refs_1_, f32[8,16,128]{2,1,0:T(8,128)S(1)} %collective-permute-done.4.refs_2_, ...), custom_call_target="tpu_custom_call" | custom-call | flops 1048576 | bytes 2097152 | tf_op jit(solution)/shard_map/pallas_call | solution.py:874
  27.6 1.4 %shard_map.137 = f32[320,128]{1,0:T(8,128)} custom-call(f32[16,8,16,128]{3,2,1,0:T(8,128)S(1)} %get-tuple-element.65.field, f32[128,256]{1,0:T(8,128)S(1)} %get-tuple-element.58.component, f32[32,128]{1,0:T(8,128)S(1)} %get-tuple-element.59.vertical, f32[2,128]{1,0:T(2,128)S(1)} %get-tuple-element.60.factor_rows), custom_call_target="tpu_custom_call" | custom-call | flops 15728640 | bytes 1048576 | tf_op jit(solution)/shard_map/pallas_call | solution.py:885
  29.0 4.2 %all-to-all-start = ((f32[32,5,2,128]{3,2,1,0:T(2,128)}), f32[32,5,2,128]{3,2,1,0:T(2,128)S(1)}, u32[]{:S(2)}, u32[]{:S(2)}) async-start(f32[32,5,2,128]{3,2,1,0:T(2,128)} %bitcast.9), calls=%async_computation | async-start | bytes 327680 | tf_op jit(solution)/shard_map/all_to_all | solution.py:889
  33.2 1.3 %collective-permute-start.8 = (f32[576,128]{1,0:T(8,128)S(1)}, f32[576,128]{1,0:T(8,128)S(1)}, u32[]{:S(2)}, u32[]{:S(2)}) collective-permute-start(f32[576,128]{1,0:T(8,128)S(1)} %get-tuple-element.66), channel_id=1, source_target_pairs={{0,1},{2,3},{4,5},{6,7},{1,0},{3,2},{5,4},{7,6},{8,9},{10,11},{12,... | collective-permute-start | bytes 884744 | tf_op jit(solution)/shard_map/ppermute | solution.py:711
  34.4 4.5 %collective-permute-start.9 = (f32[576,128]{1,0:T(8,128)S(1)}, f32[576,128]{1,0:T(8,128)S(1)}, u32[]{:S(2)}, u32[]{:S(2)}) collective-permute-start(f32[576,128]{1,0:T(8,128)S(1)} %get-tuple-element.67), channel_id=1, source_target_pairs={{1,2},{3,4},{5,6},{2,1},{4,3},{6,5},{9,10},{11,12},{13,14},{10,9},... | collective-permute-start | bytes 884744 | tf_op jit(solution)/shard_map/ppermute | solution.py:711
  38.9 1.4 %all-to-all-done = f32[32,5,2,128]{3,2,1,0:T(2,128)S(1)} async-done(((f32[32,5,2,128]{3,2,1,0:T(2,128)}), f32[32,5,2,128]{3,2,1,0:T(2,128)S(1)}, u32[]{:S(2)}, u32[]{:S(2)}) %all-to-all-start) | async-done | bytes 163872 | tf_op jit(solution)/shard_map/all_to_all | solution.py:889
  40.4 1.9 %shard_map.138 = f32[32,16,128]{2,1,0:T(8,128)} custom-call(f32[320,128]{1,0:T(8,128)S(1)} %bitcast.14), custom_call_target="tpu_custom_call" | custom-call | flops 15728640 | bytes 1048576 | tf_op jit(solution)/shard_map/pallas_call | solution.py:892
  42.3 4.3 %all-to-all-start.1 = ((f32[32,16,128]{2,1,0:T(8,128)}), f32[32,16,128]{2,1,0:T(8,128)S(1)}, u32[]{:S(2)}, u32[]{:S(2)}) async-start(f32[32,16,128]{2,1,0:T(8,128)} %shard_map.138), calls=%async_computation.1 | async-start | bytes 524288 | tf_op jit(solution)/shard_map/all_to_all | solution.py:897
  46.6 2.8 %collective-permute-done.9.y_other = f32[576,128]{1,0:T(8,128)S(1)} collective-permute-done((f32[576,128]{1,0:T(8,128)S(1)}, f32[576,128]{1,0:T(8,128)S(1)}, u32[]{:S(2)}, u32[]{:S(2)}) %collective-permute-start.9) | collective-permute-done | bytes 294944 | tf_op jit(solution)/shard_map/ppermute | solution.py:711
  50.4 4.0 %collective-permute-start.11 = (f32[320,128]{1,0:T(8,128)S(1)}, f32[320,128]{1,0:T(8,128)S(1)}, u32[]{:S(2)}, u32[]{:S(2)}) collective-permute-start(f32[320,128]{1,0:T(8,128)S(1)} %get-tuple-element.73), channel_id=1, source_target_pairs={{8,16},{16,8},{9,17},{17,9},{10,18},{18,10},{11,19},{19,11},{12,20... | collective-permute-start | bytes 491528 | tf_op jit(solution)/shard_map/ppermute | solution.py:711
  54.4 1.2 %shard_map.140.block = f32[16,8,16,128]{3,2,1,0:T(8,128)S(1)} custom-call(f32[16,8,16,128]{3,2,1,0:T(8,128)S(1)} %get-tuple-element.65.field, f32[4,16,8,128]{3,2,1,0:T(8,128)S(1)} %get-tuple-element.41.refs_1_.refs_6_.refs_0_.flow, f32[3,16,128]{2,1,0:T(8,128)S(1)} %get-tuple-element.42.refs_2_.refs_7_.refs_1_.coefficients, ...), custom_call_target="tpu_custom_call" | custom-call | flops 15728640 | bytes 2097152 | tf_op jit(solution)/shard_map/pallas_call | solution.py:917
  55.6 3.0 %shard_map.141 = (f32[4,10,16,128]{3,2,1,0:T(8,128)S(1)}, f32[2,2,8,128]{3,2,1,0:T(8,128)S(1)}, f32[2,8,16,128]{3,2,1,0:T(8,128)S(1)}, f32[16,16,8,128]{3,2,1,0:T(8,128)}) custom-call(s32[4]{0:T(128)S(1)} %pad_add_fusion.own_ref.refs_0_, f32[16,8,16,128]{3,2,1,0:T(8,128)S(1)} %shard_map.140.block, f32[16,8,16,128]{3,2,1,0:T(8,128)S(1)} %get-tuple-element.65.field, ...), custom_call_target="tpu_custom_call" | custom-call | flops 31457280 | bytes 4194304 | tf_op jit(solution)/shard_map/pallas_call | solution.py:924
  58.7 2.4 %shard_map.139 = (f32[16,16,8,128]{3,2,1,0:T(8,128)}, f32[128,8,32]{2,1,0:T(8,128)}) custom-call(f32[512,128]{1,0:T(8,128)S(1)} %bitcast.13, f32[16,8,16,128]{3,2,1,0:T(8,128)S(1)} %get-tuple-element.65.field, f32[16,128]{1,0:T(8,128)S(1)} %get-tuple-element.62.wide_rows, f32[32,128]{1,0:T(8,128)S(1)} %get-tuple-element.59.vertical), custom_call_target="tpu_custom_call" | custom-call | flops 15728640 | bytes 2097152 | tf_op jit(solution)/shard_map/pallas_call | solution.py:898
  61.1 1.8 %shard_map.143 = f32[16,16,8,128]{3,2,1,0:T(8,128)} custom-call(s32[4]{0:T(128)S(1)} %pad_add_fusion.own_ref.refs_0_, f32[4,10,16,128]{3,2,1,0:T(8,128)S(1)} %get-tuple-element.68.edges, f32[2,2,8,128]{3,2,1,0:T(8,128)S(1)} %get-tuple-element.69.ends, f32[2,8,16,128]{3,2,1,0:T(8,128)S(1)} %get-tuple-element.70.nearly, ...), custom_call_target="tpu_custom_call", output_to_operand_aliasing={{}: (4, {})} | custom-call | flops 15728640 | bytes 2097152 | tf_op jit(solution)/shard_map/pallas_call | solution.py:935
  (21 shorter events, 2.2 us)
Async XLA Ops:
  0.6 12.6 %copy-start = (f32[16,16,8,128]{3,2,1,0:T(8,128)S(1)}, f32[16,16,8,128]{3,2,1,0:T(8,128)}, u32[]{:S(2)}) copy-start(f32[16,16,8,128]{3,2,1,0:T(8,128)} %given.3) | copy-start | bytes 3145732
  2.6 13.1 %collective-permute-start.2 = (f32[16,16,128]{2,1,0:T(8,128)S(1)}, f32[16,16,128]{2,1,0:T(8,128)S(1)}, u32[]{:S(2)}, u32[]{:S(2)}) collective-permute-start(f32[16,16,128]{2,1,0:T(8,128)S(1)} %get-tuple-element.46), channel_id=1, source_target_pairs={{0,1},{2,3},{4,5},{6,7},{1,0},{3,2},{5,4},{7,6},{8,9},{10,11},{12,... | collective-permute-start | bytes 393224 | tf_op jit(solution)/shard_map/ppermute | solution.py:711
  3.9 11.8 %collective-permute-start.3 = (f32[16,16,128]{2,1,0:T(8,128)S(1)}, f32[16,16,128]{2,1,0:T(8,128)S(1)}, u32[]{:S(2)}, u32[]{:S(2)}) collective-permute-start(f32[16,16,128]{2,1,0:T(8,128)S(1)} %get-tuple-element.47), channel_id=1, source_target_pairs={{1,2},{3,4},{5,6},{2,1},{4,3},{6,5},{9,10},{11,12},{13,14},{10,9},... | collective-permute-start | bytes 393224 | tf_op jit(solution)/shard_map/ppermute | solution.py:711
  8.9 6.8 %collective-permute-start = (f32[8,16,128]{2,1,0:T(8,128)S(1)}, f32[8,16,128]{2,1,0:T(8,128)S(1)}, u32[]{:S(2)}, u32[]{:S(2)}) collective-permute-start(f32[8,16,128]{2,1,0:T(8,128)S(1)} %get-tuple-element.44), channel_id=1, source_target_pairs={{0,8},{16,24},{8,0},{24,16},{1,9},{17,25},{9,1},{25,17},{2,10},{18... | collective-permute-start | bytes 196616 | tf_op jit(solution)/shard_map/ppermute | solution.py:711
  9.2 6.5 %collective-permute-start.1 = (f32[8,16,128]{2,1,0:T(8,128)S(1)}, f32[8,16,128]{2,1,0:T(8,128)S(1)}, u32[]{:S(2)}, u32[]{:S(2)}) collective-permute-start(f32[8,16,128]{2,1,0:T(8,128)S(1)} %get-tuple-element.45), channel_id=1, source_target_pairs={{8,16},{16,8},{9,17},{17,9},{10,18},{18,10},{11,19},{19,11},{12,20... | collective-permute-start | bytes 196616 | tf_op jit(solution)/shard_map/ppermute | solution.py:711
  16.4 10.5 %collective-permute-start.6 = (f32[16,16,128]{2,1,0:T(8,128)S(1)}, f32[16,16,128]{2,1,0:T(8,128)S(1)}, u32[]{:S(2)}, u32[]{:S(2)}) collective-permute-start(f32[16,16,128]{2,1,0:T(8,128)S(1)} %get-tuple-element.52), channel_id=1, source_target_pairs={{0,1},{2,3},{4,5},{6,7},{1,0},{3,2},{5,4},{7,6},{8,9},{10,11},{12,... | collective-permute-start | bytes 393224 | tf_op jit(solution)/shard_map/ppermute | solution.py:711
  16.5 10.4 %collective-permute-start.7 = (f32[16,16,128]{2,1,0:T(8,128)S(1)}, f32[16,16,128]{2,1,0:T(8,128)S(1)}, u32[]{:S(2)}, u32[]{:S(2)}) collective-permute-start(f32[16,16,128]{2,1,0:T(8,128)S(1)} %get-tuple-element.53), channel_id=1, source_target_pairs={{1,2},{3,4},{5,6},{2,1},{4,3},{6,5},{9,10},{11,12},{13,14},{10,9},... | collective-permute-start | bytes 393224 | tf_op jit(solution)/shard_map/ppermute | solution.py:711
  20.8 6.1 %collective-permute-start.4 = (f32[8,16,128]{2,1,0:T(8,128)S(1)}, f32[8,16,128]{2,1,0:T(8,128)S(1)}, u32[]{:S(2)}, u32[]{:S(2)}) collective-permute-start(f32[8,16,128]{2,1,0:T(8,128)S(1)} %get-tuple-element.50), channel_id=1, source_target_pairs={{0,8},{16,24},{8,0},{24,16},{1,9},{17,25},{9,1},{25,17},{2,10},{18... | collective-permute-start | bytes 196616 | tf_op jit(solution)/shard_map/ppermute | solution.py:711
  20.8 6.0 %collective-permute-start.5 = (f32[8,16,128]{2,1,0:T(8,128)S(1)}, f32[8,16,128]{2,1,0:T(8,128)S(1)}, u32[]{:S(2)}, u32[]{:S(2)}) collective-permute-start(f32[8,16,128]{2,1,0:T(8,128)S(1)} %get-tuple-element.51), channel_id=1, source_target_pairs={{8,16},{16,8},{9,17},{17,9},{10,18},{18,10},{11,19},{19,11},{12,20... | collective-permute-start | bytes 196616 | tf_op jit(solution)/shard_map/ppermute | solution.py:711
  29.0 11.4 %all-to-all-start = ((f32[32,5,2,128]{3,2,1,0:T(2,128)}), f32[32,5,2,128]{3,2,1,0:T(2,128)S(1)}, u32[]{:S(2)}, u32[]{:S(2)}) async-start(f32[32,5,2,128]{3,2,1,0:T(2,128)} %bitcast.9), calls=%async_computation | async-start | bytes 327680 | tf_op jit(solution)/shard_map/all_to_all | solution.py:889
  33.2 13.4 %collective-permute-start.8 = (f32[576,128]{1,0:T(8,128)S(1)}, f32[576,128]{1,0:T(8,128)S(1)}, u32[]{:S(2)}, u32[]{:S(2)}) collective-permute-start(f32[576,128]{1,0:T(8,128)S(1)} %get-tuple-element.66), channel_id=1, source_target_pairs={{0,1},{2,3},{4,5},{6,7},{1,0},{3,2},{5,4},{7,6},{8,9},{10,11},{12,... | collective-permute-start | bytes 884744 | tf_op jit(solution)/shard_map/ppermute | solution.py:711
  34.4 15.0 %collective-permute-start.9 = (f32[576,128]{1,0:T(8,128)S(1)}, f32[576,128]{1,0:T(8,128)S(1)}, u32[]{:S(2)}, u32[]{:S(2)}) collective-permute-start(f32[576,128]{1,0:T(8,128)S(1)} %get-tuple-element.67), channel_id=1, source_target_pairs={{1,2},{3,4},{5,6},{2,1},{4,3},{6,5},{9,10},{11,12},{13,14},{10,9},... | collective-permute-start | bytes 884744 | tf_op jit(solution)/shard_map/ppermute | solution.py:711
  42.3 16.3 %all-to-all-start.1 = ((f32[32,16,128]{2,1,0:T(8,128)}), f32[32,16,128]{2,1,0:T(8,128)S(1)}, u32[]{:S(2)}, u32[]{:S(2)}) async-start(f32[32,16,128]{2,1,0:T(8,128)} %shard_map.138), calls=%async_computation.1 | async-start | bytes 524288 | tf_op jit(solution)/shard_map/all_to_all | solution.py:897
  50.0 11.1 %collective-permute-start.10 = (f32[424,128]{1,0:T(8,128)S(1)}, f32[424,128]{1,0:T(8,128)S(1)}, u32[]{:S(2)}, u32[]{:S(2)}) collective-permute-start(f32[424,128]{1,0:T(8,128)S(1)} %get-tuple-element.72), channel_id=1, source_target_pairs={{0,8},{16,24},{8,0},{24,16},{1,9},{17,25},{9,1},{25,17},{2,10},{18... | collective-permute-start | bytes 651272 | tf_op jit(solution)/shard_map/ppermute | solution.py:711
  50.4 10.7 %collective-permute-start.11 = (f32[320,128]{1,0:T(8,128)S(1)}, f32[320,128]{1,0:T(8,128)S(1)}, u32[]{:S(2)}, u32[]{:S(2)}) collective-permute-start(f32[320,128]{1,0:T(8,128)S(1)} %get-tuple-element.73), channel_id=1, source_target_pairs={{8,16},{16,8},{9,17},{17,9},{10,18},{18,10},{11,19},{19,11},{12,20... | collective-permute-start | bytes 491528 | tf_op jit(solution)/shard_map/ppermute | solution.py:711

commit v8 on v7

--- a/solution.py
+++ b/solution.py
@@ -614,6 +614,11 @@
         out[pl.ds(deep + row, ranks_d, stride=each), :] = jnp.broadcast_to(
             factor_rows[row : row + 1], (ranks_d, 128)
         )
+
+
+def snapshot_and_project_kernel(shape, ranks, *refs):
+    snapshot_kernel(shape, *refs[:8], *refs[11:14])
+    project_kernel(shape, ranks, refs[11], *refs[8:11], refs[14])
 
 
 def core_kernel(counts, got, out):
@@ -871,21 +876,26 @@
         first = field
         faces = faces_beside(faces)
     high = 2 * species + 4
-    snapshot, *y_faces = vmem_call(
-        functools.partial(snapshot_kernel, shape), [shape] + [(wide * high, up)] * 2, 1, 8,
-        flops=4 * cells, moved=8 * cells,
-    )(own, *block(field, *fixed), *faces, speeds, coefficients)
-    y_faces = swapped(*y_faces, COLUMN)
+    last_given = (*block(field, *fixed), *faces, speeds, coefficients)
+    snapshot_outs = [shape] + [(wide * high, up)] * 2
     if kernels_fit:
         own, _ = lax.optimization_barrier((own, first))
         squeeze, wide_rows, factor_rows = vmem_call(
             functools.partial(matrices_kernel, shape),
             [(wide * ranks_a, wide * species), (species, wide * ranks_a), (2, 128)], 1, 4,
         )(own, turned, east, north)
-        (sent,) = vmem_call(
-            functools.partial(project_kernel, shape, (ranks_a, ranks_d)),
-            [(devices * (deep + 2), 128)], 0, 4, flops=60 * cells, moved=4 * cells,
-        )(snapshot, squeeze, upright, factor_rows)
+        snapshot, *y_faces, sent = vmem_call(
+            functools.partial(snapshot_and_project_kernel, shape, (ranks_a, ranks_d)),
+            snapshot_outs + [(devices * (deep + 2), 128)], 1, 11,
+            flops=60 * cells, moved=8 * cells,
+        )(own, *last_given, squeeze, upright, factor_rows)
+    else:
+        snapshot, *y_faces = vmem_call(
+            functools.partial(snapshot_kernel, shape), snapshot_outs, 1, 8,
+            flops=4 * cells, moved=8 * cells,
+        )(own, *last_given)
+    y_faces = swapped(*y_faces, COLUMN)
+    if kernels_fit:
         got = lax.all_to_all(
             sent.reshape(devices, (deep + 2) // 2, 2, 128), EVERY, 0, 0, tiled=True
         )

time: 63.6 us -> 63.5 us (level)
    pallas_call x2 -> x1, Pallas kernels: 2.2 us -> 1.06 us  [body(): block(field, *fixed)]
    pallas_call x2, Pallas kernels: 2.09 us -> 3.15 us  [the longest x1 2 us: body(): vmem_call(functools.partial(snapshot_and_project_kernel, shape, (ranks_a,...]
where the time goes in v8:
time: 63.5 us; the launch traced here: 62.8 us
  starting transfers between devices  37.8 us (60%)
  Pallas kernels  19.8 us (31%)
  waiting for transfers between devices  4.3 us (7%)
  between operations  0.88 us (1%)
    ppermute x12, starting transfers between devices, swapped(): got.append(lax.ppermute(face, axes, couples + [(b, a) for a, b in couples]))  29.3 us
    all_to_all x1, starting transfers between devices, body(): got = lax.all_to_all(sent, EVERY, 0, 0, tiled=True)  4.26 us
    all_to_all x1, starting transfers between devices, body(): lax.all_to_all(sent.reshape(devices, (deep + 2) // 2, 2, 128), EVERY, 0,...  4.19 us
    pallas_call x1, Pallas kernels, body(): vmem_call(functools.partial(third_step_kernel, shape, (rows, columns)), [...  3.03 us
    ppermute x12, waiting for transfers between devices, swapped(): got.append(lax.ppermute(face, axes, couples + [(b, a) for a, b in couples]))  2.86 us
    pallas_call x1, Pallas kernels, body(): vmem_call(functools.partial(expand_kernel, shape, (ranks_a, ranks_d), own...  2.44 us
    pallas_call x1, Pallas kernels, body(): vmem_call(functools.partial(snapshot_and_project_kernel, shape, (ranks_a,...  2 us
    pallas_call x1, Pallas kernels, body(): vmem_call(functools.partial(core_kernel, (rows, columns, ranks_a, own_c,...  1.94 us
  transfers between devices with their start and end apart: 14, of which 2 were waited for; matrix products, arithmetic and copies ran while one was open for 0% of the time, Pallas kernels for 21%

profile of v8, /device:TPU:3, one launch (start us, length us, event | category | flops | bytes accessed | tf_op | source)
XLA Modules:
  0.0 62.8 jit_solution(9156727532488682880)
XLA Ops:
  0.7 1.8 %shard_map.132 = (f32[8,16,128]{2,1,0:T(8,128)S(1)}, f32[8,16,128]{2,1,0:T(8,128)S(1)}, f32[16,16,128]{2,1,0:T(8,128)S(1)}, f32[16,16,128]{2,1,0:T(8,128)S(1)}) custom-call(s32[4]{0:T(128)S(1)} %pad_add_fusion.own_ref.refs_0_, f32[16,16,8,128]{3,2,1,0:T(8,128)} %given.3), custom_call_target="tpu_custom_call" | custom-call | tf_op jit(solution)/shard_map/pallas_call | solution.py:831
  2.6 1.4 %collective-permute-start.2 = (f32[16,16,128]{2,1,0:T(8,128)S(1)}, f32[16,16,128]{2,1,0:T(8,128)S(1)}, u32[]{:S(2)}, u32[]{:S(2)}) collective-permute-start(f32[16,16,128]{2,1,0:T(8,128)S(1)} %get-tuple-element.47), channel_id=1, source_target_pairs={{0,1},{2,3},{4,5},{6,7},{1,0},{3,2},{5,4},{7,6},{8,9},{10,11},{12,... | collective-permute-start | bytes 393224 | tf_op jit(solution)/shard_map/ppermute | solution.py:716
  3.9 4.9 %collective-permute-start.3 = (f32[16,16,128]{2,1,0:T(8,128)S(1)}, f32[16,16,128]{2,1,0:T(8,128)S(1)}, u32[]{:S(2)}, u32[]{:S(2)}) collective-permute-start(f32[16,16,128]{2,1,0:T(8,128)S(1)} %get-tuple-element.48), channel_id=1, source_target_pairs={{1,2},{3,4},{5,6},{2,1},{4,3},{6,5},{9,10},{11,12},{13,14},{10,9},... | collective-permute-start | bytes 393224 | tf_op jit(solution)/shard_map/ppermute | solution.py:716
  9.2 4.1 %collective-permute-start.1 = (f32[8,16,128]{2,1,0:T(8,128)S(1)}, f32[8,16,128]{2,1,0:T(8,128)S(1)}, u32[]{:S(2)}, u32[]{:S(2)}) collective-permute-start(f32[8,16,128]{2,1,0:T(8,128)S(1)} %get-tuple-element.46), channel_id=1, source_target_pairs={{8,16},{16,8},{9,17},{17,9},{10,18},{18,10},{11,19},{19,11},{12,20... | collective-permute-start | bytes 196616 | tf_op jit(solution)/shard_map/ppermute | solution.py:716
  13.3 1.3 %shard_map.130 = (f32[16,8,16,128]{3,2,1,0:T(8,128)S(1)}, f32[16,8,16,128]{3,2,1,0:T(8,128)S(1)}, f32[4,16,8,128]{3,2,1,0:T(8,128)S(1)}, f32[3,16,128]{2,1,0:T(8...) custom-call(f32[16,16,8,128]{3,2,1,0:T(8,128)S(1)} %copy-done, ...), custom_call_target="tpu_custom_call" | custom-call | flops 1048576 | bytes 3145728 | tf_op jit(solution)/shard_map/pallas_call | solution.py:842
  14.6 1.1 %shard_map.131.refs_1_ = f32[16,8,16,128]{3,2,1,0:T(8,128)S(1)} custom-call(f32[16,8,16,128]{3,2,1,0:T(8,128)S(1)} %get-tuple-element.40.field, f32[16,8,16,128]{3,2,1,0:T(8,128)S(1)} %get-tuple-element.41.refs_0_, f32[4,16,8,128]{3,2,1,0:T(8,128)S(1)} %get-tuple-element.42.refs_1_.refs_6_.refs_0_.flow, ...), custom_call_target="tpu_custom_call" | custom-call | flops 15728640 | bytes 2097152 | tf_op jit(solution)/shard_map/pallas_call | solution.py:874
  15.7 0.7 %shard_map.133 = (f32[16,8,16,128]{3,2,1,0:T(8,128)S(1)}, f32[8,16,128]{2,1,0:T(8,128)S(1)}, f32[8,16,128]{2,1,0:T(8,128)S(1)}, f32[16,16,128]{2,1,0:T(8,128)S(1)}, f32[16,16,128]{2,1,0:T(8,128)S(1)}) custom-call(s32[4]{0:T(128)S(1)} %pad_add_fusion.own_ref.refs_0_, f32[16,8,16,128]{3,2,1,0:T(8,128)S(1)} %shard_map.131.refs_1_, ...), custom_call_target="tpu_custom_call" | custom-call | flops 1048576 | bytes 2097152 | tf_op jit(solution)/shard_map/pallas_call | solution.py:873
  16.5 4.3 %collective-permute-start.7 = (f32[16,16,128]{2,1,0:T(8,128)S(1)}, f32[16,16,128]{2,1,0:T(8,128)S(1)}, u32[]{:S(2)}, u32[]{:S(2)}) collective-permute-start(f32[16,16,128]{2,1,0:T(8,128)S(1)} %get-tuple-element.54), channel_id=1, source_target_pairs={{1,2},{3,4},{5,6},{2,1},{4,3},{6,5},{9,10},{11,12},{13,14},{10,9},... | collective-permute-start | bytes 393224 | tf_op jit(solution)/shard_map/ppermute | solution.py:716
  20.8 4.1 %collective-permute-start.5 = (f32[8,16,128]{2,1,0:T(8,128)S(1)}, f32[8,16,128]{2,1,0:T(8,128)S(1)}, u32[]{:S(2)}, u32[]{:S(2)}) collective-permute-start(f32[8,16,128]{2,1,0:T(8,128)S(1)} %get-tuple-element.52), channel_id=1, source_target_pairs={{8,16},{16,8},{9,17},{17,9},{10,18},{18,10},{11,19},{19,11},{12,20... | collective-permute-start | bytes 196616 | tf_op jit(solution)/shard_map/ppermute | solution.py:716
  24.9 0.8 %shard_map.135 = (f32[128,256]{1,0:T(8,128)S(1)}, f32[16,128]{1,0:T(8,128)S(1)}, f32[2,128]{1,0:T(2,128)S(1)}) custom-call(s32[4]{0:T(128)S(1)} %pad_add_fusion.own_ref.refs_0_, f32[8,16]{1,0:T(8,128)S(1)} %get-tuple-element.55.turned, f32[16,64]{1,0:T(8,128)S(1)} %get-tuple-element.56.east, f32[8,64]{1,0:T(8,128)S(1)} %get-tuple-element.57.north), custom_call_target="tpu_custom_call" | custom-call | tf_op jit(solution)/shard_map/pallas_call | solution.py:883
  25.7 1.1 %shard_map.134.refs_1_ = f32[16,8,16,128]{3,2,1,0:T(8,128)S(1)} custom-call(f32[16,8,16,128]{3,2,1,0:T(8,128)S(1)} %get-tuple-element.49.field, f32[16,8,16,128]{3,2,1,0:T(8,128)S(1)} %get-tuple-element.41.refs_0_, f32[4,16,8,128]{3,2,1,0:T(8,128)S(1)} %get-tuple-element.42.refs_1_.refs_6_.refs_0_.flow, ...), custom_call_target="tpu_custom_call" | custom-call | flops 15728640 | bytes 2097152 | tf_op jit(solution)/shard_map/pallas_call | solution.py:879
  26.9 2.0 %shard_map.136 = (f32[16,8,16,128]{3,2,1,0:T(8,128)S(1)}, f32[576,128]{1,0:T(8,128)S(1)}, f32[576,128]{1,0:T(8,128)S(1)}, f32[320,128]{1,0:T(8,128)}) custom-call(s32[4]{0:T(128)S(1)} %pad_add_fusion.own_ref.refs_0_, f32[16,8,16,128]{3,2,1,0:T(8,128)S(1)} %shard_map.134.refs_1_, f32[8,16,128]{2,1,0:T(8,128)S(1)} %collective-permute-done.4.refs_2_, ...), custom_call_target="tpu_custom_call" | custom-call | flops 15728640 | bytes 2097152 | tf_op jit(solution)/shard_map/pallas_call | solution.py:887
  28.9 4.2 %all-to-all-start = ((f32[32,5,2,128]{3,2,1,0:T(2,128)}), f32[32,5,2,128]{3,2,1,0:T(2,128)S(1)}, u32[]{:S(2)}, u32[]{:S(2)}) async-start(f32[32,5,2,128]{3,2,1,0:T(2,128)} %bitcast.9), calls=%async_computation | async-start | bytes 327680 | tf_op jit(solution)/shard_map/all_to_all | solution.py:899
  33.1 1.3 %collective-permute-start.8 = (f32[576,128]{1,0:T(8,128)S(1)}, f32[576,128]{1,0:T(8,128)S(1)}, u32[]{:S(2)}, u32[]{:S(2)}) collective-permute-start(f32[576,128]{1,0:T(8,128)S(1)} %get-tuple-element.68), channel_id=1, source_target_pairs={{0,1},{2,3},{4,5},{6,7},{1,0},{3,2},{5,4},{7,6},{8,9},{10,11},{12,... | collective-permute-start | bytes 884744 | tf_op jit(solution)/shard_map/ppermute | solution.py:716
  34.3 4.5 %collective-permute-start.9 = (f32[576,128]{1,0:T(8,128)S(1)}, f32[576,128]{1,0:T(8,128)S(1)}, u32[]{:S(2)}, u32[]{:S(2)}) collective-permute-start(f32[576,128]{1,0:T(8,128)S(1)} %get-tuple-element.69), channel_id=1, source_target_pairs={{1,2},{3,4},{5,6},{2,1},{4,3},{6,5},{9,10},{11,12},{13,14},{10,9},... | collective-permute-start | bytes 884744 | tf_op jit(solution)/shard_map/ppermute | solution.py:716
  38.9 1.4 %all-to-all-done = f32[32,5,2,128]{3,2,1,0:T(2,128)S(1)} async-done(((f32[32,5,2,128]{3,2,1,0:T(2,128)}), f32[32,5,2,128]{3,2,1,0:T(2,128)S(1)}, u32[]{:S(2)}, u32[]{:S(2)}) %all-to-all-start) | async-done | bytes 163872 | tf_op jit(solution)/shard_map/all_to_all | solution.py:899
  40.3 1.9 %shard_map.137 = f32[32,16,128]{2,1,0:T(8,128)} custom-call(f32[320,128]{1,0:T(8,128)S(1)} %bitcast.14), custom_call_target="tpu_custom_call" | custom-call | flops 15728640 | bytes 1048576 | tf_op jit(solution)/shard_map/pallas_call | solution.py:902
  42.2 4.3 %all-to-all-start.1 = ((f32[32,16,128]{2,1,0:T(8,128)}), f32[32,16,128]{2,1,0:T(8,128)S(1)}, u32[]{:S(2)}, u32[]{:S(2)}) async-start(f32[32,16,128]{2,1,0:T(8,128)} %shard_map.137), calls=%async_computation.1 | async-start | bytes 524288 | tf_op jit(solution)/shard_map/all_to_all | solution.py:907
  46.5 2.8 %collective-permute-done.9.y_other = f32[576,128]{1,0:T(8,128)S(1)} collective-permute-done((f32[576,128]{1,0:T(8,128)S(1)}, f32[576,128]{1,0:T(8,128)S(1)}, u32[]{:S(2)}, u32[]{:S(2)}) %collective-permute-start.9) | collective-permute-done | bytes 294944 | tf_op jit(solution)/shard_map/ppermute | solution.py:716
  50.3 4.0 %collective-permute-start.11 = (f32[320,128]{1,0:T(8,128)S(1)}, f32[320,128]{1,0:T(8,128)S(1)}, u32[]{:S(2)}, u32[]{:S(2)}) collective-permute-start(f32[320,128]{1,0:T(8,128)S(1)} %get-tuple-element.75), channel_id=1, source_target_pairs={{8,16},{16,8},{9,17},{17,9},{10,18},{18,10},{11,19},{19,11},{12,20... | collective-permute-start | bytes 491528 | tf_op jit(solution)/shard_map/ppermute | solution.py:716
  54.3 1.2 %shard_map.139.block = f32[16,8,16,128]{3,2,1,0:T(8,128)S(1)} custom-call(f32[16,8,16,128]{3,2,1,0:T(8,128)S(1)} %get-tuple-element.67.field, f32[4,16,8,128]{3,2,1,0:T(8,128)S(1)} %get-tuple-element.42.refs_1_.refs_6_.refs_0_.flow, f32[3,16,128]{2,1,0:T(8,128)S(1)} %get-tuple-element.43.refs_2_.refs_7_.refs_1_.coefficients, ...), custom_call_target="tpu_custom_call" | custom-call | flops 15728640 | bytes 2097152 | tf_op jit(solution)/shard_map/pallas_call | solution.py:927
  55.5 3.0 %shard_map.140 = (f32[4,10,16,128]{3,2,1,0:T(8,128)S(1)}, f32[2,2,8,128]{3,2,1,0:T(8,128)S(1)}, f32[2,8,16,128]{3,2,1,0:T(8,128)S(1)}, f32[16,16,8,128]{3,2,1,0:T(8,128)}) custom-call(s32[4]{0:T(128)S(1)} %pad_add_fusion.own_ref.refs_0_, f32[16,8,16,128]{3,2,1,0:T(8,128)S(1)} %shard_map.139.block, f32[16,8,16,128]{3,2,1,0:T(8,128)S(1)} %get-tuple-element.67.field, ...), custom_call_target="tpu_custom_call" | custom-call | flops 31457280 | bytes 4194304 | tf_op jit(solution)/shard_map/pallas_call | solution.py:934
  58.6 2.4 %shard_map.138 = (f32[16,16,8,128]{3,2,1,0:T(8,128)}, f32[128,8,32]{2,1,0:T(8,128)}) custom-call(f32[512,128]{1,0:T(8,128)S(1)} %bitcast.13, f32[16,8,16,128]{3,2,1,0:T(8,128)S(1)} %get-tuple-element.67.field, f32[16,128]{1,0:T(8,128)S(1)} %get-tuple-element.64.wide_rows, f32[32,128]{1,0:T(8,128)S(1)} %get-tuple-element.59.refs_9_.vertical), custom_call_target="tpu_custom_call" | custom-call | flops 15728640 | bytes 2097152 | tf_op jit(solution)/shard_map/pallas_call | solution.py:908
  61.0 1.8 %shard_map.142 = f32[16,16,8,128]{3,2,1,0:T(8,128)} custom-call(s32[4]{0:T(128)S(1)} %pad_add_fusion.own_ref.refs_0_, f32[4,10,16,128]{3,2,1,0:T(8,128)S(1)} %get-tuple-element.70.edges, f32[2,2,8,128]{3,2,1,0:T(8,128)S(1)} %get-tuple-element.71.ends, f32[2,8,16,128]{3,2,1,0:T(8,128)S(1)} %get-tuple-element.72.nearly, ...), custom_call_target="tpu_custom_call", output_to_operand_aliasing={{}: (4, {})} | custom-call | flops 15728640 | bytes 2097152 | tf_op jit(solution)/shard_map/pallas_call | solution.py:945
  (20 shorter events, 1.5 us)
Async XLA Ops:
  0.6 12.6 %copy-start = (f32[16,16,8,128]{3,2,1,0:T(8,128)S(1)}, f32[16,16,8,128]{3,2,1,0:T(8,128)}, u32[]{:S(2)}) copy-start(f32[16,16,8,128]{3,2,1,0:T(8,128)} %given.3) | copy-start | bytes 3145732
  2.6 13.1 %collective-permute-start.2 = (f32[16,16,128]{2,1,0:T(8,128)S(1)}, f32[16,16,128]{2,1,0:T(8,128)S(1)}, u32[]{:S(2)}, u32[]{:S(2)}) collective-permute-start(f32[16,16,128]{2,1,0:T(8,128)S(1)} %get-tuple-element.47), channel_id=1, source_target_pairs={{0,1},{2,3},{4,5},{6,7},{1,0},{3,2},{5,4},{7,6},{8,9},{10,11},{12,... | collective-permute-start | bytes 393224 | tf_op jit(solution)/shard_map/ppermute | solution.py:716
  3.9 11.8 %collective-permute-start.3 = (f32[16,16,128]{2,1,0:T(8,128)S(1)}, f32[16,16,128]{2,1,0:T(8,128)S(1)}, u32[]{:S(2)}, u32[]{:S(2)}) collective-permute-start(f32[16,16,128]{2,1,0:T(8,128)S(1)} %get-tuple-element.48), channel_id=1, source_target_pairs={{1,2},{3,4},{5,6},{2,1},{4,3},{6,5},{9,10},{11,12},{13,14},{10,9},... | collective-permute-start | bytes 393224 | tf_op jit(solution)/shard_map/ppermute | solution.py:716
  8.9 6.8 %collective-permute-start = (f32[8,16,128]{2,1,0:T(8,128)S(1)}, f32[8,16,128]{2,1,0:T(8,128)S(1)}, u32[]{:S(2)}, u32[]{:S(2)}) collective-permute-start(f32[8,16,128]{2,1,0:T(8,128)S(1)} %get-tuple-element.45), channel_id=1, source_target_pairs={{0,8},{16,24},{8,0},{24,16},{1,9},{17,25},{9,1},{25,17},{2,10},{18... | collective-permute-start | bytes 196616 | tf_op jit(solution)/shard_map/ppermute | solution.py:716
  9.2 6.5 %collective-permute-start.1 = (f32[8,16,128]{2,1,0:T(8,128)S(1)}, f32[8,16,128]{2,1,0:T(8,128)S(1)}, u32[]{:S(2)}, u32[]{:S(2)}) collective-permute-start(f32[8,16,128]{2,1,0:T(8,128)S(1)} %get-tuple-element.46), channel_id=1, source_target_pairs={{8,16},{16,8},{9,17},{17,9},{10,18},{18,10},{11,19},{19,11},{12,20... | collective-permute-start | bytes 196616 | tf_op jit(solution)/shard_map/ppermute | solution.py:716
  16.4 10.5 %collective-permute-start.6 = (f32[16,16,128]{2,1,0:T(8,128)S(1)}, f32[16,16,128]{2,1,0:T(8,128)S(1)}, u32[]{:S(2)}, u32[]{:S(2)}) collective-permute-start(f32[16,16,128]{2,1,0:T(8,128)S(1)} %get-tuple-element.53), channel_id=1, source_target_pairs={{0,1},{2,3},{4,5},{6,7},{1,0},{3,2},{5,4},{7,6},{8,9},{10,11},{12,... | collective-permute-start | bytes 393224 | tf_op jit(solution)/shard_map/ppermute | solution.py:716
  16.5 10.4 %collective-permute-start.7 = (f32[16,16,128]{2,1,0:T(8,128)S(1)}, f32[16,16,128]{2,1,0:T(8,128)S(1)}, u32[]{:S(2)}, u32[]{:S(2)}) collective-permute-start(f32[16,16,128]{2,1,0:T(8,128)S(1)} %get-tuple-element.54), channel_id=1, source_target_pairs={{1,2},{3,4},{5,6},{2,1},{4,3},{6,5},{9,10},{11,12},{13,14},{10,9},... | collective-permute-start | bytes 393224 | tf_op jit(solution)/shard_map/ppermute | solution.py:716
  20.8 6.1 %collective-permute-start.4 = (f32[8,16,128]{2,1,0:T(8,128)S(1)}, f32[8,16,128]{2,1,0:T(8,128)S(1)}, u32[]{:S(2)}, u32[]{:S(2)}) collective-permute-start(f32[8,16,128]{2,1,0:T(8,128)S(1)} %get-tuple-element.51), channel_id=1, source_target_pairs={{0,8},{16,24},{8,0},{24,16},{1,9},{17,25},{9,1},{25,17},{2,10},{18... | collective-permute-start | bytes 196616 | tf_op jit(solution)/shard_map/ppermute | solution.py:716
  20.8 6.0 %collective-permute-start.5 = (f32[8,16,128]{2,1,0:T(8,128)S(1)}, f32[8,16,128]{2,1,0:T(8,128)S(1)}, u32[]{:S(2)}, u32[]{:S(2)}) collective-permute-start(f32[8,16,128]{2,1,0:T(8,128)S(1)} %get-tuple-element.52), channel_id=1, source_target_pairs={{8,16},{16,8},{9,17},{17,9},{10,18},{18,10},{11,19},{19,11},{12,20... | collective-permute-start | bytes 196616 | tf_op jit(solution)/shard_map/ppermute | solution.py:716
  28.9 11.4 %all-to-all-start = ((f32[32,5,2,128]{3,2,1,0:T(2,128)}), f32[32,5,2,128]{3,2,1,0:T(2,128)S(1)}, u32[]{:S(2)}, u32[]{:S(2)}) async-start(f32[32,5,2,128]{3,2,1,0:T(2,128)} %bitcast.9), calls=%async_computation | async-start | bytes 327680 | tf_op jit(solution)/shard_map/all_to_all | solution.py:899
  33.1 13.4 %collective-permute-start.8 = (f32[576,128]{1,0:T(8,128)S(1)}, f32[576,128]{1,0:T(8,128)S(1)}, u32[]{:S(2)}, u32[]{:S(2)}) collective-permute-start(f32[576,128]{1,0:T(8,128)S(1)} %get-tuple-element.68), channel_id=1, source_target_pairs={{0,1},{2,3},{4,5},{6,7},{1,0},{3,2},{5,4},{7,6},{8,9},{10,11},{12,... | collective-permute-start | bytes 884744 | tf_op jit(solution)/shard_map/ppermute | solution.py:716
  34.3 15.0 %collective-permute-start.9 = (f32[576,128]{1,0:T(8,128)S(1)}, f32[576,128]{1,0:T(8,128)S(1)}, u32[]{:S(2)}, u32[]{:S(2)}) collective-permute-start(f32[576,128]{1,0:T(8,128)S(1)} %get-tuple-element.69), channel_id=1, source_target_pairs={{1,2},{3,4},{5,6},{2,1},{4,3},{6,5},{9,10},{11,12},{13,14},{10,9},... | collective-permute-start | bytes 884744 | tf_op jit(solution)/shard_map/ppermute | solution.py:716
  42.2 16.3 %all-to-all-start.1 = ((f32[32,16,128]{2,1,0:T(8,128)}), f32[32,16,128]{2,1,0:T(8,128)S(1)}, u32[]{:S(2)}, u32[]{:S(2)}) async-start(f32[32,16,128]{2,1,0:T(8,128)} %shard_map.137), calls=%async_computation.1 | async-start | bytes 524288 | tf_op jit(solution)/shard_map/all_to_all | solution.py:907
  49.9 11.1 %collective-permute-start.10 = (f32[424,128]{1,0:T(8,128)S(1)}, f32[424,128]{1,0:T(8,128)S(1)}, u32[]{:S(2)}, u32[]{:S(2)}) collective-permute-start(f32[424,128]{1,0:T(8,128)S(1)} %get-tuple-element.74), channel_id=1, source_target_pairs={{0,8},{16,24},{8,0},{24,16},{1,9},{17,25},{9,1},{25,17},{2,10},{18... | collective-permute-start | bytes 651272 | tf_op jit(solution)/shard_map/ppermute | solution.py:716
  50.3 10.7 %collective-permute-start.11 = (f32[320,128]{1,0:T(8,128)S(1)}, f32[320,128]{1,0:T(8,128)S(1)}, u32[]{:S(2)}, u32[]{:S(2)}) collective-permute-start(f32[320,128]{1,0:T(8,128)S(1)} %get-tuple-element.75), channel_id=1, source_target_pairs={{8,16},{16,8},{9,17},{17,9},{10,18},{18,10},{11,19},{19,11},{12,20... | collective-permute-start | bytes 491528 | tf_op jit(solution)/shard_map/ppermute | solution.py:716

commit v9 on v6

--- a/solution.py
+++ b/solution.py
@@ -478,7 +478,7 @@
 
     inmost = range(2, wide - 2)
     copies = planes_copied(
-        [inmost[at : at + 4] for at in range(0, len(inmost), 4)], ready, out, semaphores
+        [inmost[at : at + 6] for at in range(0, len(inmost), 6)], ready, out, semaphores
     )
 
     def emit_last(x, plane):
@@ -496,7 +496,7 @@
         return inner[at, 1 : deep + 1]
 
     planes_advanced(
-        range(1, wide - 1),
+        [*inmost, 1, wide - 2],
         lambda x: inner[x, 1 : deep + 1],
         last_beside,
         lambda x, side: inner[x, 2 * side : 2 * side + deep],

time: 63.4 us -> 63.4 us (level)
  no operation moved by 1% of the time
where the time goes in v9:
time: 63.4 us; the launch traced here: 62.9 us
  starting transfers between devices  37 us (58%)
  Pallas kernels  20.8 us (33%)
  waiting for transfers between devices  4.15 us (7%)
  between operations  0.89 us (1%)
    ppermute x12, starting transfers between devices, swapped(): got.append(lax.ppermute(face, axes, couples + [(b, a) for a, b in couples]))  29.4 us
    all_to_all x1, starting transfers between devices, body(): got = lax.all_to_all(sent, EVERY, 0, 0, tiled=True)  4.26 us
    all_to_all x1, starting transfers between devices, body(): lax.all_to_all(sent.reshape(devices, (deep + 2) // 2, 2, 128), EVERY, 0,...  3.42 us
    pallas_call x1, Pallas kernels, body(): vmem_call(functools.partial(third_step_kernel, shape, (rows, columns)), [...  3.03 us
    pallas_call x2, Pallas kernels, with_fetches(): call(given, *(pltpu.with_memory_space_constraint(array, pltpu.HBM) for ar...  2.8 us
    ppermute x12, waiting for transfers between devices, swapped(): got.append(lax.ppermute(face, axes, couples + [(b, a) for a, b in couples]))  2.71 us
    pallas_call x1, Pallas kernels, body(): vmem_call(functools.partial(expand_kernel, shape, (ranks_a, ranks_d), own...  2.43 us
    pallas_call x2, Pallas kernels, body(): block(field, *fixed)  2.2 us
  transfers between devices with their start and end apart: 14, of which 3 were waited for; matrix products, arithmetic and copies ran while one was open for 0% of the time, Pallas kernels for 23%

profile of v9, /device:TPU:3, one launch (start us, length us, event | category | flops | bytes accessed | tf_op | source)
XLA Modules:
  0.0 62.9 jit_solution(9122783392686291026)
XLA Ops:
  0.7 1.8 %shard_map.132 = (f32[8,16,128]{2,1,0:T(8,128)S(1)}, f32[8,16,128]{2,1,0:T(8,128)S(1)}, f32[16,16,128]{2,1,0:T(8,128)S(1)}, f32[16,16,128]{2,1,0:T(8,128)S(1)}) custom-call(s32[4]{0:T(128)S(1)} %pad_add_fusion.own_ref.refs_0_, f32[16,16,8,128]{3,2,1,0:T(8,128)} %given.3), custom_call_target="tpu_custom_call" | custom-call | tf_op jit(solution)/shard_map/pallas_call | solution.py:828
  2.6 1.4 %collective-permute-start.2 = (f32[16,16,128]{2,1,0:T(8,128)S(1)}, f32[16,16,128]{2,1,0:T(8,128)S(1)}, u32[]{:S(2)}, u32[]{:S(2)}) collective-permute-start(f32[16,16,128]{2,1,0:T(8,128)S(1)} %get-tuple-element.43), channel_id=1, source_target_pairs={{0,1},{2,3},{4,5},{6,7},{1,0},{3,2},{5,4},{7,6},{8,9},{10,11},{12,... | collective-permute-start | bytes 393224 | tf_op jit(solution)/shard_map/ppermute | solution.py:713
  3.9 4.9 %collective-permute-start.3 = (f32[16,16,128]{2,1,0:T(8,128)S(1)}, f32[16,16,128]{2,1,0:T(8,128)S(1)}, u32[]{:S(2)}, u32[]{:S(2)}) collective-permute-start(f32[16,16,128]{2,1,0:T(8,128)S(1)} %get-tuple-element.44), channel_id=1, source_target_pairs={{1,2},{3,4},{5,6},{2,1},{4,3},{6,5},{9,10},{11,12},{13,14},{10,9},... | collective-permute-start | bytes 393224 | tf_op jit(solution)/shard_map/ppermute | solution.py:713
  9.2 4.1 %collective-permute-start.1 = (f32[8,16,128]{2,1,0:T(8,128)S(1)}, f32[8,16,128]{2,1,0:T(8,128)S(1)}, u32[]{:S(2)}, u32[]{:S(2)}) collective-permute-start(f32[8,16,128]{2,1,0:T(8,128)S(1)} %get-tuple-element.42), channel_id=1, source_target_pairs={{8,16},{16,8},{9,17},{17,9},{10,18},{18,10},{11,19},{19,11},{12,20... | collective-permute-start | bytes 196616 | tf_op jit(solution)/shard_map/ppermute | solution.py:713
  13.3 1.3 %shard_map.130 = (f32[16,8,16,128]{3,2,1,0:T(8,128)S(1)}, f32[16,8,16,128]{3,2,1,0:T(8,128)S(1)}, f32[4,16,8,128]{3,2,1,0:T(8,128)S(1)}, f32[3,16,128]{2,1,0:T(8,128)S(1)}, f32[16,128]{1,0:T(8,128)S(1)}) custom-call(f32[16,16,8,128]{3,2,1,0:T(8,128)S(1)} %copy-done, f32[3,16,8,128]{3,2,1,0:T(8,128)} %refs_0_.1, f32[16,8,128]{2,1,0:T(8,128)} %refs_1_.1, ...), custom_call_target="tpu_custom_call" | custom-call | flops 1048576 | bytes 3145728 | tf_op jit(solution)/shard_map/pallas_call | solution.py:839
  14.5 1.1 %shard_map.131.refs_1_ = f32[16,8,16,128]{3,2,1,0:T(8,128)S(1)} custom-call(f32[16,8,16,128]{3,2,1,0:T(8,128)S(1)} %get-tuple-element.36.field, f32[16,8,16,128]{3,2,1,0:T(8,128)S(1)} %get-tuple-element.37.refs_0_, f32[4,16,8,128]{3,2,1,0:T(8,128)S(1)} %get-tuple-element.38.refs_1_.refs_6_.refs_0_.flow, ...), custom_call_target="tpu_custom_call" | custom-call | flops 15728640 | bytes 2097152 | tf_op jit(solution)/shard_map/pallas_call | solution.py:867
  16.4 4.3 %collective-permute-start.7 = (f32[16,16,128]{2,1,0:T(8,128)S(1)}, f32[16,16,128]{2,1,0:T(8,128)S(1)}, u32[]{:S(2)}, u32[]{:S(2)}) collective-permute-start(f32[16,16,128]{2,1,0:T(8,128)S(1)} %get-tuple-element.50), channel_id=1, source_target_pairs={{1,2},{3,4},{5,6},{2,1},{4,3},{6,5},{9,10},{11,12},{13,14},{10,9},... | collective-permute-start | bytes 393224 | tf_op jit(solution)/shard_map/ppermute | solution.py:713
  20.8 4.1 %collective-permute-start.5 = (f32[8,16,128]{2,1,0:T(8,128)S(1)}, f32[8,16,128]{2,1,0:T(8,128)S(1)}, u32[]{:S(2)}, u32[]{:S(2)}) collective-permute-start(f32[8,16,128]{2,1,0:T(8,128)S(1)} %get-tuple-element.48), channel_id=1, source_target_pairs={{8,16},{16,8},{9,17},{17,9},{10,18},{18,10},{11,19},{19,11},{12,20... | collective-permute-start | bytes 196616 | tf_op jit(solution)/shard_map/ppermute | solution.py:713
  24.9 1.5 %shard_map.136 = (f32[128,256]{1,0:T(8,128)S(1)}, f32[16,128]{1,0:T(8,128)S(1)}, f32[32,128]{1,0:T(8,128)S(1)}, f32[2,128]{1,0:T(2,128)S(1)}) custom-call(s32[4]{0:T(128)S(1)} %pad_add_fusion.own_ref.refs_0_, f32[8,16]{1,0:T(8,128)} %bitcast.16, f32[32,128]{1,0:T(8,128)} %bitcast.15, f32[16,64]{1,0:T(8,128)} %refs_2_.1, f32[8,64]{1,0:T(8,128)} %refs_3_.1), custom_call_target="tpu_custom_call" | custom-call | tf_op jit(solution)/shard_map/pallas_call | solution.py:839
  26.5 1.1 %shard_map.134.refs_1_ = f32[16,8,16,128]{3,2,1,0:T(8,128)S(1)} custom-call(f32[16,8,16,128]{3,2,1,0:T(8,128)S(1)} %get-tuple-element.45.field, f32[16,8,16,128]{3,2,1,0:T(8,128)S(1)} %get-tuple-element.37.refs_0_, f32[4,16,8,128]{3,2,1,0:T(8,128)S(1)} %get-tuple-element.38.refs_1_.refs_6_.refs_0_.flow, ...), custom_call_target="tpu_custom_call" | custom-call | flops 15728640 | bytes 2097152 | tf_op jit(solution)/shard_map/pallas_call | solution.py:875
  27.7 0.7 %shard_map.135 = (f32[16,8,16,128]{3,2,1,0:T(8,128)S(1)}, f32[576,128]{1,0:T(8,128)S(1)}, f32[576,128]{1,0:T(8,128)S(1)}) custom-call(s32[4]{0:T(128)S(1)} %pad_add_fusion.own_ref.refs_0_, f32[16,8,16,128]{3,2,1,0:T(8,128)S(1)} %shard_map.134.refs_1_, f32[8,16,128]{2,1,0:T(8,128)S(1)} %collective-permute-done.4.refs_2_, ...), custom_call_target="tpu_custom_call" | custom-call | flops 1048576 | bytes 2097152 | tf_op jit(solution)/shard_map/pallas_call | solution.py:872
  28.4 1.4 %shard_map.137 = f32[320,128]{1,0:T(8,128)} custom-call(f32[16,8,16,128]{3,2,1,0:T(8,128)S(1)} %get-tuple-element.59.field, f32[128,256]{1,0:T(8,128)S(1)} %get-tuple-element.52.component, f32[32,128]{1,0:T(8,128)S(1)} %get-tuple-element.53.vertical, f32[2,128]{1,0:T(2,128)S(1)} %get-tuple-element.54.factor_rows), custom_call_target="tpu_custom_call" | custom-call | flops 15728640 | bytes 1048576 | tf_op jit(solution)/shard_map/pallas_call | solution.py:891
  29.7 3.4 %all-to-all-start = ((f32[32,5,2,128]{3,2,1,0:T(2,128)}), f32[32,5,2,128]{3,2,1,0:T(2,128)S(1)}, u32[]{:S(2)}, u32[]{:S(2)}) async-start(f32[32,5,2,128]{3,2,1,0:T(2,128)} %bitcast.9), calls=%async_computation | async-start | bytes 327680 | tf_op jit(solution)/shard_map/all_to_all | solution.py:895
  33.2 1.3 %collective-permute-start.8 = (f32[576,128]{1,0:T(8,128)S(1)}, f32[576,128]{1,0:T(8,128)S(1)}, u32[]{:S(2)}, u32[]{:S(2)}) collective-permute-start(f32[576,128]{1,0:T(8,128)S(1)} %get-tuple-element.60), channel_id=1, source_target_pairs={{0,1},{2,3},{4,5},{6,7},{1,0},{3,2},{5,4},{7,6},{8,9},{10,11},{12,... | collective-permute-start | bytes 884744 | tf_op jit(solution)/shard_map/ppermute | solution.py:713
  34.4 4.5 %collective-permute-start.9 = (f32[576,128]{1,0:T(8,128)S(1)}, f32[576,128]{1,0:T(8,128)S(1)}, u32[]{:S(2)}, u32[]{:S(2)}) collective-permute-start(f32[576,128]{1,0:T(8,128)S(1)} %get-tuple-element.61), channel_id=1, source_target_pairs={{1,2},{3,4},{5,6},{2,1},{4,3},{6,5},{9,10},{11,12},{13,14},{10,9},... | collective-permute-start | bytes 884744 | tf_op jit(solution)/shard_map/ppermute | solution.py:713
  38.9 1.4 %all-to-all-done = f32[32,5,2,128]{3,2,1,0:T(2,128)S(1)} async-done(((f32[32,5,2,128]{3,2,1,0:T(2,128)}), f32[32,5,2,128]{3,2,1,0:T(2,128)S(1)}, u32[]{:S(2)}, u32[]{:S(2)}) %all-to-all-start) | async-done | bytes 163872 | tf_op jit(solution)/shard_map/all_to_all | solution.py:895
  40.4 2.2 %shard_map.138 = f32[32,16,128]{2,1,0:T(8,128)} custom-call(f32[320,128]{1,0:T(8,128)S(1)} %bitcast.14), custom_call_target="tpu_custom_call" | custom-call | flops 15728640 | bytes 1048576 | tf_op jit(solution)/shard_map/pallas_call | solution.py:898
  42.5 4.3 %all-to-all-start.1 = ((f32[32,16,128]{2,1,0:T(8,128)}), f32[32,16,128]{2,1,0:T(8,128)S(1)}, u32[]{:S(2)}, u32[]{:S(2)}) async-start(f32[32,16,128]{2,1,0:T(8,128)} %shard_map.138), calls=%async_computation.1 | async-start | bytes 524288 | tf_op jit(solution)/shard_map/all_to_all | solution.py:903
  46.8 2.6 %collective-permute-done.9.y_other = f32[576,128]{1,0:T(8,128)S(1)} collective-permute-done((f32[576,128]{1,0:T(8,128)S(1)}, f32[576,128]{1,0:T(8,128)S(1)}, u32[]{:S(2)}, u32[]{:S(2)}) %collective-permute-start.9) | collective-permute-done | bytes 294944 | tf_op jit(solution)/shard_map/ppermute | solution.py:713
  50.3 4.0 %collective-permute-start.11 = (f32[320,128]{1,0:T(8,128)S(1)}, f32[320,128]{1,0:T(8,128)S(1)}, u32[]{:S(2)}, u32[]{:S(2)}) collective-permute-start(f32[320,128]{1,0:T(8,128)S(1)} %get-tuple-element.67), channel_id=1, source_target_pairs={{8,16},{16,8},{9,17},{17,9},{10,18},{18,10},{11,19},{19,11},{12,20... | collective-permute-start | bytes 491528 | tf_op jit(solution)/shard_map/ppermute | solution.py:713
  54.4 1.2 %shard_map.140.block = f32[16,8,16,128]{3,2,1,0:T(8,128)S(1)} custom-call(f32[16,8,16,128]{3,2,1,0:T(8,128)S(1)} %get-tuple-element.59.field, f32[4,16,8,128]{3,2,1,0:T(8,128)S(1)} %get-tuple-element.38.refs_1_.refs_6_.refs_0_.flow, f32[3,16,128]{2,1,0:T(8,128)S(1)} %get-tuple-element.39.refs_2_.refs_7_.refs_1_.coefficients, ...), custom_call_target="tpu_custom_call" | custom-call | flops 15728640 | bytes 2097152 | tf_op jit(solution)/shard_map/pallas_call | solution.py:923
  55.6 3.0 %shard_map.141 = (f32[4,10,16,128]{3,2,1,0:T(8,128)S(1)}, f32[2,2,8,128]{3,2,1,0:T(8,128)S(1)}, f32[2,8,16,128]{3,2,1,0:T(8,128)S(1)}, f32[16,16,8,128]{3,2,1,0:T(8,128)}) custom-call(s32[4]{0:T(128)S(1)} %pad_add_fusion.own_ref.refs_0_, f32[16,8,16,128]{3,2,1,0:T(8,128)S(1)} %shard_map.140.block, f32[16,8,16,128]{3,2,1,0:T(8,128)S(1)} %get-tuple-element.59.field, ...), custom_call_target="tpu_custom_call" | custom-call | flops 31457280 | bytes 4194304 | tf_op jit(solution)/shard_map/pallas_call | solution.py:930
  58.6 2.4 %shard_map.139 = (f32[16,16,8,128]{3,2,1,0:T(8,128)}, f32[128,8,32]{2,1,0:T(8,128)}) custom-call(f32[512,128]{1,0:T(8,128)S(1)} %bitcast.13, f32[16,8,16,128]{3,2,1,0:T(8,128)S(1)} %get-tuple-element.59.field, f32[16,128]{1,0:T(8,128)S(1)} %get-tuple-element.56.wide_rows, f32[32,128]{1,0:T(8,128)S(1)} %get-tuple-element.53.vertical), custom_call_target="tpu_custom_call" | custom-call | flops 15728640 | bytes 2097152 | tf_op jit(solution)/shard_map/pallas_call | solution.py:904
  61.2 1.8 %shard_map.143 = f32[16,16,8,128]{3,2,1,0:T(8,128)} custom-call(s32[4]{0:T(128)S(1)} %pad_add_fusion.own_ref.refs_0_, f32[4,10,16,128]{3,2,1,0:T(8,128)S(1)} %get-tuple-element.62.edges, f32[2,2,8,128]{3,2,1,0:T(8,128)S(1)} %get-tuple-element.63.ends, f32[2,8,16,128]{3,2,1,0:T(8,128)S(1)} %get-tuple-element.64.nearly, ...), custom_call_target="tpu_custom_call", output_to_operand_aliasing={{}: (4, {})} | custom-call | flops 15728640 | bytes 2097152 | tf_op jit(solution)/shard_map/pallas_call | solution.py:941
  (21 shorter events, 2.3 us)
Async XLA Ops:
  0.6 12.6 %copy-start = (f32[16,16,8,128]{3,2,1,0:T(8,128)S(1)}, f32[16,16,8,128]{3,2,1,0:T(8,128)}, u32[]{:S(2)}) copy-start(f32[16,16,8,128]{3,2,1,0:T(8,128)} %given.3) | copy-start | bytes 3145732
  2.6 13.1 %collective-permute-start.2 = (f32[16,16,128]{2,1,0:T(8,128)S(1)}, f32[16,16,128]{2,1,0:T(8,128)S(1)}, u32[]{:S(2)}, u32[]{:S(2)}) collective-permute-start(f32[16,16,128]{2,1,0:T(8,128)S(1)} %get-tuple-element.43), channel_id=1, source_target_pairs={{0,1},{2,3},{4,5},{6,7},{1,0},{3,2},{5,4},{7,6},{8,9},{10,11},{12,... | collective-permute-start | bytes 393224 | tf_op jit(solution)/shard_map/ppermute | solution.py:713
  3.9 11.7 %collective-permute-start.3 = (f32[16,16,128]{2,1,0:T(8,128)S(1)}, f32[16,16,128]{2,1,0:T(8,128)S(1)}, u32[]{:S(2)}, u32[]{:S(2)}) collective-permute-start(f32[16,16,128]{2,1,0:T(8,128)S(1)} %get-tuple-element.44), channel_id=1, source_target_pairs={{1,2},{3,4},{5,6},{2,1},{4,3},{6,5},{9,10},{11,12},{13,14},{10,9},... | collective-permute-start | bytes 393224 | tf_op jit(solution)/shard_map/ppermute | solution.py:713
  8.9 6.7 %collective-permute-start = (f32[8,16,128]{2,1,0:T(8,128)S(1)}, f32[8,16,128]{2,1,0:T(8,128)S(1)}, u32[]{:S(2)}, u32[]{:S(2)}) collective-permute-start(f32[8,16,128]{2,1,0:T(8,128)S(1)} %get-tuple-element.41), channel_id=1, source_target_pairs={{0,8},{16,24},{8,0},{24,16},{1,9},{17,25},{9,1},{25,17},{2,10},{18... | collective-permute-start | bytes 196616 | tf_op jit(solution)/shard_map/ppermute | solution.py:713
  9.2 6.4 %collective-permute-start.1 = (f32[8,16,128]{2,1,0:T(8,128)S(1)}, f32[8,16,128]{2,1,0:T(8,128)S(1)}, u32[]{:S(2)}, u32[]{:S(2)}) collective-permute-start(f32[8,16,128]{2,1,0:T(8,128)S(1)} %get-tuple-element.42), channel_id=1, source_target_pairs={{8,16},{16,8},{9,17},{17,9},{10,18},{18,10},{11,19},{19,11},{12,20... | collective-permute-start | bytes 196616 | tf_op jit(solution)/shard_map/ppermute | solution.py:713
  16.3 11.3 %collective-permute-start.6 = (f32[16,16,128]{2,1,0:T(8,128)S(1)}, f32[16,16,128]{2,1,0:T(8,128)S(1)}, u32[]{:S(2)}, u32[]{:S(2)}) collective-permute-start(f32[16,16,128]{2,1,0:T(8,128)S(1)} %get-tuple-element.49), channel_id=1, source_target_pairs={{0,1},{2,3},{4,5},{6,7},{1,0},{3,2},{5,4},{7,6},{8,9},{10,11},{12,... | collective-permute-start | bytes 393224 | tf_op jit(solution)/shard_map/ppermute | solution.py:713
  16.4 11.2 %collective-permute-start.7 = (f32[16,16,128]{2,1,0:T(8,128)S(1)}, f32[16,16,128]{2,1,0:T(8,128)S(1)}, u32[]{:S(2)}, u32[]{:S(2)}) collective-permute-start(f32[16,16,128]{2,1,0:T(8,128)S(1)} %get-tuple-element.50), channel_id=1, source_target_pairs={{1,2},{3,4},{5,6},{2,1},{4,3},{6,5},{9,10},{11,12},{13,14},{10,9},... | collective-permute-start | bytes 393224 | tf_op jit(solution)/shard_map/ppermute | solution.py:713
  20.8 6.9 %collective-permute-start.4 = (f32[8,16,128]{2,1,0:T(8,128)S(1)}, f32[8,16,128]{2,1,0:T(8,128)S(1)}, u32[]{:S(2)}, u32[]{:S(2)}) collective-permute-start(f32[8,16,128]{2,1,0:T(8,128)S(1)} %get-tuple-element.47), channel_id=1, source_target_pairs={{0,8},{16,24},{8,0},{24,16},{1,9},{17,25},{9,1},{25,17},{2,10},{18... | collective-permute-start | bytes 196616 | tf_op jit(solution)/shard_map/ppermute | solution.py:713
  20.8 6.8 %collective-permute-start.5 = (f32[8,16,128]{2,1,0:T(8,128)S(1)}, f32[8,16,128]{2,1,0:T(8,128)S(1)}, u32[]{:S(2)}, u32[]{:S(2)}) collective-permute-start(f32[8,16,128]{2,1,0:T(8,128)S(1)} %get-tuple-element.48), channel_id=1, source_target_pairs={{8,16},{16,8},{9,17},{17,9},{10,18},{18,10},{11,19},{19,11},{12,20... | collective-permute-start | bytes 196616 | tf_op jit(solution)/shard_map/ppermute | solution.py:713
  29.7 10.6 %all-to-all-start = ((f32[32,5,2,128]{3,2,1,0:T(2,128)}), f32[32,5,2,128]{3,2,1,0:T(2,128)S(1)}, u32[]{:S(2)}, u32[]{:S(2)}) async-start(f32[32,5,2,128]{3,2,1,0:T(2,128)} %bitcast.9), calls=%async_computation | async-start | bytes 327680 | tf_op jit(solution)/shard_map/all_to_all | solution.py:895
  33.2 13.7 %collective-permute-start.8 = (f32[576,128]{1,0:T(8,128)S(1)}, f32[576,128]{1,0:T(8,128)S(1)}, u32[]{:S(2)}, u32[]{:S(2)}) collective-permute-start(f32[576,128]{1,0:T(8,128)S(1)} %get-tuple-element.60), channel_id=1, source_target_pairs={{0,1},{2,3},{4,5},{6,7},{1,0},{3,2},{5,4},{7,6},{8,9},{10,11},{12,... | collective-permute-start | bytes 884744 | tf_op jit(solution)/shard_map/ppermute | solution.py:713
  34.4 15.0 %collective-permute-start.9 = (f32[576,128]{1,0:T(8,128)S(1)}, f32[576,128]{1,0:T(8,128)S(1)}, u32[]{:S(2)}, u32[]{:S(2)}) collective-permute-start(f32[576,128]{1,0:T(8,128)S(1)} %get-tuple-element.61), channel_id=1, source_target_pairs={{1,2},{3,4},{5,6},{2,1},{4,3},{6,5},{9,10},{11,12},{13,14},{10,9},... | collective-permute-start | bytes 884744 | tf_op jit(solution)/shard_map/ppermute | solution.py:713
  42.5 16.1 %all-to-all-start.1 = ((f32[32,16,128]{2,1,0:T(8,128)}), f32[32,16,128]{2,1,0:T(8,128)S(1)}, u32[]{:S(2)}, u32[]{:S(2)}) async-start(f32[32,16,128]{2,1,0:T(8,128)} %shard_map.138), calls=%async_computation.1 | async-start | bytes 524288 | tf_op jit(solution)/shard_map/all_to_all | solution.py:903
  50.0 11.2 %collective-permute-start.10 = (f32[424,128]{1,0:T(8,128)S(1)}, f32[424,128]{1,0:T(8,128)S(1)}, u32[]{:S(2)}, u32[]{:S(2)}) collective-permute-start(f32[424,128]{1,0:T(8,128)S(1)} %get-tuple-element.66), channel_id=1, source_target_pairs={{0,8},{16,24},{8,0},{24,16},{1,9},{17,25},{9,1},{25,17},{2,10},{18... | collective-permute-start | bytes 651272 | tf_op jit(solution)/shard_map/ppermute | solution.py:713
  50.3 10.8 %collective-permute-start.11 = (f32[320,128]{1,0:T(8,128)S(1)}, f32[320,128]{1,0:T(8,128)S(1)}, u32[]{:S(2)}, u32[]{:S(2)}) collective-permute-start(f32[320,128]{1,0:T(8,128)S(1)} %get-tuple-element.67), channel_id=1, source_target_pairs={{8,16},{16,8},{9,17},{17,9},{10,18},{18,10},{11,19},{19,11},{12,20... | collective-permute-start | bytes 491528 | tf_op jit(solution)/shard_map/ppermute | solution.py:713
